TPU v7x, 128 devices: a whole 4x4x4 slice. The times are simulated.
128 devices in a mesh: dp: 4 (over z), seq: 32 (over y, x, core).
Axes of the slice: x: 4, y: 4, z: 4, core: 2. Of those that a mesh axis runs over, the one named last changes fastest.
Arguments:
- hidden: bfloat16 [4, 8192, 1536], P('dp', 'seq'), may hold values from -6 to 6
- cotangent: bfloat16 [4, 8192, 1536], P('dp', 'seq'), may hold values from -6 to 6
- in_w: bfloat16 [1536, 6448], P(('dp', 'seq')), may hold values from -0.15625 to 0.15625
- out_w: bfloat16 [3072, 1536], P(('dp', 'seq')), may hold values from -0.109375 to 0.109375
- conv_w: bfloat16 [4, 3328], P(None, ('dp', 'seq')), may hold values from -3 to 3
- conv_b: bfloat16 [3328], P(('dp', 'seq')), may hold values from -0.5 to 0.5
- norm_gain: bfloat16 [1536], P(('dp', 'seq')), may hold values from 0.5 to 1.5
- gate_gain: bfloat16 [3072], P(('dp', 'seq')), may hold values from 0.5 to 1.5
- dt_bias: float32 [48], replicated, may hold values from -4 to -1
- decay_rates: float32 [48], replicated, may hold values from 3.6621095e-05 to 0.2
- d_skip: float32 [48], replicated, may hold values from 0.5 to 1.5
Outputs:
- out: bfloat16 [4, 8192, 1536], P('dp', 'seq')
- d_hidden: float32 [4, 8192, 1536], P('dp', 'seq')
- d_in_w: float32 [1536, 6448], P(('dp', 'seq'))
- d_out_w: float32 [3072, 1536], P(('dp', 'seq'))
- d_conv_w: float32 [4, 3328], P(None, ('dp', 'seq'))
- d_conv_b: float32 [3328], P(('dp', 'seq'))
- d_norm_gain: float32 [1536], P(('dp', 'seq'))
- d_gate_gain: float32 [3072], P(('dp', 'seq'))
- d_dt_bias: float32 [48], replicated
- d_decay_rates: float32 [48], replicated
- d_d_skip: float32 [48], replicated
All inputs are finite; a program needn't handle non-finite values.
Results may differ from a plain program's by a relative error of at most 0.017.
Values may be sent and summed in bfloat16 or wider, within the bound.
A program may use at most 320 MiB of HBM per device.

v0:
```python
import jax
import jax.numpy as jnp
from jax import lax
from jax.sharding import PartitionSpec as P

H = 48
P_SIZE = 64
NS = 128
KW = 4
SPAN = 256
DI = 3072
CONVC = 3328


epsilon = 1e-05
highest = lax.Precision.HIGHEST


def from_behind(value, axis, steps):
    count = lax.axis_size(axis)
    first, last = (max(0, -steps), min(count, count - steps))
    return lax.ppermute(value, axis, [(source, source + steps) for source in range(first, last)])


def carried_in(value, axis, join, neutral, backward):
    count, mine = (lax.axis_size(axis), lax.axis_index(axis))
    pieces = jax.tree.map(lambda part: lax.all_gather(part, axis), value)
    if backward:
        pieces = jax.tree.map(lambda part: part[::-1], pieces)
        mine = count - 1 - mine
    so_far = jax.tree.map(
        lambda part, zero: jnp.full_like(part, 0) + jnp.asarray(zero, part.dtype), value, neutral
    )

    def lap(position, so_far):
        longer = join(so_far, jax.tree.map(lambda part: part[position], pieces))
        return jax.tree.map(lambda new, old: jnp.where(position < mine, new, old), longer, so_far)

    return lax.fori_loop(0, count - 1, lap, so_far)


def rms_scale(values, gain):
    return values * lax.rsqrt(jnp.mean(values * values, axis=-1, keepdims=True) + epsilon) * gain


def span_step(carry_state, heads_x, b_in, c_out, steps_dt, neg_rate):
    block_len = heads_x.shape[0]
    log_decay = steps_dt * neg_rate[None, :]
    cum_decay = jnp.cumsum(log_decay, axis=0)
    position = jnp.arange(block_len)
    causal = (position[:, None] >= position[None, :]).astype(jnp.float32)
    gap_decay = (
        jnp.exp((cum_decay[:, None, :] - cum_decay[None, :, :]) * causal[:, :, None])
        * causal[:, :, None]
    )
    scores = jnp.dot(c_out, b_in.T, precision=highest)
    mixing = scores[:, :, None] * gap_decay * steps_dt[None, :, :]
    within = jnp.einsum("trh,rhp->thp", mixing, heads_x, precision=highest)
    carried = jnp.exp(cum_decay)[:, :, None] * jnp.einsum(
        "tn,hpn->thp", c_out, carry_state, precision=highest
    )
    last_sum = cum_decay[-1]
    toward = jnp.exp(last_sum[None, :] - cum_decay) * steps_dt
    added_in = jnp.einsum("rh,rhp,rn->hpn", toward, heads_x, b_in, precision=highest)
    updated = jnp.exp(last_sum)[:, None, None] * carry_state + added_in
    return (updated, within + carried)


def local_core(heads_x, b_in, c_out, steps_dt, neg_rate, d_skip):
    length = heads_x.shape[0]
    blocks_n = length // SPAN
    stacked = (
        heads_x.reshape(blocks_n, SPAN, H, P_SIZE),
        b_in.reshape(blocks_n, SPAN, NS),
        c_out.reshape(blocks_n, SPAN, NS),
        steps_dt.reshape(blocks_n, SPAN, H),
    )

    def advance(carry_state, pieces):
        return span_step(carry_state, pieces[0], pieces[1], pieces[2], pieces[3], neg_rate)

    final_state, outputs = lax.scan(
        jax.checkpoint(advance), jnp.zeros((H, P_SIZE, NS), jnp.float32), stacked
    )
    cum_decay = jnp.cumsum(steps_dt * neg_rate[None, :], axis=0)
    local_out = outputs.reshape(length, H, P_SIZE) + d_skip[None, :, None] * heads_x
    return (local_out, final_state, jnp.exp(cum_decay[-1]), cum_decay)


def correction(c_out, cum_decay, incoming):
    return jnp.exp(cum_decay)[:, :, None] * jnp.einsum(
        "tn,hpn->thp", c_out, incoming, precision=highest
    )


def full_mixer(heads_x, b_in, c_out, steps_dt, neg_rate, d_skip, incoming):
    local_out, final_state, total_decay, cum_decay = local_core(
        heads_x, b_in, c_out, steps_dt, neg_rate, d_skip
    )
    return (local_out + correction(c_out, cum_decay, incoming), final_state, total_decay)


def conv_section(extended, w_conv, b_conv, dt_raw, dt_bias, decay_rates):
    length = dt_raw.shape[0]
    mixed = jnp.zeros((length, CONVC), jnp.float32) + b_conv[None, :]
    for offset in range(KW):
        mixed = mixed + w_conv[offset][None, :] * extended[offset : offset + length]
    return (jax.nn.silu(mixed), jax.nn.softplus(dt_raw + dt_bias[None, :]), -decay_rates)


def gate_section(ssd_out, gate_z, gain_gate):
    length = gate_z.shape[0]
    gated = ssd_out.reshape(length, DI) * jax.nn.silu(gate_z)
    return rms_scale(gated, gain_gate)


def forward_combine(earlier, later):
    return (earlier[0] * later[0], later[0][:, None, None] * earlier[1] + later[1])


def backward_combine(earlier, later):
    return (later[0] * earlier[0], later[1] + later[0][:, None, None] * earlier[1])


def shards(
    hidden,
    cotangent,
    in_w,
    out_w,
    conv_w,
    conv_b,
    norm_gain,
    gate_gain,
    dt_bias,
    decay_rates,
    d_skip,
):
    w_in, w_out, w_conv, b_conv, gain_norm, gain_gate = (
        lax.all_gather(in_w, ("dp", "seq"), axis=0, tiled=True),
        lax.all_gather(out_w, ("dp", "seq"), axis=0, tiled=True),
        lax.all_gather(conv_w, ("dp", "seq"), axis=1, tiled=True),
        lax.all_gather(conv_b, ("dp", "seq"), axis=0, tiled=True),
        lax.all_gather(norm_gain, ("dp", "seq"), axis=0, tiled=True),
        lax.all_gather(gate_gain, ("dp", "seq"), axis=0, tiled=True),
    )
    w_conv_f = w_conv.astype(jnp.float32)
    b_conv_f = b_conv.astype(jnp.float32)
    gain_norm_f = gain_norm.astype(jnp.float32)
    gain_gate_f = gain_gate.astype(jnp.float32)
    residual = hidden[0].astype(jnp.float32)
    length = residual.shape[0]
    normed = rms_scale(residual, gain_norm_f).astype(jnp.bfloat16)
    projected = jnp.dot(normed, w_in, preferred_element_type=jnp.float32)
    gate_z = projected[:, :DI]
    conv_in = projected[:, DI : DI + CONVC].astype(jnp.bfloat16)
    dt_raw = projected[:, DI + CONVC :]
    edge_rows = from_behind(conv_in[length - (KW - 1) :], "seq", 1)
    extended = jnp.concatenate([edge_rows, conv_in], axis=0).astype(jnp.float32)
    pre_act, steps_dt, neg_rate = conv_section(
        extended, w_conv_f, b_conv_f, dt_raw, dt_bias, decay_rates
    )
    activated = lax.optimization_barrier(pre_act.astype(jnp.bfloat16)).astype(jnp.float32)
    heads_x = activated[:, :DI].reshape(length, H, P_SIZE)
    b_in = activated[:, DI : DI + NS]
    c_out = activated[:, DI + NS :]
    local_out, final_state, total_decay, cum_decay = local_core(
        heads_x, b_in, c_out, steps_dt, neg_rate, d_skip
    )
    identity = (jnp.ones((H,), jnp.float32), jnp.zeros((H, P_SIZE, NS), jnp.float32))
    prior = carried_in((total_decay, final_state), "seq", forward_combine, identity, False)
    incoming = prior[1]
    ssd_out = local_out + correction(c_out, cum_decay, incoming)
    branch = gate_section(ssd_out, gate_z, gain_gate_f).astype(jnp.bfloat16)
    result = (residual + jnp.dot(branch, w_out, preferred_element_type=jnp.float32)).astype(
        jnp.bfloat16
    )
    w_in, w_out, w_conv, b_conv, gain_norm, gain_gate = (
        lax.all_gather(in_w, ("dp", "seq"), axis=0, tiled=True),
        lax.all_gather(out_w, ("dp", "seq"), axis=0, tiled=True),
        lax.all_gather(conv_w, ("dp", "seq"), axis=1, tiled=True),
        lax.all_gather(conv_b, ("dp", "seq"), axis=0, tiled=True),
        lax.all_gather(norm_gain, ("dp", "seq"), axis=0, tiled=True),
        lax.all_gather(gate_gain, ("dp", "seq"), axis=0, tiled=True),
    )
    w_conv_f = w_conv.astype(jnp.float32)
    b_conv_f = b_conv.astype(jnp.float32)
    gain_norm_f = gain_norm.astype(jnp.float32)
    gain_gate_f = gain_gate.astype(jnp.float32)
    grad_out = cotangent[0]
    d_branch = jnp.einsum("td,kd->tk", grad_out, w_out, preferred_element_type=jnp.float32)
    d_w_out = jnp.einsum("tk,td->kd", branch, grad_out, preferred_element_type=jnp.float32)
    gate_pull = jax.vjp(gate_section, ssd_out, gate_z, gain_gate_f)[1]
    d_ssd, d_gate_z, d_gain_gate = gate_pull(d_branch)
    d_incoming = jnp.einsum("th,thp,tn->hpn", jnp.exp(cum_decay), d_ssd, c_out, precision=highest)
    later = carried_in((total_decay, d_incoming), "seq", backward_combine, identity, True)
    carried_back = later[1]
    d_total_decay = jnp.sum(carried_back * incoming, axis=(1, 2))
    mixer_pull = jax.vjp(full_mixer, heads_x, b_in, c_out, steps_dt, neg_rate, d_skip, incoming)[1]
    d_heads_x, d_b_in, d_c_out, d_steps, d_rate, d_dskip, unused_grad = mixer_pull(
        (d_ssd, carried_back, d_total_decay)
    )
    d_act = jnp.concatenate([d_heads_x.reshape(length, DI), d_b_in, d_c_out], axis=1)
    conv_pull = jax.vjp(conv_section, extended, w_conv_f, b_conv_f, dt_raw, dt_bias, decay_rates)[1]
    d_ext, d_conv_w, d_conv_b, d_dt_raw, d_dt_bias, d_rates = conv_pull((d_act, d_steps, d_rate))
    back_rows = from_behind(d_ext[: KW - 1].astype(jnp.bfloat16), "seq", -1).astype(jnp.float32)
    d_conv_in = d_ext[KW - 1 :].at[length - (KW - 1) :].add(back_rows)
    d_projected = jnp.concatenate([d_gate_z, d_conv_in, d_dt_raw], axis=1).astype(jnp.bfloat16)
    d_normed = jnp.einsum("tj,dj->td", d_projected, w_in, preferred_element_type=jnp.float32)
    d_w_in = jnp.einsum("td,tj->dj", normed, d_projected, preferred_element_type=jnp.float32)
    norm_pull = jax.vjp(rms_scale, residual, gain_norm_f)[1]
    d_from_norm, d_gain_norm = norm_pull(d_normed)
    d_hidden = grad_out.astype(jnp.float32) + d_from_norm
    g_in, g_out, g_conv, g_bias, g_norm, g_gate = (
        lax.psum_scatter(d_w_in, ("dp", "seq"), scatter_dimension=0, tiled=True),
        lax.psum_scatter(d_w_out, ("dp", "seq"), scatter_dimension=0, tiled=True),
        lax.psum_scatter(d_conv_w, ("dp", "seq"), scatter_dimension=1, tiled=True),
        lax.psum_scatter(d_conv_b, ("dp", "seq"), scatter_dimension=0, tiled=True),
        lax.psum_scatter(d_gain_norm, ("dp", "seq"), scatter_dimension=0, tiled=True),
        lax.psum_scatter(d_gain_gate, ("dp", "seq"), scatter_dimension=0, tiled=True),
    )
    h_bias, h_rates, h_skip = lax.psum((d_dt_bias, d_rates, d_dskip), ("dp", "seq"))
    return (
        result[None],
        d_hidden[None],
        g_in,
        g_out,
        g_conv,
        g_bias,
        g_norm,
        g_gate,
        h_bias,
        h_rates,
        h_skip,
    )


def solution(mesh):
    placed = (
        P("dp", "seq", None),
        P("dp", "seq", None),
        P(("dp", "seq"), None),
        P(("dp", "seq"), None),
        P(None, ("dp", "seq")),
        P(("dp", "seq")),
        P(("dp", "seq")),
        P(("dp", "seq")),
        P(),
        P(),
        P(),
    )
    return jax.shard_map(
        shards,
        mesh=mesh,
        in_specs=placed,
        out_specs=(
            P("dp", "seq", None),
            P("dp", "seq", None),
            P(("dp", "seq"), None),
            P(("dp", "seq"), None),
            P(None, ("dp", "seq")),
            P(("dp", "seq")),
            P(("dp", "seq")),
            P(("dp", "seq")),
            P(),
            P(),
            P(),
        ),
        check_vma=False,
    )
```

profile of v0, /device:TPU:1, one launch (start us, length us, event | category | flops | bytes accessed | tf_op | source)
XLA Modules:
  0.0 1846.1 jit_solution(17709670860745395)
XLA Ops:
  11.2 69.9 %all-reduce.20 = (bf16[1536]{0:T(1024)(128)(2,1)S(1)}, bf16[3328]{0:T(1024)(128)(2,1)S(1)}, bf16[3072]{0:T(1024)(128)(2,1)}) all-reduce(bf16[1536]{0:T(1024)(128)(2,1)S(1)} %dynamic-update-slice.4, bf16[3328]{0:T(1024)(128)(2,1)S(1)} %dynamic-update-slice.3, ...), channel_id=1, replica_groups=mesh['dp'=4,'seq'=32] {'dp','seq'}, use_global_device_ids=true, to_apply=%add.11 | all-reduce | flops 7936 | bytes 31744
  81.7 33.8 %all-gather.2 = bf16[128,26,4]{1,2,0:T(4,128)(2,1)S(1)} all-gather(bf16[1,26,4]{1,2,0:T(4,128)(2,1)} %bitcast.242), channel_id=1, replica_groups=mesh['dp'=4,'seq'=32] {'dp','seq'}, dimensions={0}, use_global_device_ids=true | all-gather | bytes 26832 | tf_op jit(solution)/shard_map/all_gather | solution.py:141
  118.1 29.4 %reshape.318 = bf16[1536,6448]{1,0:T(8,128)(2,1)} reshape(bf16[128,12,6448]{2,1,0:T(8,128)(2,1)} %all-gather.16.cloned.1.call-done) | data formatting | bytes 39616512
  147.6 14.5 fusion.132
  174.2 7.0 multiply_convert_fusion
  190.1 21.5 %all-gather.4 = f32[32,1,48]{2,1,0:T(1,128)S(1)} all-gather(f32[1,1,48]{2,1,0:T(1,128)S(1)} %copy-done.67), channel_id=1, replica_groups=mesh['dp'=4,'seq'=32] {'seq'}, dimensions={0}, use_global_device_ids=true | all-gather | bytes 6336 | tf_op jit(solution)/shard_map/all_gather | solution.py:27
  219.5 122.8 %all-gather.12.cloned.1.call-done = f32[1536,64,128]{2,1,0:T(8,128)} async-done(((f32[48,64,128]{2,1,0:T(8,128)}), f32[1536,64,128]{2,1,0:T(8,128)}) %all-gather.12.cloned.1.call-update) | async-done | bytes 50331664 | tf_op jit(solution)/shard_map/all_gather | solution.py:27
  342.3 56.7 %while.19 = (s32[]{:T(128)}, f32[48,64,128]{2,1,0:T(8,128)S(1)}, s32[]{:T(128)}, f32[32,48]{1,0:T(8,128)S(1)}, f32[32,48,64,128]{3,2,1,0:T(8,128)}, /*index=5*/s32[]{:T(128)}, s32[]{:T(128)}) while((s32[]{:T(128)}, f32[48,64,128]{2,1,0:T(8,128)S(1)}, s32[]{:T(128)}, f32[32,48]{1,0:T(8,128)S(1)}, f32[32,48,64,128]{3,2,1,0:T(8,128)}, ...), condition=%wide.region_4.5_spmd.clone, body=%wide.region_3.4_spmd.clone.sunk | while | flops 1572868 | bytes 4719281 | solution.py:39
  403.2 11.6 fusion.37
  414.8 5.8 multiply_reduce_fusion.11
  420.7 8.5 multiply_reduce_fusion.7
  429.2 5.3 multiply_reduce_fusion.6
  434.5 3.7 fusion.48
  444.6 4.9 fusion.77
  449.6 145.4 %all-gather.14.cloned.1.call-done = f32[1536,64,128]{2,1,0:T(8,128)} async-done(((f32[48,64,128]{2,1,0:T(8,128)}), f32[1536,64,128]{2,1,0:T(8,128)}) %all-gather.14.cloned.1.call-update) | async-done | bytes 50331664 | tf_op jit(solution)/shard_map/all_gather | solution.py:27
  595.0 35.4 %rev.6 = f32[32,48,64,128]{3,2,1,0:T(8,128)} reverse(f32[32,48,64,128]{3,2,1,0:T(8,128)} %bitcast.220), dimensions={0} | reverse | bytes 100663296 | tf_op jit(solution)/shard_map/rev | solution.py:29
  630.4 103.6 %while.20 = (s32[]{:T(128)}, f32[48,64,128]{2,1,0:T(8,128)}, s32[]{:T(128)}, f32[32,48,64,128]{3,2,1,0:T(8,128)}, f32[32,48]{1,0:T(8,128)S(1)}, /*index=5*/s32[]{:T(128)}, s32[]{:T(128)}) while((s32[]{:T(128)}, f32[48,64,128]{2,1,0:T(8,128)}, s32[]{:T(128)}, f32[32,48,64,128]{3,2,1,0:T(8,128)}, f32[32,48]{1,0:T(8,128)S(1)}, ...), condition=%wide.region_8.9_spmd.clone, body=%wide.region_7.8_spmd.clone.sunk | while | flops 1572868 | bytes 4719281 | solution.py:39
  633.3 3.4 fusion.155
  636.6 3.4 fusion.155
  640.0 3.4 fusion.155
  646.7 3.4 fusion.155
  650.0 3.4 fusion.155
  653.4 3.4 fusion.155
  656.8 3.4 fusion.155
  660.1 3.4 fusion.155
  663.5 3.4 fusion.155
  666.8 3.4 fusion.155
  670.2 3.4 fusion.155
  673.6 3.4 fusion.155
  676.9 3.4 fusion.155
  680.3 3.4 fusion.155
  755.7 3.8 reduce-window.36
  767.4 7.4 multiply_reduce_fusion.5
  774.8 20.2 %fusion.17 = (f32[256,48]{0,1:T(8,128)}, f32[256,48]{0,1:T(8,128)}, f32[256,48]{0,1:T(8,128)}, f32[256,256]{1,0:T(8,128)}) fusion(f32[256,48]{0,1:T(8,128)S(1)} %copy-done.53, f32[256,48]{0,1:T(8,128)S(1)} %copy-done.55, f32[256,256]{1,0:T(8,128)S(1)} %fusion.133, f32[256,256]{1,0:T(8,128)S(1)} %copy-done.38, f32[256,48,64]{0,2,1:T(8,128)S(1)} %bitcast.224, ...), kind=kOutput, calls=%fused_computation.24 | convolution fusion | flops 2463002624 | bytes 7323648 | tf_op jit(solution)/shard_map/transpose(jvp())/while/body/eval_jaxpr/checkpoint/trh,rhp->thp/dot_general | solution.py:58
  806.7 4.0 reduce-window.48
  817.1 6.1 fusion.80
  823.2 12.5 bitcast_add_fusion.3
  840.9 4.4 fusion.83
  850.2 8.4 multiply_reduce_fusion.4
  861.1 4.2 pad_add_fusion
  878.3 10.0 scatter-add.4
  889.5 12.5 fusion.61
  902.1 9.4 fusion.87
  911.5 17.9 fusion.75
  929.4 444.6 %fusion = f32[16,6448]{1,0:T(8,128)} fusion(f32[1536,6448]{1,0:T(8,128)} %fusion.75), kind=kCustom, calls=%all-reduce-scatter | all-reduce-scatter fusion | flops 13205505 | bytes 40029184
  1384.6 33.2 %collective-permute-done.33 = f32[12,6448]{1,0:T(8,128)S(1)} collective-permute-done((f32[12,6448]{1,0:T(8,128)S(1)}, f32[12,6448]{1,0:T(8,128)S(1)}, u32[]{:S(2)}, u32[]{:S(2)}) %collective-permute-start.33) | collective-permute-done | bytes 309536
  1429.8 12.8 collective-permute-start.23
  1442.6 3.6 collective-permute-start.22
  1446.2 6.9 collective-permute-start.21
  1453.0 25.0 %collective-permute-start.20 = (f32[16,6448]{1,0:T(8,128)}, f32[16,6448]{1,0:T(8,128)}, u32[]{:S(2)}, u32[]{:S(2)}) collective-permute-start(f32[16,6448]{1,0:T(8,128)} %fusion), channel_id=1, source_target_pairs={{0,19},{1,20},{2,21},{3,22},{4,23},{5,24},{6,25},{7,26},{8,27},{9,... | collective-permute-start | bytes 1238024
  1478.0 22.6 %collective-permute-start.19 = (f32[16,6448]{1,0:T(8,128)}, f32[16,6448]{1,0:T(8,128)}, u32[]{:S(2)}, u32[]{:S(2)}) collective-permute-start(f32[16,6448]{1,0:T(8,128)} %fusion), channel_id=1, source_target_pairs={{0,18},{1,19},{2,20},{3,21},{4,22},{5,23},{6,24},{7,25},{8,26},{9,... | collective-permute-start | bytes 1238024
  1500.7 33.0 %collective-permute-start.18 = (f32[16,6448]{1,0:T(8,128)}, f32[16,6448]{1,0:T(8,128)}, u32[]{:S(2)}, u32[]{:S(2)}) collective-permute-start(f32[16,6448]{1,0:T(8,128)} %fusion), channel_id=1, source_target_pairs={{0,17},{1,18},{2,19},{3,20},{4,21},{5,22},{6,23},{7,24},{8,25},{9,... | collective-permute-start | bytes 1238024
  1536.9 3.6 collective-permute-start.16
  1545.1 10.7 collective-permute-start.13
  1555.8 17.0 collective-permute-done.17
  1574.8 10.0 collective-permute-done.16
  1586.8 4.1 collective-permute-start.10
  1590.9 31.5 %collective-permute-start.9 = (f32[16,6448]{1,0:T(8,128)}, f32[16,6448]{1,0:T(8,128)}, u32[]{:S(2)}, u32[]{:S(2)}) collective-permute-start(f32[16,6448]{1,0:T(8,128)} %fusion), channel_id=1, source_target_pairs={{0,8},{1,9},{2,10},{3,11},{4,12},{5,13},{6,14},{7,15},{8,16},{9,17... | collective-permute-start | bytes 1238024
  1624.5 10.0 collective-permute-start.7
  1634.5 7.4 fusion.51
  1645.6 4.0 collective-permute-start.4
  1649.6 20.8 %collective-permute-done.8 = f32[16,6448]{1,0:T(8,128)} collective-permute-done((f32[16,6448]{1,0:T(8,128)}, f32[16,6448]{1,0:T(8,128)}, u32[]{:S(2)}, u32[]{:S(2)}) %collective-permute-start.8) | collective-permute-done | bytes 412704
  1672.7 17.4 collective-permute-start.2
  1697.0 138.7 %concatenate.15 = f32[524,6448]{1,0:T(8,128)} concatenate(f32[12,6448]{1,0:T(8,128)S(1)} %copy-done.34, f32[16,6448]{1,0:T(8,128)} %collective-permute-done.32, f32[16,6448]{1,0:T(8,128)} %collective-permute-done.31, f32[16,6448]{1,0:T(8,128)} %collective-permute-done.30, f32[16,6448]{1,0:T(8,128)} %collective-permute-done.29, f32[16,6448]{1,0:T(8,128)} %collective-permute-done.28, ...), dimensions={0} | concatenate | bytes 27030016
  (452 shorter events, 285.3 us)
Async XLA Ops:
  7.2 110.9 %all-gather.16.cloned.1.call-start = ((), (), s32[]{:S(2)}) async-start(), calls=%async_computation.5 | async-start | bytes 26947584 | tf_op jit(solution)/shard_map/all_gather | solution.py:139
  7.9 334.4 %all-gather.12.cloned.1.call-start = ((), (), s32[]{:S(2)}) async-start(), calls=%async_computation.3 | async-start | bytes 51904512 | tf_op jit(solution)/shard_map/all_gather | solution.py:27
  8.6 154.4 %copy-start.62 = (f32[48]{0:T(128)}, f32[48]{0:T(128)S(1)}, u32[]{:S(2)}) copy-start(f32[48]{0:T(128)S(1)} %neg.34) | copy-start | bytes 580
  81.1 66.4 %copy-start.35 = (f32[1536]{0:T(1024)}, f32[1536]{0:T(1024)S(1)}, u32[]{:S(2)}) copy-start(f32[1536]{0:T(1024)S(1)} %convert_element_type.73) | copy-start | bytes 18436
  116.7 57.5 %copy-start.44 = (f32[3328]{0:T(1024)}, f32[3328]{0:T(1024)S(1)}, u32[]{:S(2)}) copy-start(f32[3328]{0:T(1024)S(1)} %get-tuple-element.365) | copy-start | bytes 39940
  118.0 29.5 %copy-start.60 = (f32[256]{0:T(256)}, f32[256]{0:T(256)S(1)}, u32[]{:S(2)}) copy-start(f32[256]{0:T(256)S(1)} %fusion.64) | copy-start | bytes 3076
  118.1 29.5 %copy-start.58 = (f32[256]{0:T(256)}, f32[256]{0:T(256)S(1)}, u32[]{:S(2)}) copy-start(f32[256]{0:T(256)S(1)} %fusion.120) | copy-start | bytes 3076
  118.1 29.5 %copy-start.12 = (bf16[1,256,1536]{2,1,0:T(8,128)(2,1)S(1)}, bf16[1,256,1536]{2,1,0:T(8,128)(2,1)}, u32[]{:S(2)}) copy-start(bf16[1,256,1536]{2,1,0:T(8,128)(2,1)} %param.17) | copy-start | bytes 2359300
  147.6 15.5 copy-start.63
  164.2 23.5 %copy-start.24 = (f32[48,2,128]{0,2,1:T(8,128)}, f32[48,2,128]{0,2,1:T(8,128)S(1)}, u32[]{:S(2)}) copy-start(f32[48,2,128]{0,2,1:T(8,128)S(1)} %copy.149) | copy-start | bytes 147460
  167.3 5.2 collective-permute-start
  181.2 217.9 %copy-start.4 = (bf16[256,3328]{0,1:T(8,128)(2,1)}, bf16[256,3328]{0,1:T(8,128)(2,1)S(1)}, u32[]{:S(2)}) copy-start(bf16[256,3328]{0,1:T(8,128)(2,1)S(1)} %get-tuple-element.408) | copy-start | bytes 5111812
  185.5 235.2 %all-gather.10.cloned.1.call-start = ((), (), s32[]{:S(2)}) async-start(), calls=%async_computation.1 | async-start | bytes 9510912 | tf_op jit(solution)/shard_map/all_gather | solution.py:140
  186.2 408.8 %all-gather.14.cloned.1.call-start = ((), (), s32[]{:S(2)}) async-start(), calls=%async_computation.4 | async-start | bytes 51904512 | tf_op jit(solution)/shard_map/all_gather | solution.py:27
  190.0 244.4 %copy-start.31 = (f32[256,48]{0,1:T(8,128)}, f32[256,48]{0,1:T(8,128)S(1)}, u32[]{:S(2)}) copy-start(f32[256,48]{0,1:T(8,128)S(1)} %copy.153) | copy-start | bytes 147460
  399.0 15.8 copy-start.1
  400.4 14.4 copy-start.11
  438.1 1253.6 %all-reduce.23.cloned.1.call-start = ((), (), s32[]{:S(2)}) async-start(), calls=%async_computation.6 | async-start | bytes 183296
  861.1 9.8 copy-start.64
  868.0 6.6 collective-permute-start.1
  875.7 13.8 copy-start.36
  875.7 13.8 copy-start.59
  889.5 12.5 copy-start.3
  902.0 935.5 %reduce-scatter.5.cloned.1.call-start = ((), (), s32[]{:S(2)}) async-start(), calls=%async_computation.2 | async-start | bytes 19021824 | tf_op jit(solution)/shard_map/reduce_scatter | solution.py:215
  1374.0 46.6 %collective-permute-start.32 = (f32[16,6448]{1,0:T(8,128)}, f32[16,6448]{1,0:T(8,128)}, u32[]{:S(2)}, u32[]{:S(2)}) collective-permute-start(f32[16,6448]{1,0:T(8,128)} %fusion), channel_id=1, source_target_pairs={{0,31},{1,32},{2,33},{3,34},{4,35},{5,36},{6,37},{7,38},{8,39},{9,... | collective-permute-start | bytes 1238024
  1377.2 40.7 %collective-permute-start.33 = (f32[12,6448]{1,0:T(8,128)S(1)}, f32[12,6448]{1,0:T(8,128)S(1)}, u32[]{:S(2)}, u32[]{:S(2)}) collective-permute-start(f32[12,6448]{1,0:T(8,128)S(1)} %slice.184), channel_id=1, source_target_pairs={{0,32},{1,33},{2,34},{3,35},{4,36},{5,37},{6,38},{7,39},{8,40},{9,... | collective-permute-start | bytes 928520
  1378.5 44.2 %collective-permute-start.31 = (f32[16,6448]{1,0:T(8,128)}, f32[16,6448]{1,0:T(8,128)}, u32[]{:S(2)}, u32[]{:S(2)}) collective-permute-start(f32[16,6448]{1,0:T(8,128)} %fusion), channel_id=1, source_target_pairs={{0,30},{1,31},{2,32},{3,33},{4,34},{5,35},{6,36},{7,37},{8,38},{9,... | collective-permute-start | bytes 1238024
  1380.5 44.2 %collective-permute-start.30 = (f32[16,6448]{1,0:T(8,128)}, f32[16,6448]{1,0:T(8,128)}, u32[]{:S(2)}, u32[]{:S(2)}) collective-permute-start(f32[16,6448]{1,0:T(8,128)} %fusion), channel_id=1, source_target_pairs={{0,29},{1,30},{2,31},{3,32},{4,33},{5,34},{6,35},{7,36},{8,37},{9,... | collective-permute-start | bytes 1238024
  1382.6 44.2 %collective-permute-start.29 = (f32[16,6448]{1,0:T(8,128)}, f32[16,6448]{1,0:T(8,128)}, u32[]{:S(2)}, u32[]{:S(2)}) collective-permute-start(f32[16,6448]{1,0:T(8,128)} %fusion), channel_id=1, source_target_pairs={{0,28},{1,29},{2,30},{3,31},{4,32},{5,33},{6,34},{7,35},{8,36},{9,... | collective-permute-start | bytes 1238024
  1418.6 11.2 collective-permute-start.28
  1420.6 21.9 %collective-permute-start.27 = (f32[16,6448]{1,0:T(8,128)}, f32[16,6448]{1,0:T(8,128)}, u32[]{:S(2)}, u32[]{:S(2)}) collective-permute-start(f32[16,6448]{1,0:T(8,128)} %fusion), channel_id=1, source_target_pairs={{0,26},{1,27},{2,28},{3,29},{4,30},{5,31},{6,32},{7,33},{8,34},{9,... | collective-permute-start | bytes 1238024
  1422.7 23.5 %collective-permute-start.26 = (f32[16,6448]{1,0:T(8,128)}, f32[16,6448]{1,0:T(8,128)}, u32[]{:S(2)}, u32[]{:S(2)}) collective-permute-start(f32[16,6448]{1,0:T(8,128)} %fusion), channel_id=1, source_target_pairs={{0,25},{1,26},{2,27},{3,28},{4,29},{5,30},{6,31},{7,32},{8,33},{9,... | collective-permute-start | bytes 1238024
  1424.7 28.3 %collective-permute-start.25 = (f32[16,6448]{1,0:T(8,128)}, f32[16,6448]{1,0:T(8,128)}, u32[]{:S(2)}, u32[]{:S(2)}) collective-permute-start(f32[16,6448]{1,0:T(8,128)} %fusion), channel_id=1, source_target_pairs={{0,24},{1,25},{2,26},{3,27},{4,28},{5,29},{6,30},{7,31},{8,32},{9,... | collective-permute-start | bytes 1238024
  1426.8 51.2 %collective-permute-start.24 = (f32[16,6448]{1,0:T(8,128)}, f32[16,6448]{1,0:T(8,128)}, u32[]{:S(2)}, u32[]{:S(2)}) collective-permute-start(f32[16,6448]{1,0:T(8,128)} %fusion), channel_id=1, source_target_pairs={{0,23},{1,24},{2,25},{3,26},{4,27},{5,28},{6,29},{7,30},{8,31},{9,... | collective-permute-start | bytes 1238024
  1429.8 70.9 %collective-permute-start.23 = (f32[16,6448]{1,0:T(8,128)}, f32[16,6448]{1,0:T(8,128)}, u32[]{:S(2)}, u32[]{:S(2)}) collective-permute-start(f32[16,6448]{1,0:T(8,128)} %fusion), channel_id=1, source_target_pairs={{0,22},{1,23},{2,24},{3,25},{4,26},{5,27},{6,28},{7,29},{8,30},{9,... | collective-permute-start | bytes 1238024
  1442.6 91.2 %collective-permute-start.22 = (f32[16,6448]{1,0:T(8,128)}, f32[16,6448]{1,0:T(8,128)}, u32[]{:S(2)}, u32[]{:S(2)}) collective-permute-start(f32[16,6448]{1,0:T(8,128)} %fusion), channel_id=1, source_target_pairs={{0,21},{1,22},{2,23},{3,24},{4,25},{5,26},{6,27},{7,28},{8,29},{9,... | collective-permute-start | bytes 1238024
  1446.2 90.7 %collective-permute-start.21 = (f32[16,6448]{1,0:T(8,128)}, f32[16,6448]{1,0:T(8,128)}, u32[]{:S(2)}, u32[]{:S(2)}) collective-permute-start(f32[16,6448]{1,0:T(8,128)} %fusion), channel_id=1, source_target_pairs={{0,20},{1,21},{2,22},{3,23},{4,24},{5,25},{6,26},{7,27},{8,28},{9,... | collective-permute-start | bytes 1238024
  1453.0 87.5 %collective-permute-start.20 = (f32[16,6448]{1,0:T(8,128)}, f32[16,6448]{1,0:T(8,128)}, u32[]{:S(2)}, u32[]{:S(2)}) collective-permute-start(f32[16,6448]{1,0:T(8,128)} %fusion), channel_id=1, source_target_pairs={{0,19},{1,20},{2,21},{3,22},{4,23},{5,24},{6,25},{7,26},{8,27},{9,... | collective-permute-start | bytes 1238024
  1478.0 64.6 %collective-permute-start.19 = (f32[16,6448]{1,0:T(8,128)}, f32[16,6448]{1,0:T(8,128)}, u32[]{:S(2)}, u32[]{:S(2)}) collective-permute-start(f32[16,6448]{1,0:T(8,128)} %fusion), channel_id=1, source_target_pairs={{0,18},{1,19},{2,20},{3,21},{4,22},{5,23},{6,24},{7,25},{8,26},{9,... | collective-permute-start | bytes 1238024
  1500.7 44.4 %collective-permute-start.18 = (f32[16,6448]{1,0:T(8,128)}, f32[16,6448]{1,0:T(8,128)}, u32[]{:S(2)}, u32[]{:S(2)}) collective-permute-start(f32[16,6448]{1,0:T(8,128)} %fusion), channel_id=1, source_target_pairs={{0,17},{1,18},{2,19},{3,20},{4,21},{5,22},{6,23},{7,24},{8,25},{9,... | collective-permute-start | bytes 1238024
  1533.7 39.0 %collective-permute-start.17 = (f32[16,6448]{1,0:T(8,128)}, f32[16,6448]{1,0:T(8,128)}, u32[]{:S(2)}, u32[]{:S(2)}) collective-permute-start(f32[16,6448]{1,0:T(8,128)} %fusion), channel_id=1, source_target_pairs={{0,16},{1,17},{2,18},{3,19},{4,20},{5,21},{6,22},{7,23},{8,24},{9,... | collective-permute-start | bytes 1238024
  1536.9 47.9 %collective-permute-start.16 = (f32[16,6448]{1,0:T(8,128)}, f32[16,6448]{1,0:T(8,128)}, u32[]{:S(2)}, u32[]{:S(2)}) collective-permute-start(f32[16,6448]{1,0:T(8,128)} %fusion), channel_id=1, source_target_pairs={{0,15},{1,16},{2,17},{3,18},{4,19},{5,20},{6,21},{7,22},{8,23},{9,... | collective-permute-start | bytes 1238024
  1540.5 46.3 %collective-permute-start.15 = (f32[16,6448]{1,0:T(8,128)}, f32[16,6448]{1,0:T(8,128)}, u32[]{:S(2)}, u32[]{:S(2)}) collective-permute-start(f32[16,6448]{1,0:T(8,128)} %fusion), channel_id=1, source_target_pairs={{0,14},{1,15},{2,16},{3,17},{4,18},{5,19},{6,20},{7,21},{8,22},{9,... | collective-permute-start | bytes 1238024
  1542.6 48.3 %collective-permute-start.14 = (f32[16,6448]{1,0:T(8,128)}, f32[16,6448]{1,0:T(8,128)}, u32[]{:S(2)}, u32[]{:S(2)}) collective-permute-start(f32[16,6448]{1,0:T(8,128)} %fusion), channel_id=1, source_target_pairs={{0,13},{1,14},{2,15},{3,16},{4,17},{5,18},{6,19},{7,20},{8,21},{9,... | collective-permute-start | bytes 1238024
  1545.1 77.4 %collective-permute-start.13 = (f32[16,6448]{1,0:T(8,128)}, f32[16,6448]{1,0:T(8,128)}, u32[]{:S(2)}, u32[]{:S(2)}) collective-permute-start(f32[16,6448]{1,0:T(8,128)} %fusion), channel_id=1, source_target_pairs={{0,12},{1,13},{2,14},{3,15},{4,16},{5,17},{6,18},{7,19},{8,20},{9,... | collective-permute-start | bytes 1238024
  1572.8 51.7 %collective-permute-start.12 = (f32[16,6448]{1,0:T(8,128)}, f32[16,6448]{1,0:T(8,128)}, u32[]{:S(2)}, u32[]{:S(2)}) collective-permute-start(f32[16,6448]{1,0:T(8,128)} %fusion), channel_id=1, source_target_pairs={{0,11},{1,12},{2,13},{3,14},{4,15},{5,16},{6,17},{7,18},{8,19},{9,... | collective-permute-start | bytes 1238024
  1574.8 67.1 %copy-start.61 = (f32[256]{0:T(256)S(1)}, f32[256]{0:T(256)}, u32[]{:S(2)}) copy-start(f32[256]{0:T(256)} %copy-done.60) | copy-start | bytes 3076
  1574.8 115.3 %copy-start.13 = (bf16[1,256,1536]{2,1,0:T(8,128)(2,1)S(1)}, bf16[1,256,1536]{2,1,0:T(8,128)(2,1)}, u32[]{:S(2)}) copy-start(bf16[1,256,1536]{2,1,0:T(8,128)(2,1)} %param.17) | copy-start | bytes 2359300
  1574.8 115.3 %copy-start.20 = (bf16[1,256,1536]{2,1,0:T(8,128)(2,1)S(1)}, bf16[1,256,1536]{2,1,0:T(8,128)(2,1)}, u32[]{:S(2)}) copy-start(bf16[1,256,1536]{2,1,0:T(8,128)(2,1)} %param.18) | copy-start | bytes 2359300
  1574.8 115.3 %copy-start.27 = (f32[256,1536]{1,0:T(8,128)S(1)}, f32[256,1536]{1,0:T(8,128)}, u32[]{:S(2)}) copy-start(f32[256,1536]{1,0:T(8,128)} %get-tuple-element.432) | copy-start | bytes 4718596
  1584.8 57.1 %collective-permute-start.11 = (f32[16,6448]{1,0:T(8,128)}, f32[16,6448]{1,0:T(8,128)}, u32[]{:S(2)}, u32[]{:S(2)}) collective-permute-start(f32[16,6448]{1,0:T(8,128)} %fusion), channel_id=1, source_target_pairs={{0,10},{1,11},{2,12},{3,13},{4,14},{5,15},{6,16},{7,17},{8,18},{9,... | collective-permute-start | bytes 1238024
  1586.8 56.5 %collective-permute-start.10 = (f32[16,6448]{1,0:T(8,128)}, f32[16,6448]{1,0:T(8,128)}, u32[]{:S(2)}, u32[]{:S(2)}) collective-permute-start(f32[16,6448]{1,0:T(8,128)} %fusion), channel_id=1, source_target_pairs={{0,9},{1,10},{2,11},{3,12},{4,13},{5,14},{6,15},{7,16},{8,17},{9,1... | collective-permute-start | bytes 1238024
  1590.9 54.6 %collective-permute-start.9 = (f32[16,6448]{1,0:T(8,128)}, f32[16,6448]{1,0:T(8,128)}, u32[]{:S(2)}, u32[]{:S(2)}) collective-permute-start(f32[16,6448]{1,0:T(8,128)} %fusion), channel_id=1, source_target_pairs={{0,8},{1,9},{2,10},{3,11},{4,12},{5,13},{6,14},{7,15},{8,16},{9,17... | collective-permute-start | bytes 1238024
  1622.4 47.9 %collective-permute-start.8 = (f32[16,6448]{1,0:T(8,128)}, f32[16,6448]{1,0:T(8,128)}, u32[]{:S(2)}, u32[]{:S(2)}) collective-permute-start(f32[16,6448]{1,0:T(8,128)} %fusion), channel_id=1, source_target_pairs={{0,7},{1,8},{2,9},{3,10},{4,11},{5,12},{6,13},{7,14},{8,15},{9,16}... | collective-permute-start | bytes 1238024
  1624.5 48.2 %collective-permute-start.7 = (f32[16,6448]{1,0:T(8,128)}, f32[16,6448]{1,0:T(8,128)}, u32[]{:S(2)}, u32[]{:S(2)}) collective-permute-start(f32[16,6448]{1,0:T(8,128)} %fusion), channel_id=1, source_target_pairs={{0,6},{1,7},{2,8},{3,9},{4,10},{5,11},{6,12},{7,13},{8,14},{9,15},... | collective-permute-start | bytes 1238024
  1641.9 55.1 %copy-start.34 = (f32[12,6448]{1,0:T(8,128)S(1)}, f32[12,6448]{1,0:T(8,128)}, u32[]{:S(2)}) copy-start(f32[12,6448]{1,0:T(8,128)} %copy-done.33) | copy-start | bytes 928516
  1641.9 55.0 %collective-permute-start.6 = (f32[16,6448]{1,0:T(8,128)}, f32[16,6448]{1,0:T(8,128)S(1)}, u32[]{:S(2)}, u32[]{:S(2)}) collective-permute-start(f32[16,6448]{1,0:T(8,128)} %fusion), channel_id=1, source_target_pairs={{0,5},{1,6},{2,7},{3,8},{4,9},{5,10},{6,11},{7,12},{8,13},{9,14},{... | collective-permute-start | bytes 1238024
  1643.4 53.6 %collective-permute-start.5 = (f32[16,6448]{1,0:T(8,128)}, f32[16,6448]{1,0:T(8,128)S(1)}, u32[]{:S(2)}, u32[]{:S(2)}) collective-permute-start(f32[16,6448]{1,0:T(8,128)} %fusion), channel_id=1, source_target_pairs={{0,4},{1,5},{2,6},{3,7},{4,8},{5,9},{6,10},{7,11},{8,12},{9,13},{1... | collective-permute-start | bytes 1238024
  1645.6 51.4 %collective-permute-start.4 = (f32[16,6448]{1,0:T(8,128)}, f32[16,6448]{1,0:T(8,128)S(1)}, u32[]{:S(2)}, u32[]{:S(2)}) collective-permute-start(f32[16,6448]{1,0:T(8,128)} %fusion), channel_id=1, source_target_pairs={{0,3},{1,4},{2,5},{3,6},{4,7},{5,8},{6,9},{7,10},{8,11},{9,12},{10... | collective-permute-start | bytes 1238024
  1670.4 26.6 %collective-permute-start.3 = (f32[16,6448]{1,0:T(8,128)}, f32[16,6448]{1,0:T(8,128)S(1)}, u32[]{:S(2)}, u32[]{:S(2)}) collective-permute-start(f32[16,6448]{1,0:T(8,128)} %fusion), channel_id=1, source_target_pairs={{0,2},{1,3},{2,4},{3,5},{4,6},{5,7},{6,8},{7,9},{8,10},{9,11},{10,... | collective-permute-start | bytes 1238024
  1672.7 24.2 %collective-permute-start.2 = (f32[16,6448]{1,0:T(8,128)}, f32[16,6448]{1,0:T(8,128)S(1)}, u32[]{:S(2)}, u32[]{:S(2)}) collective-permute-start(f32[16,6448]{1,0:T(8,128)} %fusion), channel_id=1, source_target_pairs={{0,1},{1,2},{2,3},{3,4},{4,5},{5,6},{6,7},{7,8},{8,9},{9,10},{10,1... | collective-permute-start | bytes 1238024
  1696.9 140.6 %copy-start.71 = (f32[48]{0:T(128)S(1)}, f32[48]{0:T(128)}, u32[]{:S(2)}) copy-start(f32[48]{0:T(128)} %get-tuple-element.550) | copy-start | bytes 580
  1696.9 141.1 %copy-start.70 = (f32[48]{0:T(128)S(1)}, f32[48]{0:T(128)}, u32[]{:S(2)}) copy-start(f32[48]{0:T(128)} %get-tuple-element.551) | copy-start | bytes 580
  1697.0 141.6 %copy-start.69 = (f32[48]{0:T(128)S(1)}, f32[48]{0:T(128)}, u32[]{:S(2)}) copy-start(f32[48]{0:T(128)} %get-tuple-element.552) | copy-start | bytes 580
  (50 other events, 253.0 us)
Sparse Core Ops, SparseCore 0:
  11.0 100.4 all-gather.15
  185.6 156.6 all-gather.11
  345.3 70.0 all-gather.9
  438.3 156.6 all-gather.13
  902.1 141.6 all-reduce.22
  1050.4 262.3 reduce-scatter.4
where the time goes:
time: 1870 us; the launch traced here: 1850 us
  blocking collectives  570 us (30%)
  waiting for transfers between devices  352 us (19%)
  local copies, waits for them, and re-layouts  280 us (15%)
  other arithmetic  244 us (13%)
  starting transfers between devices  230 us (12%)
  matrix products  154 us (8%)
    unnamed x2, blocking collectives  515 us
    all_gather x2, waiting for transfers between devices, carried_in(): pieces = jax.tree.map(lambda part: lax.all_gather(part, axis), value)  268 us
    unnamed x33, starting transfers between devices  225 us
    unnamed x166, local copies, waits for them, and re-layouts  190 us
    select_n x62, other arithmetic, lap(): jnp.where(position < mine, new, old)  158 us
    unnamed x39, waiting for transfers between devices  83.3 us
    dot_general x3, matrix products, span_step(): within = jnp.einsum('trh,rhp->thp', mixing, heads_x, precision=highest)  44.2 us
  transfers between devices with their start and end apart: 40, of which 7 were waited for; matrix products, arithmetic and copies ran while one was open for 40% of the time, Pallas kernels for 0%

commit v1 on v0

v1 whole, which is shorter than its diff:
```python
import functools
import jax
import jax.numpy as jnp
from jax import lax
from jax.experimental import pallas as pl
from jax.experimental.pallas import tpu as pltpu
from jax.sharding import PartitionSpec as P, Mesh

MESH = pl.DeviceIdType.MESH
ALL = ("z", "y", "x", "c")
ORDERS = (("z", "y", "x"), ("y", "x", "z"), ("x", "z", "y"))


class Links:
    def __init__(self, send, recv):
        self.send, self.recv, self.used, self.sent = send, recv, 0, []

    def copy(self, src, dst, device):
        k = self.used
        self.used += 1
        made = pltpu.make_async_remote_copy(
            src_ref=src, dst_ref=dst, send_sem=self.send.at[k], recv_sem=self.recv.at[k],
            device_id=device, device_id_type=MESH)
        made.start()
        self.sent.append(made)
        return made

    def finish(self):
        for made in self.sent:
            made.wait_send()


def place():
    return {name: lax.axis_index(name) for name in ALL}


def block(ref, part, core, at, have, half=None):
    z, y, x = at["z"], at["y"], at["x"]
    wide = ref.shape[-1]
    full = slice(None)
    zh, zl = (full, full) if "z" in have else (z // 2, lax.rem(z, 2))
    ys = full if "y" in have else y
    first, count = (0, wide) if "x" in have else (x * (wide // 4), wide // 4)
    if half is not None:
        if "y" in have:
            ys = pl.ds(2 * half, 2)
        elif "z" in have:
            zh = pl.ds(half, 1)
        else:
            near = -(-count // 256) * 128
            first, count = (first, near) if half == 0 else (first + near, count - near)
    cols = full if "x" in have and count == wide else pl.ds(first if isinstance(first, int) else pl.multiple_of(first, 128), count)
    return ref.at[core, zh, ys, zl, part, :, cols]


def moved(at, axis, steps):
    return {**at, axis: lax.rem(at[axis] + steps + 4, 4)}


def gather_kernel(*refs, n, rows):
    shards, fulls, refs = refs[:n], refs[n:2 * n], refs[2 * n:]
    stage, landed, unit, (send, recv, own) = refs[:n], refs[n:2 * n], refs[2 * n:3 * n], refs[3 * n:]
    at = place()
    z, y, x, c = (at[name] for name in ALL)
    to_z, to_c = 2 * lax.rem(z, 2) + x // 2, z // 2
    slot = 2 * lax.rem(x, 2) + c
    from_z = 2 * c + z // 2
    barrier = pltpu.get_barrier_semaphore()
    for axis in ("z", "y", "x"):
        for steps in (1, -1):
            pl.semaphore_signal(barrier, inc=1, device_id={axis: moved(at, axis, steps)[axis]}, device_id_type=MESH)
    pl.semaphore_signal(barrier, inc=1, device_id={"c": 1 - c}, device_id_type=MESH)
    for k in range(4):
        sx, sc = 2 * lax.rem(z, 2) + k // 2, k % 2
        other = jnp.logical_or(jnp.logical_or(sx != x, sc != c), from_z != z)

        @pl.when(other)
        def _():
            pl.semaphore_signal(barrier, inc=1, device_id=(from_z, y, sx, jnp.int32(sc)), device_id_type=MESH)
    home = jnp.logical_and(to_z == z, to_c == c)
    pl.semaphore_wait(barrier, 11 - home.astype(jnp.int32))

    links = Links(send, recv)
    first = []
    for i in range(n):
        wide = shards[i].shape[1] // 4
        for tx in range(4):
            k = links.used
            links.used += 1
            src = shards[i].at[:, pl.ds(tx * wide, wide)]
            remote = pltpu.make_async_remote_copy(
                src_ref=src, dst_ref=landed[i].at[slot], send_sem=send.at[k], recv_sem=recv.at[4 * i + slot],
                device_id=(to_z, y, jnp.int32(tx), to_c), device_id_type=MESH)
            local = pltpu.make_async_copy(src, landed[i].at[slot], recv.at[4 * i + slot])
            mine = jnp.logical_and(home, x == tx)
            pl.when(jnp.logical_not(mine))(remote.start)
            pl.when(mine)(local.start)
            first.append((remote, mine))
    kept = []
    for i in range(n):
        deep, height = rows[i], unit[i].shape[1]
        for k in range(4):
            pltpu.make_async_copy(landed[i].at[k], landed[i].at[k], recv.at[4 * i + k]).wait()
            stage[i][pl.ds(deep * k, deep), :] = landed[i][k, :deep, :].astype(jnp.float32)
        for part in range(3):
            unit[i][part] = stage[i][pl.ds(part * height, height), :].astype(jnp.bfloat16)
        for part in range(3):
            copy = pltpu.make_async_copy(unit[i].at[part], block(fulls[i], part, c, at, ()), own.at[3 * i + part])
            copy.start()
            kept.append(copy)
    sibling = {"c": 1 - c}
    streams = [(i, part) for i in range(n) for part in range(3)]
    for phase in range(3):
        near = {}
        for i, part in streams:
            have, axis = ORDERS[part][:phase], ORDERS[part][phase]
            mine = unit[i].at[part] if phase == 0 else block(fulls[i], part, c, at, have)
            there = block(fulls[i], part, c, at, have)
            near[i, part] = [links.copy(mine, there, {axis: moved(at, axis, steps)[axis]}) for steps in (1, -1)]
            if phase == 0:
                links.copy(mine, there, sibling)
        far = {}
        for i, part in streams:
            have, axis = ORDERS[part][:phase], ORDERS[part][phase]
            far[i, part] = []
            for way, steps in ((0, 1), (1, -1)):
                near[i, part][way].wait_recv()
                behind = moved(at, axis, -steps)
                piece = block(fulls[i], part, c, behind, have, way)
                far[i, part].append(links.copy(piece, piece, {axis: moved(at, axis, steps)[axis]}))
                whole = block(fulls[i], part, c, behind, have)
                links.copy(whole, whole, sibling)
        for i, part in streams:
            have, axis = ORDERS[part][:phase], ORDERS[part][phase]
            for way in (0, 1):
                far[i, part][way].wait_recv()
                piece = block(fulls[i], part, c, moved(at, axis, 2), have, way)
                links.copy(piece, piece, sibling)
        if phase == 0:
            for copy in kept:
                copy.wait()
    for made in links.sent:
        if made.device_id is sibling:
            made.wait_recv()
    links.finish()
    for remote, mine in first:
        pl.when(jnp.logical_not(mine))(remote.wait_send)


def gather(shards, rows):
    n = len(shards)
    heights = [4 * r // 3 for r in rows]
    wides = [s.shape[1] for s in shards]
    fulls = [jax.ShapeDtypeStruct((2, 2, 4, 2, 3, h, w), jnp.bfloat16) for h, w in zip(heights, wides)]
    count = n * (4 + 3 * (3 * 3 * 2 + 1 + 6))
    outs = pl.pallas_call(
        functools.partial(gather_kernel, n=n, rows=tuple(rows)),
        out_shape=fulls,
        in_specs=[pl.BlockSpec(memory_space=pltpu.VMEM)] * n,
        out_specs=[pl.BlockSpec(memory_space=pl.ANY)] * n,
        scratch_shapes=[pltpu.VMEM((3 * h, w // 4), jnp.float32) for h, w in zip(heights, wides)]
        + [pltpu.VMEM((4, s.shape[0], w // 4), jnp.bfloat16) for s, w in zip(shards, wides)]
        + [pltpu.VMEM((3, h, w // 4), jnp.bfloat16) for h, w in zip(heights, wides)]
        + [pltpu.SemaphoreType.DMA((count,)), pltpu.SemaphoreType.DMA((count,)), pltpu.SemaphoreType.DMA((3 * n,))],
        compiler_params=pltpu.CompilerParams(collective_id=0, has_side_effects=True, vmem_limit_bytes=32 << 20),
        name="gather_weights",
    )(*shards)
    return [o.reshape(128 * r, w) for o, r, w in zip(outs, rows, wides)]


def span(shape, axis, at):
    cut = [slice(None)] * 5
    if axis == "y":
        cut[1] = pl.ds(at["y"], 1)
    elif axis == "z":
        cut[0], cut[2] = pl.ds(at["z"] // 2, 1), pl.ds(lax.rem(at["z"], 2), 1)
    else:
        cut[4] = pl.ds(pl.multiple_of(at["x"] * (shape[4] // 4), 128), shape[4] // 4)
    return cut


def without(shape, axis):
    zh, y, zl, rows, wide = shape
    return {"y": (zh, 1, zl, rows, wide), "z": (1, y, 1, rows, wide), "x": (zh, y, zl, rows, wide // 4)}[axis]


def halves(shape):
    if shape[1] == 4:
        return 1, ((0, 2), (2, 2))
    if shape[0] == 2:
        return 0, ((0, 1), (1, 1))
    near = -(-shape[4] // 256) * 128
    return 4, ((0, near), (near, shape[4] - near))


def cut_half(cut, shape, half):
    dim, parts = halves(shape)
    start, size = parts[half]
    cut = list(cut)
    old = cut[dim]
    base = 0 if isinstance(old, slice) else old.start
    cut[dim] = pl.ds(pl.multiple_of(base + start, 128) if dim == 4 and not isinstance(base, int) else base + start, size)
    return cut


def half_shape(shape, half):
    dim, parts = halves(shape)
    return tuple(parts[half][1] if k == dim else size for k, size in enumerate(shape))


def add_up(out, terms, shape):
    na, nb, nc = shape[:3]

    def slab(k, carry):
        a, b, d = k // (nb * nc), lax.rem(k // nc, nb), lax.rem(k, nc)
        total = terms[0](a, b, d).astype(jnp.float32)
        for term in terms[1:]:
            total = total + term(a, b, d).astype(jnp.float32)
        out(a, b, d, total)
        return carry

    lax.fori_loop(0, na * nb * nc, slab, 0)


def start_of(cut):
    return 0 if isinstance(cut, slice) else cut.start


def slab_of(ref, cut, shape):
    z0, y0, l0, _, c0 = (start_of(s) for s in cut)
    lead = ref

    def read(a, b, d):
        return lead[z0 + a, y0 + b, l0 + d, :, pl.ds(c0, shape[4])]

    return read


def slab_to(ref, shape):
    def write(a, b, d, value):
        ref[a, b, d] = value.astype(ref.dtype)

    return write


ALL_CUT = [slice(None)] * 5


def scatter_kernel(*refs, n, rows, shapes, tall):
    parts_in, small_in, refs = refs[:n], refs[n], refs[n + 1:]
    outs, small_out, refs = refs[:n], refs[n], refs[n + 1:]
    take = iter(refs)
    near, relay, acc = {}, {}, {}
    streams = [(i, part) for i in range(n) for part in range(3)]
    for phase in range(3):
        for s in streams:
            near[s, phase] = [next(take), next(take)]
            relay[s, phase] = [next(take), next(take)]
            acc[s, phase] = next(take) if phase < 2 else None
    fin = [next(take) for _ in range(n)]
    staged = [next(take) for _ in range(n)]
    landed = [next(take) for _ in range(n)]
    rounds = [next(take) for _ in range(4)]
    send, recv, last, own = (next(take) for _ in range(4))
    at = place()
    z, y, x, c = (at[name] for name in ALL)
    to_z, to_c = 2 * lax.rem(z, 2) + x // 2, z // 2
    from_z = 2 * c + z // 2
    home = jnp.logical_and(to_z == z, to_c == c)
    barrier = pltpu.get_barrier_semaphore()
    for axis in ("z", "y", "x"):
        for steps in (1, 2, 3):
            pl.semaphore_signal(barrier, inc=1, device_id={axis: moved(at, axis, steps)[axis]}, device_id_type=MESH)
    pl.semaphore_signal(barrier, inc=1, device_id={"c": 1 - c}, device_id_type=MESH)
    for tx in range(4):
        mine = jnp.logical_and(home, x == tx)

        @pl.when(jnp.logical_not(mine))
        def _():
            pl.semaphore_signal(barrier, inc=1, device_id=(to_z, y, jnp.int32(tx), to_c), device_id_type=MESH)
    pl.semaphore_wait(barrier, 14 - home.astype(jnp.int32))

    links = Links(send, recv)

    def small_start(k):
        axis = ("c", "x", "y", "z")[k]
        rounds[k][at[axis]] = small_in[...] if k == 0 else sums[0]
        held = rounds[k].at[at[axis]]
        if k == 0:
            return [links.copy(held, held, {"c": 1 - c})]
        return [links.copy(held, held, {axis: moved(at, axis, steps)[axis]}) for steps in (1, 2, 3)]

    def small_end(k, going):
        for copy in going:
            copy.wait_recv()
        total = rounds[k][0]
        for j in range(1, 2 if k == 0 else 4):
            total = total + rounds[k][j]
        sums[0] = total

    sums = [None]
    size = {s: shapes[s[0]] for s in streams}
    source = {s: parts_in[s[0]].at[:, :, :, s[1]] for s in streams}
    going = small_start(0)
    for phase in range(3):
        sent, lent = {}, {}
        for s in streams:
            axis = ORDERS[s[1]][2 - phase]
            shape = without(size[s], axis)
            cuts = {k: span(size[s], axis, moved(at, axis, k)) for k in (0, 1, 2, 3)}
            to = {k: {axis: moved(at, axis, k)[axis]} for k in (1, 3)}
            lent[s], sent[s] = [], []
            for way, step in ((0, 1), (1, 3)):
                src = source[s].at[tuple(cut_half(cuts[2], shape, way))]
                lent[s].append(links.copy(src, relay[s, phase][way], to[step]))
            for way, step in ((0, 1), (1, 3)):
                src = source[s].at[tuple(cut_half(cuts[step], shape, 1 - way))]
                dst = near[s, phase][way].at[tuple(cut_half(ALL_CUT, shape, 1 - way))]
                sent[s].append(links.copy(src, dst, to[step]))
        small_end(phase, going)
        going = small_start(phase + 1)
        for s in streams:
            axis = ORDERS[s[1]][2 - phase]
            shape = without(size[s], axis)
            for way, step in ((0, 1), (1, 3)):
                lent[s][way].wait_recv()
                hs = half_shape(shape, way)
                cut = cut_half(span(size[s], axis, moved(at, axis, step)), shape, way)
                buf = relay[s, phase][way]
                add_up(slab_to(buf, hs), [slab_of(source[s], cut, hs), slab_of(buf, ALL_CUT, hs)], hs)
                dst = near[s, phase][way].at[tuple(cut_half(ALL_CUT, shape, way))]
                sent[s].append(links.copy(buf, dst, {axis: moved(at, axis, step)[axis]}))
        for s in streams:
            i, part = s
            axis = ORDERS[part][2 - phase]
            shape = without(size[s], axis)
            for copy in sent[s]:
                copy.wait_recv()
            terms = [slab_of(source[s], span(size[s], axis, at), shape)]
            terms += [slab_of(near[s, phase][way], ALL_CUT, shape) for way in (0, 1)]
            if phase < 2:
                add_up(slab_to(acc[s, phase], shape), terms, shape)
                source[s], size[s] = acc[s, phase], shape
            else:
                total = terms[0](0, 0, 0).astype(jnp.float32)
                for term in terms[1:]:
                    total = total + term(0, 0, 0).astype(jnp.float32)
                fin[i][pl.ds(part * shape[3], shape[3]), :] = total
    small_end(3, going)
    small_out[...] = sums[0]
    final = []
    for i in range(n):
        deep, wide = rows[i], fin[i].shape[1]
        for k in range(4):
            sx, sc = 2 * lax.rem(z, 2) + k // 2, k % 2
            staged[i][k] = jnp.zeros(staged[i].shape[1:], jnp.float32)
            staged[i][k, :deep] = fin[i][pl.ds(deep * k, deep), :]
            mine = jnp.logical_and(home, jnp.logical_and(sx == x, sc == c))
            remote = pltpu.make_async_remote_copy(
                src_ref=staged[i].at[k], dst_ref=landed[i].at[x], send_sem=own.at[4 * i + k], recv_sem=last.at[4 * i + x],
                device_id=(from_z, y, sx, jnp.int32(sc)), device_id_type=MESH)
            local = pltpu.make_async_copy(staged[i].at[k], landed[i].at[x], last.at[4 * i + x])
            pl.when(jnp.logical_not(mine))(remote.start)
            pl.when(mine)(local.start)
            final.append((remote, mine))
    for i in range(n):
        wide = fin[i].shape[1]
        for tx in range(4):
            pltpu.make_async_copy(landed[i].at[tx], landed[i].at[tx], last.at[4 * i + tx]).wait()
            outs[i][:, pl.ds(tx * wide, wide)] = landed[i][tx]
    links.finish()
    for remote, mine in final:
        pl.when(jnp.logical_not(mine))(remote.wait_send)


def scatter(halves_in, small, rows):
    n = len(halves_in)
    wides = [h.shape[1] for h in halves_in]
    heights = [4 * r // 3 for r in rows]
    ins = [h.reshape(2, 4, 2, 3, t, w) for h, t, w in zip(halves_in, heights, wides)]
    shapes = [(2, 4, 2, t, w) for t, w in zip(heights, wides)]
    tall = [-(-r // 8) * 8 for r in rows]
    scratch = []
    size = {(i, part): shapes[i] for i in range(n) for part in range(3)}
    for phase in range(3):
        for s in size:
            shape = without(size[s], ORDERS[s[1]][2 - phase])
            scratch += [pltpu.VMEM(shape, jnp.bfloat16)] * 2
            scratch += [pltpu.VMEM(half_shape(shape, way), jnp.bfloat16) for way in (0, 1)]
            if phase < 2:
                scratch += [pltpu.VMEM(shape, jnp.bfloat16)]
            size[s] = shape
    scratch += [pltpu.VMEM((3 * t, w // 4), jnp.float32) for t, w in zip(heights, wides)]
    scratch += [pltpu.VMEM((4, t, w // 4), jnp.float32) for t, w in zip(tall, wides)]
    scratch += [pltpu.VMEM((4, t, w // 4), jnp.float32) for t, w in zip(tall, wides)]
    scratch += [pltpu.VMEM((2 if k == 0 else 4,) + small.shape, jnp.float32) for k in range(4)]
    count = n * 3 * 3 * 6 + 10
    scratch += [pltpu.SemaphoreType.DMA((count,)), pltpu.SemaphoreType.DMA((count,)),
                pltpu.SemaphoreType.DMA((4 * n,)), pltpu.SemaphoreType.DMA((4 * n,))]
    outs = pl.pallas_call(
        functools.partial(scatter_kernel, n=n, rows=tuple(rows), shapes=tuple(shapes), tall=tuple(tall)),
        out_shape=[jax.ShapeDtypeStruct((t, w), jnp.float32) for t, w in zip(tall, wides)] + [jax.ShapeDtypeStruct(small.shape, jnp.float32)],
        in_specs=[pl.BlockSpec(memory_space=pltpu.VMEM)] * (n + 1),
        out_specs=[pl.BlockSpec(memory_space=pltpu.VMEM)] * (n + 1),
        scratch_shapes=scratch,
        compiler_params=pltpu.CompilerParams(collective_id=1, has_side_effects=True, vmem_limit_bytes=56 << 20),
        name="scatter_gradients",
    )(*ins, small)
    return outs


H = 48
P_SIZE = 64
NS = 128
KW = 4
DI = 3072
CONVC = 3328
PROJ = 6448
WIDE = 6656
PARAMS = 6528
SEQ = ("y", "x", "c")
epsilon = 1e-05
highest = lax.Precision.HIGHEST


def from_behind(value, steps):
    return lax.ppermute(value, SEQ, [(k, k + steps) for k in range(max(0, -steps), min(32, 32 - steps))])


def carried_in(decay, state, backward):
    mine = lax.axis_index(SEQ)
    rows = H * P_SIZE // 32
    spread = jnp.repeat(decay, P_SIZE).reshape(32, 1, rows)
    spread = jnp.pad(spread, ((0, 0), (0, 7), (0, 128 - rows)))
    packed = jnp.concatenate([state.reshape(32, rows, NS), spread], axis=1)
    blocks = lax.all_to_all(packed, SEQ, split_axis=0, concat_axis=0, tiled=True)
    decays = blocks[:, rows, :rows]
    states = blocks[:, :rows]

    def lap(carry, piece):
        return piece[0][:, None] * carry + piece[1], carry

    _, before = lax.scan(lap, jnp.zeros((rows, NS), jnp.float32), (decays, states), reverse=backward, unroll=8)
    back = lax.all_to_all(before, SEQ, split_axis=0, concat_axis=0, tiled=True)
    return back.reshape(H, P_SIZE, NS)


def rms_scale(values, gain):
    return values * lax.rsqrt(jnp.mean(values * values, axis=-1, keepdims=True) + epsilon) * gain


def span_step(heads_x, b_in, c_out, steps_dt, neg_rate):
    block_len = heads_x.shape[0]
    log_decay = steps_dt * neg_rate[None, :]
    cum_decay = jnp.cumsum(log_decay, axis=0)
    position = jnp.arange(block_len)
    causal = (position[:, None] >= position[None, :]).astype(jnp.float32)
    gap_decay = (
        jnp.exp((cum_decay[:, None, :] - cum_decay[None, :, :]) * causal[:, :, None])
        * causal[:, :, None]
    )
    scores = jnp.dot(c_out, b_in.T, precision=highest)
    mixing = scores[:, :, None] * gap_decay * steps_dt[None, :, :]
    within = jnp.einsum("trh,rhp->thp", mixing, heads_x, precision=highest)
    last_sum = cum_decay[-1]
    toward = jnp.exp(last_sum[None, :] - cum_decay) * steps_dt
    added_in = jnp.einsum("rh,rhp,rn->hpn", toward, heads_x, b_in, precision=highest)
    return (added_in, within)


def local_core(heads_x, b_in, c_out, steps_dt, neg_rate, d_skip):
    final_state, outputs = span_step(heads_x, b_in, c_out, steps_dt, neg_rate)
    cum_decay = jnp.cumsum(steps_dt * neg_rate[None, :], axis=0)
    local_out = outputs + d_skip[None, :, None] * heads_x
    return (local_out, final_state, jnp.exp(cum_decay[-1]), cum_decay)


def correction(c_out, cum_decay, incoming):
    return jnp.exp(cum_decay)[:, :, None] * jnp.einsum(
        "tn,hpn->thp", c_out, incoming, precision=highest
    )


def full_mixer(heads_x, b_in, c_out, steps_dt, neg_rate, d_skip, incoming):
    local_out, final_state, total_decay, cum_decay = local_core(
        heads_x, b_in, c_out, steps_dt, neg_rate, d_skip
    )
    return (local_out + correction(c_out, cum_decay, incoming), final_state, total_decay)


def conv_section(extended, w_conv, b_conv, dt_raw, dt_bias, decay_rates):
    length = dt_raw.shape[0]
    mixed = jnp.zeros((length, CONVC), jnp.float32) + b_conv[None, :]
    for offset in range(KW):
        mixed = mixed + w_conv[offset][None, :] * extended[offset : offset + length]
    return (jax.nn.silu(mixed), jax.nn.softplus(dt_raw + dt_bias[None, :]), -decay_rates)


def gate_section(ssd_out, gate_z, gain_gate):
    length = gate_z.shape[0]
    gated = ssd_out.reshape(length, DI) * jax.nn.silu(gate_z)
    return rms_scale(gated, gain_gate)


def swap(value):
    return lax.ppermute(value, "c", [(0, 1), (1, 0)])


def my_half(value, core):
    wide = value.shape[1] // 2
    given = swap(lax.dynamic_slice_in_dim(value, (1 - core) * wide, wide, axis=1))
    return jnp.concatenate([lax.dynamic_slice_in_dim(value, core * wide, wide, axis=1), given], axis=0)


def shards(
    hidden,
    cotangent,
    in_w,
    out_w,
    conv_w,
    conv_b,
    norm_gain,
    gate_gain,
    dt_bias,
    decay_rates,
    d_skip,
):
    core = lax.axis_index("c")
    spare = jnp.concatenate([
        jnp.pad(conv_w, ((0, 0), (0, 102))),
        jnp.pad(conv_b, (0, 102))[None],
        jnp.pad(norm_gain, (0, 116))[None],
        jnp.pad(gate_gain, (0, 104))[None],
        jnp.zeros((5, 128), jnp.bfloat16),
    ])
    shard_in = jnp.pad(jnp.concatenate([jnp.pad(in_w, ((0, 0), (0, PARAMS - PROJ))), spare], axis=1), ((0, 4), (0, 0)))
    w_in, w_out = gather([shard_in, jnp.pad(out_w, ((0, 8), (0, 0)))], [12, 24])
    spare = w_in[:, PARAMS:].reshape(128, 12, 128).astype(jnp.float32)
    w_conv_f = spare[:, :4, :26].transpose(1, 0, 2).reshape(KW, CONVC)
    b_conv_f = spare[:, 4, :26].reshape(CONVC)
    gain_norm_f = spare[:, 5, :12].reshape(1536)
    gain_gate_f = spare[:, 6, :24].reshape(DI)
    w_in = w_in * (jnp.arange(WIDE) < PROJ).astype(jnp.bfloat16)[None, :]
    residual = hidden[0].astype(jnp.float32)
    length = residual.shape[0]
    normed = rms_scale(residual, gain_norm_f).astype(jnp.bfloat16)
    projected = jnp.dot(normed, w_in, preferred_element_type=jnp.float32)
    gate_z = projected[:, :DI]
    conv_in = projected[:, DI : DI + CONVC].astype(jnp.bfloat16)
    dt_raw = projected[:, DI + CONVC : PROJ]
    edge_rows = from_behind(conv_in[length - (KW - 1) :], 1)
    extended = jnp.concatenate([edge_rows, conv_in], axis=0).astype(jnp.float32)
    pre_act, steps_dt, neg_rate = conv_section(
        extended, w_conv_f, b_conv_f, dt_raw, dt_bias, decay_rates
    )
    activated = lax.optimization_barrier(pre_act.astype(jnp.bfloat16)).astype(jnp.float32)
    heads_x = activated[:, :DI].reshape(length, H, P_SIZE)
    b_in = activated[:, DI : DI + NS]
    c_out = activated[:, DI + NS :]
    local_out, final_state, total_decay, cum_decay = local_core(
        heads_x, b_in, c_out, steps_dt, neg_rate, d_skip
    )
    incoming = carried_in(total_decay, final_state, False)
    ssd_out = local_out + correction(c_out, cum_decay, incoming)
    branch = gate_section(ssd_out, gate_z, gain_gate_f).astype(jnp.bfloat16)
    result = (residual + jnp.dot(branch, w_out, preferred_element_type=jnp.float32)).astype(
        jnp.bfloat16
    )
    grad_out = cotangent[0]
    both_out = jnp.concatenate([grad_out, swap(grad_out)], axis=0)
    d_branch = jnp.einsum("td,kd->tk", grad_out, w_out, preferred_element_type=jnp.float32)
    d_w_out = jnp.einsum("tk,td->kd", my_half(branch, core), both_out, preferred_element_type=jnp.float32).astype(jnp.bfloat16)
    gate_pull = jax.vjp(gate_section, ssd_out, gate_z, gain_gate_f)[1]
    d_ssd, d_gate_z, d_gain_gate = gate_pull(d_branch)
    d_incoming = jnp.einsum("th,thp,tn->hpn", jnp.exp(cum_decay), d_ssd, c_out, precision=highest)
    carried_back = carried_in(total_decay, d_incoming, True)
    d_total_decay = jnp.sum(carried_back * incoming, axis=(1, 2))
    mixer_pull = jax.vjp(full_mixer, heads_x, b_in, c_out, steps_dt, neg_rate, d_skip, incoming)[1]
    d_heads_x, d_b_in, d_c_out, d_steps, d_rate, d_dskip, unused_grad = mixer_pull(
        (d_ssd, carried_back, d_total_decay)
    )
    d_act = jnp.concatenate([d_heads_x.reshape(length, DI), d_b_in, d_c_out], axis=1)
    conv_pull = jax.vjp(conv_section, extended, w_conv_f, b_conv_f, dt_raw, dt_bias, decay_rates)[1]
    d_ext, d_conv_w, d_conv_b, d_dt_raw, d_dt_bias, d_rates = conv_pull((d_act, d_steps, d_rate))
    back_rows = from_behind(d_ext[: KW - 1].astype(jnp.bfloat16), -1).astype(jnp.float32)
    d_conv_in = d_ext[KW - 1 :] + jnp.pad(back_rows, ((length - (KW - 1), 0), (0, 0)))
    d_projected = jnp.concatenate(
        [d_gate_z, d_conv_in, d_dt_raw, jnp.zeros((length, WIDE - PROJ), jnp.float32)], axis=1
    ).astype(jnp.bfloat16)
    d_normed = jnp.einsum("tj,dj->td", d_projected, w_in, preferred_element_type=jnp.float32)
    both_projected = jnp.concatenate([d_projected, swap(d_projected)], axis=0)
    d_w_in = jnp.einsum("td,tj->dj", my_half(normed, core), both_projected, preferred_element_type=jnp.float32).astype(jnp.bfloat16)
    norm_pull = jax.vjp(rms_scale, residual, gain_norm_f)[1]
    d_from_norm, d_gain_norm = norm_pull(d_normed)
    d_hidden = grad_out.astype(jnp.float32) + d_from_norm
    small = jnp.concatenate([
        d_conv_w.reshape(-1), d_conv_b, d_gain_norm, d_gain_gate,
        jnp.pad(d_dt_bias, (0, 80)), jnp.pad(d_rates, (0, 80)), jnp.pad(d_dskip, (0, 80)),
        jnp.zeros((896,), jnp.float32),
    ]).reshape(176, 128)
    g_in, g_out, total = scatter([d_w_in, d_w_out], small, [12, 24])
    mine = lax.axis_index(ALL)
    d_conv_w = total[:104].reshape(KW, CONVC)
    d_conv_b = total[104:130].reshape(CONVC)
    d_gain_norm = total[130:142].reshape(1536)
    d_gain_gate = total[142:166].reshape(DI)
    return (
        result[None],
        d_hidden[None],
        g_in[:12, :PROJ],
        g_out,
        lax.dynamic_slice_in_dim(d_conv_w, 26 * mine, 26, axis=1),
        lax.dynamic_slice_in_dim(d_conv_b, 26 * mine, 26),
        lax.dynamic_slice_in_dim(d_gain_norm, 12 * mine, 12),
        lax.dynamic_slice_in_dim(d_gain_gate, 24 * mine, 24),
        total[166, :H],
        total[167, :H],
        total[168, :H],
    )


def solution(mesh):
    grid = Mesh(mesh.devices.reshape(4, 4, 4, 2), ALL)
    tokens = P("z", SEQ, None)
    placed = (
        tokens,
        tokens,
        P(ALL, None),
        P(ALL, None),
        P(None, ALL),
        P(ALL),
        P(ALL),
        P(ALL),
        P(),
        P(),
        P(),
    )
    return jax.shard_map(
        shards,
        mesh=grid,
        in_specs=placed,
        out_specs=(tokens, tokens, P(ALL, None), P(ALL, None), P(None, ALL), P(ALL), P(ALL), P(ALL), P(), P(), P()),
        check_vma=False,
    )
```

time: 1870 us -> 667 us (0.36)
  blocking collectives: 570 us -> 0 us
  waiting for transfers between devices: 352 us -> 33.2 us
  starting transfers between devices: 230 us -> 33.5 us
  Pallas kernels: 0 us -> 180 us
  local copies, waits for them, and re-layouts: 280 us -> 115 us
  other arithmetic: 244 us -> 162 us
  matrix products: 154 us -> 129 us
    unnamed x2 -> x0, blocking collectives: 515 us -> none
    all_gather x4 -> x0, waiting for transfers between devices: 268 us -> none  [the longest x2 268 us: carried_in(): pieces = jax.tree.map(lambda part: lax.all_gather(part, axis), value)]
    unnamed x33 -> x0, starting transfers between devices: 225 us -> none
    pallas_call x0 -> x2, Pallas kernels: none -> 180 us  [the longest x1 95.9 us: scatter(): pl.pallas_call(functools.partial(scatter_kernel, n=n, rows=tuple(rows), s...]
    unnamed x166 -> x135, local copies, waits for them, and re-layouts: 190 us -> 17.2 us
    select_n x62 -> x0, other arithmetic: 158 us -> none  [lap(): jnp.where(position < mine, new, old)]
    unnamed x39 -> x0, waiting for transfers between devices: 83.3 us -> none
    while x0 -> x44, other arithmetic: none -> 57.2 us
  transfers between devices with their start and end apart: 40 -> 10, of which waited for: 7 -> 3; matrix products, arithmetic and copies ran while one was open for 40% -> 28% of each run, Pallas kernels for 0% -> 0%
where the time goes in v1:
time: 667 us; the launch traced here: 655 us
  Pallas kernels  180 us (27%)
  other arithmetic  162 us (24%)
  matrix products  129 us (19%)
  local copies, waits for them, and re-layouts  115 us (17%)
  starting transfers between devices  33.5 us (5%)
  waiting for transfers between devices  33.2 us (5%)
    pallas_call x1, Pallas kernels, scatter(): pl.pallas_call(functools.partial(scatter_kernel, n=n, rows=tuple(rows), s...  95.9 us
    pallas_call x1, Pallas kernels, gather(): pl.pallas_call(functools.partial(gather_kernel, n=n, rows=tuple(rows)), o...  83.7 us
    while x44, other arithmetic  57.2 us
    dot_general x3, matrix products, span_step(): within = jnp.einsum('trh,rhp->thp', mixing, heads_x, precision=highest)  44.1 us
    all_to_all x2, waiting for transfers between devices, carried_in(): lax.all_to_all(packed, SEQ, split_axis=0, concat_axis=0, tiled=True)  23.5 us
    unnamed x135, local copies, waits for them, and re-layouts  17.2 us
    mul x1, other arithmetic, shards(): w_in = w_in * (jnp.arange(WIDE) < PROJ).astype(jnp.bfloat16)[None, :]  16.9 us
    dot_general x3, matrix products, span_step(): jnp.einsum('rh,rhp,rn->hpn', toward, heads_x, b_in, precision=highest)  15.9 us
  transfers between devices with their start and end apart: 10, of which 3 were waited for; matrix products, arithmetic and copies ran while one was open for 28% of the time, Pallas kernels for 0%

profile of v1, /device:TPU:1, one launch (start us, length us, event | category | flops | bytes accessed | tf_op | source)
XLA Modules:
  0.0 655.4 jit_solution(17559578950088060986)
XLA Ops:
  4.7 83.7 %gather_weights.1 = (bf16[2,2,4,2,3,16,6656]{6,5,4,3,2,1,0:T(8,128)(2,1)}, bf16[2,2,4,2,3,32,1536]{6,5,4,3,2,1,0:T(8,128)(2,1)S(1)}) custom-call(bf16[16,6656]{1,0:T(8,128)(2,1)S(1)} %pad.85.refs_0_, bf16[32,1536]{1,0:T(8,128)(2,1)S(1)} %pad.86.refs_1_), custom_call_target="tpu_custom_call" | custom-call | tf_op jit(solution)/shard_map/gather_weights/pallas_call | solution.py:156
  88.4 3.5 copy-done
  93.4 16.9 %broadcast_multiply_fusion = bf16[2,2,4,2,3,16,6656]{6,5,4,3,2,1,0:T(8,128)(2,1)} fusion(bf16[2,2,4,2,3,16,6656]{6,5,4,3,2,1,0:T(8,128)(2,1)} %get-tuple-element.146, bf16[6656]{0:T(1024)(128)(2,1)S(1)} %fusion.128), kind=kLoop, calls=%fused_computation.83 | loop fusion | flops 10223616 | bytes 40907776 | tf_op jit(solution)/shard_map/mul | solution.py:543
  110.6 9.8 %fusion.149 = (bf16[256,6656]{1,0:T(8,128)(2,1)S(1)}, f32[256,6656]{1,0:T(8,128)S(1)}) fusion(bf16[1536,6656]{1,0:T(8,128)(2,1)} %bitcast.499, bf16[1,256,1536]{2,1,0:T(8,128)(2,1)S(1)} %copy-done.10, f32[1536]{0:T(1024)S(1)} %mul.814, f32[256]{0:T(256)S(1)} %fusion.129), kind=kOutput, calls=%fused_computation.294 | convolution fusion | flops 5237768192 | bytes 31464448 | tf_op jit(solution)/shard_map/dot_general | solution.py:547
  120.4 2.1 collective-permute-start
  128.3 2.7 slice.448
  134.4 1.8 maximum_convert_fusion
  136.2 3.5 multiply_convert_fusion
  139.7 2.7 slice_convert_fusion.2
  142.4 2.6 copy.153
  145.0 3.1 fusion.43
  149.4 4.5 all-to-all-start
  153.9 23.5 %all-to-all-done = f32[32,104,128]{2,1,0:T(8,128)} async-done(((f32[32,104,128]{2,1,0:T(8,128)}), f32[32,104,128]{2,1,0:T(8,128)}, u32[]{:S(2)}, u32[]{:S(2)}) %all-to-all-start) | async-done | bytes 1703968 | tf_op jit(solution)/shard_map/all_to_all | solution.py:436
  177.4 2.7 slice.463
  182.9 66.4 %while.30 = (s32[]{:T(128)}, f32[96,128]{1,0:T(8,128)}, f32[4,8,96,128]{3,2,1,0:T(8,128)}, f32[4,8,96]{2,1,0:T(8,128)}, f32[4,8,96,128]{3,2,1,0:T(8,128)}, /*ind...) while((s32[]{:T(128)}, f32[96,128]{1,0:T(8,128)}, ...), condition=%wide.region_4.5_spmd.clone, body=%wide.region_3.4_spmd.clone.sunk | while | flops 294921 | bytes 2430100 | solution.py:443
  195.6 1.8 bitcast_dynamic-update-slice_fusion.44
  212.4 1.8 bitcast_dynamic-update-slice_fusion.44
  229.2 1.8 bitcast_dynamic-update-slice_fusion.44
  245.9 1.8 bitcast_dynamic-update-slice_fusion.44
  249.2 6.5 all-to-all-start.1
  256.6 1.9 slice_reduce_fusion
  260.0 2.7 mul.842
  262.7 3.5 copy.164
  266.9 3.5 copy.157
  270.4 1.8 fusion.121
  272.2 5.8 all-to-all-done.1
  278.0 3.0 fusion.104
  281.1 12.8 %fusion.51 = f32[256,48,64]{0,2,1:T(8,128)} fusion(f32[256,48,64]{0,2,1:T(8,128)S(1)} %fusion.104, f32[256,48,64]{0,2,1:T(8,128)S(1)} %bitcast.510, bf16[256,48,64]{0,2,1:T(8,128)(2,1)S(1)} %bitcast.495, f32[256,48]{0,1:T(8,128)} %get-tuple-element.286, f32[256,256]{1,0:T(8,128)} %fusion.98, f32[256,48]{0,1:T(8,128)} %copy-done.30, ...), kind=kOutput, calls=%fused_computation.127 | convolution fusion | flops 2434793472 | bytes 11681984 | tf_op jit(solution)/shard_map/trh,rhp->thp/dot_general | solution.py:464
  293.8 3.5 copy.158
  297.4 3.9 multiply_reduce_fusion.9
  301.3 6.5 multiply_reduce_fusion.6
  307.8 6.7 %multiply_reduce_fusion.5 = (f32[3072]{0:T(1024)}, f32[256,3072]{1,0:T(8,128)}, bf16[256,3072]{1,0:T(8,128)(2,1)}, bf16[256,3072]{1,0:T(8,128)(2,1)}) fusion(bf16[256,3328]{1,0:T(8,128)(2,1)S(1)} %copy-done.5, f32[256,6656]{1,0:T(8,128)} %copy-done.8, f32[256,3072]{1,0:T(8,128)S(1)} %get-tuple-element.249, f32[256]{0:T(256)S(1)} %multiply_multiply_fusion.3, ...), kind=kLoop, calls=%fused_computation.128 | loop fusion | flops 18871296 | bytes 20473856 | tf_op jit(solution)/shard_map/transpose(jvp())/reduce_sum | solution.py:474
  314.6 3.5 copy.161
  318.1 3.5 fusion.52
  323.0 6.7 %all-to-all-start.2 = ((f32[32,104,128]{2,1,0:T(8,128)}), f32[32,104,128]{2,1,0:T(8,128)}, u32[]{:S(2)}, u32[]{:S(2)}) async-start(f32[32,104,128]{2,1,0:T(8,128)} %fusion.68), calls=%async_computation.2 | async-start | bytes 3407872 | tf_op jit(solution)/shard_map/all_to_all | solution.py:436
  329.7 5.0 mul.869
  334.7 3.6 copy.165
  338.2 8.1 %convolution_bitcast_fusion.1 = f32[256,128]{1,0:T(8,128)} fusion(f32[256,48,64]{0,2,1:T(8,128)} %bitcast.500, f32[48,64,128]{2,1,0:T(8,128)} %bitcast.19), kind=kOutput, calls=%fused_computation.178 | convolution fusion | flops 1207959552 | bytes 4849664 | tf_op jit(solution)/shard_map/transpose(jvp(tn,hpn->thp))/dot_general | solution.py:479
  347.0 2.7 constant_dynamic-slice_fusion.4
  351.2 16.7 %fusion.31 = (f32[256,48]{0,1:T(8,128)}, f32[256,48]{0,1:T(8,128)}, f32[256,48]{0,1:T(8,128)}, f32[256,256]{1,0:T(8,128)S(1)}) fusion(f32[256,48]{0,1:T(8,128)} %get-tuple-element.286, f32[256,256]{1,0:T(8,128)} %fusion.98, f32[256,48]{0,1:T(8,128)} %copy-done.30, f32[256,256]{1,0:T(8,128)} %fusion.121, f32[48,64,256]{2,1,0:T(8,128)} %bitcast.488, ...), kind=kOutput, calls=%fused_computation.89 | convolution fusion | flops 2463002624 | bytes 5750784 | tf_op jit(solution)/shard_map/transpose(jvp(trh,rhp->thp))/dot_general | solution.py:464
  368.6 1.8 convolution_add_fusion.1
  370.4 2.7 slice.467
  375.9 31.9 %while.31 = (s32[]{:T(128)}, f32[96,128]{1,0:T(8,128)}, f32[4,8,96,128]{3,2,1,0:T(8,128)}, f32[4,8,96]{2,1,0:T(8,128)}, f32[4,8,96,128]{3,2,1,0:T(8,128)}, /*ind...) while((s32[]{:T(128)}, f32[96,128]{1,0:T(8,128)}, ...), condition=%wide.region_8.9_spmd.clone, body=%wide.region_7.8_spmd.clone.sunk | while | flops 294922 | bytes 2425660 | solution.py:443
  407.8 7.9 %all-to-all-start.3 = ((f32[32,96,128]{2,1,0:T(8,128)}), f32[32,96,128]{2,1,0:T(8,128)}, u32[]{:S(2)}, u32[]{:S(2)}) async-start(f32[32,96,128]{2,1,0:T(8,128)} %bitcast.506), calls=%async_computation.3 | async-start | bytes 3145728 | tf_op jit(solution)/shard_map/all_to_all | solution.py:444
  415.7 4.4 multiply_reduce_fusion.7
  420.1 7.3 %fusion.56 = bf16[1,256,1536]{2,1,0:T(8,128)(2,1)} fusion(bf16[256,3072]{1,0:T(8,128)(2,1)S(1)} %copy-done.7, bf16[3072,1536]{1,0:T(8,128)(2,1)} %bitcast.486, bf16[1,256,1536]{2,1,0:T(8,128)(2,1)S(1)} %copy-done.11), kind=kOutput, calls=%fused_computation.140 | convolution fusion | flops 2417098752 | bytes 12582912 | tf_op jit(solution)/shard_map/dot_general | solution.py:566
  427.4 6.1 convolution_convert_fusion.1
  433.5 4.0 all-to-all-done.3
  437.5 5.7 fusion.47
  443.2 7.2 %fusion.87 = f32[256,128]{1,0:T(8,128)} fusion(f32[48,64,128]{2,1,0:T(8,128)} %bitcast.30, bf16[256,48,64]{0,2,1:T(8,128)(2,1)S(1)} %bitcast.496, f32[256,48]{0,1:T(8,128)S(1)} %copy-done.29), kind=kOutput, calls=%fused_computation.179 | convolution fusion | flops 1209532416 | bytes 3325952 | tf_op jit(solution)/shard_map/transpose(jvp(rh,rhp,rn->hpn))/dot_general | solution.py:467
  450.3 2.7 multiply_reduce_fusion.10
  460.1 3.8 reduce-window.26
  466.9 3.8 reduce-window.24
  472.3 14.7 %bitcast_add_fusion = f32[256,48,64]{0,2,1:T(8,128)} fusion(f32[256,48,64]{0,2,1:T(8,128)} %get-tuple-element.294, f32[256,48,64]{0,2,1:T(8,128)} %bitcast.491, f32[48,64,256]{2,1,0:T(8,128)} %bitcast.490, f32[256,48]{0,1:T(8,128)} %get-tuple-element.286, f32[256,256]{1,0:T(8,128)} %fusion.98, f32[256,48]{0,1:T(8,128)} %copy-done.30, ...), kind=kOutput, calls=%fused_computation.125 | convolution fusion | flops 2434793472 | bytes 13254848 | tf_op jit(solution)/shard_map/transpose(jvp(trh,rhp->thp))/dot_general | solution.py:464
  487.0 3.5 copy.168
  491.9 6.6 %multiply_reduce_fusion.4 = (f32[3328]{0:T(1024)S(1)}, f32[3328]{0:T(1024)S(1)}, f32[3328]{0:T(1024)S(1)}, f32[3328]{0:T(1024)S(1)}, f32[3328]{0:T(1024)}, /*index=5*/f32[256,3328]{1,0:T(8,128)}) fusion(f32[259,3328]{1,0:T(8,128)S(1)} %maximum_convert_fusion, f32[256,3328]{1,0:T(8,128)} %get-tuple-element.251, f32[256,128]{1,0:T(8,128)} %convolution_add_fusion.1, ...), kind=kLoop, calls=%fused_computation.117 | loop fusion | flops 17022720 | bytes 23921664 | tf_op jit(solution)/shard_map/transpose(jvp())/reduce_sum | solution.py:495
  499.4 3.0 broadcast_multiply_fusion.1
  504.2 3.9 collective-permute-start.1
  511.0 2.3 fusion.46
  514.0 4.9 concatenate.55
  519.2 10.0 %fusion.70 = (f32[1536]{0:T(1024)S(1)}, f32[256]{0:T(256)S(1)}, bf16[256,1536]{1,0:T(8,128)(2,1)S(1)}, f32[256,1536]{1,0:T(8,128)S(1)}) fusion(bf16[1,256,1536]{2,1,0:T(8,128)(2,1)} %param.15, f32[256]{0:T(256)S(1)} %copy-done.54, f32[1536]{0:T(1024)S(1)} %copy-done.43, bf16[256,6656]{1,0:T(8,128)(2,1)S(1)} %concatenate.55, ...), kind=kOutput, calls=%fused_computation.160 | convolution fusion | flops 5248251904 | bytes 27028480 | tf_op jit(solution)/shard_map/tj,dj->td/dot_general | solution.py:590
  539.3 10.0 %convolution_convert_fusion = bf16[768,6656]{1,0:T(8,128)(2,1)} fusion(bf16[256,6656]{1,0:T(8,128)(2,1)} %collective-permute-done.3, bf16[256,6656]{1,0:T(8,128)(2,1)S(1)} %concatenate.55, bf16[256,768]{1,0:T(8,128)(2,1)S(1)} %collective-permute-done.2, bf16[256,768]{1,0:T(8,128)(2,1)S(1)} %get-tuple-element.279), kind=kOutput, calls=%fused_computation.81 | convolution fusion | flops 5254807552 | bytes 17825792 | tf_op jit(solution)/shard_map/td,tj->dj/dot_general | solution.py:592
  549.3 95.9 %scatter_gradients.1 = (f32[16,6656]{1,0:T(8,128)}, f32[24,1536]{1,0:T(8,128)}, f32[176,128]{1,0:T(8,128)}) custom-call(bf16[2,4,2,3,16,6656]{5,4,3,2,1,0:T(8,128)(2,1)} %bitcast.504, bf16[2,4,2,3,32,1536]{5,4,3,2,1,0:T(8,128)(2,1)} %bitcast.509, f32[176,128]{1,0:T(8,128)} %bitcast.49.refs_2_), custom_call_target="tpu_custom_call" | custom-call | tf_op jit(solution)/shard_map/scatter_gradients/pallas_call | solution.py:400
  649.4 1.8 slice.402
  (329 shorter events, 157.6 us)
Async XLA Ops:
  0.7 109.6 %copy-start.37 = (bf16[6656]{0:T(1024)(128)(2,1)}, bf16[6656]{0:T(1024)(128)(2,1)S(1)}, u32[]{:S(2)}) copy-start(bf16[6656]{0:T(1024)(128)(2,1)S(1)} %fusion.128) | copy-start | bytes 39940
  88.4 3.5 copy-start
  93.0 35.0 %copy-start.13 = (f32[128,12,128]{2,1,0:T(8,128)}, f32[128,12,128]{2,1,0:T(8,128)S(1)}, u32[]{:S(2)}) copy-start(f32[128,12,128]{2,1,0:T(8,128)S(1)} %reshape.397) | copy-start | bytes 2359300
  93.4 17.2 %copy-start.42 = (f32[1536]{0:T(1024)}, f32[1536]{0:T(1024)S(1)}, u32[]{:S(2)}) copy-start(f32[1536]{0:T(1024)S(1)} %mul.814) | copy-start | bytes 18436
  93.4 16.9 %copy-start.10 = (bf16[1,256,1536]{2,1,0:T(8,128)(2,1)S(1)}, bf16[1,256,1536]{2,1,0:T(8,128)(2,1)}, u32[]{:S(2)}) copy-start(bf16[1,256,1536]{2,1,0:T(8,128)(2,1)} %param.15) | copy-start | bytes 2359300
  110.5 9.8 %copy-start.47 = (f32[256]{0:T(256)}, f32[256]{0:T(256)S(1)}, u32[]{:S(2)}) copy-start(f32[256]{0:T(256)S(1)} %fusion.71) | copy-start | bytes 3076
  110.5 9.8 %copy-start.53 = (f32[256]{0:T(256)}, f32[256]{0:T(256)S(1)}, u32[]{:S(2)}) copy-start(f32[256]{0:T(256)S(1)} %fusion.129) | copy-start | bytes 3076
  110.5 13.8 %copy-start.61 = (f32[48]{0:T(128)S(1)}, f32[48]{0:T(128)}, u32[]{:S(2)}) copy-start(f32[48]{0:T(128)} %param.24) | copy-start | bytes 580
  110.6 14.3 %copy-start.49 = (f32[48]{0:T(128)S(1)}, f32[48]{0:T(128)}, u32[]{:S(2)}) copy-start(f32[48]{0:T(128)} %param.23) | copy-start | bytes 580
  120.4 3.9 copy-start.19
  120.4 14.0 %collective-permute-start = (bf16[3,3328]{1,0:T(4,128)(2,1)S(1)}, bf16[3,3328]{1,0:T(4,128)(2,1)}, u32[]{:S(2)}, u32[]{:S(2)}) collective-permute-start(bf16[3,3328]{1,0:T(4,128)(2,1)S(1)} %slice.447), channel_id=1, source_target_pairs={{0,1},{1,2},{2,3},{3,4},{4,5},{5,6},{6,7},{7,8},{8,9},{9,10},{10,1... | collective-permute-start | bytes 59912 | tf_op jit(solution)/shard_map/ppermute | solution.py:427
  124.4 9.9 %copy-start.16 = (f32[256,48]{0,1:T(8,128)}, f32[256,48]{0,1:T(8,128)S(1)}, u32[]{:S(2)}) copy-start(f32[256,48]{0,1:T(8,128)S(1)} %copy.187) | copy-start | bytes 147460
  125.6 8.7 %copy-start.14 = (f32[48,2,128]{2,0,1:T(8,128)}, f32[48,2,128]{2,0,1:T(8,128)S(1)}, u32[]{:S(2)}) copy-start(f32[48,2,128]{2,0,1:T(8,128)S(1)} %reduce-window.20) | copy-start | bytes 147460
  125.8 8.5 %copy-start.44 = (f32[48,2]{0,1:T(2,128)}, f32[48,2]{0,1:T(2,128)S(1)}, u32[]{:S(2)}) copy-start(f32[48,2]{0,1:T(2,128)S(1)} %slice.387) | copy-start | bytes 1156
  126.5 7.8 %copy-start.51 = (f32[48]{0:T(128)}, f32[48]{0:T(128)S(1)}, u32[]{:S(2)}) copy-start(f32[48]{0:T(128)S(1)} %slice_reduce_fusion.10) | copy-start | bytes 580
  149.4 28.0 %all-to-all-start = ((f32[32,104,128]{2,1,0:T(8,128)}), f32[32,104,128]{2,1,0:T(8,128)}, u32[]{:S(2)}, u32[]{:S(2)}) async-start(f32[32,104,128]{2,1,0:T(8,128)} %fusion.67), calls=%async_computation | async-start | bytes 3407872 | tf_op jit(solution)/shard_map/all_to_all | solution.py:436
  249.2 28.8 %all-to-all-start.1 = ((f32[32,96,128]{2,1,0:T(8,128)}), f32[32,96,128]{2,1,0:T(8,128)}, u32[]{:S(2)}, u32[]{:S(2)}) async-start(f32[32,96,128]{2,1,0:T(8,128)} %bitcast.505), calls=%async_computation.1 | async-start | bytes 3145728 | tf_op jit(solution)/shard_map/all_to_all | solution.py:444
  255.7 171.6 %collective-permute-start.5 = (bf16[256,1536]{1,0:T(8,128)(2,1)}, bf16[256,1536]{1,0:T(8,128)(2,1)}, u32[]{:S(2)}, u32[]{:S(2)}) collective-permute-start(bf16[256,1536]{1,0:T(8,128)(2,1)} %bitcast.513), channel_id=1, source_target_pairs={{0,1},{1,0},{2,3},{3,2},{4,5},{5,4},{6,7},{7,6},{8,9},{9,8},{10,11... | collective-permute-start | bytes 2359304 | tf_op jit(solution)/shard_map/ppermute | solution.py:506
  270.4 10.6 %copy-start.62 = (f32[48]{0:T(128)S(1)}, f32[48]{0:T(128)}, u32[]{:S(2)}) copy-start(f32[48]{0:T(128)} %param.25) | copy-start | bytes 580
  278.0 3.1 copy-start.2
  278.0 3.1 copy-start.9
  278.0 3.1 copy-start.26
  281.0 12.8 %copy-start.6 = (f32[256,48,64]{0,2,1:T(8,128)}, f32[256,48,64]{0,2,1:T(8,128)S(1)}, u32[]{:S(2)}) copy-start(f32[256,48,64]{0,2,1:T(8,128)S(1)} %fusion.104) | copy-start | bytes 9437188
  297.4 3.9 copy-start.21
  297.4 3.9 copy-start.39
  301.3 6.5 copy-start.1
  301.3 6.5 copy-start.5
  323.0 47.4 %all-to-all-start.2 = ((f32[32,104,128]{2,1,0:T(8,128)}), f32[32,104,128]{2,1,0:T(8,128)}, u32[]{:S(2)}, u32[]{:S(2)}) async-start(f32[32,104,128]{2,1,0:T(8,128)} %fusion.68), calls=%async_computation.2 | async-start | bytes 3407872 | tf_op jit(solution)/shard_map/all_to_all | solution.py:436
  338.2 8.1 %copy-start.40 = (f32[3072]{0:T(1024)S(1)}, f32[3072]{0:T(1024)}, u32[]{:S(2)}) copy-start(f32[3072]{0:T(1024)} %get-tuple-element.241) | copy-start | bytes 36868
  349.6 77.8 %collective-permute-start.4 = (bf16[256,1536]{1,0:T(8,128)(2,1)}, bf16[256,1536]{1,0:T(8,128)(2,1)}, u32[]{:S(2)}, u32[]{:S(2)}) collective-permute-start(bf16[256,1536]{1,0:T(8,128)(2,1)} %get-tuple-element.277), channel_id=1, source_target_pairs={{0,1},{1,0},{2,3},{3,2},{4,5},{5,4},{6,7},{7,6},{8,9},{9,8},{10,11... | collective-permute-start | bytes 2359304 | tf_op jit(solution)/shard_map/ppermute | solution.py:506
  351.2 17.4 %copy-start.24 = (f32[256,128]{1,0:T(8,128)S(1)}, f32[256,128]{1,0:T(8,128)}, u32[]{:S(2)}) copy-start(f32[256,128]{1,0:T(8,128)} %convolution_bitcast_fusion.1) | copy-start | bytes 393220
  407.8 29.7 %all-to-all-start.3 = ((f32[32,96,128]{2,1,0:T(8,128)}), f32[32,96,128]{2,1,0:T(8,128)}, u32[]{:S(2)}, u32[]{:S(2)}) async-start(f32[32,96,128]{2,1,0:T(8,128)} %bitcast.506), calls=%async_computation.3 | async-start | bytes 3145728 | tf_op jit(solution)/shard_map/all_to_all | solution.py:444
  415.7 4.4 copy-start.7
  415.7 4.4 copy-start.11
  420.1 7.3 %copy-start.20 = (bf16[256,1536]{1,0:T(8,128)(2,1)S(1)}, bf16[256,1536]{1,0:T(8,128)(2,1)}, u32[]{:S(2)}) copy-start(bf16[256,1536]{1,0:T(8,128)(2,1)} %get-tuple-element.276) | copy-start | bytes 2359300
  420.1 7.3 %copy-start.22 = (bf16[1,256,1536]{2,1,0:T(8,128)(2,1)S(1)}, bf16[1,256,1536]{2,1,0:T(8,128)(2,1)}, u32[]{:S(2)}) copy-start(bf16[1,256,1536]{2,1,0:T(8,128)(2,1)} %param.16) | copy-start | bytes 2359300
  437.5 5.7 copy-start.3
  437.5 5.7 copy-start.29
  443.2 12.9 %copy-start.45 = (f32[48,2]{0,1:T(2,128)S(1)}, f32[48,2]{0,1:T(2,128)}, u32[]{:S(2)}) copy-start(f32[48,2]{0,1:T(2,128)} %copy-done.44) | copy-start | bytes 1156
  443.2 12.9 %copy-start.50 = (f32[48]{0:T(128)S(1)}, f32[48]{0:T(128)}, u32[]{:S(2)}) copy-start(f32[48]{0:T(128)} %param.23) | copy-start | bytes 580
  491.9 7.4 %copy-start.32 = (f32[3328]{0:T(1024)S(1)}, f32[3328]{0:T(1024)}, u32[]{:S(2)}) copy-start(f32[3328]{0:T(1024)} %mul.821) | copy-start | bytes 39940
  502.4 5.6 copy-start.15
  502.4 5.6 copy-start.17
  502.4 5.6 copy-start.25
  502.4 5.6 copy-start.27
  502.4 5.6 copy-start.28
  502.5 5.6 copy-start.41
  502.5 5.6 copy-start.52
  502.5 5.6 copy-start.55
  502.5 5.6 copy-start.56
  502.5 5.6 copy-start.58
  502.5 6.4 copy-start.35
  504.2 6.8 %collective-permute-start.1 = (bf16[3,3328]{1,0:T(4,128)(2,1)}, bf16[3,3328]{1,0:T(4,128)(2,1)}, u32[]{:S(2)}, u32[]{:S(2)}) collective-permute-start(bf16[3,3328]{1,0:T(4,128)(2,1)} %slice.554), channel_id=1, source_target_pairs={{1,0},{2,1},{3,2},{4,3},{5,4},{6,5},{7,6},{8,7},{9,8},{10,9},{11,1... | collective-permute-start | bytes 59912 | tf_op jit(solution)/shard_map/ppermute | solution.py:427
  514.0 5.2 copy-start.38
  514.0 5.3 copy-start.43
  514.0 5.3 copy-start.54
  518.8 12.3 %copy-start.46 = (f32[3072]{0:T(1024)S(1)}, f32[3072]{0:T(1024)}, u32[]{:S(2)}) copy-start(f32[3072]{0:T(1024)} %get-tuple-element.197) | copy-start | bytes 36868
  518.8 13.6 %copy-start.59 = (f32[48]{0:T(128)S(1)}, f32[48]{0:T(128)}, u32[]{:S(2)}) copy-start(f32[48]{0:T(128)} %get-tuple-element.281) | copy-start | bytes 580
  518.9 16.2 %copy-start.60 = (f32[48]{0:T(128)S(1)}, f32[48]{0:T(128)}, u32[]{:S(2)}) copy-start(f32[48]{0:T(128)} %reduce_sum.266) | copy-start | bytes 580
  518.9 18.8 %copy-start.48 = (f32[256]{0:T(256)S(1)}, f32[256]{0:T(256)}, u32[]{:S(2)}) copy-start(f32[256]{0:T(256)} %copy-done.47) | copy-start | bytes 3076
  518.9 18.8 %copy-start.12 = (bf16[1,256,1536]{2,1,0:T(8,128)(2,1)S(1)}, bf16[1,256,1536]{2,1,0:T(8,128)(2,1)}, u32[]{:S(2)}) copy-start(bf16[1,256,1536]{2,1,0:T(8,128)(2,1)} %param.15) | copy-start | bytes 2359300
  518.9 18.8 %copy-start.23 = (bf16[1,256,1536]{2,1,0:T(8,128)(2,1)S(1)}, bf16[1,256,1536]{2,1,0:T(8,128)(2,1)}, u32[]{:S(2)}) copy-start(bf16[1,256,1536]{2,1,0:T(8,128)(2,1)} %param.16) | copy-start | bytes 2359300
  518.9 20.4 %collective-permute-start.3 = (bf16[256,6656]{1,0:T(8,128)(2,1)S(1)}, bf16[256,6656]{1,0:T(8,128)(2,1)}, u32[]{:S(2)}, u32[]{:S(2)}) collective-permute-start(bf16[256,6656]{1,0:T(8,128)(2,1)S(1)} %concatenate.55), channel_id=1, source_target_pairs={{0,1},{1,0},{2,3},{3,2},{4,5},{5,4},{6,7},{7,6},{8,9},{9,8},{10,11... | collective-permute-start | bytes 10223624 | tf_op jit(solution)/shard_map/ppermute | solution.py:506
  529.4 9.9 %collective-permute-start.2 = (bf16[256,768]{1,0:T(8,128)(2,1)S(1)}, bf16[256,768]{1,0:T(8,128)(2,1)S(1)}, u32[]{:S(2)}, u32[]{:S(2)}) collective-permute-start(bf16[256,768]{1,0:T(8,128)(2,1)S(1)} %get-tuple-element.280), channel_id=1, source_target_pairs={{0,1},{1,0},{2,3},{3,2},{4,5},{5,4},{6,7},{7,6},{8,9},{9,8},{10,11... | collective-permute-start | bytes 1179656 | tf_op jit(solution)/shard_map/ppermute | solution.py:506
  (9 other events, 14.9 us)

commit v2 on v1

--- a/solution.py
+++ b/solution.py
@@ -411,7 +411,6 @@
 
 H = 48
 P_SIZE = 64
-NS = 128
 KW = 4
 DI = 3072
 CONVC = 3328
@@ -420,86 +419,408 @@
 PARAMS = 6528
 SEQ = ("y", "x", "c")
 epsilon = 1e-05
-highest = lax.Precision.HIGHEST
-
-
-def from_behind(value, steps):
-    return lax.ppermute(value, SEQ, [(k, k + steps) for k in range(max(0, -steps), min(32, 32 - steps))])
-
-
-def carried_in(decay, state, backward):
-    mine = lax.axis_index(SEQ)
-    rows = H * P_SIZE // 32
-    spread = jnp.repeat(decay, P_SIZE).reshape(32, 1, rows)
-    spread = jnp.pad(spread, ((0, 0), (0, 7), (0, 128 - rows)))
-    packed = jnp.concatenate([state.reshape(32, rows, NS), spread], axis=1)
-    blocks = lax.all_to_all(packed, SEQ, split_axis=0, concat_axis=0, tiled=True)
-    decays = blocks[:, rows, :rows]
-    states = blocks[:, :rows]
-
-    def lap(carry, piece):
-        return piece[0][:, None] * carry + piece[1], carry
-
-    _, before = lax.scan(lap, jnp.zeros((rows, NS), jnp.float32), (decays, states), reverse=backward, unroll=8)
-    back = lax.all_to_all(before, SEQ, split_axis=0, concat_axis=0, tiled=True)
-    return back.reshape(H, P_SIZE, NS)
-
+
+
+TILES = 24
+
+
+def dot(a, b):
+    return jnp.dot(a, b, preferred_element_type=jnp.float32)
+
+
+def dot_nt(a, b):
+    return lax.dot_general(a, b, (((1,), (1,)), ((), ())), preferred_element_type=jnp.float32)
+
+
+def dot_tn(a, b):
+    return lax.dot_general(a, b, (((0,), (0,)), ((), ())), preferred_element_type=jnp.float32)
+
+
+def low(v):
+    return v.astype(jnp.bfloat16)
+
+
+def wide(v):
+    return v.astype(jnp.float32)
+
+
+def split3(v):
+    a = low(v)
+    b = low(v - wide(a))
+    return a, b, low(v - wide(a) - wide(b))
+
+
+def running_sums(v, backward):
+    row = lax.broadcasted_iota(jnp.int32, (256, 256), 0)
+    col = lax.broadcasted_iota(jnp.int32, (256, 256), 1)
+    ones = low(jnp.where(row <= col if backward else row >= col, 1.0, 0.0))
+    return sum(dot(ones, part) for part in split3(v))
+
+
+def sigmoid(v):
+    return 1.0 / (1.0 + jnp.exp(-v))
+
+
+def mixer_kernel(proj, db, taps, gain, skip, heads, branch, dproj, sums, headsums,
+                 act, mixed, ys, dys, dxs, shift, halo_out, halo_in, back_out, back_in,
+                 cum, ecum, toward, steps, rows_a, scores, dscores, usum, qin, qw, prods, stat, coef, db_in, dc_in,
+                 snd, rcv, ret, inc, snd2, rcv2, ret2, inc2,
+                 a_send, a_recv, h_sem):
+    f32, bf16 = jnp.float32, jnp.bfloat16
+    z = lax.axis_index("z")
+    me = 8 * lax.axis_index("y") + 2 * lax.axis_index("x") + lax.axis_index("c")
+    lane = lax.broadcasted_iota(jnp.int32, (256, 128), 1)
+    first_head = lane < 64
+
+    def device(k):
+        return (z, k // 8, lax.rem(k // 2, 4), lax.rem(k, 2))
+
+    def others(body):
+        def step(k, carry):
+            body(lax.rem(me + k, 32))
+            return carry
+        lax.fori_loop(1, 32, step, 0)
+
+    barrier = pltpu.get_barrier_semaphore()
+    others(lambda k: pl.semaphore_signal(barrier, inc=1, device_id=device(k), device_id_type=MESH))
+    pl.semaphore_wait(barrier, 31)
+
+    def exchange(e, source, target, own):
+        def go(k):
+            pltpu.make_async_remote_copy(
+                src_ref=source(k), dst_ref=target(me), send_sem=a_send.at[e, k], recv_sem=a_recv.at[e, me],
+                device_id=device(k), device_id_type=MESH).start()
+        others(go)
+        own()
+
+    def arrived(e, target):
+        others(lambda k: pltpu.make_async_copy(target(k), target(k), a_recv.at[e, k]).wait())
+
+    def left(e, source):
+        others(lambda k: pltpu.make_async_copy(source(k), source(k), a_send.at[e, k]).wait())
+
+    def neighbour(k, src, dst, steps_, on):
+        made = pltpu.make_async_remote_copy(
+            src_ref=src, dst_ref=dst, send_sem=h_sem.at[2 * k], recv_sem=h_sem.at[2 * k + 1],
+            device_id=device(lax.rem(me + steps_ + 32, 32)), device_id_type=MESH)
+        pl.when(on)(made.start)
+        return made
+
+    halo_out[...] = low(proj[240:256, DI:DI + CONVC])
+    front = neighbour(0, halo_out, halo_in, 1, me < 31)
+
+    raw = proj[:, DI + CONVC:DI + CONVC + 128] + heads[0:1, :]
+    dt = jnp.maximum(raw, 0.0) + jnp.log1p(jnp.exp(-jnp.abs(raw)))
+    total = running_sums(-heads[1:2, :] * dt, False)
+    last = total[255:256, :]
+    steps[...] = dt
+    cum[...] = total
+    ecum[...] = jnp.exp(total)
+    toward[...] = jnp.exp(last - total) * dt
+    rows_a[...] = jnp.transpose(total - jnp.log(dt))
+
+    @pl.when(me == 0)
+    def _():
+        halo_in[...] = jnp.zeros((16, CONVC), bf16)
+
+    pl.when(me > 0)(front.wait_recv)
+
+    def cols(j):
+        return pl.ds(pl.multiple_of(128 * j, 128), 128)
+
+    def conv(j, carry):
+        shift[0:8, :] = wide(halo_in[:, cols(j)])[8:16, :]
+        shift[8:264, :] = wide(low(proj[:, pl.ds(pl.multiple_of(DI + 128 * j, 128), 128)]))
+        total = taps[4:5, cols(j)] + taps[0:1, cols(j)] * shift[5:261, :]
+        for k in range(1, 4):
+            total = total + taps[k:k + 1, cols(j)] * shift[5 + k:261 + k, :]
+        mixed[j] = total
+        act[j] = low(total * sigmoid(total))
+        return carry
+
+    lax.fori_loop(0, TILES + 2, conv, 0)
+    b_in, c_out = act[TILES], act[TILES + 1]
+    scores[...] = dot_nt(c_out, b_in)
+
+    def pick(ref, j):
+        turned = pltpu.roll(ref[...], lax.rem(128 - 2 * j, 128), 1)
+        return jnp.broadcast_to(turned[:, 0:1], (256, 128)), jnp.broadcast_to(turned[:, 1:2], (256, 128))
+
+    def spread(ref, j):
+        one, two = pick(ref, j)
+        return jnp.where(first_head, one, two)
+
+    def by_head(v):
+        zero = jnp.zeros_like(v)
+        return jnp.where(first_head[:v.shape[0]], v, zero), jnp.where(first_head[:v.shape[0]], zero, v)
+
+    def fold(acc, prod, j):
+        row = lax.broadcasted_iota(jnp.int32, (256, 128), 0)
+        col = lax.broadcasted_iota(jnp.int32, (256, 128), 1)
+        pickers = low(jnp.where(lax.rem(row, 128) // 64 + 2 * j == col, 1.0, 0.0))
+        top = low(prod)
+        both = jnp.concatenate([top, low(prod - wide(top))], axis=1)
+        acc[...] += dot(both, pickers)
+
+    def give(buf, j, tile):
+        for g in range(4):
+            q = 4 * j + g
+            buf[q // 3, pl.ds(pl.multiple_of(32 * lax.rem(q, 3), 32), 32), :] = tile[32 * g:32 * g + 32]
+
+    def local_state(j, carry):
+        give(snd, j, low(dot_tn(low(spread(toward, j) * wide(act[j])), b_in)))
+        return carry
+
+    lax.fori_loop(0, TILES, local_state, 0)
+    tail = split3(last)
+    row16 = lax.broadcasted_iota(jnp.int32, (16, 128), 0)
+    decays = jnp.zeros((16, 128), f32)
+    for k in range(3):
+        decays = jnp.where(row16 == k, wide(tail[k]), decays)
+    for k in range(32):
+        snd[k, 96:112, :] = low(decays)
+
+    def whole(ref):
+        return lambda k: ref.at[k]
+
+    def piece(ref):
+        return lambda k: ref.at[pl.ds(pl.multiple_of(96 * k, 32), 96)]
+
+    def keep(dst, src):
+        dst[me] = src[me]
+
+    exchange(0, whole(snd), whole(rcv), lambda: keep(rcv, snd))
+
+    row = lax.broadcasted_iota(jnp.int32, (128, 128), 0)
+    col = lax.broadcasted_iota(jnp.int32, (128, 128), 1)
+    causal = row >= col
+
+    def weights(j):
+        out = []
+        for k, own in enumerate(pick(cum, j)):
+            line = rows_a[pl.ds(2 * j + k, 1), :]
+            first, second = own[:128], own[128:]
+            out.append((
+                jnp.exp(jnp.where(causal, first - line[:, :128], -1e30)),
+                jnp.exp(second - line[:, :128]),
+                jnp.exp(jnp.where(causal, second - line[:, 128:], -1e30))))
+        return out
+
+    places = ((slice(0, 128), slice(0, 128)), (slice(128, 256), slice(0, 128)), (slice(128, 256), slice(128, 256)))
+
+    def mixing(gaps):
+        return [[low(scores[r, c] * gap) for (r, c), gap in zip(places, head)] for head in gaps]
+
+    def inside(j, carry):
+        m = mixing(weights(j))
+        xa, xb = by_head(act[j])
+        top = dot(jnp.concatenate([m[0][0], m[1][0]], axis=1), jnp.concatenate([xa[:128], xb[:128]], axis=0))
+        low_ = dot(jnp.concatenate([m[0][1], m[0][2], m[1][1], m[1][2]], axis=1), jnp.concatenate([xa, xb], axis=0))
+        ys[j, 0:128, :] = top
+        ys[j, 128:256, :] = low_
+        return carry
+
+    head_a = 3 * me // 2
+    edge = jnp.where(lax.rem(me, 2) == 0, 64, 32)
+    row96 = lax.broadcasted_iota(jnp.int32, (96, 128), 0)
+
+    def scan(got, out, backward):
+        carry = jnp.zeros((96, 128), f32)
+        for k in (range(31, -1, -1) if backward else range(32)):
+            line = wide(rcv[k, 96:112, :])
+            line = jnp.exp(line[0:1] + line[1:2] + line[2:3])
+            line = pltpu.roll(jnp.broadcast_to(line, (8, 128)), lax.rem(128 - head_a, 128), 1)
+            factor = jnp.where(row96 < edge, jnp.broadcast_to(line[0:1, 0:1], (96, 128)), jnp.broadcast_to(line[0:1, 1:2], (96, 128)))
+            out[k] = low(carry)
+            carry = factor * carry + wide(got[k, 0:96, :])
+
+    lax.fori_loop(0, TILES // 2, inside, 0)
+    arrived(0, whole(rcv))
+    scan(rcv, ret, False)
+
+    def keep_flat(dst, src):
+        dst[pl.ds(pl.multiple_of(96 * me, 32), 96), :] = src[me]
+
+    exchange(1, whole(ret), piece(inc), lambda: keep_flat(inc, ret))
+    lax.fori_loop(TILES // 2, TILES, inside, 0)
+    arrived(1, piece(inc))
+
+    def state(ref, j):
+        return ref[pl.ds(pl.multiple_of(128 * j, 128), 128), :]
+
+    def gate(j, y):
+        gz = proj[:, cols(j)]
+        sig = sigmoid(gz)
+        full = y + skip[:, cols(j)] * wide(act[j])
+        return gz, sig, full, full * gz * sig
+
+    stat[...] = jnp.zeros((256, 128), f32)
+    coef[...] = jnp.zeros((256, 128), f32)
+
+    def gate_sums(j, carry):
+        y = ys[j] + spread(ecum, j) * dot_nt(c_out, state(inc, j))
+        ys[j] = y
+        _, _, _, gated = gate(j, y)
+        stat[...] += gated * gated
+        coef[...] += gated * (gain[:, cols(j)] * db[:, cols(j)])
+        return carry
+
+    lax.fori_loop(0, TILES, gate_sums, 0)
+    scale = lax.rsqrt(jnp.sum(stat[...], axis=1, keepdims=True) * (1.0 / DI) + epsilon)
+    factor = scale * scale * scale * (jnp.sum(coef[...], axis=1, keepdims=True) * (1.0 / DI))
+    stat[...] = jnp.broadcast_to(scale, (256, 128))
+    coef[...] = jnp.broadcast_to(factor, (256, 128))
+    sums[...] = jnp.zeros((8, CONVC), f32)
+
+    def gate_back(j, carry):
+        y = ys[j]
+        gz, sig, full, gated = gate(j, y)
+        scaled = gated * stat[...]
+        branch[:, cols(j)] = low(scaled * gain[:, cols(j)])
+        given = db[:, cols(j)]
+        sums[5:6, cols(j)] = jnp.sum(scaled * given, axis=0, keepdims=True)
+        d_gated = stat[...] * gain[:, cols(j)] * given - gated * coef[...]
+        dproj[:, cols(j)] = low(d_gated * full * (sig * (1.0 + gz * (1.0 - sig))))
+        dy = low(d_gated * gz * sig)
+        dys[j] = dy
+        dyf = wide(dy)
+        sums[6:7, cols(j)] = jnp.sum(dyf * wide(act[j]), axis=0, keepdims=True)
+        give(snd2, j, low(dot_tn(low(spread(ecum, j) * dyf), c_out)))
+        return carry
+
+    lax.fori_loop(0, TILES, gate_back, 0)
+    exchange(2, whole(snd2), whole(rcv2), lambda: keep(rcv2, snd2))
+    for ref in (usum, qin, qw):
+        ref[...] = jnp.zeros((256, 128), f32)
+    dscores[...] = jnp.zeros((256, 256), f32)
+    prods[...] = jnp.zeros((128, 128), f32)
+
+    def inside_back(j, carry):
+        gaps = weights(j)
+        m = mixing(gaps)
+        x = act[j]
+        dya, dyb = by_head(dys[j])
+        for k, dy in enumerate((dya, dyb)):
+            near = dot_nt(dy[:128], x[:128])
+            far = dot_nt(dy[128:], x)
+            part = (near, far[:, :128], far[:, 128:])
+            for (r, c), gap, value in zip(places, gaps[k], part):
+                dscores[r, c] += gap * value
+        top = dot_tn(jnp.concatenate([m[0][0], m[0][1], m[1][0], m[1][1]], axis=0), jnp.concatenate([dya, dyb], axis=0))
+        low_ = dot_tn(jnp.concatenate([m[0][2], m[1][2]], axis=0), jnp.concatenate([dya[128:], dyb[128:]], axis=0))
+        dx = jnp.concatenate([top, low_], axis=0)
+        dxs[j] = dx
+        fold(usum, wide(dys[j]) * ys[j], j)
+        fold(qin, wide(x) * dx, j)
+        return carry
+
+    lax.fori_loop(0, TILES // 2, inside_back, 0)
+    arrived(2, whole(rcv2))
+    scan(rcv2, ret2, True)
+    exchange(3, whole(ret2), piece(inc2), lambda: keep_flat(inc2, ret2))
+    lax.fori_loop(TILES // 2, TILES, inside_back, 0)
+    arrived(3, piece(inc2))
+    db_in[...] = jnp.zeros((256, 128), f32)
+    dc_in[...] = jnp.zeros((256, 128), f32)
+
+    def d_mix(j, d_act):
+        m = mixed[j]
+        sig = sigmoid(m)
+        d_m = d_act * (sig * (1.0 + m * (1.0 - sig)))
+        mixed[j] = d_m
+        back_out[:, cols(j)] = low(d_m[0:16])
+
+    def carry_back(j, carry):
+        s_in, d_s = state(inc, j), state(inc2, j)
+        x, dyf = wide(act[j]), wide(dys[j])
+        w = spread(toward, j)
+        d_w = w * dot_nt(b_in, d_s)
+        fold(qw, x * d_w, j)
+        db_in[...] += dot(low(w * x), d_s)
+        dc_in[...] += dot(low(spread(ecum, j) * dyf), s_in)
+        pair = wide(s_in) * wide(d_s)
+        prods[pl.ds(2 * j, 1), :] = jnp.sum(pair[:64], axis=0, keepdims=True)
+        prods[pl.ds(2 * j + 1, 1), :] = jnp.sum(pair[64:], axis=0, keepdims=True)
+        d_mix(j, dxs[j] + d_w + skip[:, cols(j)] * dyf)
+        return carry
+
+    lax.fori_loop(0, TILES, carry_back, 0)
+    ds = low(dscores[...])
+    d_mix(TILES, db_in[...] + dot_tn(ds, c_out))
+    d_mix(TILES + 1, dc_in[...] + dot(ds, b_in))
+    behind = neighbour(1, back_out, back_in, -1, me > 0)
+
+    q = qin[...] + qw[...]
+    d_last = ecum[255:256, :] * jnp.sum(jnp.transpose(prods[...]), axis=0, keepdims=True) + jnp.sum(qw[...], axis=0, keepdims=True)
+    at_end = lax.broadcasted_iota(jnp.int32, (256, 128), 0) == 255
+    d_l = running_sums(usum[...] - q + jnp.where(at_end, d_last, 0.0), True)
+    dt = steps[...]
+    raw = proj[:, DI + CONVC:DI + CONVC + 128] + heads[0:1, :]
+    d_raw = (q / jnp.maximum(dt, 1e-30) - heads[1:2, :] * d_l) * sigmoid(raw)
+    d_raw = jnp.where(lane < H, d_raw, 0.0)
+    headsums[...] = jnp.zeros((8, 128), f32)
+    headsums[0:1, :] = jnp.sum(d_raw, axis=0, keepdims=True)
+    headsums[1:2, :] = -jnp.sum(d_l * dt, axis=0, keepdims=True)
+    dproj[:, DI + CONVC:DI + CONVC + 128] = low(d_raw)
+    dproj[:, DI + CONVC + 128:] = jnp.zeros((256, 128), bf16)
+
+    @pl.when(me == 31)
+    def _():
+        back_in[...] = jnp.zeros((16, CONVC), bf16)
+
+    pl.when(me < 31)(behind.wait_recv)
+
+    def conv_back(j, carry):
+        d_m = mixed[j]
+        shift[0:8, :] = wide(halo_in[:, cols(j)])[8:16, :]
+        shift[8:264, :] = wide(low(proj[:, pl.ds(pl.multiple_of(DI + 128 * j, 128), 128)]))
+        for k in range(4):
+            sums[k:k + 1, cols(j)] = jnp.sum(d_m * shift[5 + k:261 + k, :], axis=0, keepdims=True)
+        sums[4:5, cols(j)] = jnp.sum(d_m, axis=0, keepdims=True)
+        shift[0:256, :] = d_m
+        shift[256:264, :] = wide(back_in[:, cols(j)])[0:8, :]
+        total = taps[3:4, cols(j)] * d_m
+        for k in range(3):
+            total = total + taps[k:k + 1, cols(j)] * shift[3 - k:259 - k, :]
+        dproj[:, pl.ds(pl.multiple_of(DI + 128 * j, 128), 128)] = low(total)
+        return carry
+
+    lax.fori_loop(0, TILES + 2, conv_back, 0)
+    pl.when(me < 31)(front.wait_send)
+    pl.when(me > 0)(behind.wait_send)
+    left(0, whole(snd))
+    left(1, whole(ret))
+    left(2, whole(snd2))
+    left(3, whole(ret2))
+
+
+def mixer(projected, d_branch, taps, gain, skip, heads):
+    f32, bf16 = jnp.float32, jnp.bfloat16
+    tile, half = (256, 128), (16, CONVC)
+    vm = pltpu.VMEM
+    scratch = [
+        vm((TILES + 2,) + tile, bf16), vm((TILES + 2,) + tile, f32), vm((TILES,) + tile, f32), vm((TILES,) + tile, bf16),
+        vm((TILES,) + tile, f32), vm((264, 128), f32), vm(half, bf16), vm(half, bf16), vm(half, bf16), vm(half, bf16),
+        vm(tile, f32), vm(tile, f32), vm(tile, f32), vm(tile, f32), vm((128, 256), f32), vm((256, 256), f32), vm((256, 256), f32),
+        vm(tile, f32), vm(tile, f32), vm(tile, f32), vm((128, 128), f32), vm(tile, f32), vm(tile, f32), vm(tile, f32), vm(tile, f32),
+    ]
+    for _ in range(2):
+        scratch += [vm((32, 112, 128), bf16), vm((32, 112, 128), bf16), vm((32, 96, 128), bf16), vm((3072, 128), bf16)]
+    scratch += [pltpu.SemaphoreType.DMA((4, 32)), pltpu.SemaphoreType.DMA((4, 32)), pltpu.SemaphoreType.DMA((4,))]
+    spec = pl.BlockSpec(memory_space=pltpu.VMEM)
+    return pl.pallas_call(
+        mixer_kernel,
+        out_shape=[jax.ShapeDtypeStruct((256, DI), bf16), jax.ShapeDtypeStruct((256, WIDE), bf16),
+                   jax.ShapeDtypeStruct((8, CONVC), f32), jax.ShapeDtypeStruct((8, 128), f32)],
+        in_specs=[spec] * 6,
+        out_specs=[spec] * 4,
+        scratch_shapes=scratch,
+        compiler_params=pltpu.CompilerParams(collective_id=2, has_side_effects=True, vmem_limit_bytes=60 << 20),
+        name="mixer",
+    )(projected, d_branch, taps, gain, skip, heads)
 
 def rms_scale(values, gain):
     return values * lax.rsqrt(jnp.mean(values * values, axis=-1, keepdims=True) + epsilon) * gain
-
-
-def span_step(heads_x, b_in, c_out, steps_dt, neg_rate):
-    block_len = heads_x.shape[0]
-    log_decay = steps_dt * neg_rate[None, :]
-    cum_decay = jnp.cumsum(log_decay, axis=0)
-    position = jnp.arange(block_len)
-    causal = (position[:, None] >= position[None, :]).astype(jnp.float32)
-    gap_decay = (
-        jnp.exp((cum_decay[:, None, :] - cum_decay[None, :, :]) * causal[:, :, None])
-        * causal[:, :, None]
-    )
-    scores = jnp.dot(c_out, b_in.T, precision=highest)
-    mixing = scores[:, :, None] * gap_decay * steps_dt[None, :, :]
-    within = jnp.einsum("trh,rhp->thp", mixing, heads_x, precision=highest)
-    last_sum = cum_decay[-1]
-    toward = jnp.exp(last_sum[None, :] - cum_decay) * steps_dt
-    added_in = jnp.einsum("rh,rhp,rn->hpn", toward, heads_x, b_in, precision=highest)
-    return (added_in, within)
-
-
-def local_core(heads_x, b_in, c_out, steps_dt, neg_rate, d_skip):
-    final_state, outputs = span_step(heads_x, b_in, c_out, steps_dt, neg_rate)
-    cum_decay = jnp.cumsum(steps_dt * neg_rate[None, :], axis=0)
-    local_out = outputs + d_skip[None, :, None] * heads_x
-    return (local_out, final_state, jnp.exp(cum_decay[-1]), cum_decay)
-
-
-def correction(c_out, cum_decay, incoming):
-    return jnp.exp(cum_decay)[:, :, None] * jnp.einsum(
-        "tn,hpn->thp", c_out, incoming, precision=highest
-    )
-
-
-def full_mixer(heads_x, b_in, c_out, steps_dt, neg_rate, d_skip, incoming):
-    local_out, final_state, total_decay, cum_decay = local_core(
-        heads_x, b_in, c_out, steps_dt, neg_rate, d_skip
-    )
-    return (local_out + correction(c_out, cum_decay, incoming), final_state, total_decay)
-
-
-def conv_section(extended, w_conv, b_conv, dt_raw, dt_bias, decay_rates):
-    length = dt_raw.shape[0]
-    mixed = jnp.zeros((length, CONVC), jnp.float32) + b_conv[None, :]
-    for offset in range(KW):
-        mixed = mixed + w_conv[offset][None, :] * extended[offset : offset + length]
-    return (jax.nn.silu(mixed), jax.nn.softplus(dt_raw + dt_bias[None, :]), -decay_rates)
-
-
-def gate_section(ssd_out, gate_z, gain_gate):
-    length = gate_z.shape[0]
-    gated = ssd_out.reshape(length, DI) * jax.nn.silu(gate_z)
-    return rms_scale(gated, gain_gate)
 
 
 def swap(value):
@@ -545,57 +866,24 @@
     length = residual.shape[0]
     normed = rms_scale(residual, gain_norm_f).astype(jnp.bfloat16)
     projected = jnp.dot(normed, w_in, preferred_element_type=jnp.float32)
-    gate_z = projected[:, :DI]
-    conv_in = projected[:, DI : DI + CONVC].astype(jnp.bfloat16)
-    dt_raw = projected[:, DI + CONVC : PROJ]
-    edge_rows = from_behind(conv_in[length - (KW - 1) :], 1)
-    extended = jnp.concatenate([edge_rows, conv_in], axis=0).astype(jnp.float32)
-    pre_act, steps_dt, neg_rate = conv_section(
-        extended, w_conv_f, b_conv_f, dt_raw, dt_bias, decay_rates
-    )
-    activated = lax.optimization_barrier(pre_act.astype(jnp.bfloat16)).astype(jnp.float32)
-    heads_x = activated[:, :DI].reshape(length, H, P_SIZE)
-    b_in = activated[:, DI : DI + NS]
-    c_out = activated[:, DI + NS :]
-    local_out, final_state, total_decay, cum_decay = local_core(
-        heads_x, b_in, c_out, steps_dt, neg_rate, d_skip
-    )
-    incoming = carried_in(total_decay, final_state, False)
-    ssd_out = local_out + correction(c_out, cum_decay, incoming)
-    branch = gate_section(ssd_out, gate_z, gain_gate_f).astype(jnp.bfloat16)
-    result = (residual + jnp.dot(branch, w_out, preferred_element_type=jnp.float32)).astype(
-        jnp.bfloat16
-    )
     grad_out = cotangent[0]
     both_out = jnp.concatenate([grad_out, swap(grad_out)], axis=0)
     d_branch = jnp.einsum("td,kd->tk", grad_out, w_out, preferred_element_type=jnp.float32)
+    taps = jnp.pad(jnp.concatenate([w_conv_f, b_conv_f[None]]), ((0, 3), (0, 0)))
+    heads = jnp.pad(jnp.stack([dt_bias, decay_rates]), ((0, 6), (0, 80)))
+    branch, d_projected, sums, head_sums = mixer(
+        projected, d_branch, taps, gain_gate_f[None], jnp.repeat(d_skip, P_SIZE)[None], heads)
+    result = (residual + jnp.dot(branch, w_out, preferred_element_type=jnp.float32)).astype(jnp.bfloat16)
     d_w_out = jnp.einsum("tk,td->kd", my_half(branch, core), both_out, preferred_element_type=jnp.float32).astype(jnp.bfloat16)
-    gate_pull = jax.vjp(gate_section, ssd_out, gate_z, gain_gate_f)[1]
-    d_ssd, d_gate_z, d_gain_gate = gate_pull(d_branch)
-    d_incoming = jnp.einsum("th,thp,tn->hpn", jnp.exp(cum_decay), d_ssd, c_out, precision=highest)
-    carried_back = carried_in(total_decay, d_incoming, True)
-    d_total_decay = jnp.sum(carried_back * incoming, axis=(1, 2))
-    mixer_pull = jax.vjp(full_mixer, heads_x, b_in, c_out, steps_dt, neg_rate, d_skip, incoming)[1]
-    d_heads_x, d_b_in, d_c_out, d_steps, d_rate, d_dskip, unused_grad = mixer_pull(
-        (d_ssd, carried_back, d_total_decay)
-    )
-    d_act = jnp.concatenate([d_heads_x.reshape(length, DI), d_b_in, d_c_out], axis=1)
-    conv_pull = jax.vjp(conv_section, extended, w_conv_f, b_conv_f, dt_raw, dt_bias, decay_rates)[1]
-    d_ext, d_conv_w, d_conv_b, d_dt_raw, d_dt_bias, d_rates = conv_pull((d_act, d_steps, d_rate))
-    back_rows = from_behind(d_ext[: KW - 1].astype(jnp.bfloat16), -1).astype(jnp.float32)
-    d_conv_in = d_ext[KW - 1 :] + jnp.pad(back_rows, ((length - (KW - 1), 0), (0, 0)))
-    d_projected = jnp.concatenate(
-        [d_gate_z, d_conv_in, d_dt_raw, jnp.zeros((length, WIDE - PROJ), jnp.float32)], axis=1
-    ).astype(jnp.bfloat16)
     d_normed = jnp.einsum("tj,dj->td", d_projected, w_in, preferred_element_type=jnp.float32)
     both_projected = jnp.concatenate([d_projected, swap(d_projected)], axis=0)
     d_w_in = jnp.einsum("td,tj->dj", my_half(normed, core), both_projected, preferred_element_type=jnp.float32).astype(jnp.bfloat16)
     norm_pull = jax.vjp(rms_scale, residual, gain_norm_f)[1]
     d_from_norm, d_gain_norm = norm_pull(d_normed)
     d_hidden = grad_out.astype(jnp.float32) + d_from_norm
+    d_skips = jnp.sum(sums[6, :DI].reshape(H, P_SIZE), axis=1)
     small = jnp.concatenate([
-        d_conv_w.reshape(-1), d_conv_b, d_gain_norm, d_gain_gate,
-        jnp.pad(d_dt_bias, (0, 80)), jnp.pad(d_rates, (0, 80)), jnp.pad(d_dskip, (0, 80)),
+        sums[:5].reshape(-1), d_gain_norm, sums[5, :DI], head_sums[:2].reshape(-1), jnp.pad(d_skips, (0, 80)),
         jnp.zeros((896,), jnp.float32),
     ]).reshape(176, 128)
     g_in, g_out, total = scatter([d_w_in, d_w_out], small, [12, 24])

time: 667 us -> 419 us (0.63); the launches traced: 655 us -> 418 us
  other arithmetic: 162 us -> 25.2 us
  Pallas kernels: 180 us -> 296 us
  local copies, waits for them, and re-layouts: 115 us -> 36.2 us
  matrix products: 129 us -> 58.5 us
  waiting for transfers between devices: 33.2 us -> 0.01 us
  starting transfers between devices: 33.5 us -> 0.96 us
    pallas_call x0 -> x1, Pallas kernels: none -> 115 us  [mixer(): pl.pallas_call(mixer_kernel, out_shape=[jax.ShapeDtypeStruct((256, DI), b...]
    dot_general x12 -> x0, matrix products: 79.5 us -> none  [the longest x3 44.1 us: span_step(): within = jnp.einsum('trh,rhp->thp', mixing, heads_x, precision=highest)]
    while x44 -> x0, other arithmetic: 57.2 us -> none
    all_to_all x4 -> x0, waiting for transfers between devices: 33.2 us -> none  [the longest x2 23.5 us: carried_in(): lax.all_to_all(packed, SEQ, split_axis=0, concat_axis=0, tiled=True)]
    all_to_all x4 -> x0, starting transfers between devices: 25.6 us -> none  [the longest x2 14.4 us: carried_in(): back = lax.all_to_all(before, SEQ, split_axis=0, concat_axis=0, tiled=True)]
    reduce_sum x8 -> x1, other arithmetic: 25.1 us -> 1.36 us  [shards(): d_skips = jnp.sum(sums[6, :DI].reshape(H, P_SIZE), axis=1)]
    mul x16 -> x0, local copies, waits for them, and re-layouts: 19.9 us -> none  [the longest x3 9.76 us: correction(): jnp.exp(cum_decay)[:, :, None]]
    slice x13 -> x1, local copies, waits for them, and re-layouts: 19 us -> 1.61 us  [shards(): d_skips = jnp.sum(sums[6, :DI].reshape(H, P_SIZE), axis=1)]
  transfers between devices with their start and end apart: 10 -> 4, of which waited for: 3 -> 0; matrix products, arithmetic and copies ran while one was open for 28% -> 11% of each run, Pallas kernels for 0% -> 0%
where the time goes in v2:
time: 419 us; the launch traced here: 418 us
  Pallas kernels  296 us (71%)
  matrix products  58.5 us (14%)
  local copies, waits for them, and re-layouts  36.2 us (9%)
  other arithmetic  25.2 us (6%)
    pallas_call x1, Pallas kernels, mixer(): pl.pallas_call(mixer_kernel, out_shape=[jax.ShapeDtypeStruct((256, DI), b...  115 us
    pallas_call x1, Pallas kernels, scatter(): pl.pallas_call(functools.partial(scatter_kernel, n=n, rows=tuple(rows), s...  98 us
    pallas_call x1, Pallas kernels, gather(): pl.pallas_call(functools.partial(gather_kernel, n=n, rows=tuple(rows)), o...  83.7 us
    mul x1, other arithmetic, shards(): w_in = w_in * (jnp.arange(WIDE) < PROJ).astype(jnp.bfloat16)[None, :]  16.9 us
    dot_general x1, matrix products, shards(): projected = jnp.dot(normed, w_in, preferred_element_type=jnp.float32)  14.4 us
    dot_general x1, matrix products, shards(): jnp.einsum('tj,dj->td', d_projected, w_in, preferred_element_type=jnp.flo...  12.5 us
    unnamed x32, local copies, waits for them, and re-layouts  11.9 us
    dot_general x1, matrix products, shards(): jnp.einsum('td,tj->dj', my_half(normed, core), both_projected, preferred_...  9.59 us
  transfers between devices with their start and end apart: 4, of which 0 were waited for; matrix products, arithmetic and copies ran while one was open for 11% of the time, Pallas kernels for 0%

profile of v2, /device:TPU:1, one launch (start us, length us, event | category | flops | bytes accessed | tf_op | source)
XLA Modules:
  0.0 418.0 jit_solution(3182971266623965115)
XLA Ops:
  0.7 0.7 pad_bitcast_fusion.2
  1.3 0.7 pad_bitcast_fusion
  2.0 0.7 pad.41
  2.7 0.1 concatenate.24
  2.8 1.0 fusion.37
  3.8 0.9 pad.46.refs_1_
  4.7 83.7 %gather_weights.1 = (bf16[2,2,4,2,3,16,6656]{6,5,4,3,2,1,0:T(8,128)(2,1)}, bf16[2,2,4,2,3,32,1536]{6,5,4,3,2,1,0:T(8,128)(2,1)S(1)}) custom-call(bf16[16,6656]{1,0:T(8,128)(2,1)S(1)} %pad.45.refs_0_, bf16[32,1536]{1,0:T(8,128)(2,1)S(1)} %pad.46.refs_1_), custom_call_target="tpu_custom_call" | custom-call | tf_op jit(solution)/shard_map/gather_weights/pallas_call | solution.py:156
  88.4 3.5 copy-done
  91.9 1.0 slice_convert_fusion
  93.0 0.1 reshape.121
  93.0 0.2 slice_reduce_fusion.2
  93.3 0.2 slice_reduce_fusion.1
  93.5 0.2 slice_reduce_fusion
  93.7 0.1 mul.116
  93.8 0.0 copy-start.1
  93.8 0.0 copy-start.8
  93.9 16.9 %broadcast_multiply_fusion = bf16[2,2,4,2,3,16,6656]{6,5,4,3,2,1,0:T(8,128)(2,1)} fusion(bf16[2,2,4,2,3,16,6656]{6,5,4,3,2,1,0:T(8,128)(2,1)} %get-tuple-element.20, bf16[6656]{0:T(1024)(128)(2,1)S(1)} %fusion.38), kind=kLoop, calls=%fused_computation.4 | loop fusion | flops 10223616 | bytes 40907776 | tf_op jit(solution)/shard_map/mul | solution.py:864
  110.7 0.2 fusion.16
  111.0 0.2 reshape.110
  111.2 0.1 broadcast_in_dim_reshape_squeeze.8
  111.4 0.7 broadcast_in_dim_reshape_squeeze.9.gain
  112.1 0.1 broadcast_in_dim.34
  112.1 0.7 broadcast_in_dim_reshape.3.skip
  112.8 0.7 select_maximum_fusion.taps
  113.5 8.1 %convolution_bitcast_fusion.db = f32[256,3072]{1,0:T(8,128)} fusion(bf16[3072,1536]{1,0:T(8,128)(2,1)} %bitcast.80, bf16[1,256,1536]{2,1,0:T(8,128)(2,1)} %param.12), kind=kOutput, calls=%fused_computation.9 | convolution fusion | flops 2415919104 | bytes 13369344 | tf_op jit(solution)/shard_map/td,kd->tk/dot_general | solution.py:871
  121.6 0.6 select_maximum_fusion.1.heads
  122.2 14.4 %fusion.29.proj = f32[256,6656]{1,0:T(8,128)} fusion(bf16[1536,6656]{1,0:T(8,128)(2,1)} %bitcast.84, bf16[1,256,1536]{2,1,0:T(8,128)(2,1)S(1)} %copy-done.1, f32[1536]{0:T(1024)S(1)} %mul.116, f32[256]{0:T(256)S(1)} %fusion.39), kind=kOutput, calls=%fused_computation.37 | convolution fusion | flops 5236064256 | bytes 28056576 | tf_op jit(solution)/shard_map/dot_general | solution.py:868
  136.6 114.7 %mixer.1 = (bf16[256,3072]{1,0:T(8,128)(2,1)}, bf16[256,6656]{1,0:T(8,128)(2,1)}, f32[8,3328]{1,0:T(8,128)}, f32[8,128]{1,0:T(8,128)}) custom-call(f32[256,6656]{1,0:T(8,128)} %fusion.29.proj, f32[256,3072]{1,0:T(8,128)} %convolution_bitcast_fusion.db, f32[8,3328]{1,0:T(8,128)} %select_maximum_fusion.taps, f32[1,3072]{1,0:T(1,128)} %broadcast_in_dim_reshape_squeeze.9.gain, ...), custom_call_target="tpu_custom_call" | custom-call | tf_op jit(solution)/shard_map/mixer/pallas_call | solution.py:811
  251.3 2.4 constant_dynamic-slice_fusion.2
  253.7 0.0 collective-permute-start.2
  253.7 0.5 collective-permute-start.3
  254.2 0.0 collective-permute-start.1
  254.2 12.5 %fusion.15 = (f32[1536]{0:T(1024)}, f32[256]{0:T(256)}, bf16[256,1536]{1,0:T(8,128)(2,1)}, f32[256,1536]{1,0:T(8,128)}) fusion(bf16[1,256,1536]{2,1,0:T(8,128)(2,1)S(1)} %copy-done.1, f32[256]{0:T(256)S(1)} %fusion.39, f32[1536]{0:T(1024)S(1)} %mul.116, bf16[256,6656]{1,0:T(8,128)(2,1)} %get-tuple-element.23, bf16[1536,6656]{1,0:T(8,128)(2,1)} %bitcast.83, ...), kind=kOutput, calls=%fused_computation.23 | convolution fusion | flops 5248251904 | bytes 27028480 | tf_op jit(solution)/shard_map/tj,dj->td/dot_general | solution.py:878
  266.7 1.9 constant_dynamic-slice_fusion.4
  268.6 0.4 collective-permute-start
  269.1 1.5 reshape.113
  270.6 1.6 slice_reduce_fusion.3
  272.2 1.4 reshape_squeeze.3
  273.6 1.4 reduce_sum.41
  275.0 1.6 constant_dynamic-update-slice_fusion.5
  276.5 1.3 constant_dynamic-update-slice_fusion.4
  277.8 1.3 constant_dynamic-update-slice_fusion.3
  279.2 0.7 multiply_multiply_fusion
  279.9 1.3 constant_dynamic-update-slice_fusion.2
  281.2 7.3 %fusion.7 = bf16[1,256,1536]{2,1,0:T(8,128)(2,1)} fusion(bf16[256,3072]{1,0:T(8,128)(2,1)S(1)} %copy-done.2, bf16[3072,1536]{1,0:T(8,128)(2,1)} %bitcast.81, bf16[1,256,1536]{2,1,0:T(8,128)(2,1)S(1)} %copy-done.1), kind=kOutput, calls=%fused_computation.12 | convolution fusion | flops 2417098752 | bytes 12582912 | tf_op jit(solution)/shard_map/dot_general | solution.py:876
  288.5 1.3 constant_dynamic-update-slice_fusion.1
  289.8 2.7 fusion.21
  292.5 1.3 constant_dynamic-update-slice_fusion
  293.8 0.0 collective-permute-done.2
  293.8 0.0 collective-permute-done.3
  293.8 6.6 %convolution_convert_fusion.1 = bf16[1536,1536]{1,0:T(8,128)(2,1)} fusion(bf16[256,1536]{1,0:T(8,128)(2,1)} %collective-permute-done.2, bf16[256,1536]{1,0:T(8,128)(2,1)S(1)} %get-tuple-element.31, bf16[256,1536]{1,0:T(8,128)(2,1)} %collective-permute-done.3, bf16[256,1536]{1,0:T(8,128)(2,1)} %bitcast.8), kind=kOutput, calls=%fused_computation.5 | convolution fusion | flops 2424569856 | bytes 7864320 | tf_op jit(solution)/shard_map/tk,td->kd/dot_general | solution.py:877
  300.4 9.6 %convolution_convert_fusion = bf16[768,6656]{1,0:T(8,128)(2,1)} fusion(bf16[256,6656]{1,0:T(8,128)(2,1)} %collective-permute-done.1, bf16[256,6656]{1,0:T(8,128)(2,1)S(1)} %copy-done.12, bf16[256,768]{1,0:T(8,128)(2,1)} %collective-permute-done, bf16[256,768]{1,0:T(8,128)(2,1)S(1)} %get-tuple-element.34), kind=kOutput, calls=%fused_computation.2 | convolution fusion | flops 5254807552 | bytes 17825792 | tf_op jit(solution)/shard_map/td,tj->dj/dot_general | solution.py:880
  310.0 98.0 %scatter_gradients.1 = (f32[16,6656]{1,0:T(8,128)}, f32[24,1536]{1,0:T(8,128)}, f32[176,128]{1,0:T(8,128)}) custom-call(bf16[2,4,2,3,16,6656]{5,4,3,2,1,0:T(8,128)(2,1)} %bitcast.85, bf16[2,4,2,3,32,1536]{5,4,3,2,1,0:T(8,128)(2,1)} %bitcast.86, f32[176,128]{1,0:T(8,128)} %bitcast.19.refs_2_), custom_call_target="tpu_custom_call" | custom-call | tf_op jit(solution)/shard_map/scatter_gradients/pallas_call | solution.py:400
  408.0 0.8 slice.61
  408.8 0.7 slice_bitcast_fusion.1
  409.5 0.7 slice_bitcast_fusion.2
  410.3 0.7 slice_bitcast_fusion.3
  411.0 1.3 slice_bitcast_fusion.4
  412.2 1.8 slice.60
  414.1 0.7 constant_dynamic-slice_fusion
  414.7 0.6 dynamic_slice.29
  415.3 0.6 dynamic_slice.31
  415.9 0.6 dynamic_slice.30
  416.5 1.6 copy.33
  (33 shorter events, 0.2 us)
Async XLA Ops:
  88.4 3.5 copy-start
  93.8 160.4 %copy-start.4 = (f32[1536]{0:T(1024)}, f32[1536]{0:T(1024)S(1)}, u32[]{:S(2)}) copy-start(f32[1536]{0:T(1024)S(1)} %mul.116) | copy-start | bytes 18436
  93.8 16.9 %copy-start.1 = (bf16[1,256,1536]{2,1,0:T(8,128)(2,1)S(1)}, bf16[1,256,1536]{2,1,0:T(8,128)(2,1)}, u32[]{:S(2)}) copy-start(bf16[1,256,1536]{2,1,0:T(8,128)(2,1)} %param.11) | copy-start | bytes 2359300
  93.8 18.2 %copy-start.8 = (f32[48]{0:T(128)S(1)}, f32[48]{0:T(128)}, u32[]{:S(2)}) copy-start(f32[48]{0:T(128)} %param.21) | copy-start | bytes 580
  111.0 143.2 %copy-start.6 = (f32[256]{0:T(256)}, f32[256]{0:T(256)S(1)}, u32[]{:S(2)}) copy-start(f32[256]{0:T(256)S(1)} %fusion.39) | copy-start | bytes 3076
  113.5 8.1 %copy-start.9 = (f32[48]{0:T(128)S(1)}, f32[48]{0:T(128)}, u32[]{:S(2)}) copy-start(f32[48]{0:T(128)} %param.20) | copy-start | bytes 580
  113.5 8.2 %copy-start.10 = (f32[48]{0:T(128)S(1)}, f32[48]{0:T(128)}, u32[]{:S(2)}) copy-start(f32[48]{0:T(128)} %param.19) | copy-start | bytes 580
  253.7 40.1 %collective-permute-start.2 = (bf16[256,1536]{1,0:T(8,128)(2,1)}, bf16[256,1536]{1,0:T(8,128)(2,1)}, u32[]{:S(2)}, u32[]{:S(2)}) collective-permute-start(bf16[256,1536]{1,0:T(8,128)(2,1)} %get-tuple-element.32), channel_id=1, source_target_pairs={{0,1},{1,0},{2,3},{3,2},{4,5},{5,4},{6,7},{7,6},{8,9},{9,8},{10,11... | collective-permute-start | bytes 2359304 | tf_op jit(solution)/shard_map/ppermute | solution.py:827
  253.7 40.1 %collective-permute-start.3 = (bf16[256,1536]{1,0:T(8,128)(2,1)}, bf16[256,1536]{1,0:T(8,128)(2,1)}, u32[]{:S(2)}, u32[]{:S(2)}) collective-permute-start(bf16[256,1536]{1,0:T(8,128)(2,1)} %bitcast.8), channel_id=1, source_target_pairs={{0,1},{1,0},{2,3},{3,2},{4,5},{5,4},{6,7},{7,6},{8,9},{9,8},{10,11... | collective-permute-start | bytes 2359304 | tf_op jit(solution)/shard_map/ppermute | solution.py:827
  254.2 27.0 %copy-start.2 = (bf16[256,3072]{1,0:T(8,128)(2,1)S(1)}, bf16[256,3072]{1,0:T(8,128)(2,1)}, u32[]{:S(2)}) copy-start(bf16[256,3072]{1,0:T(8,128)(2,1)} %get-tuple-element.22) | copy-start | bytes 4718596
  254.2 46.3 %collective-permute-start.1 = (bf16[256,6656]{1,0:T(8,128)(2,1)}, bf16[256,6656]{1,0:T(8,128)(2,1)}, u32[]{:S(2)}, u32[]{:S(2)}) collective-permute-start(bf16[256,6656]{1,0:T(8,128)(2,1)} %get-tuple-element.23), channel_id=1, source_target_pairs={{0,1},{1,0},{2,3},{3,2},{4,5},{5,4},{6,7},{7,6},{8,9},{9,8},{10,11... | collective-permute-start | bytes 10223624 | tf_op jit(solution)/shard_map/ppermute | solution.py:827
  268.6 31.8 %collective-permute-start = (bf16[256,768]{1,0:T(8,128)(2,1)}, bf16[256,768]{1,0:T(8,128)(2,1)}, u32[]{:S(2)}, u32[]{:S(2)}) collective-permute-start(bf16[256,768]{1,0:T(8,128)(2,1)} %get-tuple-element.35), channel_id=1, source_target_pairs={{0,1},{1,0},{2,3},{3,2},{4,5},{5,4},{6,7},{7,6},{8,9},{9,8},{10,11... | collective-permute-start | bytes 1179656 | tf_op jit(solution)/shard_map/ppermute | solution.py:827
  281.2 7.3 %copy-start.11 = (f32[48]{0:T(128)S(1)}, f32[48]{0:T(128)}, u32[]{:S(2)}) copy-start(f32[48]{0:T(128)} %reduce_sum.41) | copy-start | bytes 580
  281.2 8.6 %copy-start.3 = (f32[256,1536]{1,0:T(8,128)S(1)}, f32[256,1536]{1,0:T(8,128)}, u32[]{:S(2)}) copy-start(f32[256,1536]{1,0:T(8,128)} %get-tuple-element.41) | copy-start | bytes 4718596
  281.2 8.6 %copy-start.5 = (f32[1536]{0:T(1024)S(1)}, f32[1536]{0:T(1024)}, u32[]{:S(2)}) copy-start(f32[1536]{0:T(1024)} %copy-done.4) | copy-start | bytes 18436
  281.2 8.6 %copy-start.7 = (f32[256]{0:T(256)S(1)}, f32[256]{0:T(256)}, u32[]{:S(2)}) copy-start(f32[256]{0:T(256)} %copy-done.6) | copy-start | bytes 3076
  293.8 6.7 %copy-start.12 = (bf16[256,6656]{1,0:T(8,128)(2,1)S(1)}, bf16[256,6656]{1,0:T(8,128)(2,1)}, u32[]{:S(2)}) copy-start(bf16[256,6656]{1,0:T(8,128)(2,1)} %get-tuple-element.23) | copy-start | bytes 10223620

commit v3 on v2

--- a/solution.py
+++ b/solution.py
@@ -247,7 +247,7 @@
 
 
 def scatter_kernel(*refs, n, rows, shapes, tall):
-    parts_in, small_in, refs = refs[:n], refs[n], refs[n + 1:]
+    parts_in, smalls, refs = refs[:n], refs[n:n + 3], refs[n + 3:]
     outs, small_out, refs = refs[:n], refs[n], refs[n + 1:]
     take = iter(refs)
     near, relay, acc = {}, {}, {}
@@ -284,7 +284,13 @@
 
     def small_start(k):
         axis = ("c", "x", "y", "z")[k]
-        rounds[k][at[axis]] = small_in[...] if k == 0 else sums[0]
+        if k == 0:
+            start = 0
+            for part in smalls:
+                rounds[0][c, :, start:start + part.shape[1]] = part[...]
+                start += part.shape[1]
+        else:
+            rounds[k][at[axis]] = sums[0]
         held = rounds[k].at[at[axis]]
         if k == 0:
             return [links.copy(held, held, {"c": 1 - c})]
@@ -347,7 +353,17 @@
                     total = total + term(0, 0, 0).astype(jnp.float32)
                 fin[i][pl.ds(part * shape[3], shape[3]), :] = total
     small_end(3, going)
-    small_out[...] = sums[0]
+    index = 32 * z + 8 * y + 2 * x + c
+    total, start = sums[0], 0
+    for part, (each, first, count, to) in zip(smalls, ((26, 0, 8, 0), (0, 0, 8, 8), (12, 0, 1, 6))):
+        wide_ = part.shape[1]
+        value = total[:, start:start + wide_]
+        if each:
+            value = pltpu.roll(value, lax.rem(wide_ - each * index, wide_), 1)
+        small_out[to:to + count, :] = value[first:first + count, :128]
+        start += wide_
+    gate = pltpu.roll(total[:, :128 * 24], lax.rem(3072 - 24 * index, 3072), 1)
+    small_out[5:6, :] = gate[5:6, :128]
     final = []
     for i in range(n):
         deep, wide = rows[i], fin[i].shape[1]
@@ -373,7 +389,7 @@
         pl.when(jnp.logical_not(mine))(remote.wait_send)
 
 
-def scatter(halves_in, small, rows):
+def scatter(halves_in, smalls, rows):
     n = len(halves_in)
     wides = [h.shape[1] for h in halves_in]
     heights = [4 * r // 3 for r in rows]
@@ -393,19 +409,19 @@
     scratch += [pltpu.VMEM((3 * t, w // 4), jnp.float32) for t, w in zip(heights, wides)]
     scratch += [pltpu.VMEM((4, t, w // 4), jnp.float32) for t, w in zip(tall, wides)]
     scratch += [pltpu.VMEM((4, t, w // 4), jnp.float32) for t, w in zip(tall, wides)]
-    scratch += [pltpu.VMEM((2 if k == 0 else 4,) + small.shape, jnp.float32) for k in range(4)]
+    scratch += [pltpu.VMEM((2 if k == 0 else 4, 8, sum(s.shape[1] for s in smalls)), jnp.float32) for k in range(4)]
     count = n * 3 * 3 * 6 + 10
     scratch += [pltpu.SemaphoreType.DMA((count,)), pltpu.SemaphoreType.DMA((count,)),
                 pltpu.SemaphoreType.DMA((4 * n,)), pltpu.SemaphoreType.DMA((4 * n,))]
     outs = pl.pallas_call(
         functools.partial(scatter_kernel, n=n, rows=tuple(rows), shapes=tuple(shapes), tall=tuple(tall)),
-        out_shape=[jax.ShapeDtypeStruct((t, w), jnp.float32) for t, w in zip(tall, wides)] + [jax.ShapeDtypeStruct(small.shape, jnp.float32)],
-        in_specs=[pl.BlockSpec(memory_space=pltpu.VMEM)] * (n + 1),
+        out_shape=[jax.ShapeDtypeStruct((t, w), jnp.float32) for t, w in zip(tall, wides)] + [jax.ShapeDtypeStruct((16, 128), jnp.float32)],
+        in_specs=[pl.BlockSpec(memory_space=pltpu.VMEM)] * (n + 3),
         out_specs=[pl.BlockSpec(memory_space=pltpu.VMEM)] * (n + 1),
         scratch_shapes=scratch,
         compiler_params=pltpu.CompilerParams(collective_id=1, has_side_effects=True, vmem_limit_bytes=56 << 20),
         name="scatter_gradients",
-    )(*ins, small)
+    )(*ins, *smalls)
     return outs
 
 
@@ -463,33 +479,45 @@
 
 def mixer_kernel(proj, db, taps, gain, skip, heads, branch, dproj, sums, headsums,
                  act, mixed, ys, dys, dxs, shift, halo_out, halo_in, back_out, back_in,
-                 cum, ecum, toward, steps, rows_a, scores, dscores, usum, qin, qw, prods, stat, coef, db_in, dc_in,
-                 snd, rcv, ret, inc, snd2, rcv2, ret2, inc2,
-                 a_send, a_recv, h_sem):
+                 cum, ecum, toward, steps, rows_a, scores, dscores, usum, qin, qw, prods, stat, coef, db_in, dc_in, decay,
+                 skips, loc, inc, inc2, *rest):
     f32, bf16 = jnp.float32, jnp.bfloat16
-    z = lax.axis_index("z")
-    me = 8 * lax.axis_index("y") + 2 * lax.axis_index("x") + lax.axis_index("c")
+    ways, (sib_send, sib_recv, a_send, a_recv, h_sem) = (rest[:5], rest[5:10]), rest[10:]
+    z, core = lax.axis_index("z"), lax.axis_index("c")
+    chip = 4 * lax.axis_index("y") + lax.axis_index("x")
+    me = 2 * chip + core
     lane = lax.broadcasted_iota(jnp.int32, (256, 128), 1)
     first_head = lane < 64
 
     def device(k):
         return (z, k // 8, lax.rem(k // 2, 4), lax.rem(k, 2))
 
+    def same_core(k):
+        return (z, k // 4, lax.rem(k, 4), core)
+
     def others(body):
         def step(k, carry):
-            body(lax.rem(me + k, 32))
+            body(lax.rem(chip + k, 16))
             return carry
-        lax.fori_loop(1, 32, step, 0)
+        lax.fori_loop(1, 16, step, 0)
 
     barrier = pltpu.get_barrier_semaphore()
-    others(lambda k: pl.semaphore_signal(barrier, inc=1, device_id=device(k), device_id_type=MESH))
-    pl.semaphore_wait(barrier, 31)
+    others(lambda k: pl.semaphore_signal(barrier, inc=1, device_id=same_core(k), device_id_type=MESH))
+    pl.semaphore_signal(barrier, inc=1, device_id={"c": 1 - core}, device_id_type=MESH)
+    beside = jnp.where(core == 1, me + 1, me - 1)
+    inner = jnp.logical_and(beside >= 0, beside < 32)
+
+    @pl.when(inner)
+    def _():
+        pl.semaphore_signal(barrier, inc=1, device_id=device(beside), device_id_type=MESH)
+
+    pl.semaphore_wait(barrier, 16 + inner.astype(jnp.int32))
 
     def exchange(e, source, target, own):
         def go(k):
             pltpu.make_async_remote_copy(
-                src_ref=source(k), dst_ref=target(me), send_sem=a_send.at[e, k], recv_sem=a_recv.at[e, me],
-                device_id=device(k), device_id_type=MESH).start()
+                src_ref=source(k), dst_ref=target(chip), send_sem=a_send.at[e, k], recv_sem=a_recv.at[e, chip],
+                device_id=same_core(k), device_id_type=MESH).start()
         others(go)
         own()
 
@@ -498,6 +526,13 @@
 
     def left(e, source):
         others(lambda k: pltpu.make_async_copy(source(k), source(k), a_send.at[e, k]).wait())
+
+    def to_sibling(e, src, dst):
+        made = pltpu.make_async_remote_copy(
+            src_ref=src, dst_ref=dst, send_sem=sib_send.at[e], recv_sem=sib_recv.at[e],
+            device_id={"c": 1 - core}, device_id_type=MESH)
+        made.start()
+        return made
 
     def neighbour(k, src, dst, steps_, on):
         made = pltpu.make_async_remote_copy(
@@ -562,34 +597,116 @@
         both = jnp.concatenate([top, low(prod - wide(top))], axis=1)
         acc[...] += dot(both, pickers)
 
-    def give(buf, j, tile):
-        for g in range(4):
-            q = 4 * j + g
-            buf[q // 3, pl.ds(pl.multiple_of(32 * lax.rem(q, 3), 32), 32), :] = tile[32 * g:32 * g + 32]
+    def rows128(j):
+        return pl.ds(pl.multiple_of(128 * j, 128), 128)
+
+    mine, given = 12 * core, 12 * (1 - core)
+    row128 = lax.broadcasted_iota(jnp.int32, (128, 128), 0)
+    row16 = lax.broadcasted_iota(jnp.int32, (16, 128), 0)
+    decay[0:8, :] = jnp.broadcast_to(last, (8, 128))
+
+    def pair_factor(line, j):
+        turned = pltpu.roll(jnp.broadcast_to(line, (8, 128)), lax.rem(128 - 2 * j, 128), 1)
+        return jnp.where(row128 < 64, jnp.broadcast_to(turned[0:1, 0:1], (128, 128)), jnp.broadcast_to(turned[0:1, 1:2], (128, 128)))
+
+    head_a = 24 * core + 3 * chip // 2
+    edge = jnp.where(lax.rem(chip, 2) == 0, 64, 32)
+    row96 = lax.broadcasted_iota(jnp.int32, (96, 128), 0)
+
+    class Carry:
+        def __init__(self, way, backward, into):
+            self.e, self.backward, self.into = 2 * way, backward, into
+            self.sib, self.snd, self.rcv, self.ret, self.across = ways[way]
+
+        def swap(self):
+            self.first = to_sibling(self.e, loc.at[pl.ds(pl.multiple_of(1536 * (1 - core), 128), 1536)], self.sib)
+
+        def start(self):
+            self.first.wait_recv()
+            second = core == (0 if self.backward else 1)
+            other = decay[8:9, :]
+            later = jnp.exp(jnp.where(second, last, other))
+
+            def join(j, carry):
+                own, theirs = wide(loc[rows128(mine + j), :]), wide(self.sib[rows128(j), :])
+                factor = pair_factor(later, mine + j)
+                tile = low(factor * jnp.where(second, theirs, own) + jnp.where(second, own, theirs))
+                for g in range(4):
+                    q = 4 * j + g
+                    self.snd[q // 3, pl.ds(pl.multiple_of(32 * lax.rem(q, 3), 32), 32), :] = tile[32 * g:32 * g + 32]
+                return carry
+
+            lax.fori_loop(0, 12, join, 0)
+            tail = split3(last + other)
+            lines = jnp.zeros((16, 128), f32)
+            for k in range(3):
+                lines = jnp.where(row16 == k, wide(tail[k]), lines)
+            for k in range(16):
+                self.snd[k, 96:112, :] = low(lines)
+
+            def own():
+                self.rcv[chip] = self.snd[chip]
+
+            exchange(self.e, lambda k: self.snd.at[k], lambda k: self.rcv.at[k], own)
+
+        def turn(self):
+            arrived(self.e, lambda k: self.rcv.at[k])
+            carry = jnp.zeros((96, 128), f32)
+            for k in (range(15, -1, -1) if self.backward else range(16)):
+                line = wide(self.rcv[k, 96:112, :])
+                line = jnp.exp(line[0:1] + line[1:2] + line[2:3])
+                line = pltpu.roll(jnp.broadcast_to(line, (8, 128)), lax.rem(128 - head_a, 128), 1)
+                factor = jnp.where(row96 < edge, jnp.broadcast_to(line[0:1, 0:1], (96, 128)), jnp.broadcast_to(line[0:1, 1:2], (96, 128)))
+                self.ret[k] = low(carry)
+                carry = factor * carry + wide(self.rcv[k, 0:96, :])
+            start = pl.multiple_of(1536 * core, 128)
+
+            def place_(k):
+                return self.into.at[pl.ds(pl.multiple_of(start + 96 * k, 32), 96)]
+
+            def own():
+                self.into[pl.ds(pl.multiple_of(start + 96 * chip, 32), 96), :] = self.ret[chip]
+
+            self.place = place_
+            exchange(self.e + 1, lambda k: self.ret.at[k], place_, own)
+
+        def finish(self):
+            arrived(self.e + 1, self.place)
+            second = core == (0 if self.backward else 1)
+            before = jnp.exp(jnp.where(second, decay[8:9, :], last))
+
+            def part(j, carry):
+                at_ = rows128(mine + j)
+                came = self.into[at_, :]
+                passed = low(pair_factor(before, mine + j) * wide(came) + wide(jnp.where(second, self.sib[rows128(j), :], loc[at_, :])))
+                self.across[rows128(j), :] = jnp.where(second, came, passed)
+                self.into[at_, :] = jnp.where(second, passed, came)
+                return carry
+
+            lax.fori_loop(0, 12, part, 0)
+            half = pl.ds(pl.multiple_of(1536 * core, 128), 1536)
+            self.last = to_sibling(self.e + 1, self.across, self.into.at[half])
+            self.last.wait_recv()
+
+        def end(self):
+            if self.backward:
+                self.first.wait_send()
+            self.last.wait_send()
+            left(self.e, lambda k: self.snd.at[k])
+            left(self.e + 1, lambda k: self.ret.at[k])
+
+    ahead, aback = Carry(0, False, inc), Carry(1, True, inc2)
+    decays = to_sibling(4, decay.at[0:8], decay.at[8:16])
 
     def local_state(j, carry):
-        give(snd, j, low(dot_tn(low(spread(toward, j) * wide(act[j])), b_in)))
+        loc[rows128(j), :] = low(dot_tn(low(spread(toward, j) * wide(act[j])), b_in))
         return carry
 
-    lax.fori_loop(0, TILES, local_state, 0)
-    tail = split3(last)
-    row16 = lax.broadcasted_iota(jnp.int32, (16, 128), 0)
-    decays = jnp.zeros((16, 128), f32)
-    for k in range(3):
-        decays = jnp.where(row16 == k, wide(tail[k]), decays)
-    for k in range(32):
-        snd[k, 96:112, :] = low(decays)
-
-    def whole(ref):
-        return lambda k: ref.at[k]
-
-    def piece(ref):
-        return lambda k: ref.at[pl.ds(pl.multiple_of(96 * k, 32), 96)]
-
-    def keep(dst, src):
-        dst[me] = src[me]
-
-    exchange(0, whole(snd), whole(rcv), lambda: keep(rcv, snd))
+    lax.fori_loop(given, given + 12, local_state, 0)
+    ahead.swap()
+    lax.fori_loop(mine, mine + 12, local_state, 0)
+    decays.wait_recv()
+    ahead.start()
 
     row = lax.broadcasted_iota(jnp.int32, (128, 128), 0)
     col = lax.broadcasted_iota(jnp.int32, (128, 128), 1)
@@ -620,30 +737,10 @@
         ys[j, 128:256, :] = low_
         return carry
 
-    head_a = 3 * me // 2
-    edge = jnp.where(lax.rem(me, 2) == 0, 64, 32)
-    row96 = lax.broadcasted_iota(jnp.int32, (96, 128), 0)
-
-    def scan(got, out, backward):
-        carry = jnp.zeros((96, 128), f32)
-        for k in (range(31, -1, -1) if backward else range(32)):
-            line = wide(rcv[k, 96:112, :])
-            line = jnp.exp(line[0:1] + line[1:2] + line[2:3])
-            line = pltpu.roll(jnp.broadcast_to(line, (8, 128)), lax.rem(128 - head_a, 128), 1)
-            factor = jnp.where(row96 < edge, jnp.broadcast_to(line[0:1, 0:1], (96, 128)), jnp.broadcast_to(line[0:1, 1:2], (96, 128)))
-            out[k] = low(carry)
-            carry = factor * carry + wide(got[k, 0:96, :])
-
     lax.fori_loop(0, TILES // 2, inside, 0)
-    arrived(0, whole(rcv))
-    scan(rcv, ret, False)
-
-    def keep_flat(dst, src):
-        dst[pl.ds(pl.multiple_of(96 * me, 32), 96), :] = src[me]
-
-    exchange(1, whole(ret), piece(inc), lambda: keep_flat(inc, ret))
+    ahead.turn()
     lax.fori_loop(TILES // 2, TILES, inside, 0)
-    arrived(1, piece(inc))
+    ahead.finish()
 
     def state(ref, j):
         return ref[pl.ds(pl.multiple_of(128 * j, 128), 128), :]
@@ -671,6 +768,7 @@
     stat[...] = jnp.broadcast_to(scale, (256, 128))
     coef[...] = jnp.broadcast_to(factor, (256, 128))
     sums[...] = jnp.zeros((8, CONVC), f32)
+    skips[...] = jnp.zeros((128, 128), f32)
 
     def gate_back(j, carry):
         y = ys[j]
@@ -684,12 +782,15 @@
         dy = low(d_gated * gz * sig)
         dys[j] = dy
         dyf = wide(dy)
-        sums[6:7, cols(j)] = jnp.sum(dyf * wide(act[j]), axis=0, keepdims=True)
-        give(snd2, j, low(dot_tn(low(spread(ecum, j) * dyf), c_out)))
+        skips[pl.ds(j, 1), :] = jnp.sum(dyf * wide(act[j]), axis=0, keepdims=True)
+        loc[rows128(j), :] = low(dot_tn(low(spread(ecum, j) * dyf), c_out))
         return carry
 
-    lax.fori_loop(0, TILES, gate_back, 0)
-    exchange(2, whole(snd2), whole(rcv2), lambda: keep(rcv2, snd2))
+    ahead.first.wait_send()
+    lax.fori_loop(given, given + 12, gate_back, 0)
+    aback.swap()
+    lax.fori_loop(mine, mine + 12, gate_back, 0)
+    aback.start()
     for ref in (usum, qin, qw):
         ref[...] = jnp.zeros((256, 128), f32)
     dscores[...] = jnp.zeros((256, 256), f32)
@@ -715,11 +816,9 @@
         return carry
 
     lax.fori_loop(0, TILES // 2, inside_back, 0)
-    arrived(2, whole(rcv2))
-    scan(rcv2, ret2, True)
-    exchange(3, whole(ret2), piece(inc2), lambda: keep_flat(inc2, ret2))
+    aback.turn()
     lax.fori_loop(TILES // 2, TILES, inside_back, 0)
-    arrived(3, piece(inc2))
+    aback.finish()
     db_in[...] = jnp.zeros((256, 128), f32)
     dc_in[...] = jnp.zeros((256, 128), f32)
 
@@ -759,6 +858,9 @@
     d_raw = (q / jnp.maximum(dt, 1e-30) - heads[1:2, :] * d_l) * sigmoid(raw)
     d_raw = jnp.where(lane < H, d_raw, 0.0)
     headsums[...] = jnp.zeros((8, 128), f32)
+    by_pair = jnp.transpose(skips[...])
+    headsums[2:3, :] = jnp.sum(by_pair[:64], axis=0, keepdims=True)
+    headsums[3:4, :] = jnp.sum(by_pair[64:], axis=0, keepdims=True)
     headsums[0:1, :] = jnp.sum(d_raw, axis=0, keepdims=True)
     headsums[1:2, :] = -jnp.sum(d_l * dt, axis=0, keepdims=True)
     dproj[:, DI + CONVC:DI + CONVC + 128] = low(d_raw)
@@ -788,10 +890,9 @@
     lax.fori_loop(0, TILES + 2, conv_back, 0)
     pl.when(me < 31)(front.wait_send)
     pl.when(me > 0)(behind.wait_send)
-    left(0, whole(snd))
-    left(1, whole(ret))
-    left(2, whole(snd2))
-    left(3, whole(ret2))
+    decays.wait_send()
+    ahead.end()
+    aback.end()
 
 
 def mixer(projected, d_branch, taps, gain, skip, heads):
@@ -803,10 +904,13 @@
         vm((TILES,) + tile, f32), vm((264, 128), f32), vm(half, bf16), vm(half, bf16), vm(half, bf16), vm(half, bf16),
         vm(tile, f32), vm(tile, f32), vm(tile, f32), vm(tile, f32), vm((128, 256), f32), vm((256, 256), f32), vm((256, 256), f32),
         vm(tile, f32), vm(tile, f32), vm(tile, f32), vm((128, 128), f32), vm(tile, f32), vm(tile, f32), vm(tile, f32), vm(tile, f32),
+        vm((16, 128), f32),
     ]
+    scratch += [vm((128, 128), f32), vm((3072, 128), bf16), vm((3072, 128), bf16), vm((3072, 128), bf16)]
     for _ in range(2):
-        scratch += [vm((32, 112, 128), bf16), vm((32, 112, 128), bf16), vm((32, 96, 128), bf16), vm((3072, 128), bf16)]
-    scratch += [pltpu.SemaphoreType.DMA((4, 32)), pltpu.SemaphoreType.DMA((4, 32)), pltpu.SemaphoreType.DMA((4,))]
+        scratch += [vm((1536, 128), bf16), vm((16, 112, 128), bf16), vm((16, 112, 128), bf16), vm((16, 96, 128), bf16), vm((1536, 128), bf16)]
+    scratch += [pltpu.SemaphoreType.DMA((5,)), pltpu.SemaphoreType.DMA((5,)), pltpu.SemaphoreType.DMA((4, 16)),
+                pltpu.SemaphoreType.DMA((4, 16)), pltpu.SemaphoreType.DMA((4,))]
     spec = pl.BlockSpec(memory_space=pltpu.VMEM)
     return pl.pallas_call(
         mixer_kernel,
@@ -818,6 +922,7 @@
         compiler_params=pltpu.CompilerParams(collective_id=2, has_side_effects=True, vmem_limit_bytes=60 << 20),
         name="mixer",
     )(projected, d_branch, taps, gain, skip, heads)
+
 
 def rms_scale(values, gain):
     return values * lax.rsqrt(jnp.mean(values * values, axis=-1, keepdims=True) + epsilon) * gain
@@ -861,7 +966,6 @@
     b_conv_f = spare[:, 4, :26].reshape(CONVC)
     gain_norm_f = spare[:, 5, :12].reshape(1536)
     gain_gate_f = spare[:, 6, :24].reshape(DI)
-    w_in = w_in * (jnp.arange(WIDE) < PROJ).astype(jnp.bfloat16)[None, :]
     residual = hidden[0].astype(jnp.float32)
     length = residual.shape[0]
     normed = rms_scale(residual, gain_norm_f).astype(jnp.bfloat16)
@@ -881,29 +985,20 @@
     norm_pull = jax.vjp(rms_scale, residual, gain_norm_f)[1]
     d_from_norm, d_gain_norm = norm_pull(d_normed)
     d_hidden = grad_out.astype(jnp.float32) + d_from_norm
-    d_skips = jnp.sum(sums[6, :DI].reshape(H, P_SIZE), axis=1)
-    small = jnp.concatenate([
-        sums[:5].reshape(-1), d_gain_norm, sums[5, :DI], head_sums[:2].reshape(-1), jnp.pad(d_skips, (0, 80)),
-        jnp.zeros((896,), jnp.float32),
-    ]).reshape(176, 128)
-    g_in, g_out, total = scatter([d_w_in, d_w_out], small, [12, 24])
-    mine = lax.axis_index(ALL)
-    d_conv_w = total[:104].reshape(KW, CONVC)
-    d_conv_b = total[104:130].reshape(CONVC)
-    d_gain_norm = total[130:142].reshape(1536)
-    d_gain_gate = total[142:166].reshape(DI)
+    g_in, g_out, total = scatter(
+        [d_w_in, d_w_out], [sums, head_sums, jnp.pad(d_gain_norm[None], ((0, 7), (0, 0)))], [12, 24])
     return (
         result[None],
         d_hidden[None],
         g_in[:12, :PROJ],
         g_out,
-        lax.dynamic_slice_in_dim(d_conv_w, 26 * mine, 26, axis=1),
-        lax.dynamic_slice_in_dim(d_conv_b, 26 * mine, 26),
-        lax.dynamic_slice_in_dim(d_gain_norm, 12 * mine, 12),
-        lax.dynamic_slice_in_dim(d_gain_gate, 24 * mine, 24),
-        total[166, :H],
-        total[167, :H],
-        total[168, :H],
+        total[:4, :26],
+        total[4, :26],
+        total[6, :12],
+        total[5, :24],
+        total[8, :H],
+        total[9, :H],
+        jnp.stack([total[10, :H // 2], total[11, :H // 2]], axis=1).reshape(H),
     )
 
 

time: 419 us -> 378 us (0.902)
  other arithmetic: 25.2 us -> 5.17 us
  local copies, waits for them, and re-layouts: 36.2 us -> 22.8 us
  matrix products: 58.5 us -> 53.2 us
  Pallas kernels: 296 us -> 291 us
    mul x1 -> x0, other arithmetic: 16.9 us -> none  [shards(): w_in = w_in * (jnp.arange(WIDE) < PROJ).astype(jnp.bfloat16)[None, :]]
    pallas_call x1, Pallas kernels: 115 us -> 103 us  [mixer(): pl.pallas_call(mixer_kernel, out_shape=[jax.ShapeDtypeStruct((256, DI), b...]
    pallas_call x1, Pallas kernels: 98 us -> 105 us  [scatter(): pl.pallas_call(functools.partial(scatter_kernel, n=n, rows=tuple(rows), s...]
    unnamed x32 -> x23, local copies, waits for them, and re-layouts: 11.9 us -> 6.27 us
  transfers between devices with their start and end apart: 4 -> 4, of which waited for: 0 -> 0; matrix products, arithmetic and copies ran while one was open for 11% -> 7% of each run, Pallas kernels for 0% -> 0%
where the time goes in v3:
time: 378 us; the launch traced here: 374 us
  Pallas kernels  291 us (77%)
  matrix products  53.2 us (14%)
  local copies, waits for them, and re-layouts  22.8 us (6%)
  other arithmetic  5.17 us (1%)
    pallas_call x1, Pallas kernels, scatter(): pl.pallas_call(functools.partial(scatter_kernel, n=n, rows=tuple(rows), s...  105 us
    pallas_call x1, Pallas kernels, mixer(): pl.pallas_call(mixer_kernel, out_shape=[jax.ShapeDtypeStruct((256, DI), b...  103 us
    pallas_call x1, Pallas kernels, gather(): pl.pallas_call(functools.partial(gather_kernel, n=n, rows=tuple(rows)), o...  83.7 us
    dot_general x1, matrix products, shards(): projected = jnp.dot(normed, w_in, preferred_element_type=jnp.float32)  14.5 us
    dot_general x1, matrix products, shards(): jnp.einsum('tj,dj->td', d_projected, w_in, preferred_element_type=jnp.flo...  10.8 us
    dot_general x1, matrix products, shards(): jnp.einsum('td,tj->dj', my_half(normed, core), both_projected, preferred_...  10 us
  transfers between devices with their start and end apart: 4, of which 0 were waited for; matrix products, arithmetic and copies ran while one was open for 7% of the time, Pallas kernels for 0%

profile of v3, /device:TPU:1, one launch (start us, length us, event | category | flops | bytes accessed | tf_op | source)
XLA Modules:
  0.0 374.3 jit_solution(5117096851647342286)
XLA Ops:
  0.6 0.7 pad_bitcast_fusion.2
  1.3 0.7 pad_bitcast_fusion
  2.0 0.7 pad.41
  2.7 0.1 concatenate.21
  2.8 1.0 fusion.34
  3.8 0.9 pad.46.refs_1_
  4.7 83.7 %gather_weights.1 = (bf16[2,2,4,2,3,16,6656]{6,5,4,3,2,1,0:T(8,128)(2,1)}, bf16[2,2,4,2,3,32,1536]{6,5,4,3,2,1,0:T(8,128)(2,1)S(1)}) custom-call(bf16[16,6656]{1,0:T(8,128)(2,1)S(1)} %pad.45.refs_0_, bf16[32,1536]{1,0:T(8,128)(2,1)S(1)} %pad.46.refs_1_), custom_call_target="tpu_custom_call" | custom-call | tf_op jit(solution)/shard_map/gather_weights/pallas_call | solution.py:156
  88.4 0.0 copy-start
  88.4 3.6 copy-done
  92.0 1.0 slice_convert_fusion
  93.0 0.0 copy-start.1
  93.0 0.1 reshape.89
  93.1 0.0 copy-start.4
  93.1 0.2 slice_reduce_fusion.2
  93.4 0.2 slice_reduce_fusion.1
  93.6 0.2 slice_reduce_fusion
  93.8 0.1 mul.88
  93.9 0.2 copy-done.1
  94.2 0.2 fusion.13
  94.4 0.0 slice-start
  94.4 0.2 reshape.83
  94.6 0.1 broadcast_in_dim_reshape_squeeze.8
  94.8 0.7 broadcast_in_dim_reshape_squeeze.9.gain
  95.5 0.0 copy-done.4
  95.5 0.1 broadcast_in_dim.31
  95.6 0.7 broadcast_in_dim_reshape.3.skip
  96.3 14.5 %fusion.26.proj = f32[256,6656]{1,0:T(8,128)} fusion(bf16[1536,6656]{1,0:T(8,128)(2,1)} %bitcast.86, bf16[1,256,1536]{2,1,0:T(8,128)(2,1)S(1)} %copy-done.1, f32[1536]{0:T(1024)S(1)} %mul.88, f32[256]{0:T(256)S(1)} %fusion.35), kind=kOutput, calls=%fused_computation.33 | convolution fusion | flops 5236064256 | bytes 28056576 | tf_op jit(solution)/shard_map/dot_general | solution.py:972
  110.8 0.7 select_maximum_fusion.taps
  111.5 0.0 slice-done
  111.5 0.0 slice-done.1
  111.5 0.0 slice-done.2
  111.5 0.0 copy-start.5
  111.5 0.0 copy-start.6
  111.5 4.3 %convolution_bitcast_fusion.db = f32[256,3072]{1,0:T(8,128)} fusion(bf16[3072,1536]{1,0:T(8,128)(2,1)S(1)} %bitcast.80, bf16[1,256,1536]{2,1,0:T(8,128)(2,1)S(1)} %copy-done.3), kind=kOutput, calls=%fused_computation.5 | convolution fusion | flops 2415919104 | bytes 13369344 | tf_op jit(solution)/shard_map/td,kd->tk/dot_general | solution.py:975
  115.8 0.0 copy-done.5
  115.8 0.6 select_maximum_fusion.1.heads
  116.4 102.8 %mixer.1 = (bf16[256,3072]{1,0:T(8,128)(2,1)}, bf16[256,6656]{1,0:T(8,128)(2,1)}, f32[8,3328]{1,0:T(8,128)}, f32[8,128]{1,0:T(8,128)}) custom-call(f32[256,6656]{1,0:T(8,128)} %fusion.26.proj, f32[256,3072]{1,0:T(8,128)} %convolution_bitcast_fusion.db, f32[8,3328]{1,0:T(8,128)} %select_maximum_fusion.taps, f32[1,3072]{1,0:T(1,128)} %broadcast_in_dim_reshape_squeeze.9.gain, ...), custom_call_target="tpu_custom_call" | custom-call | tf_op jit(solution)/shard_map/mixer/pallas_call | solution.py:915
  219.2 1.5 constant_dynamic-slice_fusion.1
  220.7 0.1 collective-permute-start.2
  220.8 0.5 collective-permute-start.3
  221.3 0.1 collective-permute-start.1
  221.4 10.8 %fusion.12 = (f32[1536]{0:T(1024)S(1)}, f32[256]{0:T(256)S(1)}, bf16[256,1536]{1,0:T(8,128)(2,1)S(1)}, f32[256,1536]{1,0:T(8,128)S(1)}) fusion(bf16[1,256,1536]{2,1,0:T(8,128)(2,1)S(1)} %copy-done.1, f32[256]{0:T(256)S(1)} %fusion.35, f32[1536]{0:T(1024)S(1)} %mul.88, bf16[256,6656]{1,0:T(8,128)(2,1)} %get-tuple-element.23, bf16[1536,6656]{1,0:T(8,128)(2,1)} %bitcast.87), kind=kOutput, calls=%fused_computation.19 | convolution fusion | flops 5238028288 | bytes 27015168 | tf_op jit(solution)/shard_map/tj,dj->td/dot_general | solution.py:982
  232.2 0.1 constant_dynamic-slice_fusion.3
  232.3 0.5 collective-permute-start
  232.8 0.8 copy-done.2
  233.6 7.2 %fusion.4 = bf16[1,256,1536]{2,1,0:T(8,128)(2,1)} fusion(bf16[256,3072]{1,0:T(8,128)(2,1)S(1)} %copy-done.2, bf16[3072,1536]{1,0:T(8,128)(2,1)} %bitcast.77, bf16[1,256,1536]{2,1,0:T(8,128)(2,1)S(1)} %copy-done.1), kind=kOutput, calls=%fused_computation.8 | convolution fusion | flops 2417098752 | bytes 12582912 | tf_op jit(solution)/shard_map/dot_general | solution.py:980
  240.8 1.6 fusion.18
  242.4 0.6 pad.49.refs_4_
  243.1 0.0 collective-permute-done.2
  243.1 0.0 collective-permute-done.3
  243.1 6.4 %convolution_convert_fusion.1 = bf16[1536,1536]{1,0:T(8,128)(2,1)} fusion(bf16[256,1536]{1,0:T(8,128)(2,1)} %collective-permute-done.2, bf16[256,1536]{1,0:T(8,128)(2,1)S(1)} %get-tuple-element.31, bf16[256,1536]{1,0:T(8,128)(2,1)} %collective-permute-done.3, bf16[256,1536]{1,0:T(8,128)(2,1)S(1)} %bitcast.84), kind=kOutput, calls=%fused_computation.1 | convolution fusion | flops 2424569856 | bytes 7864320 | tf_op jit(solution)/shard_map/tk,td->kd/dot_general | solution.py:981
  249.5 0.0 collective-permute-done
  249.5 0.0 collective-permute-done.1
  249.5 10.0 %convolution_convert_fusion = bf16[768,6656]{1,0:T(8,128)(2,1)} fusion(bf16[256,6656]{1,0:T(8,128)(2,1)} %collective-permute-done.1, bf16[256,6656]{1,0:T(8,128)(2,1)S(1)} %copy-done.7, bf16[256,768]{1,0:T(8,128)(2,1)S(1)} %collective-permute-done, bf16[256,768]{1,0:T(8,128)(2,1)S(1)} %get-tuple-element.34), kind=kOutput, calls=%fused_computation | convolution fusion | flops 5254807552 | bytes 17825792 | tf_op jit(solution)/shard_map/td,tj->dj/dot_general | solution.py:984
  259.5 104.5 %scatter_gradients.1 = (f32[16,6656]{1,0:T(8,128)}, f32[24,1536]{1,0:T(8,128)}, f32[16,128]{1,0:T(8,128)}) custom-call(bf16[2,4,2,3,16,6656]{5,4,3,2,1,0:T(8,128)(2,1)} %bitcast.81, bf16[2,4,2,3,32,1536]{5,4,3,2,1,0:T(8,128)(2,1)} %bitcast.82, f32[8,3328]{1,0:T(8,128)} %get-tuple-element.24.refs_2_, f32[8,128]{1,0:T(8,128)} %get-tuple-element.25.refs_3_, ...), custom_call_target="tpu_custom_call" | custom-call | tf_op jit(solution)/shard_map/scatter_gradients/pallas_call | solution.py:416
  364.1 1.3 slice_bitcast_fusion.2
  365.3 1.3 slice.48
  366.6 1.3 slice_bitcast_fusion.3
  367.9 1.2 slice_bitcast_fusion.6
  369.1 1.2 slice_bitcast_fusion.7
  370.3 0.1 copy.26
  370.4 0.6 reshape.87
  371.0 1.8 slice.47
  372.8 1.6 copy.29
  (17 shorter events, 0.1 us)
Async XLA Ops:
  88.4 3.6 copy-start
  93.0 1.1 copy-start.1
  93.1 2.4 copy-start.4
  94.4 17.0 %slice-start = ((s8[9437184]{0:T(1024)(128)(4,1)}), s8[1048576]{0:T(1024)(128)(4,1)S(1)}, s32[]{:S(2)}) async-start(s8[9437184]{0:T(1024)(128)(4,1)} %bitcast.78), calls=%async_computation | async-start | bytes 2097152
  96.2 15.2 %slice-start.1 = ((s8[9437184]{0:T(1024)(128)(4,1)}), s8[4194304]{0:T(1024)(128)(4,1)S(1)}, s32[]{:S(2)}) async-start(s8[9437184]{0:T(1024)(128)(4,1)} %bitcast.78), calls=%async_computation.1 | async-start | bytes 8388608
  96.3 15.2 %slice-start.2 = ((s8[9437184]{0:T(1024)(128)(4,1)}), s8[4194304]{0:T(1024)(128)(4,1)S(1)}, s32[]{:S(2)}) async-start(s8[9437184]{0:T(1024)(128)(4,1)} %bitcast.78), calls=%async_computation.2 | async-start | bytes 8388608
  96.3 15.2 %copy-start.3 = (bf16[1,256,1536]{2,1,0:T(8,128)(2,1)S(1)}, bf16[1,256,1536]{2,1,0:T(8,128)(2,1)}, u32[]{:S(2)}) copy-start(bf16[1,256,1536]{2,1,0:T(8,128)(2,1)} %param.12) | copy-start | bytes 2359300
  111.5 4.3 %copy-start.5 = (f32[48]{0:T(128)S(1)}, f32[48]{0:T(128)}, u32[]{:S(2)}) copy-start(f32[48]{0:T(128)} %param.20) | copy-start | bytes 580
  111.5 4.3 %copy-start.6 = (f32[48]{0:T(128)S(1)}, f32[48]{0:T(128)}, u32[]{:S(2)}) copy-start(f32[48]{0:T(128)} %param.19) | copy-start | bytes 580
  220.7 22.4 %collective-permute-start.2 = (bf16[256,1536]{1,0:T(8,128)(2,1)S(1)}, bf16[256,1536]{1,0:T(8,128)(2,1)}, u32[]{:S(2)}, u32[]{:S(2)}) collective-permute-start(bf16[256,1536]{1,0:T(8,128)(2,1)S(1)} %get-tuple-element.32), channel_id=1, source_target_pairs={{0,1},{1,0},{2,3},{3,2},{4,5},{5,4},{6,7},{7,6},{8,9},{9,8},{10,11... | collective-permute-start | bytes 2359304 | tf_op jit(solution)/shard_map/ppermute | solution.py:932
  220.8 22.3 %collective-permute-start.3 = (bf16[256,1536]{1,0:T(8,128)(2,1)S(1)}, bf16[256,1536]{1,0:T(8,128)(2,1)}, u32[]{:S(2)}, u32[]{:S(2)}) collective-permute-start(bf16[256,1536]{1,0:T(8,128)(2,1)S(1)} %bitcast.83), channel_id=1, source_target_pairs={{0,1},{1,0},{2,3},{3,2},{4,5},{5,4},{6,7},{7,6},{8,9},{9,8},{10,11... | collective-permute-start | bytes 2359304 | tf_op jit(solution)/shard_map/ppermute | solution.py:932
  221.3 28.2 %collective-permute-start.1 = (bf16[256,6656]{1,0:T(8,128)(2,1)}, bf16[256,6656]{1,0:T(8,128)(2,1)}, u32[]{:S(2)}, u32[]{:S(2)}) collective-permute-start(bf16[256,6656]{1,0:T(8,128)(2,1)} %get-tuple-element.23), channel_id=1, source_target_pairs={{0,1},{1,0},{2,3},{3,2},{4,5},{5,4},{6,7},{7,6},{8,9},{9,8},{10,11... | collective-permute-start | bytes 10223624 | tf_op jit(solution)/shard_map/ppermute | solution.py:932
  232.2 1.4 copy-start.2
  232.3 17.2 %collective-permute-start = (bf16[256,768]{1,0:T(8,128)(2,1)S(1)}, bf16[256,768]{1,0:T(8,128)(2,1)S(1)}, u32[]{:S(2)}, u32[]{:S(2)}) collective-permute-start(bf16[256,768]{1,0:T(8,128)(2,1)S(1)} %get-tuple-element.35), channel_id=1, source_target_pairs={{0,1},{1,0},{2,3},{3,2},{4,5},{5,4},{6,7},{7,6},{8,9},{9,8},{10,11... | collective-permute-start | bytes 1179656 | tf_op jit(solution)/shard_map/ppermute | solution.py:932
  243.1 6.4 %copy-start.7 = (bf16[256,6656]{1,0:T(8,128)(2,1)S(1)}, bf16[256,6656]{1,0:T(8,128)(2,1)}, u32[]{:S(2)}) copy-start(bf16[256,6656]{1,0:T(8,128)(2,1)} %get-tuple-element.23) | copy-start | bytes 10223620

commit v4 on v3

--- a/solution.py
+++ b/solution.py
@@ -246,41 +246,148 @@
 ALL_CUT = [slice(None)] * 5
 
 
-def scatter_kernel(*refs, n, rows, shapes, tall):
+def scatter_scratch(rows, wides):
+    heights = [4 * r // 3 for r in rows]
+    tall = [-(-r // 8) * 8 for r in rows]
+    scratch = []
+    size = {(i, part): (2, 4, 2, heights[i], wides[i]) for i in range(len(rows)) for part in range(3)}
+    for phase in range(3):
+        for s in size:
+            shape = without(size[s], ORDERS[s[1]][2 - phase])
+            scratch += [pltpu.VMEM(shape, jnp.bfloat16)] * 2
+            scratch += [pltpu.VMEM(half_shape(shape, way), jnp.bfloat16) for way in (0, 1)]
+            if phase < 2:
+                scratch += [pltpu.VMEM(shape, jnp.bfloat16)]
+            size[s] = shape
+    scratch += [pltpu.VMEM((3 * t, w // 4), jnp.float32) for t, w in zip(heights, wides)]
+    scratch += [pltpu.VMEM((4, t, w // 4), jnp.float32) for t, w in zip(tall, wides)] * 2
+    scratch += [pltpu.SemaphoreType.DMA((4 * len(rows),))] * 2
+    return scratch
+
+
+class Scatter:
+    def __init__(self, at, links, sources, rows, wides, refs):
+        n = len(rows)
+        take = iter(refs)
+        self.at, self.links, self.rows, self.n = at, links, rows, n
+        self.streams = [(i, part) for i in range(n) for part in range(3)]
+        self.near, self.relay, self.acc = {}, {}, {}
+        for phase in range(3):
+            for s in self.streams:
+                self.near[s, phase] = [next(take), next(take)]
+                self.relay[s, phase] = [next(take), next(take)]
+                self.acc[s, phase] = next(take) if phase < 2 else None
+        self.fin, self.staged, self.landed = ([next(take) for _ in range(n)] for _ in range(3))
+        self.last, self.own = next(take), next(take)
+        self.size = {s: (2, 4, 2, 4 * rows[s[0]] // 3, wides[s[0]]) for s in self.streams}
+        self.source = {s: sources[s[0]].at[:, :, :, s[1]] for s in self.streams}
+
+    def steps(self):
+        at, links, size, source = self.at, self.links, self.size, self.source
+        for phase in range(3):
+            sent, lent = {}, {}
+            for s in self.streams:
+                axis = ORDERS[s[1]][2 - phase]
+                shape = without(size[s], axis)
+                cuts = {k: span(size[s], axis, moved(at, axis, k)) for k in (1, 2, 3)}
+                to = {k: {axis: moved(at, axis, k)[axis]} for k in (1, 3)}
+                lent[s], sent[s] = [], []
+                for way, step in ((0, 1), (1, 3)):
+                    src = source[s].at[tuple(cut_half(cuts[2], shape, way))]
+                    lent[s].append(links.copy(src, self.relay[s, phase][way], to[step]))
+                for way, step in ((0, 1), (1, 3)):
+                    src = source[s].at[tuple(cut_half(cuts[step], shape, 1 - way))]
+                    dst = self.near[s, phase][way].at[tuple(cut_half(ALL_CUT, shape, 1 - way))]
+                    sent[s].append(links.copy(src, dst, to[step]))
+            yield
+            for s in self.streams:
+                axis = ORDERS[s[1]][2 - phase]
+                shape = without(size[s], axis)
+                for way, step in ((0, 1), (1, 3)):
+                    lent[s][way].wait_recv()
+                    hs = half_shape(shape, way)
+                    cut = cut_half(span(size[s], axis, moved(at, axis, step)), shape, way)
+                    buf = self.relay[s, phase][way]
+                    add_up(slab_to(buf, hs), [slab_of(source[s], cut, hs), slab_of(buf, ALL_CUT, hs)], hs)
+                    dst = self.near[s, phase][way].at[tuple(cut_half(ALL_CUT, shape, way))]
+                    sent[s].append(links.copy(buf, dst, {axis: moved(at, axis, step)[axis]}))
+            yield
+            for s in self.streams:
+                i, part = s
+                axis = ORDERS[part][2 - phase]
+                shape = without(size[s], axis)
+                for copy in sent[s]:
+                    copy.wait_recv()
+                terms = [slab_of(source[s], span(size[s], axis, at), shape)]
+                terms += [slab_of(self.near[s, phase][way], ALL_CUT, shape) for way in (0, 1)]
+                if phase < 2:
+                    add_up(slab_to(self.acc[s, phase], shape), terms, shape)
+                    source[s], size[s] = self.acc[s, phase], shape
+                else:
+                    total = terms[0](0, 0, 0).astype(jnp.float32)
+                    for term in terms[1:]:
+                        total = total + term(0, 0, 0).astype(jnp.float32)
+                    self.fin[i][pl.ds(part * shape[3], shape[3]), :] = total
+        z, y, x, c = (at[name] for name in ALL)
+        from_z = 2 * c + z // 2
+        home = jnp.logical_and(2 * lax.rem(z, 2) + x // 2 == z, z // 2 == c)
+        final = []
+        for i in range(self.n):
+            deep = self.rows[i]
+            staged, landed = self.staged[i], self.landed[i]
+            for k in range(4):
+                sx, sc = 2 * lax.rem(z, 2) + k // 2, k % 2
+                staged[k] = jnp.zeros(staged.shape[1:], jnp.float32)
+                staged[k, :deep] = self.fin[i][pl.ds(deep * k, deep), :]
+                mine = jnp.logical_and(home, jnp.logical_and(sx == x, sc == c))
+                remote = pltpu.make_async_remote_copy(
+                    src_ref=staged.at[k], dst_ref=landed.at[x], send_sem=self.own.at[4 * i + k], recv_sem=self.last.at[4 * i + x],
+                    device_id=(from_z, y, sx, jnp.int32(sc)), device_id_type=MESH)
+                local = pltpu.make_async_copy(staged.at[k], landed.at[x], self.last.at[4 * i + x])
+                pl.when(jnp.logical_not(mine))(remote.start)
+                pl.when(mine)(local.start)
+                final.append((remote, mine))
+        self.final = final
+        yield
+
+    def finish(self, outs):
+        for i in range(self.n):
+            wide_ = self.fin[i].shape[1]
+            for tx in range(4):
+                pltpu.make_async_copy(self.landed[i].at[tx], self.landed[i].at[tx], self.last.at[4 * i + tx]).wait()
+                outs[i][:, pl.ds(tx * wide_, wide_)] = self.landed[i][tx]
+        for remote, mine in self.final:
+            pl.when(jnp.logical_not(mine))(remote.wait_send)
+
+
+def targets(at):
+    z, x, c = at["z"], at["x"], at["c"]
+    to_z, to_c = 2 * lax.rem(z, 2) + x // 2, z // 2
+    return to_z, to_c, 2 * c + z // 2, jnp.logical_and(to_z == z, to_c == c)
+
+
+def scatter_kernel(*refs, rows, wides):
+    n = len(rows)
     parts_in, smalls, refs = refs[:n], refs[n:n + 3], refs[n + 3:]
     outs, small_out, refs = refs[:n], refs[n], refs[n + 1:]
-    take = iter(refs)
-    near, relay, acc = {}, {}, {}
-    streams = [(i, part) for i in range(n) for part in range(3)]
-    for phase in range(3):
-        for s in streams:
-            near[s, phase] = [next(take), next(take)]
-            relay[s, phase] = [next(take), next(take)]
-            acc[s, phase] = next(take) if phase < 2 else None
-    fin = [next(take) for _ in range(n)]
-    staged = [next(take) for _ in range(n)]
-    landed = [next(take) for _ in range(n)]
-    rounds = [next(take) for _ in range(4)]
-    send, recv, last, own = (next(take) for _ in range(4))
+    rounds, (send, recv), refs = refs[:4], refs[4:6], refs[6:]
     at = place()
     z, y, x, c = (at[name] for name in ALL)
-    to_z, to_c = 2 * lax.rem(z, 2) + x // 2, z // 2
-    from_z = 2 * c + z // 2
-    home = jnp.logical_and(to_z == z, to_c == c)
+    to_z, to_c, _, home = targets(at)
     barrier = pltpu.get_barrier_semaphore()
     for axis in ("z", "y", "x"):
         for steps in (1, 2, 3):
             pl.semaphore_signal(barrier, inc=1, device_id={axis: moved(at, axis, steps)[axis]}, device_id_type=MESH)
     pl.semaphore_signal(barrier, inc=1, device_id={"c": 1 - c}, device_id_type=MESH)
     for tx in range(4):
-        mine = jnp.logical_and(home, x == tx)
-
-        @pl.when(jnp.logical_not(mine))
+        @pl.when(jnp.logical_not(jnp.logical_and(home, x == tx)))
         def _():
             pl.semaphore_signal(barrier, inc=1, device_id=(to_z, y, jnp.int32(tx), to_c), device_id_type=MESH)
     pl.semaphore_wait(barrier, 14 - home.astype(jnp.int32))
 
     links = Links(send, recv)
+    work = Scatter(at, links, parts_in, rows, wides, refs)
+    sums = [None]
 
     def small_start(k):
         axis = ("c", "x", "y", "z")[k]
@@ -304,54 +411,11 @@
             total = total + rounds[k][j]
         sums[0] = total
 
-    sums = [None]
-    size = {s: shapes[s[0]] for s in streams}
-    source = {s: parts_in[s[0]].at[:, :, :, s[1]] for s in streams}
     going = small_start(0)
-    for phase in range(3):
-        sent, lent = {}, {}
-        for s in streams:
-            axis = ORDERS[s[1]][2 - phase]
-            shape = without(size[s], axis)
-            cuts = {k: span(size[s], axis, moved(at, axis, k)) for k in (0, 1, 2, 3)}
-            to = {k: {axis: moved(at, axis, k)[axis]} for k in (1, 3)}
-            lent[s], sent[s] = [], []
-            for way, step in ((0, 1), (1, 3)):
-                src = source[s].at[tuple(cut_half(cuts[2], shape, way))]
-                lent[s].append(links.copy(src, relay[s, phase][way], to[step]))
-            for way, step in ((0, 1), (1, 3)):
-                src = source[s].at[tuple(cut_half(cuts[step], shape, 1 - way))]
-                dst = near[s, phase][way].at[tuple(cut_half(ALL_CUT, shape, 1 - way))]
-                sent[s].append(links.copy(src, dst, to[step]))
-        small_end(phase, going)
-        going = small_start(phase + 1)
-        for s in streams:
-            axis = ORDERS[s[1]][2 - phase]
-            shape = without(size[s], axis)
-            for way, step in ((0, 1), (1, 3)):
-                lent[s][way].wait_recv()
-                hs = half_shape(shape, way)
-                cut = cut_half(span(size[s], axis, moved(at, axis, step)), shape, way)
-                buf = relay[s, phase][way]
-                add_up(slab_to(buf, hs), [slab_of(source[s], cut, hs), slab_of(buf, ALL_CUT, hs)], hs)
-                dst = near[s, phase][way].at[tuple(cut_half(ALL_CUT, shape, way))]
-                sent[s].append(links.copy(buf, dst, {axis: moved(at, axis, step)[axis]}))
-        for s in streams:
-            i, part = s
-            axis = ORDERS[part][2 - phase]
-            shape = without(size[s], axis)
-            for copy in sent[s]:
-                copy.wait_recv()
-            terms = [slab_of(source[s], span(size[s], axis, at), shape)]
-            terms += [slab_of(near[s, phase][way], ALL_CUT, shape) for way in (0, 1)]
-            if phase < 2:
-                add_up(slab_to(acc[s, phase], shape), terms, shape)
-                source[s], size[s] = acc[s, phase], shape
-            else:
-                total = terms[0](0, 0, 0).astype(jnp.float32)
-                for term in terms[1:]:
-                    total = total + term(0, 0, 0).astype(jnp.float32)
-                fin[i][pl.ds(part * shape[3], shape[3]), :] = total
+    for k, _ in enumerate(work.steps()):
+        if k in (0, 2, 4):
+            small_end(k // 2, going)
+            going = small_start(k // 2 + 1)
     small_end(3, going)
     index = 32 * z + 8 * y + 2 * x + c
     total, start = sums[0], 0
@@ -364,65 +428,27 @@
         start += wide_
     gate = pltpu.roll(total[:, :128 * 24], lax.rem(3072 - 24 * index, 3072), 1)
     small_out[5:6, :] = gate[5:6, :128]
-    final = []
-    for i in range(n):
-        deep, wide = rows[i], fin[i].shape[1]
-        for k in range(4):
-            sx, sc = 2 * lax.rem(z, 2) + k // 2, k % 2
-            staged[i][k] = jnp.zeros(staged[i].shape[1:], jnp.float32)
-            staged[i][k, :deep] = fin[i][pl.ds(deep * k, deep), :]
-            mine = jnp.logical_and(home, jnp.logical_and(sx == x, sc == c))
-            remote = pltpu.make_async_remote_copy(
-                src_ref=staged[i].at[k], dst_ref=landed[i].at[x], send_sem=own.at[4 * i + k], recv_sem=last.at[4 * i + x],
-                device_id=(from_z, y, sx, jnp.int32(sc)), device_id_type=MESH)
-            local = pltpu.make_async_copy(staged[i].at[k], landed[i].at[x], last.at[4 * i + x])
-            pl.when(jnp.logical_not(mine))(remote.start)
-            pl.when(mine)(local.start)
-            final.append((remote, mine))
-    for i in range(n):
-        wide = fin[i].shape[1]
-        for tx in range(4):
-            pltpu.make_async_copy(landed[i].at[tx], landed[i].at[tx], last.at[4 * i + tx]).wait()
-            outs[i][:, pl.ds(tx * wide, wide)] = landed[i][tx]
+    work.finish(outs)
     links.finish()
-    for remote, mine in final:
-        pl.when(jnp.logical_not(mine))(remote.wait_send)
 
 
 def scatter(halves_in, smalls, rows):
     n = len(halves_in)
     wides = [h.shape[1] for h in halves_in]
-    heights = [4 * r // 3 for r in rows]
-    ins = [h.reshape(2, 4, 2, 3, t, w) for h, t, w in zip(halves_in, heights, wides)]
-    shapes = [(2, 4, 2, t, w) for t, w in zip(heights, wides)]
+    ins = [h.reshape(2, 4, 2, 3, 4 * r // 3, w) for h, r, w in zip(halves_in, rows, wides)]
     tall = [-(-r // 8) * 8 for r in rows]
-    scratch = []
-    size = {(i, part): shapes[i] for i in range(n) for part in range(3)}
-    for phase in range(3):
-        for s in size:
-            shape = without(size[s], ORDERS[s[1]][2 - phase])
-            scratch += [pltpu.VMEM(shape, jnp.bfloat16)] * 2
-            scratch += [pltpu.VMEM(half_shape(shape, way), jnp.bfloat16) for way in (0, 1)]
-            if phase < 2:
-                scratch += [pltpu.VMEM(shape, jnp.bfloat16)]
-            size[s] = shape
-    scratch += [pltpu.VMEM((3 * t, w // 4), jnp.float32) for t, w in zip(heights, wides)]
-    scratch += [pltpu.VMEM((4, t, w // 4), jnp.float32) for t, w in zip(tall, wides)]
-    scratch += [pltpu.VMEM((4, t, w // 4), jnp.float32) for t, w in zip(tall, wides)]
-    scratch += [pltpu.VMEM((2 if k == 0 else 4, 8, sum(s.shape[1] for s in smalls)), jnp.float32) for k in range(4)]
     count = n * 3 * 3 * 6 + 10
-    scratch += [pltpu.SemaphoreType.DMA((count,)), pltpu.SemaphoreType.DMA((count,)),
-                pltpu.SemaphoreType.DMA((4 * n,)), pltpu.SemaphoreType.DMA((4 * n,))]
-    outs = pl.pallas_call(
-        functools.partial(scatter_kernel, n=n, rows=tuple(rows), shapes=tuple(shapes), tall=tuple(tall)),
+    scratch = [pltpu.VMEM((2 if k == 0 else 4, 8, sum(s.shape[1] for s in smalls)), jnp.float32) for k in range(4)]
+    scratch += [pltpu.SemaphoreType.DMA((count,))] * 2
+    return pl.pallas_call(
+        functools.partial(scatter_kernel, rows=tuple(rows), wides=tuple(wides)),
         out_shape=[jax.ShapeDtypeStruct((t, w), jnp.float32) for t, w in zip(tall, wides)] + [jax.ShapeDtypeStruct((16, 128), jnp.float32)],
         in_specs=[pl.BlockSpec(memory_space=pltpu.VMEM)] * (n + 3),
         out_specs=[pl.BlockSpec(memory_space=pltpu.VMEM)] * (n + 1),
-        scratch_shapes=scratch,
+        scratch_shapes=scratch + scatter_scratch(rows, wides),
         compiler_params=pltpu.CompilerParams(collective_id=1, has_side_effects=True, vmem_limit_bytes=56 << 20),
         name="scatter_gradients",
     )(*ins, *smalls)
-    return outs
 
 
 H = 48
@@ -477,12 +503,24 @@
     return 1.0 / (1.0 + jnp.exp(-v))
 
 
-def mixer_kernel(proj, db, taps, gain, skip, heads, branch, dproj, sums, headsums,
-                 act, mixed, ys, dys, dxs, shift, halo_out, halo_in, back_out, back_in,
+def loop(first, count, body, unroll):
+    def step(k, carry):
+        for u in range(unroll):
+            body(first + k * unroll + u, u)
+        return carry
+    lax.fori_loop(0, count // unroll, step, 0)
+
+
+def mixer_kernel(gates, conv_in, dt_in, normed, hidden, given_out, db, taps, gain, skip, heads, w_in, w_out,
+                 out, dproj, d_norm, sums, headsums, g_z, g_o,
+                 branch, dz, sib_normed, sib_given, sib_branch, sib_dz, src_z, src_o, chunk, chunk_sem,
+                 act, ys, dys, shift, shift2, halo_out, halo_in, back_out, back_in,
                  cum, ecum, toward, steps, rows_a, scores, dscores, usum, qin, qw, prods, stat, coef, db_in, dc_in, decay,
                  skips, loc, inc, inc2, *rest):
     f32, bf16 = jnp.float32, jnp.bfloat16
-    ways, (sib_send, sib_recv, a_send, a_recv, h_sem) = (rest[:5], rest[5:10]), rest[10:]
+    snd, rcv, ret = rest[:3]
+    ways, (sib_send, sib_recv, a_send, a_recv, h_sem, rs_send, rs_recv), rest = (rest[3:5], rest[5:7]), rest[7:14], rest[14:]
+    at = place()
     z, core = lax.axis_index("z"), lax.axis_index("c")
     chip = 4 * lax.axis_index("y") + lax.axis_index("x")
     me = 2 * chip + core
@@ -511,7 +549,14 @@
     def _():
         pl.semaphore_signal(barrier, inc=1, device_id=device(beside), device_id_type=MESH)
 
-    pl.semaphore_wait(barrier, 16 + inner.astype(jnp.int32))
+    for steps_ in (1, -1):
+        pl.semaphore_signal(barrier, inc=1, device_id={"z": moved(at, "z", steps_)["z"]}, device_id_type=MESH)
+    to_z, to_c, _, home = targets(at)
+    for tx in range(4):
+        @pl.when(jnp.logical_not(jnp.logical_and(home, at["x"] == tx)))
+        def _():
+            pl.semaphore_signal(barrier, inc=1, device_id=(to_z, at["y"], jnp.int32(tx), to_c), device_id_type=MESH)
+    pl.semaphore_wait(barrier, 22 + inner.astype(jnp.int32) - home.astype(jnp.int32))
 
     def exchange(e, source, target, own):
         def go(k):
@@ -541,10 +586,14 @@
         pl.when(on)(made.start)
         return made
 
-    halo_out[...] = low(proj[240:256, DI:DI + CONVC])
+    def lanes(start, size):
+        return pl.ds(pl.multiple_of(start, 128), size)
+
+    halo_out[...] = conv_in[240:256, :]
     front = neighbour(0, halo_out, halo_in, 1, me < 31)
-
-    raw = proj[:, DI + CONVC:DI + CONVC + 128] + heads[0:1, :]
+    shared = [to_sibling(5, normed.at[:, lanes(768 * (1 - core), 768)], sib_normed), to_sibling(6, given_out, sib_given)]
+
+    raw = dt_in[...] + heads[0:1, :]
     dt = jnp.maximum(raw, 0.0) + jnp.log1p(jnp.exp(-jnp.abs(raw)))
     total = running_sums(-heads[1:2, :] * dt, False)
     last = total[255:256, :]
@@ -563,17 +612,19 @@
     def cols(j):
         return pl.ds(pl.multiple_of(128 * j, 128), 128)
 
-    def conv(j, carry):
-        shift[0:8, :] = wide(halo_in[:, cols(j)])[8:16, :]
-        shift[8:264, :] = wide(low(proj[:, pl.ds(pl.multiple_of(DI + 128 * j, 128), 128)]))
-        total = taps[4:5, cols(j)] + taps[0:1, cols(j)] * shift[5:261, :]
+    def convolved(j, u):
+        shift[u, 0:8, :] = wide(halo_in[:, cols(j)])[8:16, :]
+        shift[u, 8:264, :] = wide(conv_in[:, cols(j)])
+        total = taps[4:5, cols(j)] + taps[0:1, cols(j)] * shift[u, 5:261, :]
         for k in range(1, 4):
-            total = total + taps[k:k + 1, cols(j)] * shift[5 + k:261 + k, :]
-        mixed[j] = total
+            total = total + taps[k:k + 1, cols(j)] * shift[u, 5 + k:261 + k, :]
+        return total
+
+    def conv(j, u):
+        total = convolved(j, u)
         act[j] = low(total * sigmoid(total))
-        return carry
-
-    lax.fori_loop(0, TILES + 2, conv, 0)
+
+    loop(0, TILES + 2, conv, 2)
     b_in, c_out = act[TILES], act[TILES + 1]
     scores[...] = dot_nt(c_out, b_in)
 
@@ -616,7 +667,8 @@
     class Carry:
         def __init__(self, way, backward, into):
             self.e, self.backward, self.into = 2 * way, backward, into
-            self.sib, self.snd, self.rcv, self.ret, self.across = ways[way]
+            self.sib, self.across = ways[way]
+            self.snd, self.rcv, self.ret = snd, rcv, ret
 
         def swap(self):
             self.first = to_sibling(self.e, loc.at[pl.ds(pl.multiple_of(1536 * (1 - core), 128), 1536)], self.sib)
@@ -636,7 +688,7 @@
                     self.snd[q // 3, pl.ds(pl.multiple_of(32 * lax.rem(q, 3), 32), 32), :] = tile[32 * g:32 * g + 32]
                 return carry
 
-            lax.fori_loop(0, 12, join, 0)
+            loop(0, 12, join, 12)
             tail = split3(last + other)
             lines = jnp.zeros((16, 128), f32)
             for k in range(3):
@@ -683,7 +735,7 @@
                 self.into[at_, :] = jnp.where(second, passed, came)
                 return carry
 
-            lax.fori_loop(0, 12, part, 0)
+            loop(0, 12, part, 12)
             half = pl.ds(pl.multiple_of(1536 * core, 128), 1536)
             self.last = to_sibling(self.e + 1, self.across, self.into.at[half])
             self.last.wait_recv()
@@ -702,9 +754,9 @@
         loc[rows128(j), :] = low(dot_tn(low(spread(toward, j) * wide(act[j])), b_in))
         return carry
 
-    lax.fori_loop(given, given + 12, local_state, 0)
+    loop(given, 12, local_state, 6)
     ahead.swap()
-    lax.fori_loop(mine, mine + 12, local_state, 0)
+    loop(mine, 12, local_state, 6)
     decays.wait_recv()
     ahead.start()
 
@@ -737,16 +789,16 @@
         ys[j, 128:256, :] = low_
         return carry
 
-    lax.fori_loop(0, TILES // 2, inside, 0)
+    loop(0, TILES // 2, inside, 3)
     ahead.turn()
-    lax.fori_loop(TILES // 2, TILES, inside, 0)
+    loop(TILES // 2, TILES // 2, inside, 3)
     ahead.finish()
 
     def state(ref, j):
         return ref[pl.ds(pl.multiple_of(128 * j, 128), 128), :]
 
     def gate(j, y):
-        gz = proj[:, cols(j)]
+        gz = gates[:, cols(j)]
         sig = sigmoid(gz)
         full = y + skip[:, cols(j)] * wide(act[j])
         return gz, sig, full, full * gz * sig
@@ -762,7 +814,7 @@
         coef[...] += gated * (gain[:, cols(j)] * db[:, cols(j)])
         return carry
 
-    lax.fori_loop(0, TILES, gate_sums, 0)
+    loop(0, TILES, gate_sums, 4)
     scale = lax.rsqrt(jnp.sum(stat[...], axis=1, keepdims=True) * (1.0 / DI) + epsilon)
     factor = scale * scale * scale * (jnp.sum(coef[...], axis=1, keepdims=True) * (1.0 / DI))
     stat[...] = jnp.broadcast_to(scale, (256, 128))
@@ -778,7 +830,7 @@
         given = db[:, cols(j)]
         sums[5:6, cols(j)] = jnp.sum(scaled * given, axis=0, keepdims=True)
         d_gated = stat[...] * gain[:, cols(j)] * given - gated * coef[...]
-        dproj[:, cols(j)] = low(d_gated * full * (sig * (1.0 + gz * (1.0 - sig))))
+        dz[:, cols(j)] = low(d_gated * full * (sig * (1.0 + gz * (1.0 - sig))))
         dy = low(d_gated * gz * sig)
         dys[j] = dy
         dyf = wide(dy)
@@ -787,10 +839,73 @@
         return carry
 
     ahead.first.wait_send()
-    lax.fori_loop(given, given + 12, gate_back, 0)
+    loop(given, 12, gate_back, 4)
     aback.swap()
-    lax.fori_loop(mine, mine + 12, gate_back, 0)
+    theirs, ours = lanes(1536 * (1 - core), 1536), lanes(1536 * core, 1536)
+    shared += [to_sibling(7, branch.at[:, theirs], sib_branch), to_sibling(8, dz.at[:, theirs], sib_dz.at[:, theirs])]
+    loop(mine, 12, gate_back, 4)
+    shared += [to_sibling(9, dz.at[:, ours], sib_dz.at[:, ours])]
+    ahead.end()
     aback.start()
+    for copy in shared:
+        copy.wait_recv()
+
+    def d_w_gates(k, u):
+        zh, part = k // 8, lanes(384 * lax.rem(k, 8), 384)
+        total = dot_tn(normed[:, lanes(768 * core + 384 * zh, 384)], dz[:, part])
+        total = total + dot_tn(sib_normed[:, lanes(384 * zh, 384)], sib_dz[:, part])
+        src_z[zh, :, :, :, :, part] = low(total).reshape(4, 2, 3, 16, 384)
+
+    def d_w_out(k, u):
+        q, part = k // 4, lanes(384 * lax.rem(k, 4), 384)
+        total = dot_tn(branch[:, lanes(1536 * core + 384 * q, 384)], given_out[:, part])
+        total = total + dot_tn(sib_branch[:, lanes(384 * q, 384)], sib_given[:, part])
+        src_o[q // 2, pl.ds(2 * lax.rem(q, 2), 2), :, :, :, part] = low(total).reshape(2, 2, 3, 32, 384)
+
+    loop(0, 16, d_w_gates, 1)
+    loop(0, 16, d_w_out, 1)
+    aback.turn()
+    links = Links(rs_send, rs_recv)
+    work = Scatter(at, links, [src_z, src_o], (12, 24), (DI, 1536), rest)
+    reduce = work.steps()
+    next(reduce)
+
+    def fetch(k, slot):
+        last_ = k >= 12
+        part = jnp.minimum(k, 11)
+        a_ = pltpu.make_async_copy(
+            w_out.at[pl.ds(pl.multiple_of(1536 * lax.rem(part, 2), 128), 1536), lanes(256 * (part // 2), 256)], chunk.at[slot], chunk_sem.at[slot])
+        b_ = pltpu.make_async_copy(w_in.at[:, lanes(256 * jnp.maximum(k - 12, 0), 256)], chunk.at[slot], chunk_sem.at[slot])
+        pl.when(jnp.logical_not(last_))(a_.start)
+        pl.when(last_)(b_.start)
+
+    def fetched(slot):
+        pltpu.make_async_copy(chunk.at[slot], chunk.at[slot], chunk_sem.at[slot]).wait()
+
+    def out_part(n, u):
+        part = lanes(256 * n, 256)
+        total = wide(hidden[:, part])
+        for slot in range(2):
+            fetched(slot)
+            total = total + dot(branch[:, 1536 * slot:1536 * slot + 1536], chunk[slot])
+            fetch(2 * n + slot + 2, slot)
+        out[:, part] = low(total)
+
+    def norm_part(n, u):
+        for slot in range(2):
+            fetched(slot)
+            k = 2 * n + slot
+            for half in range(2):
+                rows_ = slice(768 * half, 768 * half + 768)
+                d_norm[:, rows_] += dot_nt(dz[:, lanes(256 * k, 256)], chunk[slot, rows_, :])
+
+            @pl.when(k + 2 < 12)
+            def _():
+                fetch(k + 14, slot)
+
+    fetch(jnp.int32(0), 0)
+    fetch(jnp.int32(1), 1)
+    d_norm[...] = jnp.zeros((256, 1536), f32)
     for ref in (usum, qin, qw):
         ref[...] = jnp.zeros((256, 128), f32)
     dscores[...] = jnp.zeros((256, 256), f32)
@@ -810,26 +925,29 @@
         top = dot_tn(jnp.concatenate([m[0][0], m[0][1], m[1][0], m[1][1]], axis=0), jnp.concatenate([dya, dyb], axis=0))
         low_ = dot_tn(jnp.concatenate([m[0][2], m[1][2]], axis=0), jnp.concatenate([dya[128:], dyb[128:]], axis=0))
         dx = jnp.concatenate([top, low_], axis=0)
-        dxs[j] = dx
         fold(usum, wide(dys[j]) * ys[j], j)
+        ys[j] = dx
         fold(qin, wide(x) * dx, j)
         return carry
 
-    lax.fori_loop(0, TILES // 2, inside_back, 0)
-    aback.turn()
-    lax.fori_loop(TILES // 2, TILES, inside_back, 0)
+    loop(0, TILES // 2, inside_back, 3)
+    next(reduce)
+    loop(TILES // 2, TILES // 2, inside_back, 3)
+    loop(0, 6, out_part, 1)
+    loop(0, 6, norm_part, 1)
+    next(reduce)
     aback.finish()
     db_in[...] = jnp.zeros((256, 128), f32)
     dc_in[...] = jnp.zeros((256, 128), f32)
 
-    def d_mix(j, d_act):
-        m = mixed[j]
+    def d_mix(j, u, d_act):
+        m = convolved(j, u)
         sig = sigmoid(m)
         d_m = d_act * (sig * (1.0 + m * (1.0 - sig)))
-        mixed[j] = d_m
+        ys[j] = d_m
         back_out[:, cols(j)] = low(d_m[0:16])
 
-    def carry_back(j, carry):
+    def carry_back(j, u):
         s_in, d_s = state(inc, j), state(inc2, j)
         x, dyf = wide(act[j]), wide(dys[j])
         w = spread(toward, j)
@@ -840,13 +958,15 @@
         pair = wide(s_in) * wide(d_s)
         prods[pl.ds(2 * j, 1), :] = jnp.sum(pair[:64], axis=0, keepdims=True)
         prods[pl.ds(2 * j + 1, 1), :] = jnp.sum(pair[64:], axis=0, keepdims=True)
-        d_mix(j, dxs[j] + d_w + skip[:, cols(j)] * dyf)
-        return carry
-
-    lax.fori_loop(0, TILES, carry_back, 0)
+        d_mix(j, u, ys[j] + d_w + skip[:, cols(j)] * dyf)
+
+    loop(0, TILES // 2, carry_back, 4)
+    next(reduce)
+    loop(TILES // 2, TILES // 2, carry_back, 4)
+    next(reduce)
     ds = low(dscores[...])
-    d_mix(TILES, db_in[...] + dot_tn(ds, c_out))
-    d_mix(TILES + 1, dc_in[...] + dot(ds, b_in))
+    d_mix(TILES, 0, db_in[...] + dot_tn(ds, c_out))
+    d_mix(TILES + 1, 1, dc_in[...] + dot(ds, b_in))
     behind = neighbour(1, back_out, back_in, -1, me > 0)
 
     q = qin[...] + qw[...]
@@ -854,7 +974,7 @@
     at_end = lax.broadcasted_iota(jnp.int32, (256, 128), 0) == 255
     d_l = running_sums(usum[...] - q + jnp.where(at_end, d_last, 0.0), True)
     dt = steps[...]
-    raw = proj[:, DI + CONVC:DI + CONVC + 128] + heads[0:1, :]
+    raw = dt_in[...] + heads[0:1, :]
     d_raw = (q / jnp.maximum(dt, 1e-30) - heads[1:2, :] * d_l) * sigmoid(raw)
     d_raw = jnp.where(lane < H, d_raw, 0.0)
     headsums[...] = jnp.zeros((8, 128), f32)
@@ -863,8 +983,9 @@
     headsums[3:4, :] = jnp.sum(by_pair[64:], axis=0, keepdims=True)
     headsums[0:1, :] = jnp.sum(d_raw, axis=0, keepdims=True)
     headsums[1:2, :] = -jnp.sum(d_l * dt, axis=0, keepdims=True)
-    dproj[:, DI + CONVC:DI + CONVC + 128] = low(d_raw)
-    dproj[:, DI + CONVC + 128:] = jnp.zeros((256, 128), bf16)
+    dproj[:, CONVC:CONVC + 128] = low(d_raw)
+    dproj[:, CONVC + 128:] = jnp.zeros((256, 128), bf16)
+    next(reduce)
 
     @pl.when(me == 31)
     def _():
@@ -872,56 +993,64 @@
 
     pl.when(me < 31)(behind.wait_recv)
 
-    def conv_back(j, carry):
-        d_m = mixed[j]
-        shift[0:8, :] = wide(halo_in[:, cols(j)])[8:16, :]
-        shift[8:264, :] = wide(low(proj[:, pl.ds(pl.multiple_of(DI + 128 * j, 128), 128)]))
+    def conv_back(j, u):
+        d_m = ys[j]
+        shift[u, 0:8, :] = wide(halo_in[:, cols(j)])[8:16, :]
+        shift[u, 8:264, :] = wide(conv_in[:, cols(j)])
         for k in range(4):
-            sums[k:k + 1, cols(j)] = jnp.sum(d_m * shift[5 + k:261 + k, :], axis=0, keepdims=True)
+            sums[k:k + 1, cols(j)] = jnp.sum(d_m * shift[u, 5 + k:261 + k, :], axis=0, keepdims=True)
         sums[4:5, cols(j)] = jnp.sum(d_m, axis=0, keepdims=True)
-        shift[0:256, :] = d_m
-        shift[256:264, :] = wide(back_in[:, cols(j)])[0:8, :]
+        shift2[u, 0:256, :] = d_m
+        shift2[u, 256:264, :] = wide(back_in[:, cols(j)])[0:8, :]
         total = taps[3:4, cols(j)] * d_m
         for k in range(3):
-            total = total + taps[k:k + 1, cols(j)] * shift[3 - k:259 - k, :]
-        dproj[:, pl.ds(pl.multiple_of(DI + 128 * j, 128), 128)] = low(total)
-        return carry
-
-    lax.fori_loop(0, TILES + 2, conv_back, 0)
+            total = total + taps[k:k + 1, cols(j)] * shift2[u, 3 - k:259 - k, :]
+        dproj[:, cols(j)] = low(total)
+
+    loop(0, TILES // 2, conv_back, 2)
+    next(reduce)
+    loop(TILES // 2, TILES // 2 + 2, conv_back, 2)
+    work.finish([g_z, g_o])
+    links.finish()
+    for copy in shared:
+        copy.wait_send()
     pl.when(me < 31)(front.wait_send)
     pl.when(me > 0)(behind.wait_send)
     decays.wait_send()
-    ahead.end()
     aback.end()
 
 
-def mixer(projected, d_branch, taps, gain, skip, heads):
+def mixer(gates, conv_in, dt_in, normed, hidden, given_out, d_branch, taps, gain, skip, heads, w_in, w_out):
     f32, bf16 = jnp.float32, jnp.bfloat16
-    tile, half = (256, 128), (16, CONVC)
+    tile, half, late = (256, 128), (16, CONVC), WIDE - DI
     vm = pltpu.VMEM
+    dma = pltpu.SemaphoreType.DMA
     scratch = [
-        vm((TILES + 2,) + tile, bf16), vm((TILES + 2,) + tile, f32), vm((TILES,) + tile, f32), vm((TILES,) + tile, bf16),
-        vm((TILES,) + tile, f32), vm((264, 128), f32), vm(half, bf16), vm(half, bf16), vm(half, bf16), vm(half, bf16),
+        vm((256, DI), bf16), vm((256, DI), bf16), vm((256, 768), bf16), vm((256, 1536), bf16), vm((256, 1536), bf16), vm((256, DI), bf16),
+        vm((2, 4, 2, 3, 16, DI), bf16), vm((2, 4, 2, 3, 32, 1536), bf16), vm((2, 1536, 256), bf16), dma((2,)),
+        vm((TILES + 2,) + tile, bf16), vm((TILES + 2,) + tile, f32), vm((TILES,) + tile, bf16),
+        vm((4, 264, 128), f32), vm((2, 264, 128), f32), vm(half, bf16), vm(half, bf16), vm(half, bf16), vm(half, bf16),
         vm(tile, f32), vm(tile, f32), vm(tile, f32), vm(tile, f32), vm((128, 256), f32), vm((256, 256), f32), vm((256, 256), f32),
         vm(tile, f32), vm(tile, f32), vm(tile, f32), vm((128, 128), f32), vm(tile, f32), vm(tile, f32), vm(tile, f32), vm(tile, f32),
-        vm((16, 128), f32),
+        vm((16, 128), f32), vm((128, 128), f32), vm((3072, 128), bf16), vm((3072, 128), bf16), vm((3072, 128), bf16),
     ]
-    scratch += [vm((128, 128), f32), vm((3072, 128), bf16), vm((3072, 128), bf16), vm((3072, 128), bf16)]
+    scratch += [vm((16, 112, 128), bf16), vm((16, 112, 128), bf16), vm((16, 96, 128), bf16)]
     for _ in range(2):
-        scratch += [vm((1536, 128), bf16), vm((16, 112, 128), bf16), vm((16, 112, 128), bf16), vm((16, 96, 128), bf16), vm((1536, 128), bf16)]
-    scratch += [pltpu.SemaphoreType.DMA((5,)), pltpu.SemaphoreType.DMA((5,)), pltpu.SemaphoreType.DMA((4, 16)),
-                pltpu.SemaphoreType.DMA((4, 16)), pltpu.SemaphoreType.DMA((4,))]
-    spec = pl.BlockSpec(memory_space=pltpu.VMEM)
+        scratch += [vm((1536, 128), bf16), vm((1536, 128), bf16)]
+    scratch += [dma((10,)), dma((10,)), dma((4, 16)), dma((4, 16)), dma((4,)), dma((108,)), dma((108,))]
+    scratch += scatter_scratch((12, 24), (DI, 1536))
+    near, far = pl.BlockSpec(memory_space=pltpu.VMEM), pl.BlockSpec(memory_space=pl.ANY)
     return pl.pallas_call(
         mixer_kernel,
-        out_shape=[jax.ShapeDtypeStruct((256, DI), bf16), jax.ShapeDtypeStruct((256, WIDE), bf16),
-                   jax.ShapeDtypeStruct((8, CONVC), f32), jax.ShapeDtypeStruct((8, 128), f32)],
-        in_specs=[spec] * 6,
-        out_specs=[spec] * 4,
+        out_shape=[jax.ShapeDtypeStruct((256, 1536), bf16), jax.ShapeDtypeStruct((256, late), bf16),
+                   jax.ShapeDtypeStruct((256, 1536), f32), jax.ShapeDtypeStruct((8, CONVC), f32), jax.ShapeDtypeStruct((8, 128), f32),
+                   jax.ShapeDtypeStruct((16, DI), f32), jax.ShapeDtypeStruct((24, 1536), f32)],
+        in_specs=[near] * 11 + [far] * 2,
+        out_specs=[near] * 7,
         scratch_shapes=scratch,
-        compiler_params=pltpu.CompilerParams(collective_id=2, has_side_effects=True, vmem_limit_bytes=60 << 20),
+        compiler_params=pltpu.CompilerParams(collective_id=2, has_side_effects=True, vmem_limit_bytes=62 << 20),
         name="mixer",
-    )(projected, d_branch, taps, gain, skip, heads)
+    )(gates, conv_in, dt_in, normed, hidden, given_out, d_branch, taps, gain, skip, heads, w_in, w_out)
 
 
 def rms_scale(values, gain):
@@ -969,28 +1098,27 @@
     residual = hidden[0].astype(jnp.float32)
     length = residual.shape[0]
     normed = rms_scale(residual, gain_norm_f).astype(jnp.bfloat16)
-    projected = jnp.dot(normed, w_in, preferred_element_type=jnp.float32)
+    gates = jnp.dot(normed, w_in[:, :DI], preferred_element_type=jnp.float32)
+    conv_in = jnp.dot(normed, w_in[:, DI : DI + CONVC], preferred_element_type=jnp.float32).astype(jnp.bfloat16)
+    dt_in = jnp.dot(normed, w_in[:, DI + CONVC : PARAMS], preferred_element_type=jnp.float32)
     grad_out = cotangent[0]
-    both_out = jnp.concatenate([grad_out, swap(grad_out)], axis=0)
     d_branch = jnp.einsum("td,kd->tk", grad_out, w_out, preferred_element_type=jnp.float32)
     taps = jnp.pad(jnp.concatenate([w_conv_f, b_conv_f[None]]), ((0, 3), (0, 0)))
     heads = jnp.pad(jnp.stack([dt_bias, decay_rates]), ((0, 6), (0, 80)))
-    branch, d_projected, sums, head_sums = mixer(
-        projected, d_branch, taps, gain_gate_f[None], jnp.repeat(d_skip, P_SIZE)[None], heads)
-    result = (residual + jnp.dot(branch, w_out, preferred_element_type=jnp.float32)).astype(jnp.bfloat16)
-    d_w_out = jnp.einsum("tk,td->kd", my_half(branch, core), both_out, preferred_element_type=jnp.float32).astype(jnp.bfloat16)
-    d_normed = jnp.einsum("tj,dj->td", d_projected, w_in, preferred_element_type=jnp.float32)
-    both_projected = jnp.concatenate([d_projected, swap(d_projected)], axis=0)
-    d_w_in = jnp.einsum("td,tj->dj", my_half(normed, core), both_projected, preferred_element_type=jnp.float32).astype(jnp.bfloat16)
+    result, d_late, d_normed, sums, head_sums, g_gates, g_out = mixer(
+        gates, conv_in, dt_in, normed, hidden[0], grad_out, d_branch, taps, gain_gate_f[None],
+        jnp.repeat(d_skip, P_SIZE)[None], heads, w_in, w_out)
+    d_normed = d_normed + jnp.einsum("tj,dj->td", d_late, w_in[:, DI:], preferred_element_type=jnp.float32)
+    both_late = jnp.concatenate([d_late, swap(d_late)], axis=0)
+    d_w_late = jnp.einsum("td,tj->dj", my_half(normed, core), both_late, preferred_element_type=jnp.float32).astype(jnp.bfloat16)
     norm_pull = jax.vjp(rms_scale, residual, gain_norm_f)[1]
     d_from_norm, d_gain_norm = norm_pull(d_normed)
     d_hidden = grad_out.astype(jnp.float32) + d_from_norm
-    g_in, g_out, total = scatter(
-        [d_w_in, d_w_out], [sums, head_sums, jnp.pad(d_gain_norm[None], ((0, 7), (0, 0)))], [12, 24])
+    g_late, total = scatter([d_w_late], [sums, head_sums, jnp.pad(d_gain_norm[None], ((0, 7), (0, 0)))], [12])
     return (
         result[None],
         d_hidden[None],
-        g_in[:12, :PROJ],
+        jnp.concatenate([g_gates[:12], g_late[:12, : PROJ - DI]], axis=1),
         g_out,
         total[:4, :26],
         total[4, :26],

time: 378 us -> 354 us (0.937)
  matrix products: 53.2 us -> 37.3 us
  Pallas kernels: 291 us -> 282 us
    dot_general x5, matrix products: 48.9 us -> 29.4 us  [the longest x1 8.37 us: shards(): jnp.einsum('tj,dj->td', d_late, w_in[:, DI:], preferred_element_type=jnp....]
    pallas_call x2, Pallas kernels: 207 us -> 198 us  [the longest x1 140 us: mixer(): pl.pallas_call(mixer_kernel, out_shape=[jax.ShapeDtypeStruct((256, 1536),...]
  transfers between devices with their start and end apart: 4 -> 2, of which waited for: 0 -> 0; matrix products, arithmetic and copies ran while one was open for 7% -> 3% of each run, Pallas kernels for 0% -> 0%
where the time goes in v4:
time: 354 us; the launch traced here: 351 us
  Pallas kernels  282 us (80%)
  matrix products  37.3 us (11%)
  local copies, waits for them, and re-layouts  24.2 us (7%)
  other arithmetic  6.19 us (2%)
    pallas_call x1, Pallas kernels, mixer(): pl.pallas_call(mixer_kernel, out_shape=[jax.ShapeDtypeStruct((256, 1536),...  140 us
    pallas_call x1, Pallas kernels, gather(): pl.pallas_call(functools.partial(gather_kernel, n=n, rows=tuple(rows)), o...  83.7 us
    pallas_call x1, Pallas kernels, scatter(): pl.pallas_call(functools.partial(scatter_kernel, rows=tuple(rows), wides=...  58.2 us
    dot_general x1, matrix products, shards(): jnp.einsum('tj,dj->td', d_late, w_in[:, DI:], preferred_element_type=jnp....  8.37 us
    dot_general x1, matrix products, shards(): jnp.dot(normed, w_in[:, DI:DI + CONVC], preferred_element_type=jnp.float32)  8.04 us
    dot_general x1, matrix products, shards(): jnp.einsum('td,kd->tk', grad_out, w_out, preferred_element_type=jnp.float32)  7.98 us
  transfers between devices with their start and end apart: 2, of which 0 were waited for; matrix products, arithmetic and copies ran while one was open for 3% of the time, Pallas kernels for 0%

profile of v4, /device:TPU:1, one launch (start us, length us, event | category | flops | bytes accessed | tf_op | source)
XLA Modules:
  0.0 350.9 jit_solution(10682521456679227323)
XLA Ops:
  0.6 0.7 pad_bitcast_fusion.2
  1.3 0.7 pad_bitcast_fusion
  2.0 0.7 pad.41
  2.7 0.1 concatenate.18
  2.8 1.0 fusion.29
  3.8 0.0 copy-start.3
  3.8 1.0 pad.46.refs_1_
  4.8 83.7 %gather_weights.1 = (bf16[2,2,4,2,3,16,6656]{6,5,4,3,2,1,0:T(8,128)(2,1)}, bf16[2,2,4,2,3,32,1536]{6,5,4,3,2,1,0:T(8,128)(2,1)S(1)}) custom-call(bf16[16,6656]{1,0:T(8,128)(2,1)S(1)} %pad.45.refs_0_, bf16[32,1536]{1,0:T(8,128)(2,1)S(1)} %pad.46.refs_1_), custom_call_target="tpu_custom_call" | custom-call | tf_op jit(solution)/shard_map/gather_weights/pallas_call | solution.py:156
  88.5 0.0 copy-start
  88.5 3.6 %copy-done = bf16[2,2,4,2,3,32,1536]{6,5,4,3,2,1,0:T(8,128)(2,1)} copy-done((bf16[2,2,4,2,3,32,1536]{6,5,4,3,2,1,0:T(8,128)(2,1)}, bf16[2,2,4,2,3,32,1536]{6,5,4,3,2,1,0:T(8,128)(2,1)S(1)}, u32[]{:S(2)}) %copy-start) | copy-done | bytes 9437208
  92.1 1.0 slice_convert_fusion
  93.1 0.1 reshape.68
  93.2 0.0 copy-start.7
  93.2 0.2 slice_reduce_fusion.2
  93.4 0.1 mul.72
  93.5 0.0 copy-done.3
  93.5 0.2 fusion.21
  93.8 0.4 copy-done.7
  94.2 0.3 fusion.17.normed
  94.5 0.0 copy-start.1
  94.5 0.0 slice-start
  94.5 2.3 fusion.27.dt_in
  96.8 8.0 %fusion.6.conv_in = bf16[256,3328]{1,0:T(8,128)(2,1)} fusion(bf16[256,1536]{1,0:T(8,128)(2,1)S(1)} %fusion.17.normed, bf16[1536,6656]{1,0:T(8,128)(2,1)} %bitcast.52), kind=kOutput, calls=%fused_computation.7 | convolution fusion | flops 2618097664 | bytes 12713984 | tf_op jit(solution)/shard_map/dot_general | solution.py:1102
  104.9 0.0 copy-done.1
  104.9 0.0 slice-done
  104.9 0.0 slice-done.1
  104.9 1.1 slice-done.4
  106.0 4.2 %fusion.4.gates = f32[256,3072]{1,0:T(8,128)} fusion(bf16[256,1536]{1,0:T(8,128)(2,1)S(1)} %fusion.17.normed, bf16[1536,6656]{1,0:T(8,128)(2,1)S(1)} %bitcast.57), kind=kOutput, calls=%fused_computation.4 | convolution fusion | flops 2415919104 | bytes 13369344 | tf_op jit(solution)/shard_map/dot_general | solution.py:1101
  110.2 1.1 slice_bitcast_fusion
  111.4 1.3 slice_reduce_fusion.1
  112.7 1.3 slice_reduce_fusion
  113.9 0.2 reshape.64
  114.1 0.1 broadcast_in_dim_reshape_squeeze.8
  114.3 0.7 broadcast_in_dim_reshape_squeeze.9.gain
  115.0 0.0 copy-done.11
  115.0 0.1 broadcast_in_dim.31
  115.1 0.7 broadcast_in_dim_reshape.3.skip
  115.8 0.7 select_maximum_fusion.taps
  116.4 8.0 %convolution_bitcast_fusion.db = f32[256,3072]{1,0:T(8,128)} fusion(bf16[3072,1536]{1,0:T(8,128)(2,1)} %bitcast.48, bf16[1,256,1536]{2,1,0:T(8,128)(2,1)S(1)} %copy-done.5), kind=kOutput, calls=%fused_computation.8 | convolution fusion | flops 2415919104 | bytes 13369344 | tf_op jit(solution)/shard_map/td,kd->tk/dot_general | solution.py:1105
  124.4 0.0 copy-done.13
  124.4 0.6 select_maximum_fusion.1.heads
  125.0 139.7 %mixer.1 = (bf16[256,1536]{1,0:T(8,128)(2,1)}, bf16[256,3584]{1,0:T(8,128)(2,1)}, f32[256,1536]{1,0:T(8,128)}, f32[8,3328]{1,0:T(8,128)}, f32[8,128]{1,0:T(8,128...) custom-call(f32[256,3072]{1,0:T(8,128)} %fusion.4.gates, bf16[256,3328]{1,0:T(8,128)(2,1)} %fusion.6.conv_in, ...), custom_call_target="tpu_custom_call" | custom-call | tf_op jit(solution)/shard_map/mixer/pallas_call | solution.py:1043
  264.7 0.1 collective-permute-start.1
  264.8 0.1 constant_dynamic-slice_fusion.1
  264.9 0.6 collective-permute-start
  265.4 8.4 %fusion.18 = (f32[1536]{0:T(1024)S(1)}, f32[256]{0:T(256)S(1)}, f32[256,1536]{1,0:T(8,128)S(1)}) fusion(f32[256]{0:T(256)S(1)} %fusion.30, bf16[1,256,1536]{2,1,0:T(8,128)(2,1)S(1)} %copy-done.4, f32[1536]{0:T(1024)S(1)} %mul.72, f32[256,1536]{1,0:T(8,128)} %get-tuple-element.25, bf16[256,3584]{1,0:T(8,128)(2,1)} %get-tuple-element.26, ...), kind=kOutput, calls=%fused_computation.21 | convolution fusion | flops 2821716224 | bytes 16791552 | tf_op jit(solution)/shard_map/tj,dj->td/dot_general | solution.py:1111
  273.8 0.6 pad.49.refs_3_
  274.5 0.0 copy-done.6
  274.5 1.6 fusion.20
  276.1 0.0 collective-permute-done
  276.1 0.0 collective-permute-done.1
  276.1 6.4 %convolution_convert_fusion = bf16[768,3584]{1,0:T(8,128)(2,1)} fusion(bf16[256,3584]{1,0:T(8,128)(2,1)} %collective-permute-done.1, bf16[256,3584]{1,0:T(8,128)(2,1)S(1)} %copy-done.14, bf16[256,768]{1,0:T(8,128)(2,1)S(1)} %collective-permute-done, bf16[256,768]{1,0:T(8,128)(2,1)S(1)} %get-tuple-element.35), kind=kOutput, calls=%fused_computation.6 | convolution fusion | flops 2830237696 | bytes 9961472 | tf_op jit(solution)/shard_map/td,tj->dj/dot_general | solution.py:1113
  282.5 58.2 %scatter_gradients.1 = (f32[16,3584]{1,0:T(8,128)}, f32[16,128]{1,0:T(8,128)}) custom-call(bf16[2,4,2,3,16,3584]{5,4,3,2,1,0:T(8,128)(2,1)} %bitcast.59, f32[8,3328]{1,0:T(8,128)} %get-tuple-element.28.refs_1_, f32[8,128]{1,0:T(8,128)} %get-tuple-element.29.refs_2_, f32[8,1536]{1,0:T(8,128)} %pad.49.refs_3_), custom_call_target="tpu_custom_call" | custom-call | tf_op jit(solution)/shard_map/scatter_gradients/pallas_call | solution.py:443
  340.7 1.3 slice_bitcast_fusion.2
  342.0 1.3 slice.68
  343.2 1.3 slice_bitcast_fusion.3
  344.5 1.2 slice_bitcast_fusion.6
  345.7 1.2 slice_bitcast_fusion.7
  346.9 0.1 copy.27
  346.9 0.6 reshape.67
  347.6 0.9 slice.67
  348.5 0.8 pad_maximum_fusion
  349.3 0.9 copy.31
  350.2 0.7 copy.32
  (33 shorter events, 0.1 us)
Async XLA Ops:
  3.8 89.8 %copy-start.3 = (bf16[1,256,1536]{2,1,0:T(8,128)(2,1)S(1)}, bf16[1,256,1536]{2,1,0:T(8,128)(2,1)}, u32[]{:S(2)}) copy-start(bf16[1,256,1536]{2,1,0:T(8,128)(2,1)} %param.11) | copy-start | bytes 2359300
  88.5 3.6 %copy-start = (bf16[2,2,4,2,3,32,1536]{6,5,4,3,2,1,0:T(8,128)(2,1)}, bf16[2,2,4,2,3,32,1536]{6,5,4,3,2,1,0:T(8,128)(2,1)S(1)}, u32[]{:S(2)}) copy-start(bf16[2,2,4,2,3,32,1536]{6,5,4,3,2,1,0:T(8,128)(2,1)S(1)} %get-tuple-element.23) | copy-start | bytes 28311556
  93.2 1.0 copy-start.7
  94.5 10.4 %copy-start.1 = (bf16[256,1536]{1,0:T(8,128)(2,1)}, bf16[256,1536]{1,0:T(8,128)(2,1)S(1)}, u32[]{:S(2)}) copy-start(bf16[256,1536]{1,0:T(8,128)(2,1)S(1)} %fusion.17.normed) | copy-start | bytes 2359300
  94.5 10.4 %slice-start = ((s8[20447232]{0:T(1024)(128)(4,1)}), s8[4194304]{0:T(1024)(128)(4,1)S(1)}, s32[]{:S(2)}) async-start(s8[20447232]{0:T(1024)(128)(4,1)} %bitcast.55), calls=%async_computation | async-start | bytes 8388608
  96.8 8.1 %slice-start.1 = ((s8[20447232]{0:T(1024)(128)(4,1)}), s8[4194304]{0:T(1024)(128)(4,1)S(1)}, s32[]{:S(2)}) async-start(s8[20447232]{0:T(1024)(128)(4,1)} %bitcast.55), calls=%async_computation.1 | async-start | bytes 8388608
  96.8 8.1 %slice-start.2 = ((s8[20447232]{0:T(1024)(128)(4,1)}), s8[4194304]{0:T(1024)(128)(4,1)S(1)}, s32[]{:S(2)}) async-start(s8[20447232]{0:T(1024)(128)(4,1)} %bitcast.55), calls=%async_computation.2 | async-start | bytes 8388608
  96.8 8.1 %slice-start.3 = ((s8[20447232]{0:T(1024)(128)(4,1)}), s8[4194304]{0:T(1024)(128)(4,1)S(1)}, s32[]{:S(2)}) async-start(s8[20447232]{0:T(1024)(128)(4,1)} %bitcast.55), calls=%async_computation.3 | async-start | bytes 8388608
  96.8 9.2 %slice-start.4 = ((s8[20447232]{0:T(1024)(128)(4,1)}), s8[3670016]{0:T(1024)(128)(4,1)S(1)}, s32[]{:S(2)}) async-start(s8[20447232]{0:T(1024)(128)(4,1)} %bitcast.55), calls=%async_computation.4 | async-start | bytes 7340032
  106.0 9.0 %copy-start.11 = (f32[48]{0:T(128)S(1)}, f32[48]{0:T(128)}, u32[]{:S(2)}) copy-start(f32[48]{0:T(128)} %param.21) | copy-start | bytes 580
  110.2 6.2 %copy-start.5 = (bf16[1,256,1536]{2,1,0:T(8,128)(2,1)S(1)}, bf16[1,256,1536]{2,1,0:T(8,128)(2,1)}, u32[]{:S(2)}) copy-start(bf16[1,256,1536]{2,1,0:T(8,128)(2,1)} %param.12) | copy-start | bytes 2359300
  116.4 8.0 %copy-start.12 = (f32[48]{0:T(128)S(1)}, f32[48]{0:T(128)}, u32[]{:S(2)}) copy-start(f32[48]{0:T(128)} %param.20) | copy-start | bytes 580
  116.4 8.0 %copy-start.13 = (f32[48]{0:T(128)S(1)}, f32[48]{0:T(128)}, u32[]{:S(2)}) copy-start(f32[48]{0:T(128)} %param.19) | copy-start | bytes 580
  125.0 139.8 %copy-start.2 = (bf16[256,1536]{1,0:T(8,128)(2,1)S(1)}, bf16[256,1536]{1,0:T(8,128)(2,1)}, u32[]{:S(2)}) copy-start(bf16[256,1536]{1,0:T(8,128)(2,1)} %copy-done.1) | copy-start | bytes 2359300
  125.0 140.4 %copy-start.4 = (bf16[1,256,1536]{2,1,0:T(8,128)(2,1)S(1)}, bf16[1,256,1536]{2,1,0:T(8,128)(2,1)}, u32[]{:S(2)}) copy-start(bf16[1,256,1536]{2,1,0:T(8,128)(2,1)} %param.11) | copy-start | bytes 2359300
  264.7 11.4 %collective-permute-start.1 = (bf16[256,3584]{1,0:T(8,128)(2,1)}, bf16[256,3584]{1,0:T(8,128)(2,1)}, u32[]{:S(2)}, u32[]{:S(2)}) collective-permute-start(bf16[256,3584]{1,0:T(8,128)(2,1)} %get-tuple-element.26), channel_id=1, source_target_pairs={{0,1},{1,0},{2,3},{3,2},{4,5},{5,4},{6,7},{7,6},{8,9},{9,8},{10,11... | collective-permute-start | bytes 5505032 | tf_op jit(solution)/shard_map/ppermute | solution.py:1061
  264.9 11.2 %collective-permute-start = (bf16[256,768]{1,0:T(8,128)(2,1)S(1)}, bf16[256,768]{1,0:T(8,128)(2,1)S(1)}, u32[]{:S(2)}, u32[]{:S(2)}) collective-permute-start(bf16[256,768]{1,0:T(8,128)(2,1)S(1)} %get-tuple-element.36), channel_id=1, source_target_pairs={{0,1},{1,0},{2,3},{3,2},{4,5},{5,4},{6,7},{7,6},{8,9},{9,8},{10,11... | collective-permute-start | bytes 1179656 | tf_op jit(solution)/shard_map/ppermute | solution.py:1061
  265.4 9.0 %copy-start.6 = (bf16[1,256,1536]{2,1,0:T(8,128)(2,1)S(1)}, bf16[1,256,1536]{2,1,0:T(8,128)(2,1)}, u32[]{:S(2)}) copy-start(bf16[1,256,1536]{2,1,0:T(8,128)(2,1)} %param.12) | copy-start | bytes 2359300
  274.5 1.6 copy-start.14
  282.5 66.0 %copy-start.9 = (f32[16,3072]{1,0:T(8,128)S(1)}, f32[16,3072]{1,0:T(8,128)}, u32[]{:S(2)}) copy-start(f32[16,3072]{1,0:T(8,128)} %get-tuple-element.27) | copy-start | bytes 589828
  340.7 8.7 %copy-start.8 = (bf16[256,1536]{1,0:T(8,128)(2,1)S(1)}, bf16[256,1536]{1,0:T(8,128)(2,1)}, u32[]{:S(2)}) copy-start(bf16[256,1536]{1,0:T(8,128)(2,1)} %get-tuple-element.24) | copy-start | bytes 2359300
  340.7 9.5 %copy-start.10 = (f32[24,1536]{1,0:T(8,128)S(1)}, f32[24,1536]{1,0:T(8,128)}, u32[]{:S(2)}) copy-start(f32[24,1536]{1,0:T(8,128)} %get-tuple-element.59) | copy-start | bytes 442372

commit v5 on v4

--- a/solution.py
+++ b/solution.py
@@ -9,6 +9,7 @@
 MESH = pl.DeviceIdType.MESH
 ALL = ("z", "y", "x", "c")
 ORDERS = (("z", "y", "x"), ("y", "x", "z"), ("x", "z", "y"))
+PARTS = range(3)
 
 
 class Links:
@@ -57,115 +58,156 @@
     return {**at, axis: lax.rem(at[axis] + steps + 4, 4)}
 
 
-def gather_kernel(*refs, n, rows):
-    shards, fulls, refs = refs[:n], refs[n:2 * n], refs[2 * n:]
-    stage, landed, unit, (send, recv, own) = refs[:n], refs[n:2 * n], refs[2 * n:3 * n], refs[3 * n:]
+def targets(at):
+    z, x, c = at["z"], at["x"], at["c"]
+    to_z, to_c = 2 * lax.rem(z, 2) + x // 2, z // 2
+    return to_z, to_c, 2 * c + z // 2, jnp.logical_and(to_z == z, to_c == c)
+
+
+class Ring:
+    def __init__(self, links, at, full, phase, share):
+        self.links, self.at, self.full, self.phase, self.share = links, at, full, phase, share
+        self.c = at["c"]
+        self.shared = []
+
+    def to_sibling(self, ref):
+        if self.share:
+            self.shared.append(self.links.copy(ref, ref, {"c": 1 - self.c}))
+
+    def start(self):
+        self.near = {}
+        for part in PARTS:
+            have, axis = ORDERS[part][:self.phase], ORDERS[part][self.phase]
+            mine = block(self.full, part, self.c, self.at, have)
+            self.near[part] = [self.links.copy(mine, mine, {axis: moved(self.at, axis, steps)[axis]}) for steps in (1, -1)]
+
+    def turn(self):
+        self.far = {}
+        for part in PARTS:
+            have, axis = ORDERS[part][:self.phase], ORDERS[part][self.phase]
+            self.far[part] = []
+            for way, steps in ((0, 1), (1, -1)):
+                self.near[part][way].wait_recv()
+                piece = block(self.full, part, self.c, moved(self.at, axis, -steps), have, way)
+                self.far[part].append(self.links.copy(piece, piece, {axis: moved(self.at, axis, steps)[axis]}))
+        for part in PARTS:
+            have, axis = ORDERS[part][:self.phase], ORDERS[part][self.phase]
+            for steps in (1, -1):
+                self.to_sibling(block(self.full, part, self.c, moved(self.at, axis, -steps), have))
+
+    def finish(self):
+        for part in PARTS:
+            have, axis = ORDERS[part][:self.phase], ORDERS[part][self.phase]
+            for way in (0, 1):
+                self.far[part][way].wait_recv()
+            self.to_sibling(block(self.full, part, self.c, moved(self.at, axis, 2), have))
+
+    def share_held(self):
+        for part in PARTS:
+            self.to_sibling(block(self.full, part, self.c, self.at, ORDERS[part][:self.phase]))
+
+    def end(self):
+        for copy in self.shared:
+            copy.wait_recv()
+
+
+def gather_kernel(*refs):
+    shards, fulls, refs = refs[:2], refs[2:4], refs[4:]
+    stages, stage_o, landed, unit, (send, recv, first_recv, own) = refs[:2], refs[2], refs[3:5], refs[5:7], refs[7:]
     at = place()
     z, y, x, c = (at[name] for name in ALL)
-    to_z, to_c = 2 * lax.rem(z, 2) + x // 2, z // 2
+    to_z, to_c, from_z, home = targets(at)
     slot = 2 * lax.rem(x, 2) + c
-    from_z = 2 * c + z // 2
     barrier = pltpu.get_barrier_semaphore()
     for axis in ("z", "y", "x"):
-        for steps in (1, -1):
+        for steps in (1, 2, 3):
             pl.semaphore_signal(barrier, inc=1, device_id={axis: moved(at, axis, steps)[axis]}, device_id_type=MESH)
     pl.semaphore_signal(barrier, inc=1, device_id={"c": 1 - c}, device_id_type=MESH)
     for k in range(4):
         sx, sc = 2 * lax.rem(z, 2) + k // 2, k % 2
-        other = jnp.logical_or(jnp.logical_or(sx != x, sc != c), from_z != z)
-
-        @pl.when(other)
+
+        @pl.when(jnp.logical_not(jnp.logical_and(home, jnp.logical_and(sx == x, sc == c))))
         def _():
             pl.semaphore_signal(barrier, inc=1, device_id=(from_z, y, sx, jnp.int32(sc)), device_id_type=MESH)
-    home = jnp.logical_and(to_z == z, to_c == c)
-    pl.semaphore_wait(barrier, 11 - home.astype(jnp.int32))
+    pl.semaphore_wait(barrier, 14 - home.astype(jnp.int32))
 
     links = Links(send, recv)
     first = []
-    for i in range(n):
+    for i in range(2):
         wide = shards[i].shape[1] // 4
         for tx in range(4):
             k = links.used
             links.used += 1
             src = shards[i].at[:, pl.ds(tx * wide, wide)]
             remote = pltpu.make_async_remote_copy(
-                src_ref=src, dst_ref=landed[i].at[slot], send_sem=send.at[k], recv_sem=recv.at[4 * i + slot],
+                src_ref=src, dst_ref=landed[i].at[slot], send_sem=send.at[k], recv_sem=first_recv.at[4 * i + slot],
                 device_id=(to_z, y, jnp.int32(tx), to_c), device_id_type=MESH)
-            local = pltpu.make_async_copy(src, landed[i].at[slot], recv.at[4 * i + slot])
+            local = pltpu.make_async_copy(src, landed[i].at[slot], first_recv.at[4 * i + slot])
             mine = jnp.logical_and(home, x == tx)
             pl.when(jnp.logical_not(mine))(remote.start)
             pl.when(mine)(local.start)
             first.append((remote, mine))
-    kept = []
-    for i in range(n):
-        deep, height = rows[i], unit[i].shape[1]
+    kept, direct = [], []
+    for i in range(2):
+        wide = stages[i].shape[1]
         for k in range(4):
-            pltpu.make_async_copy(landed[i].at[k], landed[i].at[k], recv.at[4 * i + k]).wait()
-            stage[i][pl.ds(deep * k, deep), :] = landed[i][k, :deep, :].astype(jnp.float32)
-        for part in range(3):
-            unit[i][part] = stage[i][pl.ds(part * height, height), :].astype(jnp.bfloat16)
-        for part in range(3):
-            copy = pltpu.make_async_copy(unit[i].at[part], block(fulls[i], part, c, at, ()), own.at[3 * i + part])
+            pltpu.make_async_copy(landed[i].at[k], landed[i].at[k], first_recv.at[4 * i + k]).wait()
+            stages[i][pl.ds(12 * k, 12), :] = landed[i][k, :12, :wide].astype(jnp.float32)
+            for b in range(2 * i):
+                stage_o[pl.ds(24 * k + 12 * b, 12), :] = landed[i][k, :12, wide + 384 * b:wide + 384 * b + 384].astype(jnp.float32)
+        for part in PARTS:
+            unit[i][part, :, :wide] = stages[i][pl.ds(16 * part, 16), :].astype(jnp.bfloat16)
+            for b in range(2 * i):
+                unit[i][part, :, wide + 384 * b:wide + 384 * b + 384] = stage_o[pl.ds(32 * part + 16 * b, 16), :].astype(jnp.bfloat16)
+        for part in PARTS:
+            axis = ORDERS[part][0]
+            there = block(fulls[i], part, c, at, ())
+            for steps in (1, 3, 2):
+                direct.append(links.copy(unit[i].at[part], there, {axis: moved(at, axis, steps)[axis]}))
+            copy = pltpu.make_async_copy(unit[i].at[part], there, own.at[3 * i + part])
             copy.start()
             kept.append(copy)
-    sibling = {"c": 1 - c}
-    streams = [(i, part) for i in range(n) for part in range(3)]
-    for phase in range(3):
-        near = {}
-        for i, part in streams:
-            have, axis = ORDERS[part][:phase], ORDERS[part][phase]
-            mine = unit[i].at[part] if phase == 0 else block(fulls[i], part, c, at, have)
-            there = block(fulls[i], part, c, at, have)
-            near[i, part] = [links.copy(mine, there, {axis: moved(at, axis, steps)[axis]}) for steps in (1, -1)]
-            if phase == 0:
-                links.copy(mine, there, sibling)
-        far = {}
-        for i, part in streams:
-            have, axis = ORDERS[part][:phase], ORDERS[part][phase]
-            far[i, part] = []
-            for way, steps in ((0, 1), (1, -1)):
-                near[i, part][way].wait_recv()
-                behind = moved(at, axis, -steps)
-                piece = block(fulls[i], part, c, behind, have, way)
-                far[i, part].append(links.copy(piece, piece, {axis: moved(at, axis, steps)[axis]}))
-                whole = block(fulls[i], part, c, behind, have)
-                links.copy(whole, whole, sibling)
-        for i, part in streams:
-            have, axis = ORDERS[part][:phase], ORDERS[part][phase]
-            for way in (0, 1):
-                far[i, part][way].wait_recv()
-                piece = block(fulls[i], part, c, moved(at, axis, 2), have, way)
-                links.copy(piece, piece, sibling)
-        if phase == 0:
-            for copy in kept:
-                copy.wait()
-    for made in links.sent:
-        if made.device_id is sibling:
-            made.wait_recv()
+    rings = [Ring(links, at, fulls[i], 1, False) for i in range(2)]
+    for i in range(2):
+        for copy in direct[9 * i:9 * i + 9]:
+            copy.wait_recv()
+        for copy in kept[3 * i:3 * i + 3]:
+            copy.wait()
+        rings[i].start()
+    for ring in rings:
+        ring.turn()
+    last = Ring(links, at, fulls[0], 2, True)
+    rings[0].finish()
+    last.start()
+    last.share_held()
+    rings[1].finish()
+    other = Ring(links, at, fulls[1], 2, True)
+    other.share_held()
+    last.turn()
+    last.finish()
+    last.end()
+    other.end()
     links.finish()
     for remote, mine in first:
         pl.when(jnp.logical_not(mine))(remote.wait_send)
 
 
-def gather(shards, rows):
-    n = len(shards)
-    heights = [4 * r // 3 for r in rows]
+def gather(late, early):
+    shards = (late, early)
     wides = [s.shape[1] for s in shards]
-    fulls = [jax.ShapeDtypeStruct((2, 2, 4, 2, 3, h, w), jnp.bfloat16) for h, w in zip(heights, wides)]
-    count = n * (4 + 3 * (3 * 3 * 2 + 1 + 6))
-    outs = pl.pallas_call(
-        functools.partial(gather_kernel, n=n, rows=tuple(rows)),
-        out_shape=fulls,
-        in_specs=[pl.BlockSpec(memory_space=pltpu.VMEM)] * n,
-        out_specs=[pl.BlockSpec(memory_space=pl.ANY)] * n,
-        scratch_shapes=[pltpu.VMEM((3 * h, w // 4), jnp.float32) for h, w in zip(heights, wides)]
-        + [pltpu.VMEM((4, s.shape[0], w // 4), jnp.bfloat16) for s, w in zip(shards, wides)]
-        + [pltpu.VMEM((3, h, w // 4), jnp.bfloat16) for h, w in zip(heights, wides)]
-        + [pltpu.SemaphoreType.DMA((count,)), pltpu.SemaphoreType.DMA((count,)), pltpu.SemaphoreType.DMA((3 * n,))],
+    vm, dma = pltpu.VMEM, pltpu.SemaphoreType.DMA
+    return pl.pallas_call(
+        gather_kernel,
+        out_shape=[jax.ShapeDtypeStruct((2, 2, 4, 2, 3, 16, w), jnp.bfloat16) for w in wides],
+        in_specs=[pl.BlockSpec(memory_space=pltpu.VMEM)] * 2,
+        out_specs=[pl.BlockSpec(memory_space=pl.ANY)] * 2,
+        scratch_shapes=[vm((48, wides[0] // 4), jnp.float32), vm((48, 768), jnp.float32), vm((96, 384), jnp.float32)]
+        + [vm((4, 16, w // 4), jnp.bfloat16) for w in wides]
+        + [vm((3, 16, w // 4), jnp.bfloat16) for w in wides]
+        + [dma((96,)), dma((96,)), dma((8,)), dma((6,))],
         compiler_params=pltpu.CompilerParams(collective_id=0, has_side_effects=True, vmem_limit_bytes=32 << 20),
         name="gather_weights",
     )(*shards)
-    return [o.reshape(128 * r, w) for o, r, w in zip(outs, rows, wides)]
 
 
 def span(shape, axis, at):
@@ -246,131 +288,137 @@
 ALL_CUT = [slice(None)] * 5
 
 
-def scatter_scratch(rows, wides):
-    heights = [4 * r // 3 for r in rows]
-    tall = [-(-r // 8) * 8 for r in rows]
+def scatter_scratch(wide, split):
+    vm, f32 = pltpu.VMEM, jnp.float32
     scratch = []
-    size = {(i, part): (2, 4, 2, heights[i], wides[i]) for i in range(len(rows)) for part in range(3)}
+    size = {part: (2, 4, 2, 16, wide) for part in PARTS}
     for phase in range(3):
-        for s in size:
-            shape = without(size[s], ORDERS[s[1]][2 - phase])
-            scratch += [pltpu.VMEM(shape, jnp.bfloat16)] * 2
-            scratch += [pltpu.VMEM(half_shape(shape, way), jnp.bfloat16) for way in (0, 1)]
+        for part in PARTS:
+            shape = without(size[part], ORDERS[part][2 - phase])
+            scratch += [vm(shape, jnp.bfloat16)] * (3 if phase else 2)
+            if phase == 0:
+                scratch += [vm(half_shape(shape, way), jnp.bfloat16) for way in (0, 1)]
             if phase < 2:
-                scratch += [pltpu.VMEM(shape, jnp.bfloat16)]
-            size[s] = shape
-    scratch += [pltpu.VMEM((3 * t, w // 4), jnp.float32) for t, w in zip(heights, wides)]
-    scratch += [pltpu.VMEM((4, t, w // 4), jnp.float32) for t, w in zip(tall, wides)] * 2
-    scratch += [pltpu.SemaphoreType.DMA((4 * len(rows),))] * 2
-    return scratch
+                scratch += [vm(shape, jnp.bfloat16)]
+            size[part] = shape
+    first = 768 if split else wide // 4
+    scratch += [vm((48, first), f32), vm((96, 384), f32), vm((4, 16, wide // 4), f32), vm((4, 16, wide // 4), f32)]
+    return scratch + [pltpu.SemaphoreType.DMA((4,))] * 2
 
 
 class Scatter:
-    def __init__(self, at, links, sources, rows, wides, refs):
-        n = len(rows)
+    def __init__(self, at, links, source, wide, split, refs):
         take = iter(refs)
-        self.at, self.links, self.rows, self.n = at, links, rows, n
-        self.streams = [(i, part) for i in range(n) for part in range(3)]
+        self.at, self.links, self.split = at, links, split
         self.near, self.relay, self.acc = {}, {}, {}
         for phase in range(3):
-            for s in self.streams:
-                self.near[s, phase] = [next(take), next(take)]
-                self.relay[s, phase] = [next(take), next(take)]
+            for s in PARTS:
+                self.near[s, phase] = [next(take) for _ in range(3 if phase else 2)]
+                self.relay[s] = [next(take), next(take)] if phase == 0 else self.relay[s]
                 self.acc[s, phase] = next(take) if phase < 2 else None
-        self.fin, self.staged, self.landed = ([next(take) for _ in range(n)] for _ in range(3))
-        self.last, self.own = next(take), next(take)
-        self.size = {s: (2, 4, 2, 4 * rows[s[0]] // 3, wides[s[0]]) for s in self.streams}
-        self.source = {s: sources[s[0]].at[:, :, :, s[1]] for s in self.streams}
+        self.fin, self.fin_o, self.staged, self.landed, self.last, self.own = (next(take) for _ in range(6))
+        self.size = {s: (2, 4, 2, 16, wide) for s in PARTS}
+        self.source = {s: source.at[:, :, :, s] for s in PARTS}
+
+    def add(self, phase, s, axis, shape):
+        terms = [slab_of(self.source[s], span(self.size[s], axis, self.at), shape)]
+        terms += [slab_of(buf, ALL_CUT, shape) for buf in self.near[s, phase]]
+        if phase < 2:
+            add_up(slab_to(self.acc[s, phase], shape), terms, shape)
+            self.source[s], self.size[s] = self.acc[s, phase], shape
+            return
+        total = terms[0](0, 0, 0).astype(jnp.float32)
+        for term in terms[1:]:
+            total = total + term(0, 0, 0).astype(jnp.float32)
+        first = self.fin.shape[1]
+        self.fin[pl.ds(16 * s, 16), :] = total[:, :first]
+        if self.split:
+            for b in range(2):
+                self.fin_o[pl.ds(32 * s + 16 * b, 16), :] = total[:, first + 384 * b:first + 384 * b + 384]
 
     def steps(self):
         at, links, size, source = self.at, self.links, self.size, self.source
-        for phase in range(3):
-            sent, lent = {}, {}
-            for s in self.streams:
-                axis = ORDERS[s[1]][2 - phase]
-                shape = without(size[s], axis)
-                cuts = {k: span(size[s], axis, moved(at, axis, k)) for k in (1, 2, 3)}
-                to = {k: {axis: moved(at, axis, k)[axis]} for k in (1, 3)}
-                lent[s], sent[s] = [], []
-                for way, step in ((0, 1), (1, 3)):
-                    src = source[s].at[tuple(cut_half(cuts[2], shape, way))]
-                    lent[s].append(links.copy(src, self.relay[s, phase][way], to[step]))
-                for way, step in ((0, 1), (1, 3)):
-                    src = source[s].at[tuple(cut_half(cuts[step], shape, 1 - way))]
-                    dst = self.near[s, phase][way].at[tuple(cut_half(ALL_CUT, shape, 1 - way))]
-                    sent[s].append(links.copy(src, dst, to[step]))
-            yield
-            for s in self.streams:
-                axis = ORDERS[s[1]][2 - phase]
-                shape = without(size[s], axis)
-                for way, step in ((0, 1), (1, 3)):
-                    lent[s][way].wait_recv()
-                    hs = half_shape(shape, way)
-                    cut = cut_half(span(size[s], axis, moved(at, axis, step)), shape, way)
-                    buf = self.relay[s, phase][way]
-                    add_up(slab_to(buf, hs), [slab_of(source[s], cut, hs), slab_of(buf, ALL_CUT, hs)], hs)
-                    dst = self.near[s, phase][way].at[tuple(cut_half(ALL_CUT, shape, way))]
-                    sent[s].append(links.copy(buf, dst, {axis: moved(at, axis, step)[axis]}))
-            yield
-            for s in self.streams:
-                i, part = s
-                axis = ORDERS[part][2 - phase]
-                shape = without(size[s], axis)
+        sent, lent = {}, {}
+        for s in PARTS:
+            axis = ORDERS[s][2]
+            shape = without(size[s], axis)
+            lent[s] = []
+            for way, step in ((0, 1), (1, 3)):
+                src = source[s].at[tuple(cut_half(span(size[s], axis, moved(at, axis, 2)), shape, way))]
+                lent[s].append(links.copy(src, self.relay[s][way], {axis: moved(at, axis, step)[axis]}))
+        for s in PARTS:
+            axis = ORDERS[s][2]
+            shape = without(size[s], axis)
+            sent[s] = []
+            for way, step in ((0, 1), (1, 3)):
+                src = source[s].at[tuple(cut_half(span(size[s], axis, moved(at, axis, step)), shape, 1 - way))]
+                dst = self.near[s, 0][way].at[tuple(cut_half(ALL_CUT, shape, 1 - way))]
+                sent[s].append(links.copy(src, dst, {axis: moved(at, axis, step)[axis]}))
+        yield
+        for s in PARTS:
+            axis = ORDERS[s][2]
+            shape = without(size[s], axis)
+            for way, step in ((0, 1), (1, 3)):
+                lent[s][way].wait_recv()
+                hs = half_shape(shape, way)
+                cut = cut_half(span(size[s], axis, moved(at, axis, step)), shape, way)
+                buf = self.relay[s][way]
+                add_up(slab_to(buf, hs), [slab_of(source[s], cut, hs), slab_of(buf, ALL_CUT, hs)], hs)
+                dst = self.near[s, 0][way].at[tuple(cut_half(ALL_CUT, shape, way))]
+                sent[s].append(links.copy(buf, dst, {axis: moved(at, axis, step)[axis]}))
+        yield
+        for phase in (1, 2):
+            for s in PARTS:
                 for copy in sent[s]:
                     copy.wait_recv()
-                terms = [slab_of(source[s], span(size[s], axis, at), shape)]
-                terms += [slab_of(self.near[s, phase][way], ALL_CUT, shape) for way in (0, 1)]
-                if phase < 2:
-                    add_up(slab_to(self.acc[s, phase], shape), terms, shape)
-                    source[s], size[s] = self.acc[s, phase], shape
-                else:
-                    total = terms[0](0, 0, 0).astype(jnp.float32)
-                    for term in terms[1:]:
-                        total = total + term(0, 0, 0).astype(jnp.float32)
-                    self.fin[i][pl.ds(part * shape[3], shape[3]), :] = total
+                axis = ORDERS[s][3 - phase]
+                self.add(phase - 1, s, axis, without(size[s], axis))
+                axis = ORDERS[s][2 - phase]
+                sent[s] = []
+                for k in (1, 3, 2):
+                    src = source[s].at[tuple(span(size[s], axis, moved(at, axis, k)))]
+                    sent[s].append(links.copy(src, self.near[s, phase][k - 1], {axis: moved(at, axis, k)[axis]}))
+            yield
+        for s in PARTS:
+            for copy in sent[s]:
+                copy.wait_recv()
+            axis = ORDERS[s][0]
+            self.add(2, s, axis, without(size[s], axis))
         z, y, x, c = (at[name] for name in ALL)
-        from_z = 2 * c + z // 2
-        home = jnp.logical_and(2 * lax.rem(z, 2) + x // 2 == z, z // 2 == c)
-        final = []
-        for i in range(self.n):
-            deep = self.rows[i]
-            staged, landed = self.staged[i], self.landed[i]
-            for k in range(4):
-                sx, sc = 2 * lax.rem(z, 2) + k // 2, k % 2
-                staged[k] = jnp.zeros(staged.shape[1:], jnp.float32)
-                staged[k, :deep] = self.fin[i][pl.ds(deep * k, deep), :]
-                mine = jnp.logical_and(home, jnp.logical_and(sx == x, sc == c))
-                remote = pltpu.make_async_remote_copy(
-                    src_ref=staged.at[k], dst_ref=landed.at[x], send_sem=self.own.at[4 * i + k], recv_sem=self.last.at[4 * i + x],
-                    device_id=(from_z, y, sx, jnp.int32(sc)), device_id_type=MESH)
-                local = pltpu.make_async_copy(staged.at[k], landed.at[x], self.last.at[4 * i + x])
-                pl.when(jnp.logical_not(mine))(remote.start)
-                pl.when(mine)(local.start)
-                final.append((remote, mine))
-        self.final = final
+        _, _, from_z, home = targets(at)
+        self.final = []
+        first, staged, landed = self.fin.shape[1], self.staged, self.landed
+        for k in range(4):
+            sx, sc = 2 * lax.rem(z, 2) + k // 2, k % 2
+            staged[k] = jnp.zeros(staged.shape[1:], jnp.float32)
+            staged[k, :12, :first] = self.fin[pl.ds(12 * k, 12), :]
+            for b in range(2 if self.split else 0):
+                staged[k, :12, first + 384 * b:first + 384 * b + 384] = self.fin_o[pl.ds(24 * k + 12 * b, 12), :]
+            mine = jnp.logical_and(home, jnp.logical_and(sx == x, sc == c))
+            remote = pltpu.make_async_remote_copy(
+                src_ref=staged.at[k], dst_ref=landed.at[x], send_sem=self.own.at[k], recv_sem=self.last.at[x],
+                device_id=(from_z, y, sx, jnp.int32(sc)), device_id_type=MESH)
+            local = pltpu.make_async_copy(staged.at[k], landed.at[x], self.last.at[x])
+            pl.when(jnp.logical_not(mine))(remote.start)
+            pl.when(mine)(local.start)
+            self.final.append((remote, mine))
         yield
 
-    def finish(self, outs):
-        for i in range(self.n):
-            wide_ = self.fin[i].shape[1]
-            for tx in range(4):
-                pltpu.make_async_copy(self.landed[i].at[tx], self.landed[i].at[tx], self.last.at[4 * i + tx]).wait()
-                outs[i][:, pl.ds(tx * wide_, wide_)] = self.landed[i][tx]
+    def finish(self, out, out_o=None):
+        first = self.fin.shape[1]
+        for tx in range(4):
+            pltpu.make_async_copy(self.landed.at[tx], self.landed.at[tx], self.last.at[tx]).wait()
+            out[:, pl.ds(tx * first, first)] = self.landed[tx, :, :first]
+            for b in range(2 if self.split else 0):
+                out_o[pl.ds(12 * b, 12), pl.ds(tx * 384, 384)] = self.landed[tx, :12, first + 384 * b:first + 384 * b + 384]
         for remote, mine in self.final:
             pl.when(jnp.logical_not(mine))(remote.wait_send)
 
 
-def targets(at):
-    z, x, c = at["z"], at["x"], at["c"]
-    to_z, to_c = 2 * lax.rem(z, 2) + x // 2, z // 2
-    return to_z, to_c, 2 * c + z // 2, jnp.logical_and(to_z == z, to_c == c)
-
-
-def scatter_kernel(*refs, rows, wides):
-    n = len(rows)
-    parts_in, smalls, refs = refs[:n], refs[n:n + 3], refs[n + 3:]
-    outs, small_out, refs = refs[:n], refs[n], refs[n + 1:]
-    rounds, (send, recv), refs = refs[:4], refs[4:6], refs[6:]
+SMALL = 1792
+
+
+def scatter_kernel(part_in, sums_in, heads_in, gain_in, out, small_out, core_sum, core_other, rounds_x, rounds_y, rounds_z, whole, send, recv, *refs, wide):
     at = place()
     z, y, x, c = (at[name] for name in ALL)
     to_z, to_c, _, home = targets(at)
@@ -386,69 +434,66 @@
     pl.semaphore_wait(barrier, 14 - home.astype(jnp.int32))
 
     links = Links(send, recv)
-    work = Scatter(at, links, parts_in, rows, wides, refs)
-    sums = [None]
-
-    def small_start(k):
-        axis = ("c", "x", "y", "z")[k]
-        if k == 0:
-            start = 0
-            for part in smalls:
-                rounds[0][c, :, start:start + part.shape[1]] = part[...]
-                start += part.shape[1]
-        else:
-            rounds[k][at[axis]] = sums[0]
-        held = rounds[k].at[at[axis]]
-        if k == 0:
-            return [links.copy(held, held, {"c": 1 - c})]
-        return [links.copy(held, held, {axis: moved(at, axis, steps)[axis]}) for steps in (1, 2, 3)]
-
-    def small_end(k, going):
-        for copy in going:
-            copy.wait_recv()
-        total = rounds[k][0]
-        for j in range(1, 2 if k == 0 else 4):
-            total = total + rounds[k][j]
-        sums[0] = total
-
-    going = small_start(0)
-    for k, _ in enumerate(work.steps()):
-        if k in (0, 2, 4):
-            small_end(k // 2, going)
-            going = small_start(k // 2 + 1)
-    small_end(3, going)
+    work = Scatter(at, links, part_in, wide, False, refs)
+
+    def side(core):
+        return pl.ds(pl.multiple_of(SMALL * core, 128), SMALL)
+
+    def small_steps():
+        whole[...] = jnp.zeros((8, 2 * SMALL), jnp.float32)
+        whole[:, :CONVC] = sums_in[...]
+        whole[7:8, :1536] = gain_in[...]
+        whole[:, CONVC:CONVC + 128] = heads_in[...]
+        going = [links.copy(whole.at[:, side(1 - c)], core_sum, {"c": 1 - c})]
+        yield
+        going[0].wait()
+        links.sent.remove(going[0])
+        total = core_sum[...] + whole[:, side(c)]
+        for axis, held in (("x", rounds_x), ("y", rounds_y), ("z", rounds_z)):
+            held[at[axis]] = total
+            mine = held.at[at[axis]]
+            going = [links.copy(mine, mine, {axis: moved(at, axis, steps)[axis]}) for steps in (1, 3, 2)]
+            yield
+            for copy in going:
+                copy.wait_recv()
+            total = held[0]
+            for j in range(1, 4):
+                total = total + held[j]
+        whole[:, side(c)] = total
+        going = [links.copy(whole.at[:, side(c)], core_other, {"c": 1 - c})]
+        yield
+        going[0].wait_recv()
+        whole[:, side(1 - c)] = core_other[...]
+        yield
+
+    small = small_steps()
+    next(small)
+    for _ in work.steps():
+        next(small)
     index = 32 * z + 8 * y + 2 * x + c
-    total, start = sums[0], 0
-    for part, (each, first, count, to) in zip(smalls, ((26, 0, 8, 0), (0, 0, 8, 8), (12, 0, 1, 6))):
-        wide_ = part.shape[1]
-        value = total[:, start:start + wide_]
-        if each:
-            value = pltpu.roll(value, lax.rem(wide_ - each * index, wide_), 1)
-        small_out[to:to + count, :] = value[first:first + count, :128]
-        start += wide_
-    gate = pltpu.roll(total[:, :128 * 24], lax.rem(3072 - 24 * index, 3072), 1)
-    small_out[5:6, :] = gate[5:6, :128]
-    work.finish(outs)
+    total = whole[...]
+    for first, size, each, row, count, to in ((0, CONVC, 26, 0, 5, 0), (0, DI, 24, 5, 1, 5), (0, 1536, 12, 7, 1, 6)):
+        value = pltpu.roll(total[:, first:first + size], lax.rem(size - each * index, size), 1)
+        small_out[to:to + count, :] = value[row:row + count, :128]
+    small_out[8:16, :] = total[:, CONVC:CONVC + 128]
+    work.finish(out)
     links.finish()
 
 
-def scatter(halves_in, smalls, rows):
-    n = len(halves_in)
-    wides = [h.shape[1] for h in halves_in]
-    ins = [h.reshape(2, 4, 2, 3, 4 * r // 3, w) for h, r, w in zip(halves_in, rows, wides)]
-    tall = [-(-r // 8) * 8 for r in rows]
-    count = n * 3 * 3 * 6 + 10
-    scratch = [pltpu.VMEM((2 if k == 0 else 4, 8, sum(s.shape[1] for s in smalls)), jnp.float32) for k in range(4)]
-    scratch += [pltpu.SemaphoreType.DMA((count,))] * 2
+def scatter(half_in, sums, head_sums, d_gain):
+    wide = half_in.shape[-1]
+    vm, f32 = pltpu.VMEM, jnp.float32
+    spec = pl.BlockSpec(memory_space=pltpu.VMEM)
+    scratch = [vm((8, SMALL), f32)] * 2 + [vm((4, 8, SMALL), f32)] * 3 + [vm((8, 2 * SMALL), f32)]
     return pl.pallas_call(
-        functools.partial(scatter_kernel, rows=tuple(rows), wides=tuple(wides)),
-        out_shape=[jax.ShapeDtypeStruct((t, w), jnp.float32) for t, w in zip(tall, wides)] + [jax.ShapeDtypeStruct((16, 128), jnp.float32)],
-        in_specs=[pl.BlockSpec(memory_space=pltpu.VMEM)] * (n + 3),
-        out_specs=[pl.BlockSpec(memory_space=pltpu.VMEM)] * (n + 1),
-        scratch_shapes=scratch + scatter_scratch(rows, wides),
-        compiler_params=pltpu.CompilerParams(collective_id=1, has_side_effects=True, vmem_limit_bytes=56 << 20),
+        functools.partial(scatter_kernel, wide=wide),
+        out_shape=[jax.ShapeDtypeStruct((16, wide), f32), jax.ShapeDtypeStruct((16, 128), f32)],
+        in_specs=[spec] * 4,
+        out_specs=[spec] * 2,
+        scratch_shapes=scratch + [pltpu.SemaphoreType.DMA((64,))] * 2 + scatter_scratch(wide, False),
+        compiler_params=pltpu.CompilerParams(collective_id=1, has_side_effects=True, vmem_limit_bytes=48 << 20),
         name="scatter_gradients",
-    )(*ins, *smalls)
+    )(half_in.reshape(2, 4, 2, 3, 16, wide), sums, head_sums, d_gain)
 
 
 H = 48
@@ -511,9 +556,9 @@
     lax.fori_loop(0, count // unroll, step, 0)
 
 
-def mixer_kernel(gates, conv_in, dt_in, normed, hidden, given_out, db, taps, gain, skip, heads, w_in, w_out,
-                 out, dproj, d_norm, sums, headsums, g_z, g_o,
-                 branch, dz, sib_normed, sib_given, sib_branch, sib_dz, src_z, src_o, chunk, chunk_sem,
+def mixer_kernel(conv_in, dt_in, normed, hidden, given_out, taps, gain, skip, heads, part_w,
+                 out, dproj, d_norm, sums, headsums, g_z, g_o, weights_,
+                 gates, db, branch, dz, sib_normed, sib_given, sib_branch, sib_dz, src, chunk, chunk_sem,
                  act, ys, dys, shift, shift2, halo_out, halo_in, back_out, back_in,
                  cum, ecum, toward, steps, rows_a, scores, dscores, usum, qin, qw, prods, stat, coef, db_in, dc_in, decay,
                  skips, loc, inc, inc2, *rest):
@@ -549,14 +594,14 @@
     def _():
         pl.semaphore_signal(barrier, inc=1, device_id=device(beside), device_id_type=MESH)
 
-    for steps_ in (1, -1):
+    for steps_ in (1, 2, 3):
         pl.semaphore_signal(barrier, inc=1, device_id={"z": moved(at, "z", steps_)["z"]}, device_id_type=MESH)
     to_z, to_c, _, home = targets(at)
     for tx in range(4):
         @pl.when(jnp.logical_not(jnp.logical_and(home, at["x"] == tx)))
         def _():
             pl.semaphore_signal(barrier, inc=1, device_id=(to_z, at["y"], jnp.int32(tx), to_c), device_id_type=MESH)
-    pl.semaphore_wait(barrier, 22 + inner.astype(jnp.int32) - home.astype(jnp.int32))
+    pl.semaphore_wait(barrier, 23 + inner.astype(jnp.int32) - home.astype(jnp.int32))
 
     def exchange(e, source, target, own):
         def go(k):
@@ -592,6 +637,10 @@
     halo_out[...] = conv_in[240:256, :]
     front = neighbour(0, halo_out, halo_in, 1, me < 31)
     shared = [to_sibling(5, normed.at[:, lanes(768 * (1 - core), 768)], sib_normed), to_sibling(6, given_out, sib_given)]
+
+    links = Links(rs_send, rs_recv)
+    ring = Ring(links, at, weights_, 2, True)
+    ring.start()
 
     raw = dt_in[...] + heads[0:1, :]
     dt = jnp.maximum(raw, 0.0) + jnp.log1p(jnp.exp(-jnp.abs(raw)))
@@ -791,8 +840,54 @@
 
     loop(0, TILES // 2, inside, 3)
     ahead.turn()
+    ring.turn()
     loop(TILES // 2, TILES // 2, inside, 3)
     ahead.finish()
+    ring.finish()
+    ring.end()
+
+    def fetch(k, slot):
+        first = jnp.minimum(k, 7)
+        a_ = pltpu.make_async_copy(
+            weights_.at[:, :, :, :, :, :, lanes(1536 * (first // 2) + 384 * lax.rem(first, 2), 384)],
+            chunk.at[slot].reshape(2, 2, 4, 2, 3, 16, 384), chunk_sem.at[slot])
+        pl.when(k < 8)(a_.start)
+        later = jnp.maximum(k - 8, 0)
+        for b in range(2):
+            b_ = pltpu.make_async_copy(
+                weights_.at[later // 4, :, :, :, :, :, lanes(1536 * lax.rem(later, 4) + 768 + 384 * b, 384)],
+                chunk.at[slot].reshape(2, 4, 2, 3, 32, 384).at[:, :, :, :, pl.ds(16 * b, 16)], chunk_sem.at[slot])
+            pl.when(k >= 8)(b_.start)
+
+    def stream(use):
+        def two(n, u):
+            for slot in range(2):
+                k = 2 * n + slot
+                pltpu.make_async_copy(chunk.at[slot], chunk.at[slot], chunk_sem.at[slot]).wait()
+                use(k, chunk[slot])
+
+                @pl.when(k + 2 < 16)
+                def _():
+                    fetch(k + 2, slot)
+
+        fetch(jnp.int32(0), 0)
+        fetch(jnp.int32(1), 1)
+        loop(0, 8, two, 1)
+
+    db[...] = jnp.zeros((256, DI), f32)
+
+    def before_gate(k, w):
+        @pl.when(k < 8)
+        def _():
+            gates[:, lanes(384 * jnp.minimum(k, 7), 384)] = dot(normed[...], w)
+
+        @pl.when(k >= 8)
+        def _():
+            later = jnp.maximum(k - 8, 0)
+            part = lanes(1536 * (later // 4), 1536)
+            db[:, part] += dot_nt(given_out[:, lanes(384 * lax.rem(later, 4), 384)], w)
+
+    stream(before_gate)
 
     def state(ref, j):
         return ref[pl.ds(pl.multiple_of(128 * j, 128), 128), :]
@@ -851,61 +946,42 @@
         copy.wait_recv()
 
     def d_w_gates(k, u):
-        zh, part = k // 8, lanes(384 * lax.rem(k, 8), 384)
+        zh, n = k // 8, lax.rem(k, 8)
+        part = lanes(384 * n, 384)
         total = dot_tn(normed[:, lanes(768 * core + 384 * zh, 384)], dz[:, part])
         total = total + dot_tn(sib_normed[:, lanes(384 * zh, 384)], sib_dz[:, part])
-        src_z[zh, :, :, :, :, part] = low(total).reshape(4, 2, 3, 16, 384)
+        src[zh, :, :, :, :, lanes(1536 * (n // 2) + 384 * lax.rem(n, 2), 384)] = low(total).reshape(4, 2, 3, 16, 384)
 
     def d_w_out(k, u):
-        q, part = k // 4, lanes(384 * lax.rem(k, 4), 384)
+        q, n = k // 4, lax.rem(k, 4)
+        part = lanes(384 * n, 384)
         total = dot_tn(branch[:, lanes(1536 * core + 384 * q, 384)], given_out[:, part])
         total = total + dot_tn(sib_branch[:, lanes(384 * q, 384)], sib_given[:, part])
-        src_o[q // 2, pl.ds(2 * lax.rem(q, 2), 2), :, :, :, part] = low(total).reshape(2, 2, 3, 32, 384)
+        total = low(total).reshape(2, 2, 3, 2, 16, 384)
+        for b in range(2):
+            src[q // 2, pl.ds(2 * lax.rem(q, 2), 2), :, :, :, lanes(1536 * n + 768 + 384 * b, 384)] = total[:, :, :, b]
 
     loop(0, 16, d_w_gates, 1)
     loop(0, 16, d_w_out, 1)
     aback.turn()
-    links = Links(rs_send, rs_recv)
-    work = Scatter(at, links, [src_z, src_o], (12, 24), (DI, 1536), rest)
+    work = Scatter(at, links, src, 2 * DI, True, rest)
     reduce = work.steps()
     next(reduce)
-
-    def fetch(k, slot):
-        last_ = k >= 12
-        part = jnp.minimum(k, 11)
-        a_ = pltpu.make_async_copy(
-            w_out.at[pl.ds(pl.multiple_of(1536 * lax.rem(part, 2), 128), 1536), lanes(256 * (part // 2), 256)], chunk.at[slot], chunk_sem.at[slot])
-        b_ = pltpu.make_async_copy(w_in.at[:, lanes(256 * jnp.maximum(k - 12, 0), 256)], chunk.at[slot], chunk_sem.at[slot])
-        pl.when(jnp.logical_not(last_))(a_.start)
-        pl.when(last_)(b_.start)
-
-    def fetched(slot):
-        pltpu.make_async_copy(chunk.at[slot], chunk.at[slot], chunk_sem.at[slot]).wait()
-
-    def out_part(n, u):
-        part = lanes(256 * n, 256)
-        total = wide(hidden[:, part])
-        for slot in range(2):
-            fetched(slot)
-            total = total + dot(branch[:, 1536 * slot:1536 * slot + 1536], chunk[slot])
-            fetch(2 * n + slot + 2, slot)
-        out[:, part] = low(total)
-
-    def norm_part(n, u):
-        for slot in range(2):
-            fetched(slot)
-            k = 2 * n + slot
-            for half in range(2):
-                rows_ = slice(768 * half, 768 * half + 768)
-                d_norm[:, rows_] += dot_nt(dz[:, lanes(256 * k, 256)], chunk[slot, rows_, :])
-
-            @pl.when(k + 2 < 12)
-            def _():
-                fetch(k + 14, slot)
-
-    fetch(jnp.int32(0), 0)
-    fetch(jnp.int32(1), 1)
     d_norm[...] = jnp.zeros((256, 1536), f32)
+    out_sum = db
+
+    def after_gate(k, w):
+        @pl.when(k < 8)
+        def _():
+            d_norm[...] += dot_nt(dz[:, lanes(384 * jnp.minimum(k, 7), 384)], w)
+
+        @pl.when(k >= 8)
+        def _():
+            later = jnp.maximum(k - 8, 0)
+            part = lanes(384 * lax.rem(later, 4), 384)
+            held = jnp.where(later < 4, wide(hidden[:, part]), out_sum[:, part])
+            out_sum[:, part] = held + dot(branch[:, lanes(1536 * (later // 4), 1536)], w)
+
     for ref in (usum, qin, qw):
         ref[...] = jnp.zeros((256, 128), f32)
     dscores[...] = jnp.zeros((256, 256), f32)
@@ -933,8 +1009,8 @@
     loop(0, TILES // 2, inside_back, 3)
     next(reduce)
     loop(TILES // 2, TILES // 2, inside_back, 3)
-    loop(0, 6, out_part, 1)
-    loop(0, 6, norm_part, 1)
+    stream(after_gate)
+    out[...] = low(out_sum[:, :1536])
     next(reduce)
     aback.finish()
     db_in[...] = jnp.zeros((256, 128), f32)
@@ -960,9 +1036,7 @@
         prods[pl.ds(2 * j + 1, 1), :] = jnp.sum(pair[64:], axis=0, keepdims=True)
         d_mix(j, u, ys[j] + d_w + skip[:, cols(j)] * dyf)
 
-    loop(0, TILES // 2, carry_back, 4)
-    next(reduce)
-    loop(TILES // 2, TILES // 2, carry_back, 4)
+    loop(0, TILES, carry_back, 4)
     next(reduce)
     ds = low(dscores[...])
     d_mix(TILES, 0, db_in[...] + dot_tn(ds, c_out))
@@ -1007,10 +1081,8 @@
             total = total + taps[k:k + 1, cols(j)] * shift2[u, 3 - k:259 - k, :]
         dproj[:, cols(j)] = low(total)
 
-    loop(0, TILES // 2, conv_back, 2)
-    next(reduce)
-    loop(TILES // 2, TILES // 2 + 2, conv_back, 2)
-    work.finish([g_z, g_o])
+    loop(0, TILES + 2, conv_back, 2)
+    work.finish(g_z, g_o)
     links.finish()
     for copy in shared:
         copy.wait_send()
@@ -1020,14 +1092,15 @@
     aback.end()
 
 
-def mixer(gates, conv_in, dt_in, normed, hidden, given_out, d_branch, taps, gain, skip, heads, w_in, w_out):
+def mixer(conv_in, dt_in, normed, hidden, given_out, taps, gain, skip, heads, part_w):
     f32, bf16 = jnp.float32, jnp.bfloat16
     tile, half, late = (256, 128), (16, CONVC), WIDE - DI
     vm = pltpu.VMEM
     dma = pltpu.SemaphoreType.DMA
     scratch = [
+        vm((256, DI), f32), vm((256, DI), f32),
         vm((256, DI), bf16), vm((256, DI), bf16), vm((256, 768), bf16), vm((256, 1536), bf16), vm((256, 1536), bf16), vm((256, DI), bf16),
-        vm((2, 4, 2, 3, 16, DI), bf16), vm((2, 4, 2, 3, 32, 1536), bf16), vm((2, 1536, 256), bf16), dma((2,)),
+        vm((2, 4, 2, 3, 16, 2 * DI), bf16), vm((2, 1536, 384), bf16), dma((2,)),
         vm((TILES + 2,) + tile, bf16), vm((TILES + 2,) + tile, f32), vm((TILES,) + tile, bf16),
         vm((4, 264, 128), f32), vm((2, 264, 128), f32), vm(half, bf16), vm(half, bf16), vm(half, bf16), vm(half, bf16),
         vm(tile, f32), vm(tile, f32), vm(tile, f32), vm(tile, f32), vm((128, 256), f32), vm((256, 256), f32), vm((256, 256), f32),
@@ -1037,20 +1110,22 @@
     scratch += [vm((16, 112, 128), bf16), vm((16, 112, 128), bf16), vm((16, 96, 128), bf16)]
     for _ in range(2):
         scratch += [vm((1536, 128), bf16), vm((1536, 128), bf16)]
-    scratch += [dma((10,)), dma((10,)), dma((4, 16)), dma((4, 16)), dma((4,)), dma((108,)), dma((108,))]
-    scratch += scatter_scratch((12, 24), (DI, 1536))
+    scratch += [dma((10,)), dma((10,)), dma((4, 16)), dma((4, 16)), dma((4,)), dma((64,)), dma((64,))]
+    scratch += scatter_scratch(2 * DI, True)
     near, far = pl.BlockSpec(memory_space=pltpu.VMEM), pl.BlockSpec(memory_space=pl.ANY)
     return pl.pallas_call(
         mixer_kernel,
         out_shape=[jax.ShapeDtypeStruct((256, 1536), bf16), jax.ShapeDtypeStruct((256, late), bf16),
                    jax.ShapeDtypeStruct((256, 1536), f32), jax.ShapeDtypeStruct((8, CONVC), f32), jax.ShapeDtypeStruct((8, 128), f32),
-                   jax.ShapeDtypeStruct((16, DI), f32), jax.ShapeDtypeStruct((24, 1536), f32)],
-        in_specs=[near] * 11 + [far] * 2,
-        out_specs=[near] * 7,
+                   jax.ShapeDtypeStruct((16, DI), f32), jax.ShapeDtypeStruct((24, 1536), f32),
+                   jax.ShapeDtypeStruct(part_w.shape, bf16)],
+        in_specs=[near] * 9 + [far],
+        out_specs=[near] * 7 + [far],
         scratch_shapes=scratch,
+        input_output_aliases={9: 7},
         compiler_params=pltpu.CompilerParams(collective_id=2, has_side_effects=True, vmem_limit_bytes=62 << 20),
         name="mixer",
-    )(gates, conv_in, dt_in, normed, hidden, given_out, d_branch, taps, gain, skip, heads, w_in, w_out)
+    )(conv_in, dt_in, normed, hidden, given_out, taps, gain, skip, heads, part_w)
 
 
 def rms_scale(values, gain):
@@ -1088,9 +1163,13 @@
         jnp.pad(gate_gain, (0, 104))[None],
         jnp.zeros((5, 128), jnp.bfloat16),
     ])
-    shard_in = jnp.pad(jnp.concatenate([jnp.pad(in_w, ((0, 0), (0, PARAMS - PROJ))), spare], axis=1), ((0, 4), (0, 0)))
-    w_in, w_out = gather([shard_in, jnp.pad(out_w, ((0, 8), (0, 0)))], [12, 24])
-    spare = w_in[:, PARAMS:].reshape(128, 12, 128).astype(jnp.float32)
+    late = jnp.pad(jnp.concatenate([jnp.pad(in_w[:, DI:], ((0, 0), (0, PARAMS - PROJ))), spare], axis=1), ((0, 4), (0, 0)))
+    early = jnp.concatenate([
+        in_w[:, :DI].reshape(12, 4, 768), out_w.reshape(2, 12, 4, 384).transpose(1, 2, 0, 3).reshape(12, 4, 768)
+    ], axis=2).reshape(12, 2 * DI)
+    w_late, w_early = gather(late, jnp.pad(early, ((0, 4), (0, 0))))
+    w_late = w_late.reshape(1536, WIDE - DI)
+    spare = w_late[:, PARAMS - DI:].reshape(128, 12, 128).astype(jnp.float32)
     w_conv_f = spare[:, :4, :26].transpose(1, 0, 2).reshape(KW, CONVC)
     b_conv_f = spare[:, 4, :26].reshape(CONVC)
     gain_norm_f = spare[:, 5, :12].reshape(1536)
@@ -1098,23 +1177,21 @@
     residual = hidden[0].astype(jnp.float32)
     length = residual.shape[0]
     normed = rms_scale(residual, gain_norm_f).astype(jnp.bfloat16)
-    gates = jnp.dot(normed, w_in[:, :DI], preferred_element_type=jnp.float32)
-    conv_in = jnp.dot(normed, w_in[:, DI : DI + CONVC], preferred_element_type=jnp.float32).astype(jnp.bfloat16)
-    dt_in = jnp.dot(normed, w_in[:, DI + CONVC : PARAMS], preferred_element_type=jnp.float32)
+    conv_in = jnp.dot(normed, w_late[:, :CONVC], preferred_element_type=jnp.float32).astype(jnp.bfloat16)
+    dt_in = jnp.dot(normed, w_late[:, CONVC : PARAMS - DI], preferred_element_type=jnp.float32)
     grad_out = cotangent[0]
-    d_branch = jnp.einsum("td,kd->tk", grad_out, w_out, preferred_element_type=jnp.float32)
     taps = jnp.pad(jnp.concatenate([w_conv_f, b_conv_f[None]]), ((0, 3), (0, 0)))
     heads = jnp.pad(jnp.stack([dt_bias, decay_rates]), ((0, 6), (0, 80)))
-    result, d_late, d_normed, sums, head_sums, g_gates, g_out = mixer(
-        gates, conv_in, dt_in, normed, hidden[0], grad_out, d_branch, taps, gain_gate_f[None],
-        jnp.repeat(d_skip, P_SIZE)[None], heads, w_in, w_out)
-    d_normed = d_normed + jnp.einsum("tj,dj->td", d_late, w_in[:, DI:], preferred_element_type=jnp.float32)
+    result, d_late, d_normed, sums, head_sums, g_gates, g_out, _ = mixer(
+        conv_in, dt_in, normed, hidden[0], grad_out, taps, gain_gate_f[None],
+        jnp.repeat(d_skip, P_SIZE)[None], heads, w_early)
+    d_normed = d_normed + jnp.einsum("tj,dj->td", d_late, w_late, preferred_element_type=jnp.float32)
     both_late = jnp.concatenate([d_late, swap(d_late)], axis=0)
     d_w_late = jnp.einsum("td,tj->dj", my_half(normed, core), both_late, preferred_element_type=jnp.float32).astype(jnp.bfloat16)
     norm_pull = jax.vjp(rms_scale, residual, gain_norm_f)[1]
     d_from_norm, d_gain_norm = norm_pull(d_normed)
     d_hidden = grad_out.astype(jnp.float32) + d_from_norm
-    g_late, total = scatter([d_w_late], [sums, head_sums, jnp.pad(d_gain_norm[None], ((0, 7), (0, 0)))], [12])
+    g_late, total = scatter(d_w_late, sums, head_sums, d_gain_norm[None])
     return (
         result[None],
         d_hidden[None],

time: 354 us -> 311 us (0.88)
  Pallas kernels: 282 us -> 260 us
  matrix products: 37.3 us -> 23.4 us
  local copies, waits for them, and re-layouts: 24.2 us -> 20.3 us
    pallas_call x2, Pallas kernels: 142 us -> 93.1 us  [the longest x1 50.3 us: gather(): pl.pallas_call(gather_kernel, out_shape=[jax.ShapeDtypeStruct((2, 2, 4, 2...]
    pallas_call x1, Pallas kernels: 140 us -> 167 us  [mixer(): pl.pallas_call(mixer_kernel, out_shape=[jax.ShapeDtypeStruct((256, 1536),...]
    dot_general x5 -> x3, matrix products: 31 us -> 18.6 us  [the longest x1 8.37 us: shards(): jnp.einsum('tj,dj->td', d_late, w_late, preferred_element_type=jnp.float32)]
where the time goes in v5:
time: 311 us; the launch traced here: 309 us
  Pallas kernels  260 us (84%)
  matrix products  23.4 us (8%)
  local copies, waits for them, and re-layouts  20.3 us (7%)
  other arithmetic  4.33 us (1%)
    pallas_call x1, Pallas kernels, mixer(): pl.pallas_call(mixer_kernel, out_shape=[jax.ShapeDtypeStruct((256, 1536),...  167 us
    pallas_call x1, Pallas kernels, gather(): pl.pallas_call(gather_kernel, out_shape=[jax.ShapeDtypeStruct((2, 2, 4, 2...  50.3 us
    pallas_call x1, Pallas kernels, scatter(): pl.pallas_call(functools.partial(scatter_kernel, wide=wide), out_shape=[j...  42.8 us
    dot_general x1, matrix products, shards(): jnp.einsum('tj,dj->td', d_late, w_late, preferred_element_type=jnp.float32)  8.37 us
    dot_general x1, matrix products, shards(): jnp.dot(normed, w_late[:, :CONVC], preferred_element_type=jnp.float32)  7.91 us
  transfers between devices with their start and end apart: 2, of which 0 were waited for; matrix products, arithmetic and copies ran while one was open for 3% of the time, Pallas kernels for 0%

profile of v5, /device:TPU:1, one launch (start us, length us, event | category | flops | bytes accessed | tf_op | source)
XLA Modules:
  0.0 309.4 jit_solution(10664252033892681125)
XLA Ops:
  0.6 0.9 slice.57
  1.6 0.9 slice.58
  2.5 0.7 pad_bitcast_fusion.2
  3.1 0.7 pad_bitcast_fusion
  3.8 0.7 pad.37
  4.5 0.1 concatenate.21
  4.7 0.9 reshape.72
  5.6 0.1 pad_maximum_fusion.1
  5.7 0.1 pad.66
  5.8 0.0 copy-start.5
  5.9 50.3 %gather_weights.1 = (bf16[2,2,4,2,3,16,3584]{6,5,4,3,2,1,0:T(8,128)(2,1)S(1)}, bf16[2,2,4,2,3,16,6144]{6,5,4,3,2,1,0:T(8,128)(2,1)}) custom-call(bf16[16,3584]{1,0:T(8,128)(2,1)S(1)} %pad.41.refs_0_, bf16[16,6144]{1,0:T(8,128)(2,1)S(1)} %pad.42.refs_1_), custom_call_target="tpu_custom_call" | custom-call | tf_op jit(solution)/shard_map/gather_weights/pallas_call | solution.py:199
  56.2 0.0 copy-start.1
  56.2 4.0 %copy-done.1 = bf16[2,2,4,2,3,16,3584]{6,5,4,3,2,1,0:T(8,128)(2,1)} copy-done((bf16[2,2,4,2,3,16,3584]{6,5,4,3,2,1,0:T(8,128)(2,1)}, bf16[2,2,4,2,3,16,3584]{6,5,4,3,2,1,0:T(8,128)(2,1)S(1)}, u32[]{:S(2)}) %copy-start.1) | copy-done | bytes 11010072
  60.2 0.1 slice_convert_fusion
  60.3 0.1 reshape.80
  60.4 0.0 copy-start.8
  60.4 0.2 slice_reduce_fusion.2
  60.6 0.1 mul.72
  60.7 0.0 copy-done.5
  60.7 0.2 fusion.14
  60.9 0.4 copy-done.8
  61.3 0.3 fusion.10.normed
  61.6 0.0 copy-start.3
  61.6 2.3 fusion.19.dt_in
  63.9 7.9 %fusion.2.conv_in = bf16[256,3328]{1,0:T(8,128)(2,1)} fusion(bf16[256,1536]{1,0:T(8,128)(2,1)S(1)} %fusion.10.normed, bf16[1536,3584]{1,0:T(8,128)(2,1)} %bitcast.51), kind=kOutput, calls=%fused_computation.3 | convolution fusion | flops 2618097664 | bytes 12713984 | tf_op jit(solution)/shard_map/dot_general | solution.py:1180
  71.8 0.0 copy-done.3
  71.8 1.1 slice_bitcast_fusion
  73.0 1.2 slice_reduce_fusion.1
  74.2 1.2 slice_reduce_fusion
  75.5 0.2 reshape.76
  75.7 0.1 broadcast_in_dim_reshape_squeeze.8
  75.8 0.7 broadcast_in_dim_reshape_squeeze.9.gain
  76.5 0.0 copy-done.12
  76.5 0.1 broadcast_in_dim.31
  76.6 0.7 broadcast_in_dim_reshape.3.skip
  77.3 0.7 select_maximum_fusion.taps
  78.0 0.0 copy-done.13
  78.0 0.0 copy-done.14
  78.0 0.6 select_maximum_fusion.1.heads
  78.6 166.7 %mixer.1 = (bf16[256,1536]{1,0:T(8,128)(2,1)}, bf16[256,3584]{1,0:T(8,128)(2,1)}, f32[256,1536]{1,0:T(8,128)}, f32[8,3328]{1,0:T(8,128)}, f32[8,128]{1,0:T(8,128...) custom-call(bf16[256,3328]{1,0:T(8,128)(2,1)} %fusion.2.conv_in, ...), custom_call_target="tpu_custom_call", output_to_operand_aliasing={{7}: (9, {})} | custom-call | tf_op jit(solution)/shard_map/mixer/pallas_call | solution.py:1116
  245.2 0.1 collective-permute-start.1
  245.3 0.0 copy-done.4
  245.4 0.1 constant_dynamic-slice_fusion.1
  245.4 0.6 collective-permute-start
  246.0 0.0 copy-done.6
  246.0 8.4 %fusion.11 = (f32[1536]{0:T(1024)S(1)}, f32[256]{0:T(256)S(1)}, f32[256,1536]{1,0:T(8,128)S(1)}) fusion(f32[256]{0:T(256)S(1)} %fusion.23, bf16[1,256,1536]{2,1,0:T(8,128)(2,1)S(1)} %copy-done.6, f32[1536]{0:T(1024)S(1)} %mul.72, f32[256,1536]{1,0:T(8,128)} %get-tuple-element.25, bf16[256,3584]{1,0:T(8,128)(2,1)} %get-tuple-element.26, ...), kind=kOutput, calls=%fused_computation.16 | convolution fusion | flops 2821716224 | bytes 16791552 | tf_op jit(solution)/shard_map/tj,dj->td/dot_general | solution.py:1188
  254.4 0.0 copy-done.7
  254.4 1.6 fusion.13
  256.0 0.0 collective-permute-done
  256.0 0.0 collective-permute-done.1
  256.0 0.0 copy-start
  256.0 0.0 copy-start.2
  256.1 4.8 %convolution_convert_fusion = bf16[768,3584]{1,0:T(8,128)(2,1)S(1)} fusion(bf16[256,3584]{1,0:T(8,128)(2,1)} %collective-permute-done.1, bf16[256,3584]{1,0:T(8,128)(2,1)S(1)} %copy-done.15, bf16[256,768]{1,0:T(8,128)(2,1)S(1)} %collective-permute-done, bf16[256,768]{1,0:T(8,128)(2,1)S(1)} %get-tuple-element.35), kind=kOutput, calls=%fused_computation.2 | convolution fusion | flops 2830237696 | bytes 9961472 | tf_op jit(solution)/shard_map/td,tj->dj/dot_general | solution.py:1190
  260.9 42.8 %scatter_gradients.1 = (f32[16,3584]{1,0:T(8,128)S(1)}, f32[16,128]{1,0:T(8,128)S(1)}) custom-call(bf16[2,4,2,3,16,3584]{5,4,3,2,1,0:T(8,128)(2,1)S(1)} %bitcast.48, f32[8,3328]{1,0:T(8,128)S(1)} %copy-done, f32[8,128]{1,0:T(8,128)S(1)} %copy-done.2, f32[1,1536]{1,0:T(1,128)S(1)} %reshape.78.gain_in), custom_call_target="tpu_custom_call" | custom-call | tf_op jit(solution)/shard_map/scatter_gradients/pallas_call | solution.py:488
  303.7 0.5 slice_bitcast_fusion.2
  304.3 0.6 slice.68
  304.8 0.5 slice_bitcast_fusion.3
  305.4 0.5 slice_bitcast_fusion.6
  305.9 0.5 slice_bitcast_fusion.7
  306.4 0.1 copy.27
  306.5 0.6 reshape.79
  307.1 0.8 pad_maximum_fusion
  307.9 0.9 copy.33
  308.8 0.7 copy.34
  (29 shorter events, 0.3 us)
Async XLA Ops:
  5.8 54.8 %copy-start.5 = (bf16[1,256,1536]{2,1,0:T(8,128)(2,1)S(1)}, bf16[1,256,1536]{2,1,0:T(8,128)(2,1)}, u32[]{:S(2)}) copy-start(bf16[1,256,1536]{2,1,0:T(8,128)(2,1)} %param.11) | copy-start | bytes 2359300
  56.2 4.1 %copy-start.1 = (bf16[2,2,4,2,3,16,3584]{6,5,4,3,2,1,0:T(8,128)(2,1)}, bf16[2,2,4,2,3,16,3584]{6,5,4,3,2,1,0:T(8,128)(2,1)S(1)}, u32[]{:S(2)}) copy-start(bf16[2,2,4,2,3,16,3584]{6,5,4,3,2,1,0:T(8,128)(2,1)S(1)} %get-tuple-element.22) | copy-start | bytes 33030148
  60.4 1.0 copy-start.8
  61.6 10.2 %copy-start.3 = (bf16[256,1536]{1,0:T(8,128)(2,1)}, bf16[256,1536]{1,0:T(8,128)(2,1)S(1)}, u32[]{:S(2)}) copy-start(bf16[256,1536]{1,0:T(8,128)(2,1)S(1)} %fusion.10.normed) | copy-start | bytes 2359300
  71.8 4.7 %copy-start.12 = (f32[48]{0:T(128)S(1)}, f32[48]{0:T(128)}, u32[]{:S(2)}) copy-start(f32[48]{0:T(128)} %param.21) | copy-start | bytes 580
  71.8 6.1 %copy-start.13 = (f32[48]{0:T(128)S(1)}, f32[48]{0:T(128)}, u32[]{:S(2)}) copy-start(f32[48]{0:T(128)} %param.20) | copy-start | bytes 580
  71.8 6.1 %copy-start.14 = (f32[48]{0:T(128)S(1)}, f32[48]{0:T(128)}, u32[]{:S(2)}) copy-start(f32[48]{0:T(128)} %param.19) | copy-start | bytes 580
  78.6 166.8 %copy-start.4 = (bf16[256,1536]{1,0:T(8,128)(2,1)S(1)}, bf16[256,1536]{1,0:T(8,128)(2,1)}, u32[]{:S(2)}) copy-start(bf16[256,1536]{1,0:T(8,128)(2,1)} %copy-done.3) | copy-start | bytes 2359300
  78.6 167.4 %copy-start.6 = (bf16[1,256,1536]{2,1,0:T(8,128)(2,1)S(1)}, bf16[1,256,1536]{2,1,0:T(8,128)(2,1)}, u32[]{:S(2)}) copy-start(bf16[1,256,1536]{2,1,0:T(8,128)(2,1)} %param.11) | copy-start | bytes 2359300
  245.2 10.8 %collective-permute-start.1 = (bf16[256,3584]{1,0:T(8,128)(2,1)}, bf16[256,3584]{1,0:T(8,128)(2,1)}, u32[]{:S(2)}, u32[]{:S(2)}) collective-permute-start(bf16[256,3584]{1,0:T(8,128)(2,1)} %get-tuple-element.26), channel_id=1, source_target_pairs={{0,1},{1,0},{2,3},{3,2},{4,5},{5,4},{6,7},{7,6},{8,9},{9,8},{10,11... | collective-permute-start | bytes 5505032 | tf_op jit(solution)/shard_map/ppermute | solution.py:1136
  245.4 10.6 %collective-permute-start = (bf16[256,768]{1,0:T(8,128)(2,1)S(1)}, bf16[256,768]{1,0:T(8,128)(2,1)S(1)}, u32[]{:S(2)}, u32[]{:S(2)}) collective-permute-start(bf16[256,768]{1,0:T(8,128)(2,1)S(1)} %get-tuple-element.36), channel_id=1, source_target_pairs={{0,1},{1,0},{2,3},{3,2},{4,5},{5,4},{6,7},{7,6},{8,9},{9,8},{10,11... | collective-permute-start | bytes 1179656 | tf_op jit(solution)/shard_map/ppermute | solution.py:1136
  246.0 8.4 %copy-start.7 = (bf16[1,256,1536]{2,1,0:T(8,128)(2,1)S(1)}, bf16[1,256,1536]{2,1,0:T(8,128)(2,1)}, u32[]{:S(2)}) copy-start(bf16[1,256,1536]{2,1,0:T(8,128)(2,1)} %param.12) | copy-start | bytes 2359300
  254.4 1.6 copy-start.15
  256.0 4.9 %copy-start = (f32[8,3328]{1,0:T(8,128)S(1)}, f32[8,3328]{1,0:T(8,128)}, u32[]{:S(2)}) copy-start(f32[8,3328]{1,0:T(8,128)} %get-tuple-element.28.sums_in) | copy-start | bytes 319492
  256.0 4.9 %copy-start.2 = (f32[8,128]{1,0:T(8,128)S(1)}, f32[8,128]{1,0:T(8,128)}, u32[]{:S(2)}) copy-start(f32[8,128]{1,0:T(8,128)} %get-tuple-element.29.heads_in) | copy-start | bytes 12292
  260.9 46.2 %copy-start.10 = (f32[16,3072]{1,0:T(8,128)S(1)}, f32[16,3072]{1,0:T(8,128)}, u32[]{:S(2)}) copy-start(f32[16,3072]{1,0:T(8,128)} %get-tuple-element.27) | copy-start | bytes 589828
  303.7 4.2 %copy-start.9 = (bf16[256,1536]{1,0:T(8,128)(2,1)S(1)}, bf16[256,1536]{1,0:T(8,128)(2,1)}, u32[]{:S(2)}) copy-start(bf16[256,1536]{1,0:T(8,128)(2,1)} %get-tuple-element.24) | copy-start | bytes 2359300
  303.7 5.1 %copy-start.11 = (f32[24,1536]{1,0:T(8,128)S(1)}, f32[24,1536]{1,0:T(8,128)}, u32[]{:S(2)}) copy-start(f32[24,1536]{1,0:T(8,128)} %get-tuple-element.59) | copy-start | bytes 442372

commit v6 on v5

--- a/solution.py
+++ b/solution.py
@@ -26,9 +26,12 @@
         self.sent.append(made)
         return made
 
-    def finish(self):
+    def settle(self):
         for made in self.sent:
             made.wait_send()
+        self.sent = []
+
+    finish = settle
 
 
 def place():
@@ -112,7 +115,7 @@
 
 
 def gather_kernel(*refs):
-    shards, fulls, refs = refs[:2], refs[2:4], refs[4:]
+    (in_w, out_w, conv_w, conv_b, norm_gain, gate_gain), fulls, shards, (late, early), refs = refs[:6], refs[6:8], refs[8:10], refs[10:12], refs[12:]
     stages, stage_o, landed, unit, (send, recv, first_recv, own) = refs[:2], refs[2], refs[3:5], refs[5:7], refs[7:]
     at = place()
     z, y, x, c = (at[name] for name in ALL)
@@ -129,6 +132,25 @@
         @pl.when(jnp.logical_not(jnp.logical_and(home, jnp.logical_and(sx == x, sc == c))))
         def _():
             pl.semaphore_signal(barrier, inc=1, device_id=(from_z, y, sx, jnp.int32(sc)), device_id_type=MESH)
+
+    def wide_(ref):
+        return ref[...].astype(jnp.float32)
+
+    late[...] = jnp.zeros(late.shape, jnp.float32)
+    early[...] = jnp.zeros(early.shape, jnp.float32)
+    late[0:12, 0:3376] = in_w[:, 3072:6448].astype(jnp.float32)
+    late[0:4, 3456:3482] = wide_(conv_w)
+    late[4:5, 3456:3482] = wide_(conv_b)
+    late[5:6, 3456:3468] = wide_(norm_gain)
+    late[6:7, 3456:3480] = wide_(gate_gain)
+    held = wide_(out_w)
+    for tx in range(4):
+        early[0:12, 1536 * tx:1536 * tx + 768] = in_w[:, 768 * tx:768 * tx + 768].astype(jnp.float32)
+        for b in range(2):
+            start = 1536 * tx + 768 + 384 * b
+            early[0:12, start:start + 384] = held[12 * b:12 * b + 12, 384 * tx:384 * tx + 384]
+    shards[0][...] = late[...].astype(jnp.bfloat16)
+    shards[1][...] = early[...].astype(jnp.bfloat16)
     pl.semaphore_wait(barrier, 14 - home.astype(jnp.int32))
 
     links = Links(send, recv)
@@ -192,22 +214,22 @@
         pl.when(jnp.logical_not(mine))(remote.wait_send)
 
 
-def gather(late, early):
-    shards = (late, early)
-    wides = [s.shape[1] for s in shards]
+def gather(in_w, out_w, conv_w, conv_b, norm_gain, gate_gain):
+    wides = (3584, 6144)
     vm, dma = pltpu.VMEM, pltpu.SemaphoreType.DMA
     return pl.pallas_call(
         gather_kernel,
         out_shape=[jax.ShapeDtypeStruct((2, 2, 4, 2, 3, 16, w), jnp.bfloat16) for w in wides],
-        in_specs=[pl.BlockSpec(memory_space=pltpu.VMEM)] * 2,
+        in_specs=[pl.BlockSpec(memory_space=pltpu.VMEM)] * 6,
         out_specs=[pl.BlockSpec(memory_space=pl.ANY)] * 2,
-        scratch_shapes=[vm((48, wides[0] // 4), jnp.float32), vm((48, 768), jnp.float32), vm((96, 384), jnp.float32)]
+        scratch_shapes=[vm((16, w), jnp.bfloat16) for w in wides] + [vm((16, w), jnp.float32) for w in wides]
+        + [vm((48, wides[0] // 4), jnp.float32), vm((48, 768), jnp.float32), vm((96, 384), jnp.float32)]
         + [vm((4, 16, w // 4), jnp.bfloat16) for w in wides]
         + [vm((3, 16, w // 4), jnp.bfloat16) for w in wides]
         + [dma((96,)), dma((96,)), dma((8,)), dma((6,))],
-        compiler_params=pltpu.CompilerParams(collective_id=0, has_side_effects=True, vmem_limit_bytes=32 << 20),
+        compiler_params=pltpu.CompilerParams(collective_id=0, has_side_effects=True, vmem_limit_bytes=60 << 20),
         name="gather_weights",
-    )(*shards)
+    )(in_w, out_w, conv_w, conv_b[None], norm_gain[None], gate_gain[None])
 
 
 def span(shape, axis, at):
@@ -288,7 +310,7 @@
 ALL_CUT = [slice(None)] * 5
 
 
-def scatter_scratch(wide, split):
+def scatter_scratch(wide):
     vm, f32 = pltpu.VMEM, jnp.float32
     scratch = []
     size = {part: (2, 4, 2, 16, wide) for part in PARTS}
@@ -298,25 +320,32 @@
             scratch += [vm(shape, jnp.bfloat16)] * (3 if phase else 2)
             if phase == 0:
                 scratch += [vm(half_shape(shape, way), jnp.bfloat16) for way in (0, 1)]
-            if phase < 2:
-                scratch += [vm(shape, jnp.bfloat16)]
             size[part] = shape
-    first = 768 if split else wide // 4
-    scratch += [vm((48, first), f32), vm((96, 384), f32), vm((4, 16, wide // 4), f32), vm((4, 16, wide // 4), f32)]
+    return scratch
+
+
+def last_scratch(wide, first):
+    vm, f32 = pltpu.VMEM, jnp.float32
+    scratch = [vm((48, first), f32), vm((96, 384) if wide > 4 * first else (8, 128), f32), vm((4, 16, wide // 4), f32), vm((4, 16, wide // 4), f32)]
     return scratch + [pltpu.SemaphoreType.DMA((4,))] * 2
 
 
 class Scatter:
-    def __init__(self, at, links, source, wide, split, refs):
+    def __init__(self, at, links, source, wide, split, refs, last, narrow=None):
         take = iter(refs)
         self.at, self.links, self.split = at, links, split
-        self.near, self.relay, self.acc = {}, {}, {}
+        self.near, self.relay = {}, {}
         for phase in range(3):
             for s in PARTS:
                 self.near[s, phase] = [next(take) for _ in range(3 if phase else 2)]
                 self.relay[s] = [next(take), next(take)] if phase == 0 else self.relay[s]
-                self.acc[s, phase] = next(take) if phase < 2 else None
-        self.fin, self.fin_o, self.staged, self.landed, self.last, self.own = (next(take) for _ in range(6))
+        if narrow:
+            def less(ref):
+                return ref.at[:, :, :, :, pl.ds(0, ref.shape[4] * wide // narrow)]
+
+            self.near = {key: [less(ref) for ref in held] for key, held in self.near.items()}
+            self.relay = {key: [less(ref) for ref in held] for key, held in self.relay.items()}
+        self.fin, self.fin_o, self.staged, self.landed, self.last, self.own = last
         self.size = {s: (2, 4, 2, 16, wide) for s in PARTS}
         self.source = {s: source.at[:, :, :, s] for s in PARTS}
 
@@ -324,8 +353,9 @@
         terms = [slab_of(self.source[s], span(self.size[s], axis, self.at), shape)]
         terms += [slab_of(buf, ALL_CUT, shape) for buf in self.near[s, phase]]
         if phase < 2:
-            add_up(slab_to(self.acc[s, phase], shape), terms, shape)
-            self.source[s], self.size[s] = self.acc[s, phase], shape
+            held = self.near[s, phase][0]
+            add_up(slab_to(held, shape), terms, shape)
+            self.source[s], self.size[s] = held, shape
             return
         total = terms[0](0, 0, 0).astype(jnp.float32)
         for term in terms[1:]:
@@ -404,11 +434,12 @@
             self.final.append((remote, mine))
         yield
 
-    def finish(self, out, out_o=None):
+    def finish(self, out, base, limit, out_o=None):
         first = self.fin.shape[1]
         for tx in range(4):
             pltpu.make_async_copy(self.landed.at[tx], self.landed.at[tx], self.last.at[tx]).wait()
-            out[:, pl.ds(tx * first, first)] = self.landed[tx, :, :first]
+            count = min(first, limit - tx * first)
+            out[:, base + tx * first:base + tx * first + count] = self.landed[tx, :12, :count]
             for b in range(2 if self.split else 0):
                 out_o[pl.ds(12 * b, 12), pl.ds(tx * 384, 384)] = self.landed[tx, :12, first + 384 * b:first + 384 * b + 384]
         for remote, mine in self.final:
@@ -418,82 +449,58 @@
 SMALL = 1792
 
 
-def scatter_kernel(part_in, sums_in, heads_in, gain_in, out, small_out, core_sum, core_other, rounds_x, rounds_y, rounds_z, whole, send, recv, *refs, wide):
-    at = place()
-    z, y, x, c = (at[name] for name in ALL)
-    to_z, to_c, _, home = targets(at)
-    barrier = pltpu.get_barrier_semaphore()
-    for axis in ("z", "y", "x"):
-        for steps in (1, 2, 3):
-            pl.semaphore_signal(barrier, inc=1, device_id={axis: moved(at, axis, steps)[axis]}, device_id_type=MESH)
-    pl.semaphore_signal(barrier, inc=1, device_id={"c": 1 - c}, device_id_type=MESH)
-    for tx in range(4):
-        @pl.when(jnp.logical_not(jnp.logical_and(home, x == tx)))
-        def _():
-            pl.semaphore_signal(barrier, inc=1, device_id=(to_z, y, jnp.int32(tx), to_c), device_id_type=MESH)
-    pl.semaphore_wait(barrier, 14 - home.astype(jnp.int32))
-
-    links = Links(send, recv)
-    work = Scatter(at, links, part_in, wide, False, refs)
+def small_steps(at, links, whole, core_sum, core_other, rounds):
+    c = at["c"]
 
     def side(core):
         return pl.ds(pl.multiple_of(SMALL * core, 128), SMALL)
 
-    def small_steps():
-        whole[...] = jnp.zeros((8, 2 * SMALL), jnp.float32)
-        whole[:, :CONVC] = sums_in[...]
-        whole[7:8, :1536] = gain_in[...]
-        whole[:, CONVC:CONVC + 128] = heads_in[...]
-        going = [links.copy(whole.at[:, side(1 - c)], core_sum, {"c": 1 - c})]
+    going = [links.copy(whole.at[:, side(1 - c)], core_sum, {"c": 1 - c})]
+    yield
+    going[0].wait_recv()
+    total = core_sum[...] + whole[:, side(c)]
+    for axis, held in zip(("x", "y", "z"), rounds):
+        held[at[axis]] = total
+        mine = held.at[at[axis]]
+        going = [links.copy(mine, mine, {axis: moved(at, axis, steps)[axis]}) for steps in (1, 3, 2)]
         yield
-        going[0].wait()
-        links.sent.remove(going[0])
-        total = core_sum[...] + whole[:, side(c)]
-        for axis, held in (("x", rounds_x), ("y", rounds_y), ("z", rounds_z)):
-            held[at[axis]] = total
-            mine = held.at[at[axis]]
-            going = [links.copy(mine, mine, {axis: moved(at, axis, steps)[axis]}) for steps in (1, 3, 2)]
-            yield
-            for copy in going:
-                copy.wait_recv()
-            total = held[0]
-            for j in range(1, 4):
-                total = total + held[j]
-        whole[:, side(c)] = total
-        going = [links.copy(whole.at[:, side(c)], core_other, {"c": 1 - c})]
-        yield
-        going[0].wait_recv()
-        whole[:, side(1 - c)] = core_other[...]
-        yield
-
-    small = small_steps()
-    next(small)
-    for _ in work.steps():
-        next(small)
-    index = 32 * z + 8 * y + 2 * x + c
+        for copy in going:
+            copy.wait_recv()
+        total = held[0]
+        for j in range(1, 4):
+            total = total + held[j]
+    whole[:, side(c)] = total
+    going = [links.copy(whole.at[:, side(c)], core_other, {"c": 1 - c})]
+    yield
+    going[0].wait_recv()
+    links.settle()
+    whole[:, side(1 - c)] = core_other[...]
+    yield
+
+
+def own_slices(at, whole, d_taps, d_bias, d_norm_gain, d_gate_gain, d_dt_bias, d_rates, d_skip):
+    index = 32 * at["z"] + 8 * at["y"] + 2 * at["x"] + at["c"]
     total = whole[...]
-    for first, size, each, row, count, to in ((0, CONVC, 26, 0, 5, 0), (0, DI, 24, 5, 1, 5), (0, 1536, 12, 7, 1, 6)):
-        value = pltpu.roll(total[:, first:first + size], lax.rem(size - each * index, size), 1)
-        small_out[to:to + count, :] = value[row:row + count, :128]
-    small_out[8:16, :] = total[:, CONVC:CONVC + 128]
-    work.finish(out)
-    links.finish()
-
-
-def scatter(half_in, sums, head_sums, d_gain):
-    wide = half_in.shape[-1]
-    vm, f32 = pltpu.VMEM, jnp.float32
-    spec = pl.BlockSpec(memory_space=pltpu.VMEM)
-    scratch = [vm((8, SMALL), f32)] * 2 + [vm((4, 8, SMALL), f32)] * 3 + [vm((8, 2 * SMALL), f32)]
-    return pl.pallas_call(
-        functools.partial(scatter_kernel, wide=wide),
-        out_shape=[jax.ShapeDtypeStruct((16, wide), f32), jax.ShapeDtypeStruct((16, 128), f32)],
-        in_specs=[spec] * 4,
-        out_specs=[spec] * 2,
-        scratch_shapes=scratch + [pltpu.SemaphoreType.DMA((64,))] * 2 + scatter_scratch(wide, False),
-        compiler_params=pltpu.CompilerParams(collective_id=1, has_side_effects=True, vmem_limit_bytes=48 << 20),
-        name="scatter_gradients",
-    )(half_in.reshape(2, 4, 2, 3, 16, wide), sums, head_sums, d_gain)
+
+    def own(size, each):
+        return pltpu.roll(total[:, :size], lax.rem(size - each * index, size), 1)
+
+    value = own(CONVC, 26)
+    d_taps[...] = value[0:4, :26]
+    d_bias[...] = value[4:5, :26]
+    d_gate_gain[...] = own(DI, 24)[5:6, :24]
+    d_norm_gain[...] = own(1536, 12)[7:8, :12]
+    by_head = total[:, CONVC:CONVC + 128]
+    d_dt_bias[...] = by_head[0:1, :48]
+    d_rates[...] = by_head[1:2, :48]
+    row = lax.broadcasted_iota(jnp.int32, (128, 128), 0)
+    col = lax.broadcasted_iota(jnp.int32, (128, 128), 1)
+    heads = jnp.zeros((8, 128), jnp.float32)
+    for b in range(2):
+        ones = jnp.where(2 * row + b == col, 1.0, 0.0).astype(jnp.bfloat16)
+        for part in split3(jnp.broadcast_to(by_head[2 + b:3 + b], (8, 128))):
+            heads = heads + jnp.dot(part, ones, preferred_element_type=jnp.float32)
+    d_skip[...] = heads[0:1, :48]
 
 
 H = 48
@@ -509,6 +516,7 @@
 
 
 TILES = 24
+BUFFERS = 3
 
 
 def dot(a, b):
@@ -556,15 +564,18 @@
     lax.fori_loop(0, count // unroll, step, 0)
 
 
-def mixer_kernel(conv_in, dt_in, normed, hidden, given_out, taps, gain, skip, heads, part_w,
-                 out, dproj, d_norm, sums, headsums, g_z, g_o, weights_,
-                 gates, db, branch, dz, sib_normed, sib_given, sib_branch, sib_dz, src, chunk, chunk_sem,
+def mixer_kernel(normed, given_out, taps, gain, norm_gain, dt_bias, rates, d_skip, hidden_in, w_late, part_w,
+                 out, d_hidden, g_in, g_o, o_taps, o_bias, o_norm, o_gate, o_dt, o_rates, o_skip, weights_,
+                 skip, heads,
+                 conv_in, dt_in, dproj, sums, headsums,
+                 gates, db, branch, dz, sib_normed, sib_given, sib_branch, sib_dz, src, chunk, chunk_sem, flipped, out_sem, ready,
                  act, ys, dys, shift, shift2, halo_out, halo_in, back_out, back_in,
                  cum, ecum, toward, steps, rows_a, scores, dscores, usum, qin, qw, prods, stat, coef, db_in, dc_in, decay,
                  skips, loc, inc, inc2, *rest):
     f32, bf16 = jnp.float32, jnp.bfloat16
-    snd, rcv, ret = rest[:3]
-    ways, (sib_send, sib_recv, a_send, a_recv, h_sem, rs_send, rs_recv), rest = (rest[3:5], rest[5:7]), rest[7:14], rest[14:]
+    snd, rcv, ret, sib, across = rest[:5]
+    (sib_send, sib_recv, a_send, a_recv, h_sem, rs_send, rs_recv, l_send, l_recv, t_send, t_recv), rest = rest[5:16], rest[16:]
+    whole, core_sum, core_other, rounds, last_early, last_late, rest = rest[0], rest[1], rest[2], rest[3:6], rest[6:12], rest[12:18], rest[18:]
     at = place()
     z, core = lax.axis_index("z"), lax.axis_index("c")
     chip = 4 * lax.axis_index("y") + lax.axis_index("x")
@@ -634,13 +645,73 @@
     def lanes(start, size):
         return pl.ds(pl.multiple_of(start, 128), size)
 
+    links = Links(rs_send, rs_recv)
+    ring = Ring(links, at, weights_, 2, True)
+    ring.start()
+
+    def from_late(k, slot):
+        pltpu.make_async_copy(
+            w_late.at[:, :, :, :, :, :, lanes(384 * k, 384)],
+            chunk.at[slot].reshape(2, 2, 4, 2, 3, 16, 384), chunk_sem.at[slot]).start()
+
+    def from_gates(k, slot):
+        pltpu.make_async_copy(
+            weights_.at[:, :, :, :, :, :, lanes(1536 * (k // 2) + 384 * lax.rem(k, 2), 384)],
+            chunk.at[slot].reshape(2, 2, 4, 2, 3, 16, 384), chunk_sem.at[slot]).start()
+
+    def from_out(k, slot):
+        for b in range(2):
+            pltpu.make_async_copy(
+                weights_.at[k // 4, :, :, :, :, :, lanes(1536 * lax.rem(k, 4) + 768 + 384 * b, 384)],
+                chunk.at[slot].reshape(2, 4, 2, 3, 32, 384).at[:, :, :, :, pl.ds(16 * b, 16)], chunk_sem.at[slot]).start()
+
+    def prefetch(fetch):
+        for slot in range(BUFFERS):
+            fetch(jnp.int32(slot), slot)
+
+    def stream(fetch, count, use):
+        def round_(n, u):
+            for slot in range(BUFFERS):
+                k = BUFFERS * n + slot
+
+                @pl.when(k < count)
+                def _():
+                    pltpu.make_async_copy(chunk.at[slot], chunk.at[slot], chunk_sem.at[slot]).wait()
+                    use(k, chunk[slot])
+
+                @pl.when(k + BUFFERS < count)
+                def _():
+                    fetch(k + BUFFERS, slot)
+
+        loop(0, -(-count // BUFFERS), round_, 1)
+
+    prefetch(from_late)
+
+    def project(k, w):
+        value = dot(normed[...], w)
+
+        @pl.when(k < 8)
+        def _():
+            conv_in[:, lanes(384 * jnp.minimum(k, 7), 384)] = low(value)
+
+        @pl.when(k == 8)
+        def _():
+            conv_in[:, 3072:CONVC] = low(value[:, :256])
+            dt_in[...] = value[:, 256:]
+
+    stream(from_late, 9, project)
     halo_out[...] = conv_in[240:256, :]
     front = neighbour(0, halo_out, halo_in, 1, me < 31)
     shared = [to_sibling(5, normed.at[:, lanes(768 * (1 - core), 768)], sib_normed), to_sibling(6, given_out, sib_given)]
 
-    links = Links(rs_send, rs_recv)
-    ring = Ring(links, at, weights_, 2, True)
-    ring.start()
+
+    heads[...] = jnp.zeros((8, 128), f32)
+    for k, ref in enumerate((dt_bias, rates, d_skip)):
+        heads[k:k + 1, :H] = ref[...]
+    by_head_ = heads[2:3, :]
+    for j in range(TILES):
+        skip[:, 128 * j:128 * j + 128] = jnp.where(
+            lane[0:1] < 64, jnp.broadcast_to(by_head_[:, 2 * j:2 * j + 1], (1, 128)), jnp.broadcast_to(by_head_[:, 2 * j + 1:2 * j + 2], (1, 128)))
 
     raw = dt_in[...] + heads[0:1, :]
     dt = jnp.maximum(raw, 0.0) + jnp.log1p(jnp.exp(-jnp.abs(raw)))
@@ -716,7 +787,7 @@
     class Carry:
         def __init__(self, way, backward, into):
             self.e, self.backward, self.into = 2 * way, backward, into
-            self.sib, self.across = ways[way]
+            self.sib, self.across = sib, across
             self.snd, self.rcv, self.ret = snd, rcv, ret
 
         def swap(self):
@@ -846,48 +917,18 @@
     ring.finish()
     ring.end()
 
-    def fetch(k, slot):
-        first = jnp.minimum(k, 7)
-        a_ = pltpu.make_async_copy(
-            weights_.at[:, :, :, :, :, :, lanes(1536 * (first // 2) + 384 * lax.rem(first, 2), 384)],
-            chunk.at[slot].reshape(2, 2, 4, 2, 3, 16, 384), chunk_sem.at[slot])
-        pl.when(k < 8)(a_.start)
-        later = jnp.maximum(k - 8, 0)
-        for b in range(2):
-            b_ = pltpu.make_async_copy(
-                weights_.at[later // 4, :, :, :, :, :, lanes(1536 * lax.rem(later, 4) + 768 + 384 * b, 384)],
-                chunk.at[slot].reshape(2, 4, 2, 3, 32, 384).at[:, :, :, :, pl.ds(16 * b, 16)], chunk_sem.at[slot])
-            pl.when(k >= 8)(b_.start)
-
-    def stream(use):
-        def two(n, u):
-            for slot in range(2):
-                k = 2 * n + slot
-                pltpu.make_async_copy(chunk.at[slot], chunk.at[slot], chunk_sem.at[slot]).wait()
-                use(k, chunk[slot])
-
-                @pl.when(k + 2 < 16)
-                def _():
-                    fetch(k + 2, slot)
-
-        fetch(jnp.int32(0), 0)
-        fetch(jnp.int32(1), 1)
-        loop(0, 8, two, 1)
-
+    prefetch(from_gates)
     db[...] = jnp.zeros((256, DI), f32)
 
-    def before_gate(k, w):
-        @pl.when(k < 8)
-        def _():
-            gates[:, lanes(384 * jnp.minimum(k, 7), 384)] = dot(normed[...], w)
-
-        @pl.when(k >= 8)
-        def _():
-            later = jnp.maximum(k - 8, 0)
-            part = lanes(1536 * (later // 4), 1536)
-            db[:, part] += dot_nt(given_out[:, lanes(384 * lax.rem(later, 4), 384)], w)
-
-    stream(before_gate)
+    def make_gates(k, w):
+        gates[:, lanes(384 * k, 384)] = dot(normed[...], w)
+
+    def make_db(k, w):
+        db[:, lanes(1536 * (k // 4), 1536)] += dot_nt(given_out[:, lanes(384 * lax.rem(k, 4), 384)], w)
+
+    stream(from_gates, 8, make_gates)
+    prefetch(from_out)
+    stream(from_out, 8, make_db)
 
     def state(ref, j):
         return ref[pl.ds(pl.multiple_of(128 * j, 128), 128), :]
@@ -934,53 +975,63 @@
         return carry
 
     ahead.first.wait_send()
+    ahead.end()
     loop(given, 12, gate_back, 4)
     aback.swap()
     theirs, ours = lanes(1536 * (1 - core), 1536), lanes(1536 * core, 1536)
     shared += [to_sibling(7, branch.at[:, theirs], sib_branch), to_sibling(8, dz.at[:, theirs], sib_dz.at[:, theirs])]
     loop(mine, 12, gate_back, 4)
     shared += [to_sibling(9, dz.at[:, ours], sib_dz.at[:, ours])]
-    ahead.end()
     aback.start()
     for copy in shared:
         copy.wait_recv()
 
-    def d_w_gates(k, u):
-        zh, n = k // 8, lax.rem(k, 8)
-        part = lanes(384 * n, 384)
-        total = dot_tn(normed[:, lanes(768 * core + 384 * zh, 384)], dz[:, part])
-        total = total + dot_tn(sib_normed[:, lanes(384 * zh, 384)], sib_dz[:, part])
-        src[zh, :, :, :, :, lanes(1536 * (n // 2) + 384 * lax.rem(n, 2), 384)] = low(total).reshape(4, 2, 3, 16, 384)
-
-    def d_w_out(k, u):
-        q, n = k // 4, lax.rem(k, 4)
-        part = lanes(384 * n, 384)
-        total = dot_tn(branch[:, lanes(1536 * core + 384 * q, 384)], given_out[:, part])
-        total = total + dot_tn(sib_branch[:, lanes(384 * q, 384)], sib_given[:, part])
-        total = low(total).reshape(2, 2, 3, 2, 16, 384)
-        for b in range(2):
-            src[q // 2, pl.ds(2 * lax.rem(q, 2), 2), :, :, :, lanes(1536 * n + 768 + 384 * b, 384)] = total[:, :, :, b]
-
-    loop(0, 16, d_w_gates, 1)
-    loop(0, 16, d_w_out, 1)
+    def flip(own, theirs):
+        flipped[:, :256] = low(jnp.transpose(wide(own)))
+        flipped[:, 256:] = low(jnp.transpose(wide(theirs)))
+
+    def flip_normed(zh):
+        flip(normed[:, lanes(768 * core + 384 * zh, 384)], sib_normed[:, 384 * zh:384 * zh + 384])
+
+    for zh in range(2):
+        flip_normed(zh)
+
+        def d_w_gates(n, u):
+            part = lanes(384 * n, 384)
+            total = dot(flipped[:, :256], dz[:, part]) + dot(flipped[:, 256:], sib_dz[:, part])
+            src[zh, :, :, :, :, lanes(1536 * (n // 2) + 384 * lax.rem(n, 2), 384)] = low(total).reshape(4, 2, 3, 16, 384)
+
+        loop(0, 8, d_w_gates, 2)
+    for q in range(4):
+        flip(branch[:, lanes(1536 * core + 384 * q, 384)], sib_branch[:, 384 * q:384 * q + 384])
+
+        def d_w_out(n, u):
+            part = lanes(384 * n, 384)
+            total = dot(flipped[:, :256], given_out[:, part]) + dot(flipped[:, 256:], sib_given[:, part])
+            total = low(total).reshape(2, 2, 3, 2, 16, 384)
+            for b in range(2):
+                src[q // 2, 2 * (q % 2):2 * (q % 2) + 2, :, :, :, lanes(1536 * n + 768 + 384 * b, 384)] = total[:, :, :, b]
+
+        loop(0, 4, d_w_out, 2)
+    hidden = sib_given
+    hidden_load = pltpu.make_async_copy(hidden_in, hidden, out_sem.at[2])
+    hidden_load.start()
+    prefetch(from_gates)
     aback.turn()
-    work = Scatter(at, links, src, 2 * DI, True, rest)
+    work = Scatter(at, links, src, 2 * DI, True, rest, last_early)
     reduce = work.steps()
     next(reduce)
-    d_norm[...] = jnp.zeros((256, 1536), f32)
+    d_norm = gates
+    d_norm[:, :1536] = jnp.zeros((256, 1536), f32)
     out_sum = db
 
-    def after_gate(k, w):
-        @pl.when(k < 8)
-        def _():
-            d_norm[...] += dot_nt(dz[:, lanes(384 * jnp.minimum(k, 7), 384)], w)
-
-        @pl.when(k >= 8)
-        def _():
-            later = jnp.maximum(k - 8, 0)
-            part = lanes(384 * lax.rem(later, 4), 384)
-            held = jnp.where(later < 4, wide(hidden[:, part]), out_sum[:, part])
-            out_sum[:, part] = held + dot(branch[:, lanes(1536 * (later // 4), 1536)], w)
+    def norm_gates(k, w):
+        d_norm[:, :1536] += dot_nt(dz[:, lanes(384 * k, 384)], w)
+
+    def make_out(k, w):
+        part = lanes(384 * lax.rem(k, 4), 384)
+        held = jnp.where(k < 4, wide(hidden[:, part]), out_sum[:, part])
+        out_sum[:, part] = held + dot(branch[:, lanes(1536 * (k // 4), 1536)], w)
 
     for ref in (usum, qin, qw):
         ref[...] = jnp.zeros((256, 128), f32)
@@ -1009,8 +1060,7 @@
     loop(0, TILES // 2, inside_back, 3)
     next(reduce)
     loop(TILES // 2, TILES // 2, inside_back, 3)
-    stream(after_gate)
-    out[...] = low(out_sum[:, :1536])
+    stream(from_gates, 8, norm_gates)
     next(reduce)
     aback.finish()
     db_in[...] = jnp.zeros((256, 128), f32)
@@ -1036,7 +1086,7 @@
         prods[pl.ds(2 * j + 1, 1), :] = jnp.sum(pair[64:], axis=0, keepdims=True)
         d_mix(j, u, ys[j] + d_w + skip[:, cols(j)] * dyf)
 
-    loop(0, TILES, carry_back, 4)
+    loop(0, TILES, carry_back, 3)
     next(reduce)
     ds = low(dscores[...])
     d_mix(TILES, 0, db_in[...] + dot_tn(ds, c_out))
@@ -1081,65 +1131,135 @@
             total = total + taps[k:k + 1, cols(j)] * shift2[u, 3 - k:259 - k, :]
         dproj[:, cols(j)] = low(total)
 
-    loop(0, TILES + 2, conv_back, 2)
-    work.finish(g_z, g_o)
-    links.finish()
+    links.settle()
+    for axis in ("z", "y", "x"):
+        for steps_ in (1, 2, 3):
+            pl.semaphore_signal(ready, inc=1, device_id={axis: moved(at, axis, steps_)[axis]}, device_id_type=MESH)
+    loop(0, TILES // 2, conv_back, 2)
+    shared += [to_sibling(10, dproj.at[:, :1536], sib_dz.at[:, :1536])]
+    loop(TILES // 2, TILES // 2 + 2, conv_back, 2)
+    shared += [to_sibling(11, dproj.at[:, 1536:], sib_dz.at[:, 1536:])]
+    work.finish(g_in, 0, DI, g_o)
+    for copy in shared[-2:]:
+        copy.wait_recv()
+
+    prefetch(from_late)
+    for zh in range(2):
+        flip_normed(zh)
+
+        def d_w_late(n, u):
+            part = lanes(384 * n, 384)
+            total = dot(flipped[:, :256], dproj[:, part]) + dot(flipped[:, 256:], sib_dz[:, part])
+            src[zh, :, :, :, :, part] = low(total).reshape(4, 2, 3, 16, 384)
+
+        loop(0, 9, d_w_late, 3)
+    for k in range(2):
+        src[k, :, :, :, :, 3456:3584] = jnp.zeros((4, 2, 3, 16, 128), bf16)
+    pl.semaphore_wait(ready, 9)
+    after = Links(l_send, l_recv)
+    width = WIDE - DI
+    work = Scatter(at, after, src.at[:, :, :, :, :, pl.ds(0, width)], width, False, rest, last_late, 2 * DI)
+    reduce = work.steps()
+    next(reduce)
+
+    def norm_late(k, w):
+        d_norm[:, :1536] += dot_nt(dproj[:, lanes(384 * k, 384)], w)
+
+    stream(from_late, 9, norm_late)
+    prefetch(from_out)
+
+    hidden_load.wait()
+    stat[...] = jnp.zeros((256, 128), f32)
+    coef[...] = jnp.zeros((256, 128), f32)
+
+    def norm_sums(j, u):
+        v = wide(hidden[:, cols(j)])
+        stat[...] += v * v
+        coef[...] += v * (norm_gain[:, cols(j)] * d_norm[:, cols(j)])
+
+    loop(0, 12, norm_sums, 4)
+    scale = lax.rsqrt(jnp.sum(stat[...], axis=1, keepdims=True) * (1.0 / 1536) + epsilon)
+    factor = scale * scale * scale * (jnp.sum(coef[...], axis=1, keepdims=True) * (1.0 / 1536))
+    stat[...] = jnp.broadcast_to(scale, (256, 128))
+    coef[...] = jnp.broadcast_to(factor, (256, 128))
+
+    def norm_back(j, u):
+        v, dn = wide(hidden[:, cols(j)]), d_norm[:, cols(j)]
+        sums[7:8, cols(j)] = jnp.sum(dn * v * stat[...], axis=0, keepdims=True)
+        d_norm[:, cols(j)] = wide(given_out[:, cols(j)]) + stat[...] * norm_gain[:, cols(j)] * dn - v * coef[...]
+
+    loop(0, 12, norm_back, 4)
+    hidden_copy = pltpu.make_async_copy(d_norm.at[:, :1536], d_hidden, out_sem.at[1])
+    hidden_copy.start()
+    whole[:, :CONVC] = sums[...]
+    whole[:, CONVC:CONVC + 128] = headsums[...]
+    whole[:, CONVC + 128:] = jnp.zeros((8, 128), f32)
+    tiny = Links(t_send, t_recv)
+    small = small_steps(at, tiny, whole, core_sum, core_other, rounds)
+    next(small)
+    next(reduce)
+    next(small)
+    stream(from_out, 8, make_out)
+    sib_branch[...] = low(out_sum[:, :1536])
+    out_copy = pltpu.make_async_copy(sib_branch, out, out_sem.at[0])
+    out_copy.start()
+    for _ in reduce:
+        next(small)
+    next(small)
+    own_slices(at, whole, o_taps, o_bias, o_norm, o_gate, o_dt, o_rates, o_skip)
+    work.finish(g_in, DI, PROJ - DI)
+    after.finish()
+    tiny.finish()
     for copy in shared:
         copy.wait_send()
+    out_copy.wait()
+    hidden_copy.wait()
     pl.when(me < 31)(front.wait_send)
     pl.when(me > 0)(behind.wait_send)
     decays.wait_send()
     aback.end()
 
 
-def mixer(conv_in, dt_in, normed, hidden, given_out, taps, gain, skip, heads, part_w):
+def mixer(normed, given_out, taps, gain, norm_gain, dt_bias, rates, d_skip, hidden, w_late, part_w):
     f32, bf16 = jnp.float32, jnp.bfloat16
     tile, half, late = (256, 128), (16, CONVC), WIDE - DI
     vm = pltpu.VMEM
     dma = pltpu.SemaphoreType.DMA
     scratch = [
+        vm((1, DI), f32), vm((8, 128), f32),
+        vm((256, CONVC), bf16), vm(tile, f32), vm((256, late), bf16), vm((8, CONVC), f32), vm((8, 128), f32),
         vm((256, DI), f32), vm((256, DI), f32),
-        vm((256, DI), bf16), vm((256, DI), bf16), vm((256, 768), bf16), vm((256, 1536), bf16), vm((256, 1536), bf16), vm((256, DI), bf16),
-        vm((2, 4, 2, 3, 16, 2 * DI), bf16), vm((2, 1536, 384), bf16), dma((2,)),
+        vm((256, DI), bf16), vm((256, DI), bf16), vm((256, 768), bf16), vm((256, 1536), bf16), vm((256, 1536), bf16), vm((256, late), bf16),
+        vm((2, 4, 2, 3, 16, 2 * DI), bf16), vm((BUFFERS, 1536, 384), bf16), dma((BUFFERS,)), vm((384, 512), bf16), dma((3,)), pltpu.SemaphoreType.REGULAR,
         vm((TILES + 2,) + tile, bf16), vm((TILES + 2,) + tile, f32), vm((TILES,) + tile, bf16),
-        vm((4, 264, 128), f32), vm((2, 264, 128), f32), vm(half, bf16), vm(half, bf16), vm(half, bf16), vm(half, bf16),
+        vm((3, 264, 128), f32), vm((2, 264, 128), f32), vm(half, bf16), vm(half, bf16), vm(half, bf16), vm(half, bf16),
         vm(tile, f32), vm(tile, f32), vm(tile, f32), vm(tile, f32), vm((128, 256), f32), vm((256, 256), f32), vm((256, 256), f32),
         vm(tile, f32), vm(tile, f32), vm(tile, f32), vm((128, 128), f32), vm(tile, f32), vm(tile, f32), vm(tile, f32), vm(tile, f32),
         vm((16, 128), f32), vm((128, 128), f32), vm((3072, 128), bf16), vm((3072, 128), bf16), vm((3072, 128), bf16),
     ]
     scratch += [vm((16, 112, 128), bf16), vm((16, 112, 128), bf16), vm((16, 96, 128), bf16)]
-    for _ in range(2):
-        scratch += [vm((1536, 128), bf16), vm((1536, 128), bf16)]
-    scratch += [dma((10,)), dma((10,)), dma((4, 16)), dma((4, 16)), dma((4,)), dma((64,)), dma((64,))]
-    scratch += scatter_scratch(2 * DI, True)
+    scratch += [vm((1536, 128), bf16), vm((1536, 128), bf16)]
+    scratch += [dma((12,)), dma((12,)), dma((4, 16)), dma((4, 16)), dma((4,)), dma((64,)), dma((64,)), dma((40,)), dma((40,)), dma((12,)), dma((12,))]
+    scratch += [vm((8, 2 * SMALL), f32), vm((8, SMALL), f32), vm((8, SMALL), f32)] + [vm((4, 8, SMALL), f32)] * 3
+    scratch += last_scratch(2 * DI, 768) + last_scratch(late, late // 4) + scatter_scratch(2 * DI)
     near, far = pl.BlockSpec(memory_space=pltpu.VMEM), pl.BlockSpec(memory_space=pl.ANY)
     return pl.pallas_call(
         mixer_kernel,
-        out_shape=[jax.ShapeDtypeStruct((256, 1536), bf16), jax.ShapeDtypeStruct((256, late), bf16),
-                   jax.ShapeDtypeStruct((256, 1536), f32), jax.ShapeDtypeStruct((8, CONVC), f32), jax.ShapeDtypeStruct((8, 128), f32),
-                   jax.ShapeDtypeStruct((16, DI), f32), jax.ShapeDtypeStruct((24, 1536), f32),
-                   jax.ShapeDtypeStruct(part_w.shape, bf16)],
-        in_specs=[near] * 9 + [far],
-        out_specs=[near] * 7 + [far],
+        out_shape=[jax.ShapeDtypeStruct((256, 1536), bf16), jax.ShapeDtypeStruct((256, 1536), f32),
+                   jax.ShapeDtypeStruct((12, PROJ), f32), jax.ShapeDtypeStruct((24, 1536), f32)]
+        + [jax.ShapeDtypeStruct(size, f32) for size in ((4, 26), (1, 26), (1, 12), (1, 24), (1, H), (1, H), (1, H))]
+        + [jax.ShapeDtypeStruct(part_w.shape, bf16)],
+        in_specs=[near] * 8 + [far] * 3,
+        out_specs=[far] * 2 + [near] * 9 + [far],
         scratch_shapes=scratch,
-        input_output_aliases={9: 7},
-        compiler_params=pltpu.CompilerParams(collective_id=2, has_side_effects=True, vmem_limit_bytes=62 << 20),
+        input_output_aliases={10: 11},
+        compiler_params=pltpu.CompilerParams(collective_id=2, has_side_effects=True, vmem_limit_bytes=63 << 20),
         name="mixer",
-    )(conv_in, dt_in, normed, hidden, given_out, taps, gain, skip, heads, part_w)
+    )(normed, given_out, taps, gain, norm_gain, dt_bias, rates, d_skip, hidden, w_late, part_w)
 
 
 def rms_scale(values, gain):
     return values * lax.rsqrt(jnp.mean(values * values, axis=-1, keepdims=True) + epsilon) * gain
-
-
-def swap(value):
-    return lax.ppermute(value, "c", [(0, 1), (1, 0)])
-
-
-def my_half(value, core):
-    wide = value.shape[1] // 2
-    given = swap(lax.dynamic_slice_in_dim(value, (1 - core) * wide, wide, axis=1))
-    return jnp.concatenate([lax.dynamic_slice_in_dim(value, core * wide, wide, axis=1), given], axis=0)
 
 
 def shards(
@@ -1155,55 +1275,30 @@
     decay_rates,
     d_skip,
 ):
-    core = lax.axis_index("c")
-    spare = jnp.concatenate([
-        jnp.pad(conv_w, ((0, 0), (0, 102))),
-        jnp.pad(conv_b, (0, 102))[None],
-        jnp.pad(norm_gain, (0, 116))[None],
-        jnp.pad(gate_gain, (0, 104))[None],
-        jnp.zeros((5, 128), jnp.bfloat16),
-    ])
-    late = jnp.pad(jnp.concatenate([jnp.pad(in_w[:, DI:], ((0, 0), (0, PARAMS - PROJ))), spare], axis=1), ((0, 4), (0, 0)))
-    early = jnp.concatenate([
-        in_w[:, :DI].reshape(12, 4, 768), out_w.reshape(2, 12, 4, 384).transpose(1, 2, 0, 3).reshape(12, 4, 768)
-    ], axis=2).reshape(12, 2 * DI)
-    w_late, w_early = gather(late, jnp.pad(early, ((0, 4), (0, 0))))
-    w_late = w_late.reshape(1536, WIDE - DI)
-    spare = w_late[:, PARAMS - DI:].reshape(128, 12, 128).astype(jnp.float32)
+    w_late, w_early = gather(in_w, out_w, conv_w, conv_b, norm_gain, gate_gain)
+    spare = w_late[:, :, :, :, :, :, PARAMS - DI:].reshape(128, 12, 128).astype(jnp.float32)
     w_conv_f = spare[:, :4, :26].transpose(1, 0, 2).reshape(KW, CONVC)
     b_conv_f = spare[:, 4, :26].reshape(CONVC)
     gain_norm_f = spare[:, 5, :12].reshape(1536)
     gain_gate_f = spare[:, 6, :24].reshape(DI)
     residual = hidden[0].astype(jnp.float32)
-    length = residual.shape[0]
     normed = rms_scale(residual, gain_norm_f).astype(jnp.bfloat16)
-    conv_in = jnp.dot(normed, w_late[:, :CONVC], preferred_element_type=jnp.float32).astype(jnp.bfloat16)
-    dt_in = jnp.dot(normed, w_late[:, CONVC : PARAMS - DI], preferred_element_type=jnp.float32)
-    grad_out = cotangent[0]
     taps = jnp.pad(jnp.concatenate([w_conv_f, b_conv_f[None]]), ((0, 3), (0, 0)))
-    heads = jnp.pad(jnp.stack([dt_bias, decay_rates]), ((0, 6), (0, 80)))
-    result, d_late, d_normed, sums, head_sums, g_gates, g_out, _ = mixer(
-        conv_in, dt_in, normed, hidden[0], grad_out, taps, gain_gate_f[None],
-        jnp.repeat(d_skip, P_SIZE)[None], heads, w_early)
-    d_normed = d_normed + jnp.einsum("tj,dj->td", d_late, w_late, preferred_element_type=jnp.float32)
-    both_late = jnp.concatenate([d_late, swap(d_late)], axis=0)
-    d_w_late = jnp.einsum("td,tj->dj", my_half(normed, core), both_late, preferred_element_type=jnp.float32).astype(jnp.bfloat16)
-    norm_pull = jax.vjp(rms_scale, residual, gain_norm_f)[1]
-    d_from_norm, d_gain_norm = norm_pull(d_normed)
-    d_hidden = grad_out.astype(jnp.float32) + d_from_norm
-    g_late, total = scatter(d_w_late, sums, head_sums, d_gain_norm[None])
+    result, d_hidden, g_in, g_out, d_taps, d_bias, d_norm_gain, d_gate_gain, d_dt, d_rates, d_skips, _ = mixer(
+        normed, cotangent[0], taps, gain_gate_f[None], gain_norm_f[None],
+        dt_bias[None], decay_rates[None], d_skip[None], hidden[0], w_late, w_early)
     return (
         result[None],
         d_hidden[None],
-        jnp.concatenate([g_gates[:12], g_late[:12, : PROJ - DI]], axis=1),
+        g_in,
         g_out,
-        total[:4, :26],
-        total[4, :26],
-        total[6, :12],
-        total[5, :24],
-        total[8, :H],
-        total[9, :H],
-        jnp.stack([total[10, :H // 2], total[11, :H // 2]], axis=1).reshape(H),
+        d_taps,
+        d_bias[0],
+        d_norm_gain[0],
+        d_gate_gain[0],
+        d_dt[0],
+        d_rates[0],
+        d_skips[0],
     )
 
 

time: 311 us -> 274 us (0.88)
  matrix products: 23.4 us -> 0 us
  local copies, waits for them, and re-layouts: 20.3 us -> 11 us
    pallas_call x1 -> x0, Pallas kernels: 42.8 us -> none  [scatter(): pl.pallas_call(functools.partial(scatter_kernel, wide=wide), out_shape=[j...]
    pallas_call x1, Pallas kernels: 167 us -> 205 us  [mixer(): pl.pallas_call(mixer_kernel, out_shape=[jax.ShapeDtypeStruct((256, 1536),...]
    dot_general x4 -> x0, matrix products: 23.4 us -> none  [the longest x1 8.37 us: shards(): jnp.einsum('tj,dj->td', d_late, w_late, preferred_element_type=jnp.float32)]
    unnamed x36 -> x33, local copies, waits for them, and re-layouts: 6.16 us -> 8.44 us
  transfers between devices with their start and end apart: 2 -> 0, of which waited for: 0 -> 0; matrix products, arithmetic and copies ran while one was open for 3% -> 0% of each run, Pallas kernels for 0% -> 0%
where the time goes in v6:
time: 274 us; the launch traced here: 273 us
  Pallas kernels  257 us (94%)
  local copies, waits for them, and re-layouts  11 us (4%)
  other arithmetic  4.25 us (2%)
    pallas_call x1, Pallas kernels, mixer(): pl.pallas_call(mixer_kernel, out_shape=[jax.ShapeDtypeStruct((256, 1536),...  205 us
    pallas_call x1, Pallas kernels, gather(): pl.pallas_call(gather_kernel, out_shape=[jax.ShapeDtypeStruct((2, 2, 4, 2...  52.2 us
    unnamed x33, local copies, waits for them, and re-layouts  8.44 us

profile of v6, /device:TPU:1, one launch (start us, length us, event | category | flops | bytes accessed | tf_op | source)
XLA Modules:
  0.0 273.2 jit_solution(10713801850081861973)
XLA Ops:
  0.6 1.4 fusion
  2.0 52.2 %gather_weights.1 = (bf16[2,2,4,2,3,16,3584]{6,5,4,3,2,1,0:T(8,128)(2,1)}, bf16[2,2,4,2,3,16,6144]{6,5,4,3,2,1,0:T(8,128)(2,1)}) custom-call(bf16[12,6448]{1,0:T(8,128)(2,1)} %refs_0_.1, bf16[24,1536]{1,0:T(8,128)(2,1)} %refs_1_.1, bf16[4,26]{1,0:T(4,128)(2,1)} %refs_2_.1, bf16[1,26]{1,0:T(2,128)(2,1)} %bitcast.28, bf16[1,12]{1,0:T(2,128)(2,1)} %bitcast.29, ...), custom_call_target="tpu_custom_call" | custom-call | tf_op jit(solution)/shard_map/gather_weights/pallas_call | solution.py:220
  54.2 1.1 slice_convert_fusion
  55.3 0.1 reshape.38
  55.4 0.0 copy-start
  55.4 0.2 slice_reduce_fusion
  55.6 0.7 broadcast_in_dim_reshape_squeeze.11.gain
  56.3 0.2 slice_reduce_fusion.1
  56.5 0.1 broadcast_in_dim_reshape_squeeze.10
  56.6 0.2 fusion.3
  56.9 0.2 reshape.37
  57.1 0.7 broadcast_in_dim_reshape_squeeze.12.norm_gain
  57.8 0.1 mul.24
  57.9 0.7 select_maximum_fusion.taps
  58.6 0.0 copy-done
  58.6 1.1 fusion.2.normed
  59.7 205.0 %mixer.1 = (bf16[256,1536]{1,0:T(8,128)(2,1)}, f32[256,1536]{1,0:T(8,128)}, f32[12,6448]{1,0:T(8,128)}, f32[24,1536]{1,0:T(8,128)}, f32[4,26]{1,0:T(4,128)}, /*i...) custom-call(bf16[256,1536]{1,0:T(8,128)(2,1)} %fusion.2.normed, ...), custom_call_target="tpu_custom_call", output_to_operand_aliasing={{11}: (10, {})} | custom-call | tf_op jit(solution)/shard_map/mixer/pallas_call | solution.py:1246
  264.7 0.0 copy-start.1
  264.7 2.2 copy.40
  266.9 0.0 copy-done.1
  266.9 0.0 copy-start.2
  266.9 0.0 copy-start.3
  266.9 0.0 copy-start.4
  266.9 0.0 copy-start.10
  266.9 0.0 copy-start.9
  266.9 0.0 copy-start.8
  267.0 0.0 copy-start.7
  267.0 0.0 copy-start.6
  267.0 0.0 copy-start.5
  267.0 1.1 copy.41
  268.1 0.0 copy-done.2
  268.1 0.8 copy.42
  268.9 0.0 copy-done.3
  268.9 0.7 copy.43
  269.6 0.0 copy-done.4
  269.6 0.6 copy.44
  270.1 0.0 copy-done.10
  270.1 0.5 copy.45
  270.6 0.0 copy-done.9
  270.7 0.5 copy.46
  271.2 0.0 copy-done.8
  271.2 0.5 copy.47
  271.7 0.0 copy-done.7
  271.7 0.5 copy.48
  272.2 0.0 copy-done.6
  272.2 0.5 copy.49
  272.7 0.0 copy-done.5
  272.7 0.5 copy.50
  (3 shorter events, 0.1 us)
Async XLA Ops:
  55.4 3.3 %copy-start = (bf16[1,256,1536]{2,1,0:T(8,128)(2,1)S(1)}, bf16[1,256,1536]{2,1,0:T(8,128)(2,1)}, u32[]{:S(2)}) copy-start(bf16[1,256,1536]{2,1,0:T(8,128)(2,1)} %param.11) | copy-start | bytes 2359300
  264.7 2.2 copy-start.1
  266.9 1.2 copy-start.2
  266.9 2.0 copy-start.3
  266.9 2.6 copy-start.4
  266.9 3.2 %copy-start.10 = (f32[1,26]{1,0:T(1,128)S(1)}, f32[1,26]{1,0:T(1,128)}, u32[]{:S(2)}) copy-start(f32[1,26]{1,0:T(1,128)} %get-tuple-element.31) | copy-start | bytes 316
  266.9 3.7 %copy-start.9 = (f32[1,12]{1,0:T(1,128)S(1)}, f32[1,12]{1,0:T(1,128)}, u32[]{:S(2)}) copy-start(f32[1,12]{1,0:T(1,128)} %get-tuple-element.32) | copy-start | bytes 148
  266.9 4.2 %copy-start.8 = (f32[1,24]{1,0:T(1,128)S(1)}, f32[1,24]{1,0:T(1,128)}, u32[]{:S(2)}) copy-start(f32[1,24]{1,0:T(1,128)} %get-tuple-element.33) | copy-start | bytes 292
  267.0 4.7 %copy-start.7 = (f32[1,48]{1,0:T(1,128)S(1)}, f32[1,48]{1,0:T(1,128)}, u32[]{:S(2)}) copy-start(f32[1,48]{1,0:T(1,128)} %get-tuple-element.34) | copy-start | bytes 580
  267.0 5.2 %copy-start.6 = (f32[1,48]{1,0:T(1,128)S(1)}, f32[1,48]{1,0:T(1,128)}, u32[]{:S(2)}) copy-start(f32[1,48]{1,0:T(1,128)} %get-tuple-element.35) | copy-start | bytes 580
  267.0 5.7 %copy-start.5 = (f32[1,48]{1,0:T(1,128)S(1)}, f32[1,48]{1,0:T(1,128)}, u32[]{:S(2)}) copy-start(f32[1,48]{1,0:T(1,128)} %get-tuple-element.36) | copy-start | bytes 580

commit v7 on v6

--- a/solution.py
+++ b/solution.py
@@ -910,11 +910,11 @@
         return carry
 
     loop(0, TILES // 2, inside, 3)
+    ring.turn()
     ahead.turn()
-    ring.turn()
     loop(TILES // 2, TILES // 2, inside, 3)
+    ring.finish()
     ahead.finish()
-    ring.finish()
     ring.end()
 
     prefetch(from_gates)
@@ -1057,9 +1057,7 @@
         fold(qin, wide(x) * dx, j)
         return carry
 
-    loop(0, TILES // 2, inside_back, 3)
-    next(reduce)
-    loop(TILES // 2, TILES // 2, inside_back, 3)
+    loop(0, TILES, inside_back, 3)
     stream(from_gates, 8, norm_gates)
     next(reduce)
     aback.finish()
@@ -1086,8 +1084,9 @@
         prods[pl.ds(2 * j + 1, 1), :] = jnp.sum(pair[64:], axis=0, keepdims=True)
         d_mix(j, u, ys[j] + d_w + skip[:, cols(j)] * dyf)
 
-    loop(0, TILES, carry_back, 3)
+    loop(0, 15, carry_back, 3)
     next(reduce)
+    loop(15, 9, carry_back, 3)
     ds = low(dscores[...])
     d_mix(TILES, 0, db_in[...] + dot_tn(ds, c_out))
     d_mix(TILES + 1, 1, dc_in[...] + dot(ds, b_in))
@@ -1131,15 +1130,15 @@
             total = total + taps[k:k + 1, cols(j)] * shift2[u, 3 - k:259 - k, :]
         dproj[:, cols(j)] = low(total)
 
+    loop(0, TILES // 2, conv_back, 2)
+    shared += [to_sibling(10, dproj.at[:, :1536], sib_dz.at[:, :1536])]
+    loop(TILES // 2, TILES // 2 + 2, conv_back, 2)
+    shared += [to_sibling(11, dproj.at[:, 1536:], sib_dz.at[:, 1536:])]
+    next(reduce)
     links.settle()
     for axis in ("z", "y", "x"):
         for steps_ in (1, 2, 3):
             pl.semaphore_signal(ready, inc=1, device_id={axis: moved(at, axis, steps_)[axis]}, device_id_type=MESH)
-    loop(0, TILES // 2, conv_back, 2)
-    shared += [to_sibling(10, dproj.at[:, :1536], sib_dz.at[:, :1536])]
-    loop(TILES // 2, TILES // 2 + 2, conv_back, 2)
-    shared += [to_sibling(11, dproj.at[:, 1536:], sib_dz.at[:, 1536:])]
-    work.finish(g_in, 0, DI, g_o)
     for copy in shared[-2:]:
         copy.wait_recv()
 
@@ -1155,6 +1154,7 @@
         loop(0, 9, d_w_late, 3)
     for k in range(2):
         src[k, :, :, :, :, 3456:3584] = jnp.zeros((4, 2, 3, 16, 128), bf16)
+    work.finish(g_in, 0, DI, g_o)
     pl.semaphore_wait(ready, 9)
     after = Links(l_send, l_recv)
     width = WIDE - DI

time: 274 us -> 263 us (0.960)
  Pallas kernels: 257 us -> 246 us
    pallas_call x1, Pallas kernels: 205 us -> 194 us  [mixer(): pl.pallas_call(mixer_kernel, out_shape=[jax.ShapeDtypeStruct((256, 1536),...]
where the time goes in v7:
time: 263 us; the launch traced here: 262 us
  Pallas kernels  246 us (94%)
  local copies, waits for them, and re-layouts  11 us (4%)
  other arithmetic  4.25 us (2%)
    pallas_call x1, Pallas kernels, mixer(): pl.pallas_call(mixer_kernel, out_shape=[jax.ShapeDtypeStruct((256, 1536),...  194 us
    pallas_call x1, Pallas kernels, gather(): pl.pallas_call(gather_kernel, out_shape=[jax.ShapeDtypeStruct((2, 2, 4, 2...  52.2 us
    unnamed x33, local copies, waits for them, and re-layouts  8.44 us

profile of v7, /device:TPU:1, one launch (start us, length us, event | category | flops | bytes accessed | tf_op | source)
XLA Modules:
  0.0 262.4 jit_solution(6526315943077428506)
XLA Ops:
  0.6 1.4 fusion
  2.0 52.2 %gather_weights.1 = (bf16[2,2,4,2,3,16,3584]{6,5,4,3,2,1,0:T(8,128)(2,1)}, bf16[2,2,4,2,3,16,6144]{6,5,4,3,2,1,0:T(8,128)(2,1)}) custom-call(bf16[12,6448]{1,0:T(8,128)(2,1)} %refs_0_.1, bf16[24,1536]{1,0:T(8,128)(2,1)} %refs_1_.1, bf16[4,26]{1,0:T(4,128)(2,1)} %refs_2_.1, bf16[1,26]{1,0:T(2,128)(2,1)} %bitcast.28, bf16[1,12]{1,0:T(2,128)(2,1)} %bitcast.29, ...), custom_call_target="tpu_custom_call" | custom-call | tf_op jit(solution)/shard_map/gather_weights/pallas_call | solution.py:220
  54.2 1.1 slice_convert_fusion
  55.3 0.1 reshape.38
  55.4 0.0 copy-start
  55.4 0.2 slice_reduce_fusion
  55.6 0.7 broadcast_in_dim_reshape_squeeze.11.gain
  56.3 0.2 slice_reduce_fusion.1
  56.5 0.1 broadcast_in_dim_reshape_squeeze.10
  56.6 0.2 fusion.3
  56.9 0.2 reshape.37
  57.1 0.7 broadcast_in_dim_reshape_squeeze.12.norm_gain
  57.8 0.1 mul.24
  57.9 0.7 select_maximum_fusion.taps
  58.6 0.0 copy-done
  58.6 1.1 fusion.2.normed
  59.7 194.1 %mixer.1 = (bf16[256,1536]{1,0:T(8,128)(2,1)}, f32[256,1536]{1,0:T(8,128)}, f32[12,6448]{1,0:T(8,128)}, f32[24,1536]{1,0:T(8,128)}, f32[4,26]{1,0:T(4,128)}, /*i...) custom-call(bf16[256,1536]{1,0:T(8,128)(2,1)} %fusion.2.normed, ...), custom_call_target="tpu_custom_call", output_to_operand_aliasing={{11}: (10, {})} | custom-call | tf_op jit(solution)/shard_map/mixer/pallas_call | solution.py:1246
  253.9 0.0 copy-start.1
  253.9 2.2 copy.40
  256.0 0.0 copy-done.1
  256.1 0.0 copy-start.2
  256.1 0.0 copy-start.3
  256.1 0.0 copy-start.4
  256.1 0.0 copy-start.10
  256.1 0.0 copy-start.9
  256.1 0.0 copy-start.8
  256.1 0.0 copy-start.7
  256.1 0.0 copy-start.6
  256.1 0.0 copy-start.5
  256.1 1.1 copy.41
  257.3 0.0 copy-done.2
  257.3 0.8 copy.42
  258.0 0.0 copy-done.3
  258.0 0.7 copy.43
  258.7 0.0 copy-done.4
  258.7 0.6 copy.44
  259.3 0.0 copy-done.10
  259.3 0.5 copy.45
  259.8 0.0 copy-done.9
  259.8 0.5 copy.46
  260.3 0.0 copy-done.8
  260.3 0.5 copy.47
  260.8 0.0 copy-done.7
  260.8 0.5 copy.48
  261.3 0.0 copy-done.6
  261.3 0.5 copy.49
  261.8 0.0 copy-done.5
  261.8 0.5 copy.50
  (3 shorter events, 0.1 us)
Async XLA Ops:
  55.4 3.3 %copy-start = (bf16[1,256,1536]{2,1,0:T(8,128)(2,1)S(1)}, bf16[1,256,1536]{2,1,0:T(8,128)(2,1)}, u32[]{:S(2)}) copy-start(bf16[1,256,1536]{2,1,0:T(8,128)(2,1)} %param.11) | copy-start | bytes 2359300
  253.9 2.2 copy-start.1
  256.1 1.2 copy-start.2
  256.1 2.0 copy-start.3
  256.1 2.6 %copy-start.4 = (f32[4,26]{1,0:T(4,128)S(1)}, f32[4,26]{1,0:T(4,128)}, u32[]{:S(2)}) copy-start(f32[4,26]{1,0:T(4,128)} %get-tuple-element.54) | copy-start | bytes 1252
  256.1 3.2 %copy-start.10 = (f32[1,26]{1,0:T(1,128)S(1)}, f32[1,26]{1,0:T(1,128)}, u32[]{:S(2)}) copy-start(f32[1,26]{1,0:T(1,128)} %get-tuple-element.31) | copy-start | bytes 316
  256.1 3.7 %copy-start.9 = (f32[1,12]{1,0:T(1,128)S(1)}, f32[1,12]{1,0:T(1,128)}, u32[]{:S(2)}) copy-start(f32[1,12]{1,0:T(1,128)} %get-tuple-element.32) | copy-start | bytes 148
  256.1 4.2 %copy-start.8 = (f32[1,24]{1,0:T(1,128)S(1)}, f32[1,24]{1,0:T(1,128)}, u32[]{:S(2)}) copy-start(f32[1,24]{1,0:T(1,128)} %get-tuple-element.33) | copy-start | bytes 292
  256.1 4.7 %copy-start.7 = (f32[1,48]{1,0:T(1,128)S(1)}, f32[1,48]{1,0:T(1,128)}, u32[]{:S(2)}) copy-start(f32[1,48]{1,0:T(1,128)} %get-tuple-element.34) | copy-start | bytes 580
  256.1 5.2 %copy-start.6 = (f32[1,48]{1,0:T(1,128)S(1)}, f32[1,48]{1,0:T(1,128)}, u32[]{:S(2)}) copy-start(f32[1,48]{1,0:T(1,128)} %get-tuple-element.35) | copy-start | bytes 580
  256.1 5.7 %copy-start.5 = (f32[1,48]{1,0:T(1,128)S(1)}, f32[1,48]{1,0:T(1,128)}, u32[]{:S(2)}) copy-start(f32[1,48]{1,0:T(1,128)} %get-tuple-element.36) | copy-start | bytes 580

commit v8 on v7

--- a/solution.py
+++ b/solution.py
@@ -1002,6 +1002,7 @@
             src[zh, :, :, :, :, lanes(1536 * (n // 2) + 384 * lax.rem(n, 2), 384)] = low(total).reshape(4, 2, 3, 16, 384)
 
         loop(0, 8, d_w_gates, 2)
+    aback.turn()
     for q in range(4):
         flip(branch[:, lanes(1536 * core + 384 * q, 384)], sib_branch[:, 384 * q:384 * q + 384])
 
@@ -1017,7 +1018,6 @@
     hidden_load = pltpu.make_async_copy(hidden_in, hidden, out_sem.at[2])
     hidden_load.start()
     prefetch(from_gates)
-    aback.turn()
     work = Scatter(at, links, src, 2 * DI, True, rest, last_early)
     reduce = work.steps()
     next(reduce)

time: 263 us -> 261 us (level)
  no operation moved by 1% of the time
where the time goes in v8:
time: 261 us
  Pallas kernels  245 us (94%)
  local copies, waits for them, and re-layouts  11 us (4%)
  other arithmetic  4.25 us (2%)
    pallas_call x1, Pallas kernels, mixer(): pl.pallas_call(mixer_kernel, out_shape=[jax.ShapeDtypeStruct((256, 1536),...  192 us
    pallas_call x1, Pallas kernels, gather(): pl.pallas_call(gather_kernel, out_shape=[jax.ShapeDtypeStruct((2, 2, 4, 2...  52.2 us
    unnamed x33, local copies, waits for them, and re-layouts  8.44 us

profile of v8, /device:TPU:1, one launch (start us, length us, event | category | flops | bytes accessed | tf_op | source)
XLA Modules:
  0.0 260.6 jit_solution(3892903533132020026)
XLA Ops:
  0.6 1.4 fusion
  2.0 52.2 %gather_weights.1 = (bf16[2,2,4,2,3,16,3584]{6,5,4,3,2,1,0:T(8,128)(2,1)}, bf16[2,2,4,2,3,16,6144]{6,5,4,3,2,1,0:T(8,128)(2,1)}) custom-call(bf16[12,6448]{1,0:T(8,128)(2,1)} %refs_0_.1, bf16[24,1536]{1,0:T(8,128)(2,1)} %refs_1_.1, bf16[4,26]{1,0:T(4,128)(2,1)} %refs_2_.1, bf16[1,26]{1,0:T(2,128)(2,1)} %bitcast.28, bf16[1,12]{1,0:T(2,128)(2,1)} %bitcast.29, ...), custom_call_target="tpu_custom_call" | custom-call | tf_op jit(solution)/shard_map/gather_weights/pallas_call | solution.py:220
  54.2 1.1 slice_convert_fusion
  55.3 0.1 reshape.38
  55.4 0.0 copy-start
  55.4 0.2 slice_reduce_fusion
  55.6 0.7 broadcast_in_dim_reshape_squeeze.11.gain
  56.3 0.2 slice_reduce_fusion.1
  56.5 0.1 broadcast_in_dim_reshape_squeeze.10
  56.6 0.2 fusion.3
  56.9 0.2 reshape.37
  57.1 0.7 broadcast_in_dim_reshape_squeeze.12.norm_gain
  57.8 0.1 mul.24
  57.9 0.7 select_maximum_fusion.taps
  58.6 0.0 copy-done
  58.6 1.1 fusion.2.normed
  59.7 192.4 %mixer.1 = (bf16[256,1536]{1,0:T(8,128)(2,1)}, f32[256,1536]{1,0:T(8,128)}, f32[12,6448]{1,0:T(8,128)}, f32[24,1536]{1,0:T(8,128)}, f32[4,26]{1,0:T(4,128)}, /*i...) custom-call(bf16[256,1536]{1,0:T(8,128)(2,1)} %fusion.2.normed, ...), custom_call_target="tpu_custom_call", output_to_operand_aliasing={{11}: (10, {})} | custom-call | tf_op jit(solution)/shard_map/mixer/pallas_call | solution.py:1246
  252.1 0.0 copy-start.1
  252.1 2.2 copy.40
  254.3 0.0 copy-done.1
  254.3 0.0 copy-start.2
  254.3 0.0 copy-start.3
  254.3 0.0 copy-start.4
  254.3 0.0 copy-start.10
  254.3 0.0 copy-start.9
  254.3 0.0 copy-start.8
  254.3 0.0 copy-start.7
  254.3 0.0 copy-start.6
  254.4 0.0 copy-start.5
  254.4 1.1 copy.41
  255.5 0.0 copy-done.2
  255.5 0.8 copy.42
  256.3 0.0 copy-done.3
  256.3 0.7 copy.43
  256.9 0.0 copy-done.4
  256.9 0.6 copy.44
  257.5 0.0 copy-done.10
  257.5 0.5 copy.45
  258.0 0.0 copy-done.9
  258.0 0.5 copy.46
  258.5 0.0 copy-done.8
  258.5 0.5 copy.47
  259.1 0.0 copy-done.7
  259.1 0.5 copy.48
  259.6 0.0 copy-done.6
  259.6 0.5 copy.49
  260.1 0.0 copy-done.5
  260.1 0.5 copy.50
  (3 shorter events, 0.1 us)
Async XLA Ops:
  55.4 3.3 %copy-start = (bf16[1,256,1536]{2,1,0:T(8,128)(2,1)S(1)}, bf16[1,256,1536]{2,1,0:T(8,128)(2,1)}, u32[]{:S(2)}) copy-start(bf16[1,256,1536]{2,1,0:T(8,128)(2,1)} %param.11) | copy-start | bytes 2359300
  252.1 2.2 copy-start.1
  254.3 1.2 copy-start.2
  254.3 2.0 copy-start.3
  254.3 2.6 %copy-start.4 = (f32[4,26]{1,0:T(4,128)S(1)}, f32[4,26]{1,0:T(4,128)}, u32[]{:S(2)}) copy-start(f32[4,26]{1,0:T(4,128)} %get-tuple-element.54) | copy-start | bytes 1252
  254.3 3.2 %copy-start.10 = (f32[1,26]{1,0:T(1,128)S(1)}, f32[1,26]{1,0:T(1,128)}, u32[]{:S(2)}) copy-start(f32[1,26]{1,0:T(1,128)} %get-tuple-element.31) | copy-start | bytes 316
  254.3 3.7 %copy-start.9 = (f32[1,12]{1,0:T(1,128)S(1)}, f32[1,12]{1,0:T(1,128)}, u32[]{:S(2)}) copy-start(f32[1,12]{1,0:T(1,128)} %get-tuple-element.32) | copy-start | bytes 148
  254.3 4.2 %copy-start.8 = (f32[1,24]{1,0:T(1,128)S(1)}, f32[1,24]{1,0:T(1,128)}, u32[]{:S(2)}) copy-start(f32[1,24]{1,0:T(1,128)} %get-tuple-element.33) | copy-start | bytes 292
  254.3 4.7 %copy-start.7 = (f32[1,48]{1,0:T(1,128)S(1)}, f32[1,48]{1,0:T(1,128)}, u32[]{:S(2)}) copy-start(f32[1,48]{1,0:T(1,128)} %get-tuple-element.34) | copy-start | bytes 580
  254.3 5.2 %copy-start.6 = (f32[1,48]{1,0:T(1,128)S(1)}, f32[1,48]{1,0:T(1,128)}, u32[]{:S(2)}) copy-start(f32[1,48]{1,0:T(1,128)} %get-tuple-element.35) | copy-start | bytes 580
  254.4 5.7 %copy-start.5 = (f32[1,48]{1,0:T(1,128)S(1)}, f32[1,48]{1,0:T(1,128)}, u32[]{:S(2)}) copy-start(f32[1,48]{1,0:T(1,128)} %get-tuple-element.36) | copy-start | bytes 580

commit v9 on v8

--- a/solution.py
+++ b/solution.py
@@ -612,7 +612,6 @@
         @pl.when(jnp.logical_not(jnp.logical_and(home, at["x"] == tx)))
         def _():
             pl.semaphore_signal(barrier, inc=1, device_id=(to_z, at["y"], jnp.int32(tx), to_c), device_id_type=MESH)
-    pl.semaphore_wait(barrier, 23 + inner.astype(jnp.int32) - home.astype(jnp.int32))
 
     def exchange(e, source, target, own):
         def go(k):
@@ -645,66 +644,16 @@
     def lanes(start, size):
         return pl.ds(pl.multiple_of(start, 128), size)
 
-    links = Links(rs_send, rs_recv)
-    ring = Ring(links, at, weights_, 2, True)
-    ring.start()
-
     def from_late(k, slot):
         pltpu.make_async_copy(
             w_late.at[:, :, :, :, :, :, lanes(384 * k, 384)],
             chunk.at[slot].reshape(2, 2, 4, 2, 3, 16, 384), chunk_sem.at[slot]).start()
 
-    def from_gates(k, slot):
-        pltpu.make_async_copy(
-            weights_.at[:, :, :, :, :, :, lanes(1536 * (k // 2) + 384 * lax.rem(k, 2), 384)],
-            chunk.at[slot].reshape(2, 2, 4, 2, 3, 16, 384), chunk_sem.at[slot]).start()
-
-    def from_out(k, slot):
-        for b in range(2):
-            pltpu.make_async_copy(
-                weights_.at[k // 4, :, :, :, :, :, lanes(1536 * lax.rem(k, 4) + 768 + 384 * b, 384)],
-                chunk.at[slot].reshape(2, 4, 2, 3, 32, 384).at[:, :, :, :, pl.ds(16 * b, 16)], chunk_sem.at[slot]).start()
-
     def prefetch(fetch):
         for slot in range(BUFFERS):
             fetch(jnp.int32(slot), slot)
 
-    def stream(fetch, count, use):
-        def round_(n, u):
-            for slot in range(BUFFERS):
-                k = BUFFERS * n + slot
-
-                @pl.when(k < count)
-                def _():
-                    pltpu.make_async_copy(chunk.at[slot], chunk.at[slot], chunk_sem.at[slot]).wait()
-                    use(k, chunk[slot])
-
-                @pl.when(k + BUFFERS < count)
-                def _():
-                    fetch(k + BUFFERS, slot)
-
-        loop(0, -(-count // BUFFERS), round_, 1)
-
     prefetch(from_late)
-
-    def project(k, w):
-        value = dot(normed[...], w)
-
-        @pl.when(k < 8)
-        def _():
-            conv_in[:, lanes(384 * jnp.minimum(k, 7), 384)] = low(value)
-
-        @pl.when(k == 8)
-        def _():
-            conv_in[:, 3072:CONVC] = low(value[:, :256])
-            dt_in[...] = value[:, 256:]
-
-    stream(from_late, 9, project)
-    halo_out[...] = conv_in[240:256, :]
-    front = neighbour(0, halo_out, halo_in, 1, me < 31)
-    shared = [to_sibling(5, normed.at[:, lanes(768 * (1 - core), 768)], sib_normed), to_sibling(6, given_out, sib_given)]
-
-
     heads[...] = jnp.zeros((8, 128), f32)
     for k, ref in enumerate((dt_bias, rates, d_skip)):
         heads[k:k + 1, :H] = ref[...]
@@ -712,6 +661,56 @@
     for j in range(TILES):
         skip[:, 128 * j:128 * j + 128] = jnp.where(
             lane[0:1] < 64, jnp.broadcast_to(by_head_[:, 2 * j:2 * j + 1], (1, 128)), jnp.broadcast_to(by_head_[:, 2 * j + 1:2 * j + 2], (1, 128)))
+
+    pl.semaphore_wait(barrier, 23 + inner.astype(jnp.int32) - home.astype(jnp.int32))
+    links = Links(rs_send, rs_recv)
+    ring = Ring(links, at, weights_, 2, True)
+    ring.start()
+
+    def from_gates(k, slot):
+        pltpu.make_async_copy(
+            weights_.at[:, :, :, :, :, :, lanes(1536 * (k // 2) + 384 * lax.rem(k, 2), 384)],
+            chunk.at[slot].reshape(2, 2, 4, 2, 3, 16, 384), chunk_sem.at[slot]).start()
+
+    def from_out(k, slot):
+        for b in range(2):
+            pltpu.make_async_copy(
+                weights_.at[k // 4, :, :, :, :, :, lanes(1536 * lax.rem(k, 4) + 768 + 384 * b, 384)],
+                chunk.at[slot].reshape(2, 4, 2, 3, 32, 384).at[:, :, :, :, pl.ds(16 * b, 16)], chunk_sem.at[slot]).start()
+
+    def stream(fetch, count, use):
+        def round_(n, u):
+            for slot in range(BUFFERS):
+                k = BUFFERS * n + slot
+
+                @pl.when(k < count)
+                def _():
+                    pltpu.make_async_copy(chunk.at[slot], chunk.at[slot], chunk_sem.at[slot]).wait()
+                    use(k, chunk[slot])
+
+                @pl.when(k + BUFFERS < count)
+                def _():
+                    fetch(k + BUFFERS, slot)
+
+        loop(0, -(-count // BUFFERS), round_, 1)
+
+    def project(k, w):
+        value = dot(normed[...], w)
+
+        @pl.when(k < 8)
+        def _():
+            conv_in[:, lanes(384 * jnp.minimum(k, 7), 384)] = low(value)
+
+        @pl.when(k == 8)
+        def _():
+            conv_in[:, 3072:CONVC] = low(value[:, :256])
+            dt_in[...] = value[:, 256:]
+
+    stream(from_late, 9, project)
+    halo_out[...] = conv_in[240:256, :]
+    front = neighbour(0, halo_out, halo_in, 1, me < 31)
+    shared = [to_sibling(5, normed.at[:, lanes(768 * (1 - core), 768)], sib_normed), to_sibling(6, given_out, sib_given)]
+
 
     raw = dt_in[...] + heads[0:1, :]
     dt = jnp.maximum(raw, 0.0) + jnp.log1p(jnp.exp(-jnp.abs(raw)))
@@ -950,7 +949,7 @@
         coef[...] += gated * (gain[:, cols(j)] * db[:, cols(j)])
         return carry
 
-    loop(0, TILES, gate_sums, 4)
+    loop(0, TILES, gate_sums, 6)
     scale = lax.rsqrt(jnp.sum(stat[...], axis=1, keepdims=True) * (1.0 / DI) + epsilon)
     factor = scale * scale * scale * (jnp.sum(coef[...], axis=1, keepdims=True) * (1.0 / DI))
     stat[...] = jnp.broadcast_to(scale, (256, 128))

time: 261 us -> 261 us (level)
  no operation moved by 1% of the time
where the time goes in v9:
time: 261 us; the launch traced here: 260 us
  Pallas kernels  244 us (93%)
  local copies, waits for them, and re-layouts  11 us (4%)
  other arithmetic  4.25 us (2%)
    pallas_call x1, Pallas kernels, mixer(): pl.pallas_call(mixer_kernel, out_shape=[jax.ShapeDtypeStruct((256, 1536),...  192 us
    pallas_call x1, Pallas kernels, gather(): pl.pallas_call(gather_kernel, out_shape=[jax.ShapeDtypeStruct((2, 2, 4, 2...  52.2 us
    unnamed x33, local copies, waits for them, and re-layouts  8.44 us

profile of v9, /device:TPU:1, one launch (start us, length us, event | category | flops | bytes accessed | tf_op | source)
XLA Modules:
  0.0 260.2 jit_solution(633420292746503329)
XLA Ops:
  0.6 1.4 fusion
  2.0 52.2 %gather_weights.1 = (bf16[2,2,4,2,3,16,3584]{6,5,4,3,2,1,0:T(8,128)(2,1)}, bf16[2,2,4,2,3,16,6144]{6,5,4,3,2,1,0:T(8,128)(2,1)}) custom-call(bf16[12,6448]{1,0:T(8,128)(2,1)} %refs_0_.1, bf16[24,1536]{1,0:T(8,128)(2,1)} %refs_1_.1, bf16[4,26]{1,0:T(4,128)(2,1)} %refs_2_.1, bf16[1,26]{1,0:T(2,128)(2,1)} %bitcast.28, bf16[1,12]{1,0:T(2,128)(2,1)} %bitcast.29, ...), custom_call_target="tpu_custom_call" | custom-call | tf_op jit(solution)/shard_map/gather_weights/pallas_call | solution.py:220
  54.2 1.1 slice_convert_fusion
  55.3 0.1 reshape.38
  55.4 0.0 copy-start
  55.4 0.2 slice_reduce_fusion
  55.6 0.7 broadcast_in_dim_reshape_squeeze.11.gain
  56.3 0.2 slice_reduce_fusion.1
  56.5 0.1 broadcast_in_dim_reshape_squeeze.10
  56.6 0.2 fusion.3
  56.9 0.2 reshape.37
  57.1 0.7 broadcast_in_dim_reshape_squeeze.12.norm_gain
  57.8 0.1 mul.24
  57.9 0.7 select_maximum_fusion.taps
  58.6 0.0 copy-done
  58.6 1.1 fusion.2.normed
  59.7 191.9 %mixer.1 = (bf16[256,1536]{1,0:T(8,128)(2,1)}, f32[256,1536]{1,0:T(8,128)}, f32[12,6448]{1,0:T(8,128)}, f32[24,1536]{1,0:T(8,128)}, f32[4,26]{1,0:T(4,128)}, /*i...) custom-call(bf16[256,1536]{1,0:T(8,128)(2,1)} %fusion.2.normed, ...), custom_call_target="tpu_custom_call", output_to_operand_aliasing={{11}: (10, {})} | custom-call | tf_op jit(solution)/shard_map/mixer/pallas_call | solution.py:1245
  251.7 0.0 copy-start.1
  251.7 2.2 copy.40
  253.9 0.0 copy-done.1
  253.9 0.0 copy-start.2
  253.9 0.0 copy-start.3
  253.9 0.0 copy-start.4
  253.9 0.0 copy-start.10
  253.9 0.0 copy-start.9
  253.9 0.0 copy-start.8
  253.9 0.0 copy-start.7
  253.9 0.0 copy-start.6
  253.9 0.0 copy-start.5
  254.0 1.1 copy.41
  255.1 0.0 copy-done.2
  255.1 0.8 copy.42
  255.9 0.0 copy-done.3
  255.9 0.7 copy.43
  256.5 0.0 copy-done.4
  256.5 0.6 copy.44
  257.1 0.0 copy-done.10
  257.1 0.5 copy.45
  257.6 0.0 copy-done.9
  257.6 0.5 copy.46
  258.1 0.0 copy-done.8
  258.1 0.5 copy.47
  258.6 0.0 copy-done.7
  258.7 0.5 copy.48
  259.2 0.0 copy-done.6
  259.2 0.5 copy.49
  259.7 0.0 copy-done.5
  259.7 0.5 copy.50
  (3 shorter events, 0.1 us)
Async XLA Ops:
  55.4 3.3 %copy-start = (bf16[1,256,1536]{2,1,0:T(8,128)(2,1)S(1)}, bf16[1,256,1536]{2,1,0:T(8,128)(2,1)}, u32[]{:S(2)}) copy-start(bf16[1,256,1536]{2,1,0:T(8,128)(2,1)} %param.11) | copy-start | bytes 2359300
  251.7 2.2 copy-start.1
  253.9 1.2 copy-start.2
  253.9 2.0 copy-start.3
  253.9 2.6 %copy-start.4 = (f32[4,26]{1,0:T(4,128)S(1)}, f32[4,26]{1,0:T(4,128)}, u32[]{:S(2)}) copy-start(f32[4,26]{1,0:T(4,128)} %get-tuple-element.54) | copy-start | bytes 1252
  253.9 3.2 %copy-start.10 = (f32[1,26]{1,0:T(1,128)S(1)}, f32[1,26]{1,0:T(1,128)}, u32[]{:S(2)}) copy-start(f32[1,26]{1,0:T(1,128)} %get-tuple-element.31) | copy-start | bytes 316
  253.9 3.7 %copy-start.9 = (f32[1,12]{1,0:T(1,128)S(1)}, f32[1,12]{1,0:T(1,128)}, u32[]{:S(2)}) copy-start(f32[1,12]{1,0:T(1,128)} %get-tuple-element.32) | copy-start | bytes 148
  253.9 4.2 %copy-start.8 = (f32[1,24]{1,0:T(1,128)S(1)}, f32[1,24]{1,0:T(1,128)}, u32[]{:S(2)}) copy-start(f32[1,24]{1,0:T(1,128)} %get-tuple-element.33) | copy-start | bytes 292
  253.9 4.7 %copy-start.7 = (f32[1,48]{1,0:T(1,128)S(1)}, f32[1,48]{1,0:T(1,128)}, u32[]{:S(2)}) copy-start(f32[1,48]{1,0:T(1,128)} %get-tuple-element.34) | copy-start | bytes 580
  253.9 5.2 %copy-start.6 = (f32[1,48]{1,0:T(1,128)S(1)}, f32[1,48]{1,0:T(1,128)}, u32[]{:S(2)}) copy-start(f32[1,48]{1,0:T(1,128)} %get-tuple-element.35) | copy-start | bytes 580
  253.9 5.7 %copy-start.5 = (f32[1,48]{1,0:T(1,128)S(1)}, f32[1,48]{1,0:T(1,128)}, u32[]{:S(2)}) copy-start(f32[1,48]{1,0:T(1,128)} %get-tuple-element.36) | copy-start | bytes 580
